TPU v7x, 32 devices: a whole 2x2x4 slice. The times are simulated.
32 devices in a mesh: node: 16 (over z, y, x), head: 2 (over core).
Axes of the slice: x: 2, y: 2, z: 4, core: 2. Of those that a mesh axis runs over, the one named last changes fastest.
Arguments:
- node_queries: bfloat16 [4096, 1024], P('node', 'head'), may hold values from -56 to 56, as said below
- node_keys: bfloat16 [4096, 1024], P('node', 'head'), may hold values from -56 to 56, as said below
- node_values: bfloat16 [4096, 1024], P('node', 'head'), may hold values from -6 to 6
- tile_index: int32 [4, 32, 2], P(None, 'node'), may hold values from 0 to 1
- tile_count: int32 [4, 32], P(None, 'node'), may hold values from 0 to 2, as said below
- out_weight: bfloat16 [1024, 1024], replicated, may hold values from -0.1875 to 0.1875
Outputs:
- updated: bfloat16 [1024, 4096], P('head', 'node')
Inputs may be any that keep to these rules, and one draw needn't show every extreme that they name: `node_queries`: queries, each row usually of order one; some rows may carry a large entry at a head's first column. `node_keys`: keys, likewise. `tile_index`: tile numbers may repeat within a row. `tile_count`: 2 is reached in every draw.
All inputs are finite; a program needn't handle non-finite values.
Results may differ from a plain program's by a relative error of at most 0.015.
Values may be sent and summed in bfloat16 or wider, within the bound.
No kernel may reach another device: no remote copies, remote signals or barrier semaphores. Data moves between devices by JAX's collectives and lax.ppermute only.
A program may use at most 64 MiB of HBM per device.

v0:
```python
import jax
import jax.numpy as jnp
from jax import lax
from jax.sharding import PartitionSpec as P

HD = 128
TILE = 128
SLOTS = 2
STEPS = 4


def shifted(value, axis, steps):
    count = lax.axis_size(axis)
    pairs = [(source, (source + steps) % count) for source in range(count)]
    return lax.ppermute(value, axis, pairs)


def attend(carried, queries, key_block, value_block, index_rows, count_rows):
    running_max, running_sum, weighted = carried
    tile_total = queries.shape[0]
    head_total = queries.shape[2]
    score_scale = HD ** (-0.5)
    key_tiles = key_block.reshape(tile_total, TILE, head_total, HD)[index_rows].astype(jnp.float32)
    value_tiles = value_block.reshape(tile_total, TILE, head_total, HD)[index_rows].astype(
        jnp.float32
    )
    scores = jnp.einsum("trhd,tjkhd->thrjk", queries.astype(jnp.float32), key_tiles) * score_scale
    usable = (jnp.arange(SLOTS, dtype=jnp.int32)[None, :] < count_rows[:, None])[
        :, None, None, :, None
    ]
    scores = jnp.where(usable, scores, -jnp.inf)
    new_max = jnp.maximum(running_max, jnp.max(scores, axis=(3, 4)))
    factor = jnp.exp(running_max - new_max)
    weights = jnp.exp(scores - new_max[..., None, None])
    running_sum = running_sum * factor + jnp.sum(weights, axis=(3, 4))
    rounded = weights.astype(jnp.bfloat16).astype(jnp.float32)
    weighted = weighted * factor[..., None] + jnp.einsum("thrjk,tjkhd->thrd", rounded, value_tiles)
    return (new_max, running_sum, weighted)


def on_device(node_queries, node_keys, node_values, tile_index, tile_count, out_weight):
    dest_rows, feature_width = node_queries.shape
    head_total = feature_width // HD
    tile_total = dest_rows // TILE
    score_scale = HD ** (-0.5)
    queries = node_queries.reshape(tile_total, TILE, head_total, HD)
    own_keys = node_keys.reshape(tile_total, TILE, head_total, HD)
    own_values = node_values.reshape(tile_total, TILE, head_total, HD)
    self_score = jnp.sum(queries.astype(jnp.float32) * own_keys.astype(jnp.float32), axis=-1)
    self_score = jnp.transpose(self_score, (0, 2, 1)) * score_scale
    start_values = jnp.transpose(own_values, (0, 2, 1, 3)).astype(jnp.float32)
    carried = (self_score, jnp.ones_like(self_score), start_values)
    visiting = (node_keys, node_values)
    for turn_index in range(STEPS):
        if turn_index > 0:
            visiting = shifted((visiting[0], visiting[1]), "node", 1)
        carried = attend(
            carried,
            queries,
            visiting[0],
            visiting[1],
            tile_index[turn_index],
            tile_count[turn_index],
        )
    mixed = carried[2] / carried[1][..., None]
    mixed = (
        jnp.transpose(mixed, (0, 2, 1, 3)).reshape(dest_rows, feature_width).astype(jnp.bfloat16)
    )
    head_position = lax.axis_index("head")
    own_rows = lax.dynamic_slice_in_dim(out_weight, head_position * feature_width, feature_width, 0)
    return lax.psum_scatter(
        jnp.transpose(jnp.dot(mixed, own_rows, preferred_element_type=jnp.float32)).astype(
            jnp.bfloat16
        ),
        "head",
        scatter_dimension=0,
        tiled=True,
    )


def solution(mesh):
    return jax.shard_map(
        on_device,
        mesh=mesh,
        in_specs=(
            P("node", "head"),
            P("node", "head"),
            P("node", "head"),
            P(None, "node", None),
            P(None, "node"),
            P(),
        ),
        out_specs=P("head", "node"),
        check_vma=False,
    )
```

profile of v0, /device:TPU:0, one launch (start us, length us, event | category | flops | bytes accessed | tf_op | source)
XLA Modules:
  0.0 101.5 jit_solution(9032445704743700886)
XLA Ops:
  6.5 2.9 %collective-permute-start = (bf16[256,512]{1,0:T(8,128)(2,1)}, bf16[256,512]{1,0:T(8,128)(2,1)}, u32[]{:S(2)}, u32[]{:S(2)}) collective-permute-start(bf16[256,512]{1,0:T(8,128)(2,1)} %param.7), channel_id=1, source_target_pairs={{0,2},{2,4},{4,6},{6,8},{8,10},{10,12},{12,14},{14,16},{16,18},{18... | collective-permute-start | bytes 786440 | tf_op jit(solution)/shard_map/ppermute | solution.py:15
  9.5 1.5 %collective-permute-start.1 = (bf16[256,512]{1,0:T(8,128)(2,1)}, bf16[256,512]{1,0:T(8,128)(2,1)}, u32[]{:S(2)}, u32[]{:S(2)}) collective-permute-start(bf16[256,512]{1,0:T(8,128)(2,1)} %param.8), channel_id=1, source_target_pairs={{0,2},{2,4},{4,6},{6,8},{8,10},{10,12},{12,14},{14,16},{16,18},{18... | collective-permute-start | bytes 786440 | tf_op jit(solution)/shard_map/ppermute | solution.py:15
  11.0 1.0 reshape.246
  12.0 1.0 %reshape.244 = bf16[2,128,4,128]{3,2,1,0:T(4,128)(2,1)S(1)} reshape(bf16[256,512]{1,0:T(8,128)(2,1)} %param.8) | data formatting | bytes 524288 | tf_op jit(solution)/shard_map/reshape | solution.py:48
  13.0 1.1 %slice_reduce_fusion.1 = (s32[2,2]{1,0:T(2,128)S(1)}, s32[2,2]{1,0:T(2,128)S(1)}, s32[2,2]{1,0:T(2,128)S(1)}, s32[2,2]{1,0:T(2,128)S(1)}) fusion(s32[4,2,2]{0,2,1:T(2,128)} %param.9), kind=kLoop, calls=%fused_computation.91 | loop fusion | bytes 128 | tf_op jit(solution)/shard_map/slice | solution.py:62
  14.2 1.0 %slice_reduce_fusion.5 = (s32[2]{0:T(128)S(1)}, s32[2]{0:T(128)S(1)}, s32[2]{0:T(128)S(1)}, s32[2]{0:T(128)S(1)}) fusion(s32[4,2]{0,1:T(2,128)} %param.10), kind=kLoop, calls=%fused_computation.96 | loop fusion | bytes 64 | tf_op jit(solution)/shard_map/slice | solution.py:63
  15.3 1.0 %reshape.245 = bf16[2,128,4,128]{3,2,1,0:T(4,128)(2,1)S(1)} reshape(bf16[256,512]{1,0:T(8,128)(2,1)} %param.6) | data formatting | bytes 524288 | tf_op jit(solution)/shard_map/reshape | solution.py:46
  16.6 0.4 multiply_reduce_fusion
  17.1 1.4 %gather_fusion = bf16[4,128,4,128]{3,1,2,0:T(8,128)(2,1)} fusion(bf16[2,128,4,128]{3,1,2,0:T(8,128)(2,1)S(1)} %copy.155, s32[1024]{0:T(1024)S(1)} %pad_clamp_fusion.3), kind=kCustom, calls=%fused_computation | custom fusion | bytes 1048592 | tf_op jit(solution)/shard_map/gather | solution.py:23
  18.5 1.7 %gather_fusion.1 = bf16[4,128,4,128]{3,2,1,0:T(4,128)(2,1)} fusion(bf16[2,128,4,128]{3,2,1,0:T(4,128)(2,1)S(1)} %reshape.244, s32[1024]{0:T(1024)S(1)} %pad_clamp_fusion.3), kind=kCustom, calls=%fused_computation.1 | custom fusion | bytes 1048592 | tf_op jit(solution)/shard_map/gather | solution.py:24
  20.4 2.3 %fusion.58 = (f32[2,4,128]{2,1,0:T(4,128)S(1)}, f32[2,4,128,2,128]{2,4,3,1,0:T(8,128)}) fusion(bf16[2,128,4,128,1]{3,2,1,0,4:T(4,128)(2,1)S(1)} %bitcast.141, bf16[2,2,128,4,128]{4,2,3,1,0:T(8,128)(2,1)} %bitcast.146, pred[2,2]{1,0:T(4,128)(4,1)S(1)} %get-tuple-element.37), kind=kOutput, calls=%fused_computation.107 | convolution fusion | flops 67894272 | bytes 1839108 | tf_op jit(solution)/shard_map/trhd,tjkhd->thrjk/dot_general | solution.py:27
  22.8 1.0 reshape.247
  23.8 1.9 %collective-permute-done.1 = bf16[256,512]{1,0:T(8,128)(2,1)} collective-permute-done((bf16[256,512]{1,0:T(8,128)(2,1)}, bf16[256,512]{1,0:T(8,128)(2,1)}, u32[]{:S(2)}, u32[]{:S(2)}) %collective-permute-start.1) | collective-permute-done | bytes 262176 | tf_op jit(solution)/shard_map/ppermute | solution.py:15
  25.7 1.0 reshape.248
  26.8 1.4 %gather_fusion.2 = bf16[4,128,4,128]{3,1,2,0:T(8,128)(2,1)} fusion(bf16[2,128,4,128]{3,1,2,0:T(8,128)(2,1)S(1)} %copy.160, s32[1024]{0:T(1024)S(1)} %pad_clamp_fusion.2), kind=kCustom, calls=%fused_computation.2 | custom fusion | bytes 1048592 | tf_op jit(solution)/shard_map/gather | solution.py:23
  28.2 1.4 %gather_fusion.3 = bf16[4,128,4,128]{3,1,2,0:T(8,128)(2,1)} fusion(bf16[2,128,4,128]{3,1,2,0:T(8,128)(2,1)S(1)} %copy.163, s32[1024]{0:T(1024)S(1)} %pad_clamp_fusion.2), kind=kCustom, calls=%fused_computation.3 | custom fusion | bytes 1048592 | tf_op jit(solution)/shard_map/gather | solution.py:24
  29.6 1.1 %collective-permute-start.3 = (bf16[256,512]{1,0:T(8,128)(2,1)}, bf16[256,512]{1,0:T(8,128)(2,1)}, u32[]{:S(2)}, u32[]{:S(2)}) collective-permute-start(bf16[256,512]{1,0:T(8,128)(2,1)} %collective-permute-done.1), channel_id=1, source_target_pairs={{0,2},{2,4},{4,6},{6,8},{8,10},{10,12},{12,14},{14,16},{16,18},{18... | collective-permute-start | bytes 786440 | tf_op jit(solution)/shard_map/ppermute | solution.py:15
  30.7 1.4 %fusion.57 = (f32[2,4,128]{2,1,0:T(4,128)S(1)}, f32[2,4,128,2,128]{2,4,3,1,0:T(8,128)S(1)}) fusion(bf16[2,128,4,128,1]{3,2,1,0,4:T(4,128)(2,1)} %bitcast.142, bf16[2,2,128,4,128]{4,2,3,1,0:T(8,128)(2,1)} %bitcast.147, pred[2,2]{1,0:T(4,128)(4,1)S(1)} %get-tuple-element.36), kind=kOutput, calls=%fused_computation.106 | convolution fusion | flops 67894272 | bytes 1839108 | tf_op jit(solution)/shard_map/trhd,tjkhd->thrjk/dot_general | solution.py:27
  32.2 10.6 %collective-permute-done.2 = bf16[256,512]{1,0:T(8,128)(2,1)} collective-permute-done((bf16[256,512]{1,0:T(8,128)(2,1)}, bf16[256,512]{1,0:T(8,128)(2,1)}, u32[]{:S(2)}, u32[]{:S(2)}) %collective-permute-start.2) | collective-permute-done | bytes 262176 | tf_op jit(solution)/shard_map/ppermute | solution.py:15
  42.8 1.7 %reshape.249 = bf16[2,128,4,128]{3,2,1,0:T(4,128)(2,1)} reshape(bf16[256,512]{1,0:T(8,128)(2,1)} %collective-permute-done.2) | data formatting | bytes 524288 | tf_op jit(solution)/shard_map/reshape | solution.py:23
  44.5 1.7 %copy.166 = bf16[2,128,4,128]{3,1,2,0:T(8,128)(2,1)} copy(bf16[2,128,4,128]{3,2,1,0:T(4,128)(2,1)} %reshape.249) | data formatting | bytes 524288 | tf_op jit(solution)/shard_map/reshape | solution.py:23
  46.2 0.5 collective-permute-done.3
  46.6 1.7 %reshape.250 = bf16[2,128,4,128]{3,2,1,0:T(4,128)(2,1)} reshape(bf16[256,512]{1,0:T(8,128)(2,1)} %collective-permute-done.3) | data formatting | bytes 524288 | tf_op jit(solution)/shard_map/reshape | solution.py:24
  48.4 1.7 %copy.169 = bf16[2,128,4,128]{3,1,2,0:T(8,128)(2,1)} copy(bf16[2,128,4,128]{3,2,1,0:T(4,128)(2,1)} %reshape.250) | data formatting | bytes 524288 | tf_op jit(solution)/shard_map/reshape | solution.py:24
  50.1 2.4 %gather_fusion.4 = bf16[4,128,4,128]{3,1,2,0:T(8,128)(2,1)} fusion(bf16[2,128,4,128]{3,1,2,0:T(8,128)(2,1)} %copy.166, s32[1024]{0:T(1024)S(1)} %pad_clamp_fusion.1), kind=kCustom, calls=%fused_computation.4 | custom fusion | bytes 1048592 | tf_op jit(solution)/shard_map/gather | solution.py:23
  52.4 2.4 %gather_fusion.5 = bf16[4,128,4,128]{3,1,2,0:T(8,128)(2,1)} fusion(bf16[2,128,4,128]{3,1,2,0:T(8,128)(2,1)} %copy.169, s32[1024]{0:T(1024)S(1)} %pad_clamp_fusion.1), kind=kCustom, calls=%fused_computation.5 | custom fusion | bytes 1048592 | tf_op jit(solution)/shard_map/gather | solution.py:24
  54.8 2.5 %fusion.56 = (f32[2,4,128]{2,1,0:T(4,128)S(1)}, f32[2,4,128,2,128]{2,4,3,1,0:T(8,128)}) fusion(bf16[2,128,4,128,1]{3,2,1,0,4:T(4,128)(2,1)} %bitcast.143, bf16[2,2,128,4,128]{4,2,3,1,0:T(8,128)(2,1)} %bitcast.148, pred[2,2]{1,0:T(4,128)(4,1)S(1)} %get-tuple-element.35), kind=kOutput, calls=%fused_computation.105 | convolution fusion | flops 67894272 | bytes 1839108 | tf_op jit(solution)/shard_map/trhd,tjkhd->thrjk/dot_general | solution.py:27
  57.2 10.7 %collective-permute-done.4 = bf16[256,512]{1,0:T(8,128)(2,1)} collective-permute-done((bf16[256,512]{1,0:T(8,128)(2,1)}, bf16[256,512]{1,0:T(8,128)(2,1)}, u32[]{:S(2)}, u32[]{:S(2)}) %collective-permute-start.4) | collective-permute-done | bytes 262176 | tf_op jit(solution)/shard_map/ppermute | solution.py:15
  67.9 1.7 %reshape.251 = bf16[2,128,4,128]{3,2,1,0:T(4,128)(2,1)} reshape(bf16[256,512]{1,0:T(8,128)(2,1)} %collective-permute-done.4) | data formatting | bytes 524288 | tf_op jit(solution)/shard_map/reshape | solution.py:23
  69.6 1.7 %copy.172 = bf16[2,128,4,128]{3,1,2,0:T(8,128)(2,1)} copy(bf16[2,128,4,128]{3,2,1,0:T(4,128)(2,1)} %reshape.251) | data formatting | bytes 524288 | tf_op jit(solution)/shard_map/reshape | solution.py:23
  71.4 2.4 %gather_fusion.6 = bf16[4,128,4,128]{3,1,2,0:T(8,128)(2,1)} fusion(bf16[2,128,4,128]{3,1,2,0:T(8,128)(2,1)} %copy.172, s32[1024]{0:T(1024)S(1)} %pad_clamp_fusion), kind=kCustom, calls=%fused_computation.6 | custom fusion | bytes 1048592 | tf_op jit(solution)/shard_map/gather | solution.py:23
  73.7 2.5 %fusion.55 = (f32[2,4,128]{2,1,0:T(4,128)S(1)}, f32[2,4,128,2,128]{2,4,3,1,0:T(8,128)}) fusion(bf16[2,128,4,128,1]{3,2,1,0,4:T(4,128)(2,1)} %bitcast.144, bf16[2,2,128,4,128]{4,2,3,1,0:T(8,128)(2,1)} %bitcast.149, pred[2,2]{1,0:T(4,128)(4,1)S(1)} %get-tuple-element.34), kind=kOutput, calls=%fused_computation.104 | convolution fusion | flops 67894272 | bytes 1839108 | tf_op jit(solution)/shard_map/trhd,tjkhd->thrjk/dot_general | solution.py:27
  76.3 0.2 fusion.22
  76.5 1.2 %convolution_bitcast_fusion.1 = f32[2,128,4,128]{3,1,2,0:T(8,128)} fusion(f32[2,4,128,2,128]{2,4,3,1,0:T(8,128)S(1)} %copy-done.1, bf16[2,2,128,4,128]{4,2,3,1,0:T(8,128)(2,1)S(1)} %bitcast.139, f32[2,4,128]{2,1,0:T(4,128)S(1)} %get-tuple-element.19), kind=kOutput, calls=%fused_computation.22 | convolution fusion | flops 67633152 | bytes 2101248 | tf_op jit(solution)/shard_map/thrjk,tjkhd->thrd/dot_general | solution.py:37
  77.6 1.7 %reshape.252 = bf16[2,128,4,128]{3,2,1,0:T(4,128)(2,1)} reshape(bf16[256,512]{1,0:T(8,128)(2,1)} %collective-permute-done.5) | data formatting | bytes 524288 | tf_op jit(solution)/shard_map/reshape | solution.py:24
  79.4 1.7 %copy.175 = bf16[2,128,4,128]{3,1,2,0:T(8,128)(2,1)} copy(bf16[2,128,4,128]{3,2,1,0:T(4,128)(2,1)} %reshape.252) | data formatting | bytes 524288 | tf_op jit(solution)/shard_map/reshape | solution.py:24
  81.0 2.4 %gather_fusion.7 = bf16[4,128,4,128]{3,1,2,0:T(8,128)(2,1)} fusion(bf16[2,128,4,128]{3,1,2,0:T(8,128)(2,1)} %copy.175, s32[1024]{0:T(1024)S(1)} %pad_clamp_fusion), kind=kCustom, calls=%fused_computation.7 | custom fusion | bytes 1048592 | tf_op jit(solution)/shard_map/gather | solution.py:24
  83.4 1.4 %fusion.24 = f32[2,4,128]{2,1,0:T(4,128)S(1)} fusion(f32[2,4,128,2,128]{2,4,3,1,0:T(8,128)} %get-tuple-element.23, f32[2,4,128]{2,1,0:T(4,128)S(1)} %get-tuple-element.18), kind=kLoop, calls=%fused_computation.45 | loop fusion | flops 523264 | bytes 1056768 | tf_op jit(solution)/shard_map/reduce_sum | solution.py:35
  84.8 1.7 %convolution_bitcast_fusion = f32[2,128,4,128]{3,1,2,0:T(8,128)S(1)} fusion(f32[2,4,128,2,128]{2,4,3,1,0:T(8,128)} %get-tuple-element.23, bf16[2,2,128,4,128]{4,2,3,1,0:T(8,128)(2,1)} %bitcast.140, f32[2,4,128]{2,1,0:T(4,128)S(1)} %get-tuple-element.18), kind=kOutput, calls=%fused_computation.21 | convolution fusion | flops 67633152 | bytes 2101248 | tf_op jit(solution)/shard_map/thrjk,tjkhd->thrd/dot_general | solution.py:37
  86.6 0.2 fusion.20
  86.8 0.4 convolution_bitcast_fusion.2
  87.1 0.7 copy-done.4
  87.8 0.2 fusion.18
  88.0 0.1 copy-done.7
  88.1 1.1 %fusion.16 = bf16[2,128,4,128]{3,1,2,0:T(8,128)(2,1)S(1)} fusion(f32[2,128,4,128]{3,1,2,0:T(8,128)S(1)} %convolution_bitcast_fusion, f32[2,128,4,128]{3,1,2,0:T(8,128)S(1)} %copy-done.7, f32[2,128,4,128]{3,1,2,0:T(8,128)S(1)} %convolution_bitcast_fusion.2, f32[2,4,128,2,128]{2,4,3,1,0:T(8,128)S(1)} %copy-done.4, ...), kind=kOutput, calls=%fused_computation.33 | convolution fusion | flops 69074944 | bytes 3694592 | tf_op jit(solution)/shard_map/thrjk,tjkhd->thrd/dot_general | solution.py:37
  89.2 0.2 copy.178
  89.4 1.3 %convolution_convert_fusion = bf16[1024,256]{1,0:T(8,128)(2,1)} fusion(bf16[1024,1024]{1,0:T(8,128)(2,1)S(1)} %copy-done, s32[]{:T(128)S(6)} %select_n.72, bf16[32,8,4,128]{3,2,1,0:T(4,128)(2,1)S(1)} %bitcast.150), kind=kOutput, calls=%fused_computation.20 | convolution fusion | flops 268697600 | bytes 1835012 | tf_op jit(solution)/shard_map/dot_general | solution.py:72
  90.7 4.0 %reduce-scatter.2.cloned.1.call-done = bf16[512,256]{1,0:T(8,128)(2,1)} async-done(((bf16[1024,256]{1,0:T(8,128)(2,1)}), bf16[512,256]{1,0:T(8,128)(2,1)}) %reduce-scatter.2.cloned.1.call-update) | async-done | bytes 262160 | tf_op jit(solution)/shard_map/reduce_scatter | solution.py:71
  (39 shorter events, 0.8 us)
Async XLA Ops:
  6.5 82.9 %copy-start = (bf16[1024,1024]{1,0:T(8,128)(2,1)S(1)}, bf16[1024,1024]{1,0:T(8,128)(2,1)}, u32[]{:S(2)}) copy-start(bf16[1024,1024]{1,0:T(8,128)(2,1)} %param.11) | copy-start | bytes 6291460
  6.5 88.2 %reduce-scatter.2.cloned.1.call-start = ((), (), s32[]{:S(2)}) async-start(), calls=%async_computation.1 | async-start | bytes 786432 | tf_op jit(solution)/shard_map/reduce_scatter | solution.py:71
  6.5 16.2 %collective-permute-start = (bf16[256,512]{1,0:T(8,128)(2,1)}, bf16[256,512]{1,0:T(8,128)(2,1)}, u32[]{:S(2)}, u32[]{:S(2)}) collective-permute-start(bf16[256,512]{1,0:T(8,128)(2,1)} %param.7), channel_id=1, source_target_pairs={{0,2},{2,4},{4,6},{6,8},{8,10},{10,12},{12,14},{14,16},{16,18},{18... | collective-permute-start | bytes 786440 | tf_op jit(solution)/shard_map/ppermute | solution.py:15
  9.5 16.2 %collective-permute-start.1 = (bf16[256,512]{1,0:T(8,128)(2,1)}, bf16[256,512]{1,0:T(8,128)(2,1)}, u32[]{:S(2)}, u32[]{:S(2)}) collective-permute-start(bf16[256,512]{1,0:T(8,128)(2,1)} %param.8), channel_id=1, source_target_pairs={{0,2},{2,4},{4,6},{6,8},{8,10},{10,12},{12,14},{14,16},{16,18},{18... | collective-permute-start | bytes 786440 | tf_op jit(solution)/shard_map/ppermute | solution.py:15
  16.3 6.5 %copy-start.5 = (bf16[2,128,4,128]{3,2,1,0:T(4,128)(2,1)}, bf16[2,128,4,128]{3,2,1,0:T(4,128)(2,1)S(1)}, u32[]{:S(2)}) copy-start(bf16[2,128,4,128]{3,2,1,0:T(4,128)(2,1)S(1)} %reshape.245) | copy-start | bytes 786436
  29.6 13.2 %collective-permute-start.2 = (bf16[256,512]{1,0:T(8,128)(2,1)}, bf16[256,512]{1,0:T(8,128)(2,1)}, u32[]{:S(2)}, u32[]{:S(2)}) collective-permute-start(bf16[256,512]{1,0:T(8,128)(2,1)} %collective-permute-done), channel_id=1, source_target_pairs={{0,2},{2,4},{4,6},{6,8},{8,10},{10,12},{12,14},{14,16},{16,18},{18... | collective-permute-start | bytes 786440 | tf_op jit(solution)/shard_map/ppermute | solution.py:15
  29.6 17.0 %collective-permute-start.3 = (bf16[256,512]{1,0:T(8,128)(2,1)}, bf16[256,512]{1,0:T(8,128)(2,1)}, u32[]{:S(2)}, u32[]{:S(2)}) collective-permute-start(bf16[256,512]{1,0:T(8,128)(2,1)} %collective-permute-done.1), channel_id=1, source_target_pairs={{0,2},{2,4},{4,6},{6,8},{8,10},{10,12},{12,14},{14,16},{16,18},{18... | collective-permute-start | bytes 786440 | tf_op jit(solution)/shard_map/ppermute | solution.py:15
  54.8 13.2 %collective-permute-start.4 = (bf16[256,512]{1,0:T(8,128)(2,1)}, bf16[256,512]{1,0:T(8,128)(2,1)}, u32[]{:S(2)}, u32[]{:S(2)}) collective-permute-start(bf16[256,512]{1,0:T(8,128)(2,1)} %collective-permute-done.2), channel_id=1, source_target_pairs={{0,2},{2,4},{4,6},{6,8},{8,10},{10,12},{12,14},{14,16},{16,18},{18... | collective-permute-start | bytes 786440 | tf_op jit(solution)/shard_map/ppermute | solution.py:15
  54.8 22.9 %collective-permute-start.5 = (bf16[256,512]{1,0:T(8,128)(2,1)}, bf16[256,512]{1,0:T(8,128)(2,1)}, u32[]{:S(2)}, u32[]{:S(2)}) collective-permute-start(bf16[256,512]{1,0:T(8,128)(2,1)} %collective-permute-done.3), channel_id=1, source_target_pairs={{0,2},{2,4},{4,6},{6,8},{8,10},{10,12},{12,14},{14,16},{16,18},{18... | collective-permute-start | bytes 786440 | tf_op jit(solution)/shard_map/ppermute | solution.py:15
  73.7 2.5 %copy-start.1 = (f32[2,4,128,2,128]{2,4,3,1,0:T(8,128)S(1)}, f32[2,4,128,2,128]{2,4,3,1,0:T(8,128)}, u32[]{:S(2)}) copy-start(f32[2,4,128,2,128]{2,4,3,1,0:T(8,128)} %get-tuple-element.25) | copy-start | bytes 3145732
  73.7 2.7 %copy-start.3 = (bf16[4,128,4,128]{3,1,2,0:T(8,128)(2,1)S(1)}, bf16[4,128,4,128]{3,1,2,0:T(8,128)(2,1)}, u32[]{:S(2)}) copy-start(bf16[4,128,4,128]{3,1,2,0:T(8,128)(2,1)} %gather_fusion.5) | copy-start | bytes 1572868
  83.4 3.4 %copy-start.2 = (bf16[4,128,4,128]{3,1,2,0:T(8,128)(2,1)S(1)}, bf16[4,128,4,128]{3,1,2,0:T(8,128)(2,1)}, u32[]{:S(2)}) copy-start(bf16[4,128,4,128]{3,1,2,0:T(8,128)(2,1)} %gather_fusion.3) | copy-start | bytes 1572868
  86.6 1.2 %copy-start.4 = (f32[2,4,128,2,128]{2,4,3,1,0:T(8,128)S(1)}, f32[2,4,128,2,128]{2,4,3,1,0:T(8,128)}, u32[]{:S(2)}) copy-start(f32[2,4,128,2,128]{2,4,3,1,0:T(8,128)} %get-tuple-element.29) | copy-start | bytes 3145732
  86.6 1.4 %copy-start.6 = (bf16[4,128,4,128]{3,2,1,0:T(4,128)(2,1)S(1)}, bf16[4,128,4,128]{3,2,1,0:T(4,128)(2,1)}, u32[]{:S(2)}) copy-start(bf16[4,128,4,128]{3,2,1,0:T(4,128)(2,1)} %gather_fusion.1) | copy-start | bytes 1572868
  86.6 1.5 %copy-start.7 = (f32[2,128,4,128]{3,1,2,0:T(8,128)S(1)}, f32[2,128,4,128]{3,1,2,0:T(8,128)}, u32[]{:S(2)}) copy-start(f32[2,128,4,128]{3,1,2,0:T(8,128)} %convolution_bitcast_fusion.1) | copy-start | bytes 1572868
Sparse Core Ops, SparseCore 0:
  90.8 3.8 reduce-scatter.1
where the time goes:
time: 102 us
  local copies, waits for them, and re-layouts  37.9 us (37%)
  waiting for transfers between devices  27.7 us (27%)
  matrix products  14.4 us (14%)
  between operations  13.6 us (13%)
  starting transfers between devices  5.55 us (5%)
  other arithmetic  2.51 us (2%)
    ppermute x6, waiting for transfers between devices, shifted(): return lax.ppermute(value, axis, pairs)  23.6 us
    dot_general x4, matrix products, attend(): jnp.einsum('trhd,tjkhd->thrjk', queries.astype(jnp.float32), key_tiles)  8.74 us
    gather x4, local copies, waits for them, and re-layouts, attend(): value_block.reshape(tile_total, TILE, head_total, HD)[index_rows]  7.9 us
    reshape x6, local copies, waits for them, and re-layouts, attend(): key_block.reshape(tile_total, TILE, head_total, HD)[index_rows]  7.89 us
    reshape x6, local copies, waits for them, and re-layouts, attend(): value_block.reshape(tile_total, TILE, head_total, HD)[index_rows]  7.84 us
    gather x4, local copies, waits for them, and re-layouts, attend(): key_block.reshape(tile_total, TILE, head_total, HD)[index_rows]  7.61 us
    ppermute x6, starting transfers between devices, shifted(): return lax.ppermute(value, axis, pairs)  5.55 us
    dot_general x4, matrix products, attend(): jnp.einsum('thrjk,tjkhd->thrd', rounded, value_tiles)  4.34 us
  transfers between devices with their start and end apart: 7, of which 5 were waited for; matrix products, arithmetic and copies ran while one was open for 29% of the time, Pallas kernels for 0%

commit v1 on v0

v1 whole, which is shorter than its diff:
```python
import functools

import jax
import jax.numpy as jnp
from jax import lax
from jax.experimental import pallas as pl
from jax.experimental.pallas import tpu as pltpu
from jax.sharding import Mesh, PartitionSpec as P

HEADS = 8
HD = 128
TILE = 128
SLOTS = 2
STEPS = 4
LOG2E = 1.4426950408889634
SCALE = LOG2E * HD ** (-0.5)
MASKED = -1e30
EXTRA = 16
VMEM = pl.BlockSpec(memory_space=pltpu.VMEM)
SMEM = pl.BlockSpec(memory_space=pltpu.SMEM)
ANY = pl.BlockSpec(memory_space=pl.ANY)
PARAMS = pltpu.CompilerParams(vmem_limit_bytes=48 * 1024 * 1024)


def use_rows(index_ref, count_ref, tiles):
    row = lax.broadcasted_iota(jnp.int32, (EXTRA, HD), 0)
    uses = jnp.zeros((EXTRA, HD), jnp.float32)
    for turn in range(STEPS):
        for dest in range(tiles):
            for source in range(tiles):
                times = jnp.float32(0)
                for slot in range(SLOTS):
                    used = (slot < count_ref[turn, dest]) & (index_ref[turn, dest, slot] == source)
                    times += jnp.where(used, 1.0, 0.0)
                uses = jnp.where(row == (turn * tiles + dest) * tiles + source, times, uses)
    return uses


def pack_kernel(query_ref, key_ref, value_ref, index_ref, count_ref, kv_ref, q_ref):
    rows, width = query_ref.shape
    tiles = rows // TILE
    uses = use_rows(index_ref, count_ref, tiles).astype(jnp.bfloat16)
    for head in range(width // HD):
        cols = slice(head * HD, (head + 1) * HD)
        kv_ref[head, :rows] = key_ref[:, cols]
        for tile in range(tiles):
            part = value_ref[tile * TILE : (tile + 1) * TILE, cols]
            kv_ref[head, rows + tile * TILE : rows + (tile + 1) * TILE] = part.T
        q_ref[head, :rows] = query_ref[:, cols]
        q_ref[head, rows:] = uses


def source_scores(kv_ref, place, q_ref, dest, turn, rows):
    tiles = rows // TILE
    queries = q_ref[dest, :rows]
    keys = kv_ref[place, :rows]
    raw = (
        lax.dot_general(keys, queries, (((1,), (1,)), ((), ())), preferred_element_type=jnp.float32)
        * SCALE
    )
    parts = []
    for source in range(tiles):
        bias = []
        for tile in range(tiles):
            at = rows + (turn * tiles + tile) * tiles + source
            times = q_ref[dest, at : at + 1].astype(jnp.float32)
            bias.append(jnp.where(times > 0.5, times - 1.0, MASKED))
        parts.append(
            raw[source * TILE : (source + 1) * TILE] + jnp.concatenate(bias, axis=1)
        )
    return raw, jnp.concatenate(parts, axis=0)


def slab_values(kv_ref, place, rows):
    return jnp.concatenate(
        [kv_ref[place, rows + at : rows + at + TILE] for at in range(0, rows, TILE)], axis=1
    )


def add_sources(scores, values, top, total, mixed):
    for score, value in zip(scores, values):
        weights = jnp.exp2(score - top)
        total = total + jnp.sum(weights, axis=0, keepdims=True)
        mixed = mixed + jnp.dot(
            value, weights.astype(jnp.bfloat16), preferred_element_type=jnp.float32
        )
    return total, mixed


def near_kernel(head_total, kv_ref, q_ref, weight_ref, mixed_ref, state_ref, turned_ref, held, sem):
    group = kv_ref.shape[0]
    rows = kv_ref.shape[1] // 2
    me = lax.axis_index("head")
    depth = weight_ref.shape[0] // head_total
    features = weight_ref.shape[1] // head_total
    copies = []
    for other in range(head_total):
        start = pl.multiple_of(jnp.bitwise_xor(me, other) * depth, depth)
        cols = pl.ds(pl.multiple_of(me * features, features), features)
        copies.append(
            pltpu.make_async_copy(
                weight_ref.at[pl.ds(start, depth), cols], held.at[other], sem.at[other]
            )
        )
        copies[-1].start()
    eye = lax.broadcasted_iota(jnp.int32, (TILE, TILE), 0) == lax.broadcasted_iota(
        jnp.int32, (TILE, TILE), 1
    )
    for dest in range(group):
        scores, values = [], []
        for turn in range(STEPS):
            place = dest - turn
            if place < 0:
                continue
            raw, score = source_scores(kv_ref, place, q_ref, dest, turn, rows)
            if turn == 0:
                own = jnp.concatenate(
                    [
                        jnp.sum(
                            jnp.where(eye, raw[at : at + TILE, at : at + TILE], 0.0),
                            axis=0,
                            keepdims=True,
                        )
                        for at in range(0, rows, TILE)
                    ],
                    axis=1,
                )
            scores.append(score)
            values.append(slab_values(kv_ref, place, rows))
        top = own
        for score in scores:
            top = jnp.maximum(top, jnp.max(score, axis=0, keepdims=True))
        weight = jnp.exp2(own - top)
        total, mixed = add_sources(
            scores, values, top, weight, weight * values[0].astype(jnp.float32)
        )
        mixed_ref[dest] = mixed
        state_ref[dest, 0:1] = top
        state_ref[dest, 1:2] = total
    for other in range(head_total):
        copies[other].wait()
        turned_ref[other] = held[other].T


def far_kernel(offsets, q_ref, mixed_ref, state_ref, *refs):
    far_refs, out_ref = refs[:-1], refs[-1]
    group, _, rows = mixed_ref.shape
    for dest in range(group):
        scores, values = [], []
        for turn in range(STEPS):
            place = dest - turn
            if place >= 0:
                continue
            offset = -(place // group)
            slot = place % group - max(0, offset * group - STEPS + 1)
            far = far_refs[offsets.index(offset)]
            _, score = source_scores(far, slot, q_ref, dest, turn, rows)
            scores.append(score)
            values.append(slab_values(far, slot, rows))
        top = state_ref[dest, 0:1]
        total = state_ref[dest, 1:2]
        mixed = mixed_ref[dest]
        if scores:
            before = top
            for score in scores:
                top = jnp.maximum(top, jnp.max(score, axis=0, keepdims=True))
            factor = jnp.exp2(before - top)
            total, mixed = add_sources(scores, values, top, total * factor, mixed * factor)
        out_ref[dest] = (mixed / total).astype(out_ref.dtype)


def project_kernel(turned_ref, *refs):
    mix_refs, out_ref = refs[:-1], refs[-1]
    result = None
    for other, mix_ref in enumerate(mix_refs):
        part = jnp.dot(turned_ref[other], mix_ref[...], preferred_element_type=jnp.float32)
        result = part if result is None else result + part
    out_ref[...] = result.astype(out_ref.dtype)


def on_device(node_queries, node_keys, node_values, tile_index, tile_count, out_weight):
    rows, width = node_queries.shape
    group = width // HD
    groups = lax.axis_size("group")
    head_total = lax.axis_size("head")
    depth, feature_total = out_weight.shape
    features = feature_total // head_total
    bf16, f32 = jnp.bfloat16, jnp.float32
    shape = jax.ShapeDtypeStruct

    kv, q = pl.pallas_call(
        pack_kernel,
        out_shape=(
            shape((group, 2 * rows, HD), bf16),
            shape((group, rows + EXTRA, HD), bf16),
        ),
        in_specs=[VMEM, VMEM, VMEM, SMEM, SMEM],
        out_specs=(VMEM, VMEM),
        compiler_params=PARAMS,
        name="pack",
    )(node_queries, node_keys, node_values, tile_index, tile_count)

    kv = lax.all_to_all(kv, "place", 0, 0)
    offsets = list(range(1, -(-(STEPS - 1) // group) + 1))
    far = []
    for offset in offsets:
        first = max(0, offset * group - STEPS + 1)
        pairs = [(source, (source + offset) % groups) for source in range(groups)]
        far.append(lax.ppermute(kv[first:], "group", pairs))
    q = lax.all_to_all(q, "place", 0, 0)

    mixed, state, turned = pl.pallas_call(
        functools.partial(near_kernel, head_total),
        out_shape=(
            shape((group, HD, rows), f32),
            shape((group, 8, rows), f32),
            shape((head_total, features, depth // head_total), bf16),
        ),
        in_specs=[VMEM, VMEM, ANY],
        out_specs=(VMEM, VMEM, VMEM),
        scratch_shapes=[
            pltpu.VMEM((head_total, depth // head_total, features), bf16),
            pltpu.SemaphoreType.DMA((head_total,)),
        ],
        compiler_params=PARAMS,
        name="near",
    )(kv, q, out_weight)

    mix = pl.pallas_call(
        functools.partial(far_kernel, offsets),
        out_shape=shape((group, HD, rows), bf16),
        in_specs=[VMEM] * (3 + len(far)),
        out_specs=VMEM,
        compiler_params=PARAMS,
        name="far",
    )(q, mixed, state, *far)

    mix = lax.all_to_all(mix, "place", 0, 0).reshape(width, rows)
    mixes = [mix]
    for other in range(1, head_total):
        pairs = [(source, source ^ other) for source in range(head_total)]
        mixes.append(lax.ppermute(mix, "head", pairs))
    return pl.pallas_call(
        project_kernel,
        out_shape=shape((features, rows), bf16),
        in_specs=[VMEM] * (1 + head_total),
        out_specs=VMEM,
        compiler_params=PARAMS,
        name="project",
    )(turned, *mixes)


def solution(mesh):
    nodes, heads = mesh.devices.shape
    place = HEADS // heads
    split = Mesh(
        mesh.devices.reshape(nodes // place, place, heads), ("group", "place", "head")
    )
    node = ("group", "place")
    return jax.shard_map(
        on_device,
        mesh=split,
        in_specs=(
            P(node, "head"),
            P(node, "head"),
            P(node, "head"),
            P(None, node, None),
            P(None, node),
            P(),
        ),
        out_specs=P("head", node),
        check_vma=False,
    )
```

time: 102 us -> 43.3 us (0.42)
  local copies, waits for them, and re-layouts: 37.9 us -> 4.56 us
  blocking collectives: 0 us -> 30.1 us
  waiting for transfers between devices: 27.7 us -> 1.54 us
  matrix products: 14.4 us -> 0 us
  between operations: 13.6 us -> 0.04 us
  Pallas kernels: 0 us -> 5.15 us
  starting transfers between devices: 5.55 us -> 1.63 us
  other arithmetic: 2.51 us -> 0 us
    all_to_all x0 -> x3, blocking collectives: none -> 30.1 us  [the longest x1 13.5 us: on_device(): kv = lax.all_to_all(kv, 'place', 0, 0)]
    ppermute x6 -> x2, waiting for transfers between devices: 23.6 us -> 1.54 us  [the longest x1 1.53 us: on_device(): mixes.append(lax.ppermute(mix, 'head', pairs))]
    reshape x16 -> x0, local copies, waits for them, and re-layouts: 18.8 us -> none  [the longest x6 7.89 us: attend(): key_block.reshape(tile_total, TILE, head_total, HD)[index_rows]]
    gather x8 -> x0, local copies, waits for them, and re-layouts: 15.5 us -> none  [the longest x4 7.9 us: attend(): value_block.reshape(tile_total, TILE, head_total, HD)[index_rows]]
    dot_general x9 -> x0, matrix products: 14.4 us -> none  [the longest x4 8.74 us: attend(): jnp.einsum('trhd,tjkhd->thrjk', queries.astype(jnp.float32), key_tiles)]
    pallas_call x0 -> x4, Pallas kernels: none -> 5.15 us  [the longest x1 2.22 us: on_device(): pl.pallas_call(functools.partial(near_kernel, head_total), out_shape=(sha...]
    reduce_scatter x1 -> x0, waiting for transfers between devices: 3.99 us -> none  [on_device(): lax.psum_scatter(jnp.transpose(jnp.dot(mixed, own_rows, preferred_element...]
    ppermute x6 -> x2, starting transfers between devices: 5.55 us -> 1.63 us  [the longest x1 1.63 us: on_device(): far.append(lax.ppermute(kv[first:], 'group', pairs))]
  transfers between devices with their start and end apart: 7 -> 2, of which waited for: 5 -> 1; matrix products, arithmetic and copies ran while one was open for 29% -> 0% of each run, Pallas kernels for 0% -> 5%
where the time goes in v1:
time: 43.3 us; the launch traced here: 43 us
  blocking collectives  30.1 us (70%)
  Pallas kernels  5.15 us (12%)
  local copies, waits for them, and re-layouts  4.56 us (11%)
  starting transfers between devices  1.63 us (4%)
  waiting for transfers between devices  1.54 us (4%)
    all_to_all x1, blocking collectives, on_device(): kv = lax.all_to_all(kv, 'place', 0, 0)  13.5 us
    all_to_all x1, blocking collectives, on_device(): q = lax.all_to_all(q, 'place', 0, 0)  8.46 us
    all_to_all x1, blocking collectives, on_device(): mix = lax.all_to_all(mix, 'place', 0, 0).reshape(width, rows)  8.11 us
    unnamed x10, local copies, waits for them, and re-layouts  4.54 us
    pallas_call x1, Pallas kernels, on_device(): pl.pallas_call(functools.partial(near_kernel, head_total), out_shape=(sha...  2.22 us
    ppermute x1, starting transfers between devices, on_device(): far.append(lax.ppermute(kv[first:], 'group', pairs))  1.63 us
    ppermute x1, waiting for transfers between devices, on_device(): mixes.append(lax.ppermute(mix, 'head', pairs))  1.53 us
    pallas_call x1, Pallas kernels, on_device(): pl.pallas_call(project_kernel, out_shape=shape((features, rows), bf16), i...  1.14 us
  transfers between devices with their start and end apart: 2, of which 1 were waited for; matrix products, arithmetic and copies ran while one was open for 0% of the time, Pallas kernels for 5%

profile of v1, /device:TPU:0, one launch (start us, length us, event | category | flops | bytes accessed | tf_op | source)
XLA Modules:
  0.0 43.0 jit_solution(595479792532362725)
XLA Ops:
  0.0 0.0 copy-start
  0.0 0.9 %copy.7.index_ref = s32[4,2,2]{2,1,0:T(2,128)S(1)} copy(s32[4,2,2]{0,2,1:T(2,128)} %param.9) | data formatting | bytes 128 | tf_op args[3]
  0.9 0.8 %copy.8.count_ref = s32[4,2]{1,0:T(4,128)S(1)} copy(s32[4,2]{0,1:T(2,128)} %param.10) | data formatting | bytes 64 | tf_op args[4]
  1.7 0.0 copy-start.1
  1.7 0.9 %copy-done.1 = bf16[256,512]{1,0:T(8,128)(2,1)S(1)} copy-done((bf16[256,512]{1,0:T(8,128)(2,1)S(1)}, bf16[256,512]{1,0:T(8,128)(2,1)}, u32[]{:S(2)}) %copy-start.1) | copy-done | bytes 262168
  2.6 0.0 copy-start.2
  2.6 0.9 %copy-done.2 = bf16[256,512]{1,0:T(8,128)(2,1)S(1)} copy-done((bf16[256,512]{1,0:T(8,128)(2,1)S(1)}, bf16[256,512]{1,0:T(8,128)(2,1)}, u32[]{:S(2)}) %copy-start.2) | copy-done | bytes 262168
  3.6 0.0 copy-start.3
  3.6 0.9 %copy-done.3 = bf16[256,512]{1,0:T(8,128)(2,1)S(1)} copy-done((bf16[256,512]{1,0:T(8,128)(2,1)S(1)}, bf16[256,512]{1,0:T(8,128)(2,1)}, u32[]{:S(2)}) %copy-start.3) | copy-done | bytes 262168
  4.5 0.8 %pack.1 = (bf16[4,512,128]{2,1,0:T(8,128)(2,1)S(1)}, bf16[4,272,128]{2,1,0:T(8,128)(2,1)S(1)}) custom-call(bf16[256,512]{1,0:T(8,128)(2,1)S(1)} %copy-done.1, bf16[256,512]{1,0:T(8,128)(2,1)S(1)} %copy-done.2, bf16[256,512]{1,0:T(8,128)(2,1)S(1)} %copy-done.3, s32[4,2,2]{2,1,0:T(2,128)S(1)} %copy.7.index_ref, s32[4,2]{1,0:T(4,128)S(1)} %copy.8.count_ref), custom_call_target="tpu_custom_call" | custom-call | tf_op jit(solution)/shard_map/pack/pallas_call | solution.py:191
  5.3 13.5 %all_to_all.15.kv_ref = bf16[4,512,128]{2,1,0:T(8,128)(2,1)S(1)} all-to-all(bf16[4,512,128]{2,1,0:T(8,128)(2,1)S(1)} %get-tuple-element.10), channel_id=1, replica_groups=mesh['group'=4,'place'=4,'head'=2] {'place'}, dimensions={0} | all-to-all | bytes 1048576 | tf_op jit(solution)/shard_map/all_to_all | solution.py:203
  18.8 1.6 %collective-permute-start = (bf16[3,512,128]{2,1,0:T(8,128)(2,1)S(1)}, bf16[3,512,128]{2,1,0:T(8,128)(2,1)S(1)}, u32[]{:S(2)}, u32[]{:S(2)}) collective-permute-start(bf16[3,512,128]{2,1,0:T(8,128)(2,1)S(1)} %slice.4), channel_id=1, source_target_pairs={{0,8},{8,16},{16,24},{24,0},{1,9},{9,17},{17,25},{25,1},{2,10},{10... | collective-permute-start | bytes 1179656 | tf_op jit(solution)/shard_map/ppermute | solution.py:209
  20.5 8.5 %all_to_all.16.q_ref = bf16[4,272,128]{2,1,0:T(8,128)(2,1)S(1)} all-to-all(bf16[4,272,128]{2,1,0:T(8,128)(2,1)S(1)} %get-tuple-element.11), channel_id=1, replica_groups=mesh['group'=4,'place'=4,'head'=2] {'place'}, dimensions={0} | all-to-all | bytes 557056 | tf_op jit(solution)/shard_map/all_to_all | solution.py:210
  28.9 0.0 copy-done
  28.9 2.2 %near.1 = (f32[4,128,256]{2,1,0:T(8,128)S(1)}, f32[4,8,256]{2,1,0:T(8,128)S(1)}, bf16[2,512,512]{2,1,0:T(8,128)(2,1)S(1)}) custom-call(bf16[4,512,128]{2,1,0:T(8,128)(2,1)S(1)} %all_to_all.15.kv_ref, bf16[4,272,128]{2,1,0:T(8,128)(2,1)S(1)} %all_to_all.16.q_ref, bf16[1024,1024]{1,0:T(8,128)(2,1)S(1)} %copy-done), custom_call_target="tpu_custom_call" | custom-call | tf_op jit(solution)/shard_map/near/pallas_call | solution.py:212
  31.2 0.0 collective-permute-done.refs_0_
  31.2 1.0 %far.1 = bf16[4,128,256]{2,1,0:T(8,128)(2,1)S(1)} custom-call(bf16[4,272,128]{2,1,0:T(8,128)(2,1)S(1)} %all_to_all.16.q_ref, f32[4,128,256]{2,1,0:T(8,128)S(1)} %get-tuple-element.13.mixed_ref, f32[4,8,256]{2,1,0:T(8,128)S(1)} %get-tuple-element.14.state_ref, bf16[3,512,128]{2,1,0:T(8,128)(2,1)S(1)} %collective-permute-done.refs_0_), custom_call_target="tpu_custom_call" | custom-call | tf_op jit(solution)/shard_map/far/pallas_call | solution.py:229
  32.2 8.1 %all_to_all.17 = bf16[4,128,256]{2,1,0:T(8,128)(2,1)S(1)} all-to-all(bf16[4,128,256]{2,1,0:T(8,128)(2,1)S(1)} %far.1), channel_id=1, replica_groups=mesh['group'=4,'place'=4,'head'=2] {'place'}, dimensions={0} | all-to-all | bytes 524288 | tf_op jit(solution)/shard_map/all_to_all | solution.py:238
  40.3 0.0 collective-permute-start.1
  40.3 1.5 %collective-permute-done.1.refs_1_ = bf16[512,256]{1,0:T(8,128)(2,1)S(1)} collective-permute-done((bf16[512,256]{1,0:T(8,128)(2,1)S(1)}, bf16[512,256]{1,0:T(8,128)(2,1)S(1)}, u32[]{:S(2)}, u32[]{:S(2)}) %collective-permute-start.1) | collective-permute-done | bytes 262176 | tf_op jit(solution)/shard_map/ppermute | solution.py:242
  41.8 1.1 %project.1 = bf16[512,256]{1,0:T(8,128)(2,1)} custom-call(bf16[2,512,512]{2,1,0:T(8,128)(2,1)S(1)} %get-tuple-element.12.turned_ref, bf16[512,256]{1,0:T(8,128)(2,1)S(1)} %bitcast.2, bf16[512,256]{1,0:T(8,128)(2,1)S(1)} %collective-permute-done.1.refs_1_), custom_call_target="tpu_custom_call" | custom-call | tf_op jit(solution)/shard_map/project/pallas_call | solution.py:243
  (1 shorter events, 0.0 us)
Async XLA Ops:
  0.0 28.9 %copy-start = (bf16[1024,1024]{1,0:T(8,128)(2,1)S(1)}, bf16[1024,1024]{1,0:T(8,128)(2,1)}, u32[]{:S(2)}) copy-start(bf16[1024,1024]{1,0:T(8,128)(2,1)} %weight_ref.1) | copy-start | bytes 6291460
  1.7 0.9 %copy-start.1 = (bf16[256,512]{1,0:T(8,128)(2,1)S(1)}, bf16[256,512]{1,0:T(8,128)(2,1)}, u32[]{:S(2)}) copy-start(bf16[256,512]{1,0:T(8,128)(2,1)} %query_ref.1) | copy-start | bytes 786436
  2.6 0.9 %copy-start.2 = (bf16[256,512]{1,0:T(8,128)(2,1)S(1)}, bf16[256,512]{1,0:T(8,128)(2,1)}, u32[]{:S(2)}) copy-start(bf16[256,512]{1,0:T(8,128)(2,1)} %key_ref.1) | copy-start | bytes 786436
  3.6 0.9 %copy-start.3 = (bf16[256,512]{1,0:T(8,128)(2,1)S(1)}, bf16[256,512]{1,0:T(8,128)(2,1)}, u32[]{:S(2)}) copy-start(bf16[256,512]{1,0:T(8,128)(2,1)} %value_ref.1) | copy-start | bytes 786436
  18.8 12.3 %collective-permute-start = (bf16[3,512,128]{2,1,0:T(8,128)(2,1)S(1)}, bf16[3,512,128]{2,1,0:T(8,128)(2,1)S(1)}, u32[]{:S(2)}, u32[]{:S(2)}) collective-permute-start(bf16[3,512,128]{2,1,0:T(8,128)(2,1)S(1)} %slice.4), channel_id=1, source_target_pairs={{0,8},{8,16},{16,24},{24,0},{1,9},{9,17},{17,25},{25,1},{2,10},{10... | collective-permute-start | bytes 1179656 | tf_op jit(solution)/shard_map/ppermute | solution.py:209
  40.3 1.5 %collective-permute-start.1 = (bf16[512,256]{1,0:T(8,128)(2,1)S(1)}, bf16[512,256]{1,0:T(8,128)(2,1)S(1)}, u32[]{:S(2)}, u32[]{:S(2)}) collective-permute-start(bf16[512,256]{1,0:T(8,128)(2,1)S(1)} %bitcast.1), channel_id=1, source_target_pairs={{0,1},{1,0},{2,3},{3,2},{4,5},{5,4},{6,7},{7,6},{8,9},{9,8},{10,11... | collective-permute-start | bytes 786440 | tf_op jit(solution)/shard_map/ppermute | solution.py:242

commit v2 on v1

v2 whole, which is shorter than its diff:
```python
import functools

import jax
import jax.numpy as jnp
from jax import lax
from jax.experimental import pallas as pl
from jax.experimental.pallas import tpu as pltpu
from jax.sharding import Mesh, PartitionSpec as P

HEADS = 8
HD = 128
TILE = 128
SLOTS = 2
STEPS = 4
LOG2E = 1.4426950408889634
SCALE = LOG2E * HD ** (-0.5)
MASKED = -1e30
EXTRA = 16
VMEM = pl.BlockSpec(memory_space=pltpu.VMEM)
HBM = pl.BlockSpec(memory_space=pltpu.HBM)
PARAMS = pltpu.CompilerParams(vmem_limit_bytes=48 * 1024 * 1024)


def use_rows(index_ref, count_ref, tiles):
    row = lax.broadcasted_iota(jnp.int32, (EXTRA, HD), 0)
    uses = jnp.zeros((EXTRA, HD), jnp.float32)
    for turn in range(STEPS):
        for dest in range(tiles):
            for source in range(tiles):
                times = jnp.float32(0)
                for slot in range(SLOTS):
                    used = (slot < count_ref[dest, turn]) & (index_ref[dest, slot, turn] == source)
                    times += jnp.where(used, 1.0, 0.0)
                uses = jnp.where(row == (turn * tiles + dest) * tiles + source, times, uses)
    return uses


def pack_kernel(query_ref, key_ref, value_ref, index_ref, count_ref, *refs):
    out_refs, (values, index, count, sem) = refs[:-4], refs[-4:]
    rows, width = query_ref.shape
    group = width // HD
    tiles = rows // TILE
    place = lax.axis_index("place")
    value_copy = pltpu.make_async_copy(value_ref, values, sem.at[0])
    value_copy.start()
    table_copies = [
        pltpu.make_async_copy(index_ref, index, sem.at[1]),
        pltpu.make_async_copy(count_ref, count, sem.at[2]),
    ]
    for copy in table_copies:
        copy.start()
    copies = []
    for step in range(group):
        cols = pl.ds(pl.multiple_of(jnp.bitwise_xor(place, step) * HD, HD), HD)
        out = out_refs[step]
        copies += [
            pltpu.make_async_copy(
                key_ref.at[:, cols], out.at[pl.ds(0, rows)], sem.at[3 + 2 * step]
            ),
            pltpu.make_async_copy(
                query_ref.at[:, cols], out.at[pl.ds(2 * rows, rows)], sem.at[4 + 2 * step]
            ),
        ]
    for copy in copies:
        copy.start()
    for copy in table_copies:
        copy.wait()
    uses = use_rows(index, count, tiles).astype(jnp.bfloat16)
    value_copy.wait()
    for step in range(group):
        cols = pl.ds(pl.multiple_of(jnp.bitwise_xor(place, step) * HD, HD), HD)
        out = out_refs[step]
        out[3 * rows :] = uses
        for at in range(0, rows, TILE):
            out[rows + at : rows + at + TILE] = values[at : at + TILE, cols].T
    for copy in copies:
        copy.wait()


def source_scores(keys, query_uses, turn, rows):
    tiles = rows // TILE
    raw = (
        lax.dot_general(
            keys, query_uses[:rows], (((1,), (1,)), ((), ())), preferred_element_type=jnp.float32
        )
        * SCALE
    )
    parts = []
    for source in range(tiles):
        bias = []
        for tile in range(tiles):
            at = rows + (turn * tiles + tile) * tiles + source
            times = query_uses[at : at + 1].astype(jnp.float32)
            bias.append(jnp.where(times > 0.5, times - 1.0, MASKED))
        parts.append(
            raw[source * TILE : (source + 1) * TILE] + jnp.concatenate(bias, axis=1)
        )
    return raw, jnp.concatenate(parts, axis=0)


def slab_values(kv_ref, slot, rows):
    return jnp.concatenate(
        [kv_ref[slot, rows + at : rows + at + TILE] for at in range(0, rows, TILE)], axis=1
    )


def add_sources(scores, values, top, total, mixed):
    for score, value in zip(scores, values):
        weights = jnp.exp2(score - top)
        total = total + jnp.sum(weights, axis=0, keepdims=True)
        mixed = mixed + jnp.dot(
            value, weights.astype(jnp.bfloat16), preferred_element_type=jnp.float32
        )
    return total, mixed


def near_kernel(*refs, group, head_total):
    got_refs, weight_ref = refs[:group], refs[group]
    query_ref, mixed_ref, state_ref, turned_ref, kv, held, sem = refs[group + 1 :]
    rows = mixed_ref.shape[2]
    place = lax.axis_index("place")
    me = lax.axis_index("head")
    depth = weight_ref.shape[0] // head_total
    features = weight_ref.shape[1] // head_total
    copies = []
    for other in range(head_total):
        start = pl.multiple_of(jnp.bitwise_xor(me, other) * depth, depth)
        cols = pl.ds(pl.multiple_of(me * features, features), features)
        copies.append(
            pltpu.make_async_copy(
                weight_ref.at[pl.ds(start, depth), cols], held.at[other], sem.at[other]
            )
        )
        copies[-1].start()
    for step in range(group):
        slab = jnp.bitwise_xor(place, step)
        kv[slab] = got_refs[step][: 2 * rows]
        query_ref[slab] = got_refs[step][2 * rows :]
    eye = lax.broadcasted_iota(jnp.int32, (TILE, TILE), 0) == lax.broadcasted_iota(
        jnp.int32, (TILE, TILE), 1
    )
    for dest in range(group):
        scores, values = [], []
        query_uses = query_ref[dest]
        for turn in range(STEPS):
            slab = dest - turn
            if slab < 0:
                continue
            raw, score = source_scores(kv[slab, :rows], query_uses, turn, rows)
            if turn == 0:
                own = jnp.concatenate(
                    [
                        jnp.sum(
                            jnp.where(eye, raw[at : at + TILE, at : at + TILE], 0.0),
                            axis=0,
                            keepdims=True,
                        )
                        for at in range(0, rows, TILE)
                    ],
                    axis=1,
                )
            scores.append(score)
            values.append(slab_values(kv, slab, rows))
        top = own
        for score in scores:
            top = jnp.maximum(top, jnp.max(score, axis=0, keepdims=True))
        weight = jnp.exp2(own - top)
        total, mixed = add_sources(
            scores, values, top, weight, weight * values[0].astype(jnp.float32)
        )
        mixed_ref[dest] = mixed
        state_ref[dest, 0:1] = top
        state_ref[dest, 1:2] = total
    for other in range(head_total):
        copies[other].wait()
        turned_ref[other] = held[other].T


def halo_steps(group, first):
    return [[k for k in range(group) if place ^ k >= first] for place in range(group)]


def pick(place, choices):
    result = jnp.int32(choices[-1])
    for at, choice in enumerate(choices[:-1]):
        result = jnp.where(place == at, jnp.int32(choice), result)
    return result


def far_kernel(*refs, group, halos):
    query_ref, mixed_ref, state_ref = refs[:3]
    messages = sum(group - first for _, first in halos)
    far_refs = refs[3 : 3 + messages]
    out_refs = refs[3 + messages : 3 + messages + group]
    far, done = refs[3 + messages + group :]
    rows = mixed_ref.shape[2]
    place = lax.axis_index("place")
    slots = {}
    base = 0
    for offset, first in halos:
        steps = halo_steps(group, first)
        for at in range(group - first):
            slab = pick(place, [p ^ steps[p][at] for p in range(group)])
            far[base + slab - first] = far_refs[base + at][...]
            slots[offset, first + at] = base + at
        base += group - first
    for dest in range(group):
        scores, values = [], []
        query_uses = query_ref[dest]
        for turn in range(STEPS):
            slab = dest - turn
            if slab >= 0:
                continue
            slot = slots[-(slab // group), slab % group]
            scores.append(source_scores(far[slot, :rows], query_uses, turn, rows)[1])
            values.append(slab_values(far, slot, rows))
        top = state_ref[dest, 0:1]
        total = state_ref[dest, 1:2]
        mixed = mixed_ref[dest]
        if scores:
            before = top
            for score in scores:
                top = jnp.maximum(top, jnp.max(score, axis=0, keepdims=True))
            factor = jnp.exp2(before - top)
            total, mixed = add_sources(scores, values, top, total * factor, mixed * factor)
        done[dest] = (mixed / total).astype(done.dtype)
    for step in range(group):
        out_refs[step][...] = done[jnp.bitwise_xor(place, step)]


def project_kernel(turned_ref, *refs, group, head_total):
    mix_refs, out_ref, mix = refs[:-2], refs[-2], refs[-1]
    place = lax.axis_index("place")
    for other in range(head_total):
        for step in range(group):
            mix[other, jnp.bitwise_xor(place, step)] = mix_refs[other * group + step][...]
    result = None
    for other in range(head_total):
        part = jnp.dot(
            turned_ref[other],
            mix[other].reshape(turned_ref.shape[2], out_ref.shape[1]),
            preferred_element_type=jnp.float32,
        )
        result = part if result is None else result + part
    out_ref[...] = result.astype(out_ref.dtype)


def swapped(value, axis, step):
    count = lax.axis_size(axis)
    return lax.ppermute(value, axis, [(source, source ^ step) for source in range(count)])


def on_device(node_queries, node_keys, node_values, tile_index, tile_count, out_weight):
    rows, width = node_queries.shape
    group = width // HD
    groups = lax.axis_size("group")
    head_total = lax.axis_size("head")
    depth, feature_total = out_weight.shape
    features = feature_total // head_total
    bf16, f32 = jnp.bfloat16, jnp.float32
    shape = jax.ShapeDtypeStruct
    place = lax.axis_index("place")

    packed = pl.pallas_call(
        pack_kernel,
        out_shape=[shape((3 * rows + EXTRA, HD), bf16)] * group,
        in_specs=[HBM] * 5,
        out_specs=[VMEM] * group,
        scratch_shapes=[
            pltpu.VMEM((rows, width), bf16),
            pltpu.SMEM((rows // TILE, SLOTS, STEPS), jnp.int32),
            pltpu.SMEM((rows // TILE, STEPS), jnp.int32),
            pltpu.SemaphoreType.DMA((3 + 2 * group,)),
        ],
        compiler_params=PARAMS,
        name="pack",
    )(
        *[
            pltpu.with_memory_space_constraint(array, pltpu.HBM)
            for array in (
                node_queries,
                node_keys,
                node_values,
                jnp.transpose(tile_index, (1, 2, 0)),
                jnp.transpose(tile_count, (1, 0)),
            )
        ],
    )

    got = [packed[0]] + [swapped(packed[step], "place", step) for step in range(1, group)]
    halos = []
    for offset in range(1, -(-(STEPS - 1) // group) + 1):
        halos.append((offset, max(0, offset * group - STEPS + 1)))
    far = []
    for offset, first in halos:
        steps = halo_steps(group, first)
        pairs = [(source, (source + offset) % groups) for source in range(groups)]
        for at in range(group - first):
            piece = got[steps[-1][at]][: 2 * rows]
            for p in range(group - 1):
                if steps[p][at] != steps[-1][at]:
                    piece = jnp.where(place == p, got[steps[p][at]][: 2 * rows], piece)
            piece, *got = lax.optimization_barrier([piece, *got])
            if at > 1:
                far[-2], piece = lax.optimization_barrier((far[-2], piece))
            far.append(lax.ppermute(piece, "group", pairs))

    queries, mixed, state, turned = pl.pallas_call(
        functools.partial(near_kernel, group=group, head_total=head_total),
        out_shape=(
            shape((group, rows + EXTRA, HD), bf16),
            shape((group, HD, rows), f32),
            shape((group, 8, rows), f32),
            shape((head_total, features, depth // head_total), bf16),
        ),
        in_specs=[VMEM] * group + [HBM],
        out_specs=(VMEM, VMEM, VMEM, VMEM),
        scratch_shapes=[
            pltpu.VMEM((group, 2 * rows, HD), bf16),
            pltpu.VMEM((head_total, depth // head_total, features), bf16),
            pltpu.SemaphoreType.DMA((head_total,)),
        ],
        compiler_params=PARAMS,
        name="near",
    )(*got, out_weight)

    mix = pl.pallas_call(
        functools.partial(far_kernel, group=group, halos=halos),
        out_shape=[shape((HD, rows), bf16)] * group,
        in_specs=[VMEM] * (3 + len(far)),
        out_specs=[VMEM] * group,
        scratch_shapes=[
            pltpu.VMEM((len(far), 2 * rows, HD), bf16),
            pltpu.VMEM((group, HD, rows), bf16),
        ],
        compiler_params=PARAMS,
        name="far",
    )(queries, mixed, state, *far)

    mixes = [mix[0]] + [swapped(mix[step], "place", step) for step in range(1, group)]
    for other in range(1, head_total):
        mixes += [swapped(mixes[step], "head", other) for step in range(group)]
    return pl.pallas_call(
        functools.partial(project_kernel, group=group, head_total=head_total),
        out_shape=shape((features, rows), bf16),
        in_specs=[VMEM] * (1 + head_total * group),
        out_specs=VMEM,
        scratch_shapes=[pltpu.VMEM((head_total, group, HD, rows), bf16)],
        compiler_params=PARAMS,
        name="project",
    )(turned, *mixes)


def solution(mesh):
    nodes, heads = mesh.devices.shape
    place = HEADS // heads
    split = Mesh(
        mesh.devices.reshape(nodes // place, place, heads), ("group", "place", "head")
    )
    node = ("group", "place")
    return jax.shard_map(
        on_device,
        mesh=split,
        in_specs=(
            P(node, "head"),
            P(node, "head"),
            P(node, "head"),
            P(None, node, None),
            P(None, node),
            P(),
        ),
        out_specs=P("head", node),
        check_vma=False,
    )
```

time: 43.3 us -> 40.1 us (0.926)
  blocking collectives: 30.1 us -> 0 us
  waiting for transfers between devices: 1.54 us -> 21.2 us
  starting transfers between devices: 1.63 us -> 11.4 us
  local copies, waits for them, and re-layouts: 4.56 us -> 1.59 us
  Pallas kernels: 5.15 us -> 5.69 us
    all_to_all x3 -> x0, blocking collectives: 30.1 us -> none  [the longest x1 13.5 us: on_device(): kv = lax.all_to_all(kv, 'place', 0, 0)]
    ppermute x2 -> x13, waiting for transfers between devices: 1.54 us -> 21.2 us  [the longest x10 14.1 us: swapped(): lax.ppermute(value, axis, [(source, source ^ step) for source in range(co...]
    ppermute x2 -> x13, starting transfers between devices: 1.63 us -> 11.4 us  [the longest x10 8.11 us: swapped(): lax.ppermute(value, axis, [(source, source ^ step) for source in range(co...]
    unnamed x10 -> x2, local copies, waits for them, and re-layouts: 4.54 us -> 1.59 us
    pallas_call x4, Pallas kernels: 5.15 us -> 5.69 us  [the longest x1 2.24 us: on_device(): pl.pallas_call(functools.partial(near_kernel, group=group, head_total=hea...]
  transfers between devices with their start and end apart: 2 -> 13, of which waited for: 1 -> 8; matrix products, arithmetic and copies ran while one was open for 0% -> 0% of each run, Pallas kernels for 5% -> 6%
where the time goes in v2:
time: 40.1 us; the launch traced here: 40 us
  waiting for transfers between devices  21.2 us (53%)
  starting transfers between devices  11.4 us (28%)
  Pallas kernels  5.69 us (14%)
  local copies, waits for them, and re-layouts  1.59 us (4%)
    ppermute x10, waiting for transfers between devices, swapped(): lax.ppermute(value, axis, [(source, source ^ step) for source in range(co...  14.1 us
    ppermute x10, starting transfers between devices, swapped(): lax.ppermute(value, axis, [(source, source ^ step) for source in range(co...  8.11 us
    ppermute x3, waiting for transfers between devices, on_device(): far.append(lax.ppermute(piece, 'group', pairs))  7.09 us
    ppermute x3, starting transfers between devices, on_device(): far.append(lax.ppermute(piece, 'group', pairs))  3.26 us
    pallas_call x1, Pallas kernels, on_device(): pl.pallas_call(functools.partial(near_kernel, group=group, head_total=hea...  2.24 us
    unnamed x2, local copies, waits for them, and re-layouts  1.59 us
    pallas_call x1, Pallas kernels, on_device(): pl.pallas_call(pack_kernel, out_shape=[shape((3 * rows + EXTRA, HD), bf16...  1.21 us
    pallas_call x1, Pallas kernels, on_device(): pl.pallas_call(functools.partial(project_kernel, group=group, head_total=...  1.19 us
  transfers between devices with their start and end apart: 13, of which 8 were waited for; matrix products, arithmetic and copies ran while one was open for 0% of the time, Pallas kernels for 6%

profile of v2, /device:TPU:0, one launch (start us, length us, event | category | flops | bytes accessed | tf_op | source)
XLA Modules:
  0.0 40.0 jit_solution(15994184682969981850)
XLA Ops:
  0.0 1.2 %pack.1 = (bf16[784,128]{1,0:T(8,128)(2,1)S(1)}, bf16[784,128]{1,0:T(8,128)(2,1)S(1)}, bf16[784,128]{1,0:T(8,128)(2,1)S(1)}, bf16[784,128]{1,0:T(8,128)(2,1)S(1)}) custom-call(bf16[256,512]{1,0:T(8,128)(2,1)} %query_ref.1, bf16[256,512]{1,0:T(8,128)(2,1)} %key_ref.1, bf16[256,512]{1,0:T(8,128)(2,1)} %value_ref.1, s32[2,2,4]{2,1,0:T(2,128)} %bitcast.2, ...), custom_call_target="tpu_custom_call" | custom-call | tf_op jit(solution)/shard_map/pack/pallas_call | solution.py:264
  1.2 3.0 %collective-permute-start = (bf16[784,128]{1,0:T(8,128)(2,1)S(1)}, bf16[784,128]{1,0:T(8,128)(2,1)S(1)}, u32[]{:S(2)}, u32[]{:S(2)}) collective-permute-start(bf16[784,128]{1,0:T(8,128)(2,1)S(1)} %get-tuple-element.34), channel_id=1, source_target_pairs={{0,2},{2,0},{4,6},{6,4},{1,3},{3,1},{5,7},{7,5},{8,10},{10,8},{12,... | collective-permute-start | bytes 602120 | tf_op jit(solution)/shard_map/ppermute | solution.py:250
  4.2 1.5 %collective-permute-start.1 = (bf16[784,128]{1,0:T(8,128)(2,1)S(1)}, bf16[784,128]{1,0:T(8,128)(2,1)S(1)}, u32[]{:S(2)}, u32[]{:S(2)}) collective-permute-start(bf16[784,128]{1,0:T(8,128)(2,1)S(1)} %get-tuple-element.36), channel_id=1, source_target_pairs={{0,4},{2,6},{4,0},{6,2},{1,5},{3,7},{5,1},{7,3},{8,12},{10,14},{12... | collective-permute-start | bytes 602120 | tf_op jit(solution)/shard_map/ppermute | solution.py:250
  5.7 0.0 collective-permute-start.2
  5.8 4.3 %collective-permute-done.refs_1_ = bf16[784,128]{1,0:T(8,128)(2,1)S(1)} collective-permute-done((bf16[784,128]{1,0:T(8,128)(2,1)S(1)}, bf16[784,128]{1,0:T(8,128)(2,1)S(1)}, u32[]{:S(2)}, u32[]{:S(2)}) %collective-permute-start) | collective-permute-done | bytes 200736 | tf_op jit(solution)/shard_map/ppermute | solution.py:250
  10.1 4.9 %collective-permute-done.1.refs_2_ = bf16[784,128]{1,0:T(8,128)(2,1)S(1)} collective-permute-done((bf16[784,128]{1,0:T(8,128)(2,1)S(1)}, bf16[784,128]{1,0:T(8,128)(2,1)S(1)}, u32[]{:S(2)}, u32[]{:S(2)}) %collective-permute-start.1) | collective-permute-done | bytes 200736 | tf_op jit(solution)/shard_map/ppermute | solution.py:250
  15.0 0.0 collective-permute-done.2.refs_3_
  15.0 1.6 %collective-permute-start.3 = (bf16[512,128]{1,0:T(8,128)(2,1)S(1)}, bf16[512,128]{1,0:T(8,128)(2,1)S(1)}, u32[]{:S(2)}, u32[]{:S(2)}) collective-permute-start(bf16[512,128]{1,0:T(8,128)(2,1)S(1)} %slice_select_fusion), channel_id=1, source_target_pairs={{0,8},{8,16},{16,24},{24,0},{1,9},{9,17},{17,25},{25,1},{2,10},{10... | collective-permute-start | bytes 393224 | tf_op jit(solution)/shard_map/ppermute | solution.py:306
  16.7 1.6 %collective-permute-start.4 = (bf16[512,128]{1,0:T(8,128)(2,1)S(1)}, bf16[512,128]{1,0:T(8,128)(2,1)S(1)}, u32[]{:S(2)}, u32[]{:S(2)}) collective-permute-start(bf16[512,128]{1,0:T(8,128)(2,1)S(1)} %select_select_fusion.1), channel_id=1, source_target_pairs={{0,8},{8,16},{16,24},{24,0},{1,9},{9,17},{17,25},{25,1},{2,10},{10... | collective-permute-start | bytes 393224 | tf_op jit(solution)/shard_map/ppermute | solution.py:306
  18.3 4.2 %collective-permute-done.3.refs_3_ = bf16[512,128]{1,0:T(8,128)(2,1)S(1)} collective-permute-done((bf16[512,128]{1,0:T(8,128)(2,1)S(1)}, bf16[512,128]{1,0:T(8,128)(2,1)S(1)}, u32[]{:S(2)}, u32[]{:S(2)}) %collective-permute-start.3) | collective-permute-done | bytes 131104 | tf_op jit(solution)/shard_map/ppermute | solution.py:306
  22.5 0.0 collective-permute-start.5
  22.5 0.0 copy-start
  22.5 1.6 %copy-done = bf16[1024,1024]{1,0:T(8,128)(2,1)S(1)} copy-done((bf16[1024,1024]{1,0:T(8,128)(2,1)S(1)}, bf16[1024,1024]{1,0:T(8,128)(2,1)}, u32[]{:S(2)}) %copy-start) | copy-done | bytes 2097176
  24.1 2.2 %near.1 = (bf16[4,272,128]{2,1,0:T(8,128)(2,1)S(1)}, f32[4,128,256]{2,1,0:T(8,128)S(1)}, f32[4,8,256]{2,1,0:T(8,128)S(1)}, bf16[2,512,512]{2,1,0:T(8,128)(2,1)S(1)}) custom-call(bf16[784,128]{1,0:T(8,128)(2,1)S(1)} %get-tuple-element.46.refs_0_, bf16[784,128]{1,0:T(8,128)(2,1)S(1)} %collective-permute-done.refs_1_, ...), custom_call_target="tpu_custom_call" | custom-call | tf_op jit(solution)/shard_map/near/pallas_call | solution.py:308
  26.3 0.0 collective-permute-done.4.refs_4_
  26.3 2.9 %collective-permute-done.5.refs_5_ = bf16[512,128]{1,0:T(8,128)(2,1)S(1)} collective-permute-done((bf16[512,128]{1,0:T(8,128)(2,1)S(1)}, bf16[512,128]{1,0:T(8,128)(2,1)S(1)}, u32[]{:S(2)}, u32[]{:S(2)}) %collective-permute-start.5) | collective-permute-done | bytes 131104 | tf_op jit(solution)/shard_map/ppermute | solution.py:306
  29.2 1.0 %far.1 = (bf16[128,256]{1,0:T(8,128)(2,1)S(1)}, bf16[128,256]{1,0:T(8,128)(2,1)S(1)}, bf16[128,256]{1,0:T(8,128)(2,1)S(1)}, bf16[128,256]{1,0:T(8,128)(2,1)S(1)}) custom-call(bf16[4,272,128]{2,1,0:T(8,128)(2,1)S(1)} %get-tuple-element.51.refs_0_, f32[4,128,256]{2,1,0:T(8,128)S(1)} %get-tuple-element.52.refs_1_, f32[4,8,256]{2,1,0:T(8,128)S(1)} %get-tuple-element.53.refs_2_, ...), custom_call_target="tpu_custom_call" | custom-call | tf_op jit(solution)/shard_map/far/pallas_call | solution.py:327
  30.3 1.5 %collective-permute-start.6 = (bf16[128,256]{1,0:T(8,128)(2,1)S(1)}, bf16[128,256]{1,0:T(8,128)(2,1)S(1)}, u32[]{:S(2)}, u32[]{:S(2)}) collective-permute-start(bf16[128,256]{1,0:T(8,128)(2,1)S(1)} %get-tuple-element.60), channel_id=1, source_target_pairs={{0,2},{2,0},{4,6},{6,4},{1,3},{3,1},{5,7},{7,5},{8,10},{10,8},{12,... | collective-permute-start | bytes 196616 | tf_op jit(solution)/shard_map/ppermute | solution.py:250
  31.8 0.6 %collective-permute-start.7 = (bf16[128,256]{1,0:T(8,128)(2,1)S(1)}, bf16[128,256]{1,0:T(8,128)(2,1)S(1)}, u32[]{:S(2)}, u32[]{:S(2)}) collective-permute-start(bf16[128,256]{1,0:T(8,128)(2,1)S(1)} %get-tuple-element.61), channel_id=1, source_target_pairs={{0,4},{2,6},{4,0},{6,2},{1,5},{3,7},{5,1},{7,3},{8,12},{10,14},{12... | collective-permute-start | bytes 196616 | tf_op jit(solution)/shard_map/ppermute | solution.py:250
  32.4 1.5 %collective-permute-start.8 = (bf16[128,256]{1,0:T(8,128)(2,1)S(1)}, bf16[128,256]{1,0:T(8,128)(2,1)S(1)}, u32[]{:S(2)}, u32[]{:S(2)}) collective-permute-start(bf16[128,256]{1,0:T(8,128)(2,1)S(1)} %get-tuple-element.62), channel_id=1, source_target_pairs={{0,6},{2,4},{4,2},{6,0},{1,7},{3,5},{5,3},{7,1},{8,14},{10,12},{12... | collective-permute-start | bytes 196616 | tf_op jit(solution)/shard_map/ppermute | solution.py:250
  33.8 0.0 collective-permute-start.9
  33.8 0.8 %collective-permute-done.6.refs_1_ = bf16[128,256]{1,0:T(8,128)(2,1)S(1)} collective-permute-done((bf16[128,256]{1,0:T(8,128)(2,1)S(1)}, bf16[128,256]{1,0:T(8,128)(2,1)S(1)}, u32[]{:S(2)}, u32[]{:S(2)}) %collective-permute-start.6) | collective-permute-done | bytes 65568 | tf_op jit(solution)/shard_map/ppermute | solution.py:250
  34.6 0.0 collective-permute-start.10
  34.6 1.4 %collective-permute-done.7.refs_2_ = bf16[128,256]{1,0:T(8,128)(2,1)S(1)} collective-permute-done((bf16[128,256]{1,0:T(8,128)(2,1)S(1)}, bf16[128,256]{1,0:T(8,128)(2,1)S(1)}, u32[]{:S(2)}, u32[]{:S(2)}) %collective-permute-start.7) | collective-permute-done | bytes 65568 | tf_op jit(solution)/shard_map/ppermute | solution.py:250
  36.1 0.0 collective-permute-start.11
  36.1 1.4 %collective-permute-done.8.refs_3_ = bf16[128,256]{1,0:T(8,128)(2,1)S(1)} collective-permute-done((bf16[128,256]{1,0:T(8,128)(2,1)S(1)}, bf16[128,256]{1,0:T(8,128)(2,1)S(1)}, u32[]{:S(2)}, u32[]{:S(2)}) %collective-permute-start.8) | collective-permute-done | bytes 65568 | tf_op jit(solution)/shard_map/ppermute | solution.py:250
  37.5 0.0 collective-permute-start.12
  37.5 0.0 collective-permute-done.9.refs_4_
  37.5 0.0 collective-permute-done.10.refs_5_
  37.5 0.0 collective-permute-done.11.refs_6_
  37.5 1.2 %collective-permute-done.12.refs_7_ = bf16[128,256]{1,0:T(8,128)(2,1)S(1)} collective-permute-done((bf16[128,256]{1,0:T(8,128)(2,1)S(1)}, bf16[128,256]{1,0:T(8,128)(2,1)S(1)}, u32[]{:S(2)}, u32[]{:S(2)}) %collective-permute-start.12) | collective-permute-done | bytes 65568 | tf_op jit(solution)/shard_map/ppermute | solution.py:250
  38.8 1.2 %project.1 = bf16[512,256]{1,0:T(8,128)(2,1)} custom-call(bf16[2,512,512]{2,1,0:T(8,128)(2,1)S(1)} %get-tuple-element.50.turned_ref, bf16[128,256]{1,0:T(8,128)(2,1)S(1)} %get-tuple-element.59.refs_0_, bf16[128,256]{1,0:T(8,128)(2,1)S(1)} %collective-permute-done.6.refs_1_, bf16[128,256]{1,0:T(8,128)(2,1)S(1)} %collective-permute-done.7.refs_2_, ...), custom_call_target="tpu_custom_call" | custom-call | tf_op jit(solution)/shard_map/project/pallas_call | solution.py:343
  (3 shorter events, 0.1 us)
Async XLA Ops:
  1.2 8.8 %collective-permute-start = (bf16[784,128]{1,0:T(8,128)(2,1)S(1)}, bf16[784,128]{1,0:T(8,128)(2,1)S(1)}, u32[]{:S(2)}, u32[]{:S(2)}) collective-permute-start(bf16[784,128]{1,0:T(8,128)(2,1)S(1)} %get-tuple-element.34), channel_id=1, source_target_pairs={{0,2},{2,0},{4,6},{6,4},{1,3},{3,1},{5,7},{7,5},{8,10},{10,8},{12,... | collective-permute-start | bytes 602120 | tf_op jit(solution)/shard_map/ppermute | solution.py:250
  4.2 10.8 %collective-permute-start.1 = (bf16[784,128]{1,0:T(8,128)(2,1)S(1)}, bf16[784,128]{1,0:T(8,128)(2,1)S(1)}, u32[]{:S(2)}, u32[]{:S(2)}) collective-permute-start(bf16[784,128]{1,0:T(8,128)(2,1)S(1)} %get-tuple-element.36), channel_id=1, source_target_pairs={{0,4},{2,6},{4,0},{6,2},{1,5},{3,7},{5,1},{7,3},{8,12},{10,14},{12... | collective-permute-start | bytes 602120 | tf_op jit(solution)/shard_map/ppermute | solution.py:250
  5.7 9.2 %collective-permute-start.2 = (bf16[784,128]{1,0:T(8,128)(2,1)S(1)}, bf16[784,128]{1,0:T(8,128)(2,1)S(1)}, u32[]{:S(2)}, u32[]{:S(2)}) collective-permute-start(bf16[784,128]{1,0:T(8,128)(2,1)S(1)} %get-tuple-element.37), channel_id=1, source_target_pairs={{0,6},{2,4},{4,2},{6,0},{1,7},{3,5},{5,3},{7,1},{8,14},{10,12},{12... | collective-permute-start | bytes 602120 | tf_op jit(solution)/shard_map/ppermute | solution.py:250
  15.0 7.5 %collective-permute-start.3 = (bf16[512,128]{1,0:T(8,128)(2,1)S(1)}, bf16[512,128]{1,0:T(8,128)(2,1)S(1)}, u32[]{:S(2)}, u32[]{:S(2)}) collective-permute-start(bf16[512,128]{1,0:T(8,128)(2,1)S(1)} %slice_select_fusion), channel_id=1, source_target_pairs={{0,8},{8,16},{16,24},{24,0},{1,9},{9,17},{17,25},{25,1},{2,10},{10... | collective-permute-start | bytes 393224 | tf_op jit(solution)/shard_map/ppermute | solution.py:306
  16.7 9.7 %collective-permute-start.4 = (bf16[512,128]{1,0:T(8,128)(2,1)S(1)}, bf16[512,128]{1,0:T(8,128)(2,1)S(1)}, u32[]{:S(2)}, u32[]{:S(2)}) collective-permute-start(bf16[512,128]{1,0:T(8,128)(2,1)S(1)} %select_select_fusion.1), channel_id=1, source_target_pairs={{0,8},{8,16},{16,24},{24,0},{1,9},{9,17},{17,25},{25,1},{2,10},{10... | collective-permute-start | bytes 393224 | tf_op jit(solution)/shard_map/ppermute | solution.py:306
  22.5 6.8 %collective-permute-start.5 = (bf16[512,128]{1,0:T(8,128)(2,1)S(1)}, bf16[512,128]{1,0:T(8,128)(2,1)S(1)}, u32[]{:S(2)}, u32[]{:S(2)}) collective-permute-start(bf16[512,128]{1,0:T(8,128)(2,1)S(1)} %select_select_fusion), channel_id=1, source_target_pairs={{0,8},{8,16},{16,24},{24,0},{1,9},{9,17},{17,25},{25,1},{2,10},{10... | collective-permute-start | bytes 393224 | tf_op jit(solution)/shard_map/ppermute | solution.py:306
  22.5 1.6 %copy-start = (bf16[1024,1024]{1,0:T(8,128)(2,1)S(1)}, bf16[1024,1024]{1,0:T(8,128)(2,1)}, u32[]{:S(2)}) copy-start(bf16[1024,1024]{1,0:T(8,128)(2,1)} %refs_4_.1) | copy-start | bytes 6291460
  30.3 4.3 %collective-permute-start.6 = (bf16[128,256]{1,0:T(8,128)(2,1)S(1)}, bf16[128,256]{1,0:T(8,128)(2,1)S(1)}, u32[]{:S(2)}, u32[]{:S(2)}) collective-permute-start(bf16[128,256]{1,0:T(8,128)(2,1)S(1)} %get-tuple-element.60), channel_id=1, source_target_pairs={{0,2},{2,0},{4,6},{6,4},{1,3},{3,1},{5,7},{7,5},{8,10},{10,8},{12,... | collective-permute-start | bytes 196616 | tf_op jit(solution)/shard_map/ppermute | solution.py:250
  31.8 4.3 %collective-permute-start.7 = (bf16[128,256]{1,0:T(8,128)(2,1)S(1)}, bf16[128,256]{1,0:T(8,128)(2,1)S(1)}, u32[]{:S(2)}, u32[]{:S(2)}) collective-permute-start(bf16[128,256]{1,0:T(8,128)(2,1)S(1)} %get-tuple-element.61), channel_id=1, source_target_pairs={{0,4},{2,6},{4,0},{6,2},{1,5},{3,7},{5,1},{7,3},{8,12},{10,14},{12... | collective-permute-start | bytes 196616 | tf_op jit(solution)/shard_map/ppermute | solution.py:250
  32.4 5.2 %collective-permute-start.8 = (bf16[128,256]{1,0:T(8,128)(2,1)S(1)}, bf16[128,256]{1,0:T(8,128)(2,1)S(1)}, u32[]{:S(2)}, u32[]{:S(2)}) collective-permute-start(bf16[128,256]{1,0:T(8,128)(2,1)S(1)} %get-tuple-element.62), channel_id=1, source_target_pairs={{0,6},{2,4},{4,2},{6,0},{1,7},{3,5},{5,3},{7,1},{8,14},{10,12},{12... | collective-permute-start | bytes 196616 | tf_op jit(solution)/shard_map/ppermute | solution.py:250
  33.8 3.7 %collective-permute-start.9 = (bf16[128,256]{1,0:T(8,128)(2,1)S(1)}, bf16[128,256]{1,0:T(8,128)(2,1)S(1)}, u32[]{:S(2)}, u32[]{:S(2)}) collective-permute-start(bf16[128,256]{1,0:T(8,128)(2,1)S(1)} %get-tuple-element.59.refs_0_), channel_id=1, source_target_pairs={{0,1},{1,0},{2,3},{3,2},{4,5},{5,4},{6,7},{7,6},{8,9},{9,8},{10,11... | collective-permute-start | bytes 196616 | tf_op jit(solution)/shard_map/ppermute | solution.py:250
  34.6 2.9 %collective-permute-start.10 = (bf16[128,256]{1,0:T(8,128)(2,1)S(1)}, bf16[128,256]{1,0:T(8,128)(2,1)S(1)}, u32[]{:S(2)}, u32[]{:S(2)}) collective-permute-start(bf16[128,256]{1,0:T(8,128)(2,1)S(1)} %collective-permute-done.6.refs_1_), channel_id=1, source_target_pairs={{0,1},{1,0},{2,3},{3,2},{4,5},{5,4},{6,7},{7,6},{8,9},{9,8},{10,11... | collective-permute-start | bytes 196616 | tf_op jit(solution)/shard_map/ppermute | solution.py:250
  36.1 1.5 %collective-permute-start.11 = (bf16[128,256]{1,0:T(8,128)(2,1)S(1)}, bf16[128,256]{1,0:T(8,128)(2,1)S(1)}, u32[]{:S(2)}, u32[]{:S(2)}) collective-permute-start(bf16[128,256]{1,0:T(8,128)(2,1)S(1)} %collective-permute-done.7.refs_2_), channel_id=1, source_target_pairs={{0,1},{1,0},{2,3},{3,2},{4,5},{5,4},{6,7},{7,6},{8,9},{9,8},{10,11... | collective-permute-start | bytes 196616 | tf_op jit(solution)/shard_map/ppermute | solution.py:250
  37.5 1.3 %collective-permute-start.12 = (bf16[128,256]{1,0:T(8,128)(2,1)S(1)}, bf16[128,256]{1,0:T(8,128)(2,1)S(1)}, u32[]{:S(2)}, u32[]{:S(2)}) collective-permute-start(bf16[128,256]{1,0:T(8,128)(2,1)S(1)} %collective-permute-done.8.refs_3_), channel_id=1, source_target_pairs={{0,1},{1,0},{2,3},{3,2},{4,5},{5,4},{6,7},{7,6},{8,9},{9,8},{10,11... | collective-permute-start | bytes 196616 | tf_op jit(solution)/shard_map/ppermute | solution.py:250

commit v3 on v2

--- a/solution.py
+++ b/solution.py
@@ -16,6 +16,7 @@
 SCALE = LOG2E * HD ** (-0.5)
 MASKED = -1e30
 EXTRA = 16
+COST = 10**9
 VMEM = pl.BlockSpec(memory_space=pltpu.VMEM)
 HBM = pl.BlockSpec(memory_space=pltpu.HBM)
 PARAMS = pltpu.CompilerParams(vmem_limit_bytes=48 * 1024 * 1024)
@@ -180,6 +181,10 @@
     return [[k for k in range(group) if place ^ k >= first] for place in range(group)]
 
 
+def message_parts(total):
+    return [(0, total)] if total < 3 else [(0, total - 1), (total - 1, total)]
+
+
 def pick(place, choices):
     result = jnp.int32(choices[-1])
     for at, choice in enumerate(choices[:-1]):
@@ -187,53 +192,70 @@
     return result
 
 
-def far_kernel(*refs, group, halos):
-    query_ref, mixed_ref, state_ref = refs[:3]
-    messages = sum(group - first for _, first in halos)
-    far_refs = refs[3 : 3 + messages]
-    out_refs = refs[3 + messages : 3 + messages + group]
-    far, done = refs[3 + messages + group :]
+def far_kernel(*refs, group, halo, at, last):
+    query_ref, mixed_ref, state_ref, far_ref = refs[:4]
+    if last:
+        out_refs, (mixed_out, state_out, done) = refs[4:-3], refs[-3:]
+    else:
+        mixed_out, state_out = refs[4:]
     rows = mixed_ref.shape[2]
     place = lax.axis_index("place")
-    slots = {}
-    base = 0
-    for offset, first in halos:
-        steps = halo_steps(group, first)
-        for at in range(group - first):
-            slab = pick(place, [p ^ steps[p][at] for p in range(group)])
-            far[base + slab - first] = far_refs[base + at][...]
-            slots[offset, first + at] = base + at
-        base += group - first
-    for dest in range(group):
-        scores, values = [], []
-        query_uses = query_ref[dest]
-        for turn in range(STEPS):
-            slab = dest - turn
-            if slab >= 0:
-                continue
-            slot = slots[-(slab // group), slab % group]
-            scores.append(source_scores(far[slot, :rows], query_uses, turn, rows)[1])
-            values.append(slab_values(far, slot, rows))
-        top = state_ref[dest, 0:1]
-        total = state_ref[dest, 1:2]
-        mixed = mixed_ref[dest]
-        if scores:
-            before = top
-            for score in scores:
-                top = jnp.maximum(top, jnp.max(score, axis=0, keepdims=True))
-            factor = jnp.exp2(before - top)
-            total, mixed = add_sources(scores, values, top, total * factor, mixed * factor)
-        done[dest] = (mixed / total).astype(done.dtype)
-    for step in range(group):
-        out_refs[step][...] = done[jnp.bitwise_xor(place, step)]
+    offset, first = halo
+    steps = halo_steps(group, first)
+    mixed_out[...] = mixed_ref[...]
+    state_out[...] = state_ref[...]
+    for low in range(far_ref.shape[0]):
+        slabs = [p ^ steps[p][at + low] for p in range(group)]
+        mine = pick(place, slabs)
+        for slab in sorted(set(slabs)):
+
+            @pl.when(mine == slab)
+            def _(low=low, slab=slab):
+                value = slab_values(far_ref, low, rows)
+                for dest in range(group):
+                    turn = dest + offset * group - slab
+                    if turn >= STEPS:
+                        continue
+                    score = source_scores(far_ref[low, :rows], query_ref[dest], turn, rows)[1]
+                    before = state_out[dest, 0:1]
+                    top = jnp.maximum(before, jnp.max(score, axis=0, keepdims=True))
+                    factor = jnp.exp2(before - top)
+                    total, mixed = add_sources(
+                        [score],
+                        [value],
+                        top,
+                        state_out[dest, 1:2] * factor,
+                        mixed_out[dest] * factor,
+                    )
+                    mixed_out[dest] = mixed
+                    state_out[dest, 0:1] = top
+                    state_out[dest, 1:2] = total
+
+    if last:
+        for dest in range(group):
+            done[dest] = (mixed_out[dest] / state_out[dest, 1:2]).astype(done.dtype)
+        for steps, out_ref in zip(stage_steps(group), out_refs):
+            for low, step in enumerate(steps):
+                out_ref[low * HD : (low + 1) * HD] = done[jnp.bitwise_xor(place, step)]
+
+
+def stage_steps(group):
+    stages, bit = [[0]], 1
+    while bit < group:
+        stages.append([step for step in range(group) if step & -step == bit])
+        bit *= 2
+    return stages
 
 
 def project_kernel(turned_ref, *refs, group, head_total):
     mix_refs, out_ref, mix = refs[:-2], refs[-2], refs[-1]
     place = lax.axis_index("place")
     for other in range(head_total):
-        for step in range(group):
-            mix[other, jnp.bitwise_xor(place, step)] = mix_refs[other * group + step][...]
+        step = 0
+        for mix_ref in mix_refs[other :: head_total]:
+            for low in range(0, mix_ref.shape[0], HD):
+                mix[other, jnp.bitwise_xor(place, step)] = mix_ref[low : low + HD]
+                step += 1
     result = None
     for other in range(head_total):
         part = jnp.dot(
@@ -287,23 +309,33 @@
         ],
     )
 
-    got = [packed[0]] + [swapped(packed[step], "place", step) for step in range(1, group)]
     halos = []
     for offset in range(1, -(-(STEPS - 1) // group) + 1):
         halos.append((offset, max(0, offset * group - STEPS + 1)))
-    far = []
-    for offset, first in halos:
-        steps = halo_steps(group, first)
-        pairs = [(source, (source + offset) % groups) for source in range(groups)]
-        for at in range(group - first):
-            piece = got[steps[-1][at]][: 2 * rows]
-            for p in range(group - 1):
-                if steps[p][at] != steps[-1][at]:
-                    piece = jnp.where(place == p, got[steps[p][at]][: 2 * rows], piece)
-            piece, *got = lax.optimization_barrier([piece, *got])
-            if at > 1:
-                far[-2], piece = lax.optimization_barrier((far[-2], piece))
-            far.append(lax.ppermute(piece, "group", pairs))
+    got, far = [packed[0]], []
+    waiting = [
+        (halo, part, max(row[part[1] - 1] for row in halo_steps(group, halo[1])))
+        for halo in halos
+        for part in message_parts(group - halo[1])
+    ]
+    for step in range(group):
+        if step:
+            got.append(swapped(packed[step], "place", step))
+        for (offset, first), (at, until), needed in waiting:
+            if needed != step:
+                continue
+            steps = halo_steps(group, first)
+            pairs = [(source, (source + offset) % groups) for source in range(groups)]
+            parts = []
+            for low in range(at, until):
+                piece = got[steps[-1][low]][: 2 * rows]
+                for p in range(group - 1):
+                    if steps[p][low] != steps[-1][low]:
+                        piece = jnp.where(place == p, got[steps[p][low]][: 2 * rows], piece)
+                parts.append(piece)
+            message = jnp.stack(parts)
+            message, *got = lax.optimization_barrier([message, *got])
+            far.append(((offset, first), at, lax.ppermute(message, "group", pairs)))
 
     queries, mixed, state, turned = pl.pallas_call(
         functools.partial(near_kernel, group=group, head_total=head_total),
@@ -321,29 +353,55 @@
             pltpu.SemaphoreType.DMA((head_total,)),
         ],
         compiler_params=PARAMS,
+        cost_estimate=pl.CostEstimate(flops=1, transcendentals=1, bytes_accessed=1),
         name="near",
-    )(*got, out_weight)
-
-    mix = pl.pallas_call(
-        functools.partial(far_kernel, group=group, halos=halos),
-        out_shape=[shape((HD, rows), bf16)] * group,
-        in_specs=[VMEM] * (3 + len(far)),
-        out_specs=[VMEM] * group,
-        scratch_shapes=[
-            pltpu.VMEM((len(far), 2 * rows, HD), bf16),
-            pltpu.VMEM((group, HD, rows), bf16),
-        ],
-        compiler_params=PARAMS,
-        name="far",
-    )(queries, mixed, state, *far)
-
-    mixes = [mix[0]] + [swapped(mix[step], "place", step) for step in range(1, group)]
-    for other in range(1, head_total):
-        mixes += [swapped(mixes[step], "head", other) for step in range(group)]
+    )(*got, pltpu.with_memory_space_constraint(out_weight, pltpu.HBM))
+
+    for number, (halo, at, message) in enumerate(far):
+        last = number == len(far) - 1
+        state_shapes = [shape(mixed.shape, f32), shape(state.shape, f32)]
+        stages = stage_steps(group)
+        outs = pl.pallas_call(
+            functools.partial(far_kernel, group=group, halo=halo, at=at, last=last),
+            out_shape=[shape((HD * len(steps), rows), bf16) for steps in stages]
+            if last
+            else state_shapes,
+            in_specs=[VMEM] * 4,
+            out_specs=[VMEM] * (len(stages) if last else 2),
+            scratch_shapes=[
+                pltpu.VMEM(mixed.shape, f32),
+                pltpu.VMEM(state.shape, f32),
+                pltpu.VMEM((group, HD, rows), bf16),
+            ]
+            if last
+            else [],
+            compiler_params=PARAMS,
+            cost_estimate=pl.CostEstimate(
+                flops=COST, transcendentals=1, bytes_accessed=1
+            ),
+            name="far",
+        )(queries, mixed, state, message)
+        if not last:
+            mixed, state = outs
+
+    mine, pieces = [outs[0]], {}
+    for steps, fresh in zip(stages[1:], outs[1:]):
+        bit = steps[0]
+        sent = [fresh] + [pieces[head, step] for head in range(1, bit) for step in steps]
+        got_mix = swapped(jnp.concatenate(sent) if len(sent) > 1 else fresh, "place", bit)
+        if len(steps) == 1:
+            mine.append(got_mix)
+            continue
+        for at, (head, step) in enumerate((h, s) for h in range(bit) for s in steps):
+            pieces[head ^ bit, step ^ bit] = got_mix[at * HD : (at + 1) * HD]
+        mine[0] = jnp.concatenate([mine[0]] + [pieces[head, 0] for head in range(bit, 2 * bit)])
+    mixes = []
+    for entry in mine:
+        mixes += [entry] + [swapped(entry, "head", other) for other in range(1, head_total)]
     return pl.pallas_call(
         functools.partial(project_kernel, group=group, head_total=head_total),
         out_shape=shape((features, rows), bf16),
-        in_specs=[VMEM] * (1 + head_total * group),
+        in_specs=[VMEM] * (1 + len(mixes)),
         out_specs=VMEM,
         scratch_shapes=[pltpu.VMEM((head_total, group, HD, rows), bf16)],
         compiler_params=PARAMS,

time: 40.1 us -> 38.5 us (0.960)
  Pallas kernels: 5.69 us -> 7.61 us
  starting transfers between devices: 11.4 us -> 9.76 us
  local copies, waits for them, and re-layouts: 1.59 us -> 0.01 us
    ppermute x3 -> x2, waiting for transfers between devices: 7.09 us -> 2.19 us  [on_device(): far.append(((offset, first), at, lax.ppermute(message, 'group', pairs)))]
    ppermute x10 -> x7, waiting for transfers between devices: 14.1 us -> 18.6 us  [swapped(): lax.ppermute(value, axis, [(source, source ^ step) for source in range(co...]
    ppermute x10 -> x7, starting transfers between devices: 8.11 us -> 6.51 us  [swapped(): lax.ppermute(value, axis, [(source, source ^ step) for source in range(co...]
    unnamed x2 -> x0, local copies, waits for them, and re-layouts: 1.59 us -> none
    pallas_call x1 -> x2, Pallas kernels: 1.05 us -> 2.24 us  [on_device(): pl.pallas_call(functools.partial(far_kernel, group=group, halo=halo, at=a...]
    pallas_call x1, Pallas kernels: 2.24 us -> 2.97 us  [on_device(): pl.pallas_call(functools.partial(near_kernel, group=group, head_total=hea...]
    ppermute x3 -> x2, starting transfers between devices: 3.26 us -> 3.26 us  [on_device(): far.append(((offset, first), at, lax.ppermute(message, 'group', pairs)))]
  transfers between devices with their start and end apart: 13 -> 9, of which waited for: 8 -> 7; matrix products, arithmetic and copies ran while one was open for 0% -> 0% of each run, Pallas kernels for 6% -> 11%
where the time goes in v3:
time: 38.5 us; the launch traced here: 38.4 us
  waiting for transfers between devices  20.8 us (54%)
  starting transfers between devices  9.76 us (25%)
  Pallas kernels  7.61 us (20%)
    ppermute x7, waiting for transfers between devices, swapped(): lax.ppermute(value, axis, [(source, source ^ step) for source in range(co...  18.6 us
    ppermute x7, starting transfers between devices, swapped(): lax.ppermute(value, axis, [(source, source ^ step) for source in range(co...  6.51 us
    ppermute x2, starting transfers between devices, on_device(): far.append(((offset, first), at, lax.ppermute(message, 'group', pairs)))  3.26 us
    pallas_call x1, Pallas kernels, on_device(): pl.pallas_call(functools.partial(near_kernel, group=group, head_total=hea...  2.97 us
    pallas_call x2, Pallas kernels, on_device(): pl.pallas_call(functools.partial(far_kernel, group=group, halo=halo, at=a...  2.24 us
    ppermute x2, waiting for transfers between devices, on_device(): far.append(((offset, first), at, lax.ppermute(message, 'group', pairs)))  2.19 us
    pallas_call x1, Pallas kernels, on_device(): pl.pallas_call(pack_kernel, out_shape=[shape((3 * rows + EXTRA, HD), bf16...  1.21 us
    pallas_call x1, Pallas kernels, on_device(): pl.pallas_call(functools.partial(project_kernel, group=group, head_total=...  1.19 us
  transfers between devices with their start and end apart: 9, of which 7 were waited for; matrix products, arithmetic and copies ran while one was open for 0% of the time, Pallas kernels for 11%

profile of v3, /device:TPU:0, one launch (start us, length us, event | category | flops | bytes accessed | tf_op | source)
XLA Modules:
  0.0 38.4 jit_solution(9322414383595181609)
XLA Ops:
  0.0 1.2 %pack.1 = (bf16[784,128]{1,0:T(8,128)(2,1)S(1)}, bf16[784,128]{1,0:T(8,128)(2,1)S(1)}, bf16[784,128]{1,0:T(8,128)(2,1)S(1)}, bf16[784,128]{1,0:T(8,128)(2,1)S(1)}) custom-call(bf16[256,512]{1,0:T(8,128)(2,1)} %query_ref.1, bf16[256,512]{1,0:T(8,128)(2,1)} %key_ref.1, bf16[256,512]{1,0:T(8,128)(2,1)} %value_ref.1, s32[2,2,4]{2,1,0:T(2,128)} %bitcast.8, ...), custom_call_target="tpu_custom_call" | custom-call | tf_op jit(solution)/shard_map/pack/pallas_call | solution.py:286
  1.2 3.0 %collective-permute-start.1 = (bf16[784,128]{1,0:T(8,128)(2,1)S(1)}, bf16[784,128]{1,0:T(8,128)(2,1)S(1)}, u32[]{:S(2)}, u32[]{:S(2)}) collective-permute-start(bf16[784,128]{1,0:T(8,128)(2,1)S(1)} %get-tuple-element.28), channel_id=1, source_target_pairs={{0,2},{2,0},{4,6},{6,4},{1,3},{3,1},{5,7},{7,5},{8,10},{10,8},{12,... | collective-permute-start | bytes 602120 | tf_op jit(solution)/shard_map/ppermute | solution.py:272
  4.2 1.5 %collective-permute-start.2 = (bf16[784,128]{1,0:T(8,128)(2,1)S(1)}, bf16[784,128]{1,0:T(8,128)(2,1)S(1)}, u32[]{:S(2)}, u32[]{:S(2)}) collective-permute-start(bf16[784,128]{1,0:T(8,128)(2,1)S(1)} %get-tuple-element.30), channel_id=1, source_target_pairs={{0,4},{2,6},{4,0},{6,2},{1,5},{3,7},{5,1},{7,3},{8,12},{10,14},{12... | collective-permute-start | bytes 602120 | tf_op jit(solution)/shard_map/ppermute | solution.py:272
  5.7 0.0 collective-permute-start
  5.8 4.3 %collective-permute-done.1.refs_1_ = bf16[784,128]{1,0:T(8,128)(2,1)S(1)} collective-permute-done((bf16[784,128]{1,0:T(8,128)(2,1)S(1)}, bf16[784,128]{1,0:T(8,128)(2,1)S(1)}, u32[]{:S(2)}, u32[]{:S(2)}) %collective-permute-start.1) | collective-permute-done | bytes 200736 | tf_op jit(solution)/shard_map/ppermute | solution.py:272
  10.0 4.9 %collective-permute-done.2.refs_2_ = bf16[784,128]{1,0:T(8,128)(2,1)S(1)} collective-permute-done((bf16[784,128]{1,0:T(8,128)(2,1)S(1)}, bf16[784,128]{1,0:T(8,128)(2,1)S(1)}, u32[]{:S(2)}, u32[]{:S(2)}) %collective-permute-start.2) | collective-permute-done | bytes 200736 | tf_op jit(solution)/shard_map/ppermute | solution.py:272
  15.0 1.6 %collective-permute-start.3 = (bf16[2,512,128]{2,1,0:T(8,128)(2,1)S(1)}, bf16[2,512,128]{2,1,0:T(8,128)(2,1)S(1)}, u32[]{:S(2)}, u32[]{:S(2)}) collective-permute-start(bf16[2,512,128]{2,1,0:T(8,128)(2,1)S(1)} %pad_maximum_fusion), channel_id=1, source_target_pairs={{0,8},{8,16},{16,24},{24,0},{1,9},{9,17},{17,25},{25,1},{2,10},{10... | collective-permute-start | bytes 786440 | tf_op jit(solution)/shard_map/ppermute | solution.py:338
  16.7 0.0 collective-permute-done.refs_3_
  16.7 1.6 %collective-permute-start.4 = (bf16[1,512,128]{2,1,0:T(8,128)(2,1)S(1)}, bf16[1,512,128]{2,1,0:T(8,128)(2,1)S(1)}, u32[]{:S(2)}, u32[]{:S(2)}) collective-permute-start(bf16[1,512,128]{2,1,0:T(8,128)(2,1)S(1)} %fusion.1), channel_id=1, source_target_pairs={{0,8},{8,16},{16,24},{24,0},{1,9},{9,17},{17,25},{25,1},{2,10},{10... | collective-permute-start | bytes 393224 | tf_op jit(solution)/shard_map/ppermute | solution.py:338
  18.3 3.0 %near.1 = (bf16[4,272,128]{2,1,0:T(8,128)(2,1)S(1)}, f32[4,128,256]{2,1,0:T(8,128)S(1)}, f32[4,8,256]{2,1,0:T(8,128)S(1)}, bf16[2,512,512]{2,1,0:T(8,128)(2,1)S(1)}) custom-call(bf16[784,128]{1,0:T(8,128)(2,1)S(1)} %get-tuple-element.34.refs_0_, bf16[784,128]{1,0:T(8,128)(2,1)S(1)} %collective-permute-done.1.refs_1_, ...), custom_call_target="tpu_custom_call" | custom-call | flops 1 | bytes 1 | tf_op jit(solution)/shard_map/near/pallas_call | solution.py:340
  21.3 2.0 %collective-permute-done.3.refs_3_ = bf16[2,512,128]{2,1,0:T(8,128)(2,1)S(1)} collective-permute-done((bf16[2,512,128]{2,1,0:T(8,128)(2,1)S(1)}, bf16[2,512,128]{2,1,0:T(8,128)(2,1)S(1)}, u32[]{:S(2)}, u32[]{:S(2)}) %collective-permute-start.3) | collective-permute-done | bytes 262176 | tf_op jit(solution)/shard_map/ppermute | solution.py:338
  23.3 1.2 %far.2 = (f32[4,128,256]{2,1,0:T(8,128)S(1)}, f32[4,8,256]{2,1,0:T(8,128)S(1)}) custom-call(bf16[4,272,128]{2,1,0:T(8,128)(2,1)S(1)} %get-tuple-element.39.refs_0_, f32[4,128,256]{2,1,0:T(8,128)S(1)} %get-tuple-element.40.refs_1_, f32[4,8,256]{2,1,0:T(8,128)S(1)} %get-tuple-element.41.refs_2_, bf16[2,512,128]{2,1,0:T(8,128)(2,1)S(1)} %collective-permute-done.3.refs_3_), custom_call_target="tpu_custom_call" | custom-call | flops 1000000000 | bytes 1 | tf_op jit(solution)/shard_map/far/pallas_call | solution.py:364
  24.4 0.2 collective-permute-done.4.refs_3_
  24.7 1.1 %far.3 = (bf16[128,256]{1,0:T(8,128)(2,1)S(1)}, bf16[256,256]{1,0:T(8,128)(2,1)S(1)}, bf16[128,256]{1,0:T(8,128)(2,1)S(1)}) custom-call(bf16[4,272,128]{2,1,0:T(8,128)(2,1)S(1)} %get-tuple-element.39.refs_0_, f32[4,128,256]{2,1,0:T(8,128)S(1)} %get-tuple-element.43.refs_1_, f32[4,8,256]{2,1,0:T(8,128)S(1)} %get-tuple-element.44.refs_2_, ...), custom_call_target="tpu_custom_call" | custom-call | flops 1000000000 | bytes 1 | tf_op jit(solution)/shard_map/far/pallas_call | solution.py:364
  25.8 0.5 %collective-permute-start.5 = (bf16[256,256]{1,0:T(8,128)(2,1)S(1)}, bf16[256,256]{1,0:T(8,128)(2,1)S(1)}, u32[]{:S(2)}, u32[]{:S(2)}) collective-permute-start(bf16[256,256]{1,0:T(8,128)(2,1)S(1)} %get-tuple-element.47), channel_id=1, source_target_pairs={{0,2},{2,0},{4,6},{6,4},{1,3},{3,1},{5,7},{7,5},{8,10},{10,8},{12,... | collective-permute-start | bytes 393224 | tf_op jit(solution)/shard_map/ppermute | solution.py:272
  26.3 4.5 %collective-permute-done.5 = bf16[256,256]{1,0:T(8,128)(2,1)S(1)} collective-permute-done((bf16[256,256]{1,0:T(8,128)(2,1)S(1)}, bf16[256,256]{1,0:T(8,128)(2,1)S(1)}, u32[]{:S(2)}, u32[]{:S(2)}) %collective-permute-start.5) | collective-permute-done | bytes 131104 | tf_op jit(solution)/shard_map/ppermute | solution.py:272
  30.8 1.4 %collective-permute-start.7 = (bf16[256,256]{1,0:T(8,128)(2,1)S(1)}, bf16[256,256]{1,0:T(8,128)(2,1)S(1)}, u32[]{:S(2)}, u32[]{:S(2)}) collective-permute-start(bf16[256,256]{1,0:T(8,128)(2,1)S(1)} %pad_maximum_fusion.2), channel_id=1, source_target_pairs={{0,4},{2,6},{4,0},{6,2},{1,5},{3,7},{5,1},{7,3},{8,12},{10,14},{12... | collective-permute-start | bytes 393224 | tf_op jit(solution)/shard_map/ppermute | solution.py:272
  32.2 0.1 collective-permute-start.6
  32.3 3.6 %collective-permute-done.7.refs_2_ = bf16[256,256]{1,0:T(8,128)(2,1)S(1)} collective-permute-done((bf16[256,256]{1,0:T(8,128)(2,1)S(1)}, bf16[256,256]{1,0:T(8,128)(2,1)S(1)}, u32[]{:S(2)}, u32[]{:S(2)}) %collective-permute-start.7) | collective-permute-done | bytes 131104 | tf_op jit(solution)/shard_map/ppermute | solution.py:272
  35.9 0.0 collective-permute-start.8
  35.9 0.0 collective-permute-done.6.refs_1_
  35.9 1.3 %collective-permute-done.8.refs_3_ = bf16[256,256]{1,0:T(8,128)(2,1)S(1)} collective-permute-done((bf16[256,256]{1,0:T(8,128)(2,1)S(1)}, bf16[256,256]{1,0:T(8,128)(2,1)S(1)}, u32[]{:S(2)}, u32[]{:S(2)}) %collective-permute-start.8) | collective-permute-done | bytes 131104 | tf_op jit(solution)/shard_map/ppermute | solution.py:272
  37.2 1.2 %project.1 = bf16[512,256]{1,0:T(8,128)(2,1)} custom-call(bf16[2,512,512]{2,1,0:T(8,128)(2,1)S(1)} %get-tuple-element.38.turned_ref, bf16[256,256]{1,0:T(8,128)(2,1)S(1)} %pad_maximum_fusion.1.refs_0_, bf16[256,256]{1,0:T(8,128)(2,1)S(1)} %collective-permute-done.6.refs_1_, bf16[256,256]{1,0:T(8,128)(2,1)S(1)} %collective-permute-done.7.refs_2_, ...), custom_call_target="tpu_custom_call" | custom-call | tf_op jit(solution)/shard_map/project/pallas_call | solution.py:401
  (6 shorter events, 0.1 us)
Async XLA Ops:
  1.2 8.8 %collective-permute-start.1 = (bf16[784,128]{1,0:T(8,128)(2,1)S(1)}, bf16[784,128]{1,0:T(8,128)(2,1)S(1)}, u32[]{:S(2)}, u32[]{:S(2)}) collective-permute-start(bf16[784,128]{1,0:T(8,128)(2,1)S(1)} %get-tuple-element.28), channel_id=1, source_target_pairs={{0,2},{2,0},{4,6},{6,4},{1,3},{3,1},{5,7},{7,5},{8,10},{10,8},{12,... | collective-permute-start | bytes 602120 | tf_op jit(solution)/shard_map/ppermute | solution.py:272
  4.2 10.8 %collective-permute-start.2 = (bf16[784,128]{1,0:T(8,128)(2,1)S(1)}, bf16[784,128]{1,0:T(8,128)(2,1)S(1)}, u32[]{:S(2)}, u32[]{:S(2)}) collective-permute-start(bf16[784,128]{1,0:T(8,128)(2,1)S(1)} %get-tuple-element.30), channel_id=1, source_target_pairs={{0,4},{2,6},{4,0},{6,2},{1,5},{3,7},{5,1},{7,3},{8,12},{10,14},{12... | collective-permute-start | bytes 602120 | tf_op jit(solution)/shard_map/ppermute | solution.py:272
  5.7 10.9 %collective-permute-start = (bf16[784,128]{1,0:T(8,128)(2,1)S(1)}, bf16[784,128]{1,0:T(8,128)(2,1)S(1)}, u32[]{:S(2)}, u32[]{:S(2)}) collective-permute-start(bf16[784,128]{1,0:T(8,128)(2,1)S(1)} %get-tuple-element.27), channel_id=1, source_target_pairs={{0,6},{2,4},{4,2},{6,0},{1,7},{3,5},{5,3},{7,1},{8,14},{10,12},{12... | collective-permute-start | bytes 602120 | tf_op jit(solution)/shard_map/ppermute | solution.py:272
  15.0 8.2 %collective-permute-start.3 = (bf16[2,512,128]{2,1,0:T(8,128)(2,1)S(1)}, bf16[2,512,128]{2,1,0:T(8,128)(2,1)S(1)}, u32[]{:S(2)}, u32[]{:S(2)}) collective-permute-start(bf16[2,512,128]{2,1,0:T(8,128)(2,1)S(1)} %pad_maximum_fusion), channel_id=1, source_target_pairs={{0,8},{8,16},{16,24},{24,0},{1,9},{9,17},{17,25},{25,1},{2,10},{10... | collective-permute-start | bytes 786440 | tf_op jit(solution)/shard_map/ppermute | solution.py:338
  16.7 8.0 %collective-permute-start.4 = (bf16[1,512,128]{2,1,0:T(8,128)(2,1)S(1)}, bf16[1,512,128]{2,1,0:T(8,128)(2,1)S(1)}, u32[]{:S(2)}, u32[]{:S(2)}) collective-permute-start(bf16[1,512,128]{2,1,0:T(8,128)(2,1)S(1)} %fusion.1), channel_id=1, source_target_pairs={{0,8},{8,16},{16,24},{24,0},{1,9},{9,17},{17,25},{25,1},{2,10},{10... | collective-permute-start | bytes 393224 | tf_op jit(solution)/shard_map/ppermute | solution.py:338
  25.8 5.0 %collective-permute-start.5 = (bf16[256,256]{1,0:T(8,128)(2,1)S(1)}, bf16[256,256]{1,0:T(8,128)(2,1)S(1)}, u32[]{:S(2)}, u32[]{:S(2)}) collective-permute-start(bf16[256,256]{1,0:T(8,128)(2,1)S(1)} %get-tuple-element.47), channel_id=1, source_target_pairs={{0,2},{2,0},{4,6},{6,4},{1,3},{3,1},{5,7},{7,5},{8,10},{10,8},{12,... | collective-permute-start | bytes 393224 | tf_op jit(solution)/shard_map/ppermute | solution.py:272
  30.8 5.0 %collective-permute-start.7 = (bf16[256,256]{1,0:T(8,128)(2,1)S(1)}, bf16[256,256]{1,0:T(8,128)(2,1)S(1)}, u32[]{:S(2)}, u32[]{:S(2)}) collective-permute-start(bf16[256,256]{1,0:T(8,128)(2,1)S(1)} %pad_maximum_fusion.2), channel_id=1, source_target_pairs={{0,4},{2,6},{4,0},{6,2},{1,5},{3,7},{5,1},{7,3},{8,12},{10,14},{12... | collective-permute-start | bytes 393224 | tf_op jit(solution)/shard_map/ppermute | solution.py:272
  32.2 3.7 %collective-permute-start.6 = (bf16[256,256]{1,0:T(8,128)(2,1)S(1)}, bf16[256,256]{1,0:T(8,128)(2,1)S(1)}, u32[]{:S(2)}, u32[]{:S(2)}) collective-permute-start(bf16[256,256]{1,0:T(8,128)(2,1)S(1)} %pad_maximum_fusion.1.refs_0_), channel_id=1, source_target_pairs={{0,1},{1,0},{2,3},{3,2},{4,5},{5,4},{6,7},{7,6},{8,9},{9,8},{10,11... | collective-permute-start | bytes 393224 | tf_op jit(solution)/shard_map/ppermute | solution.py:272
  35.9 1.3 %collective-permute-start.8 = (bf16[256,256]{1,0:T(8,128)(2,1)S(1)}, bf16[256,256]{1,0:T(8,128)(2,1)S(1)}, u32[]{:S(2)}, u32[]{:S(2)}) collective-permute-start(bf16[256,256]{1,0:T(8,128)(2,1)S(1)} %collective-permute-done.7.refs_2_), channel_id=1, source_target_pairs={{0,1},{1,0},{2,3},{3,2},{4,5},{5,4},{6,7},{7,6},{8,9},{9,8},{10,11... | collective-permute-start | bytes 393224 | tf_op jit(solution)/shard_map/ppermute | solution.py:272

commit v4 on v3

--- a/solution.py
+++ b/solution.py
@@ -181,6 +181,14 @@
     return [[k for k in range(group) if place ^ k >= first] for place in range(group)]
 
 
+def hops(step):
+    return step.bit_count()
+
+
+def sending_order(group):
+    return sorted(range(group), key=lambda step: (step > 0, -hops(step), step))
+
+
 def message_parts(total):
     return [(0, total)] if total < 3 else [(0, total - 1), (total - 1, total)]
 
@@ -234,28 +242,16 @@
     if last:
         for dest in range(group):
             done[dest] = (mixed_out[dest] / state_out[dest, 1:2]).astype(done.dtype)
-        for steps, out_ref in zip(stage_steps(group), out_refs):
-            for low, step in enumerate(steps):
-                out_ref[low * HD : (low + 1) * HD] = done[jnp.bitwise_xor(place, step)]
-
-
-def stage_steps(group):
-    stages, bit = [[0]], 1
-    while bit < group:
-        stages.append([step for step in range(group) if step & -step == bit])
-        bit *= 2
-    return stages
+        for step, out_ref in zip(sending_order(group), out_refs):
+            out_ref[...] = done[jnp.bitwise_xor(place, step)]
 
 
 def project_kernel(turned_ref, *refs, group, head_total):
     mix_refs, out_ref, mix = refs[:-2], refs[-2], refs[-1]
     place = lax.axis_index("place")
     for other in range(head_total):
-        step = 0
-        for mix_ref in mix_refs[other :: head_total]:
-            for low in range(0, mix_ref.shape[0], HD):
-                mix[other, jnp.bitwise_xor(place, step)] = mix_ref[low : low + HD]
-                step += 1
+        for at, step in enumerate(sending_order(group)):
+            mix[other, jnp.bitwise_xor(place, step)] = mix_refs[other * group + at][...]
     result = None
     for other in range(head_total):
         part = jnp.dot(
@@ -320,7 +316,10 @@
     ]
     for step in range(group):
         if step:
-            got.append(swapped(packed[step], "place", step))
+            block = packed[step]
+            if hops(step) > 1:
+                block, got[1] = lax.optimization_barrier((block, got[1]))
+            got.append(swapped(block, "place", step))
         for (offset, first), (at, until), needed in waiting:
             if needed != step:
                 continue
@@ -360,14 +359,11 @@
     for number, (halo, at, message) in enumerate(far):
         last = number == len(far) - 1
         state_shapes = [shape(mixed.shape, f32), shape(state.shape, f32)]
-        stages = stage_steps(group)
         outs = pl.pallas_call(
             functools.partial(far_kernel, group=group, halo=halo, at=at, last=last),
-            out_shape=[shape((HD * len(steps), rows), bf16) for steps in stages]
-            if last
-            else state_shapes,
+            out_shape=[shape((HD, rows), bf16)] * group if last else state_shapes,
             in_specs=[VMEM] * 4,
-            out_specs=[VMEM] * (len(stages) if last else 2),
+            out_specs=[VMEM] * (group if last else 2),
             scratch_shapes=[
                 pltpu.VMEM(mixed.shape, f32),
                 pltpu.VMEM(state.shape, f32),
@@ -384,20 +380,10 @@
         if not last:
             mixed, state = outs
 
-    mine, pieces = [outs[0]], {}
-    for steps, fresh in zip(stages[1:], outs[1:]):
-        bit = steps[0]
-        sent = [fresh] + [pieces[head, step] for head in range(1, bit) for step in steps]
-        got_mix = swapped(jnp.concatenate(sent) if len(sent) > 1 else fresh, "place", bit)
-        if len(steps) == 1:
-            mine.append(got_mix)
-            continue
-        for at, (head, step) in enumerate((h, s) for h in range(bit) for s in steps):
-            pieces[head ^ bit, step ^ bit] = got_mix[at * HD : (at + 1) * HD]
-        mine[0] = jnp.concatenate([mine[0]] + [pieces[head, 0] for head in range(bit, 2 * bit)])
-    mixes = []
-    for entry in mine:
-        mixes += [entry] + [swapped(entry, "head", other) for other in range(1, head_total)]
+    order = sending_order(group)
+    mixes = [outs[0]] + [swapped(out, "place", step) for step, out in zip(order[1:], outs[1:])]
+    for other in range(1, head_total):
+        mixes += [swapped(mix, "head", other) for mix in mixes[:group]]
     return pl.pallas_call(
         functools.partial(project_kernel, group=group, head_total=head_total),
         out_shape=shape((features, rows), bf16),

time: 38.5 us -> 34.7 us (0.901)
  waiting for transfers between devices: 20.8 us -> 13.6 us
  starting transfers between devices: 9.76 us -> 13.2 us
    ppermute x7 -> x10, waiting for transfers between devices: 18.6 us -> 12.6 us  [swapped(): lax.ppermute(value, axis, [(source, source ^ step) for source in range(co...]
    ppermute x7 -> x10, starting transfers between devices: 6.51 us -> 9.95 us  [swapped(): lax.ppermute(value, axis, [(source, source ^ step) for source in range(co...]
    ppermute x2, waiting for transfers between devices: 2.19 us -> 1.03 us  [on_device(): far.append(((offset, first), at, lax.ppermute(message, 'group', pairs)))]
  transfers between devices with their start and end apart: 9 -> 12, of which waited for: 7 -> 8; matrix products, arithmetic and copies ran while one was open for 0% -> 0% of each run, Pallas kernels for 11% -> 12%
where the time goes in v4:
time: 34.7 us; the launch traced here: 34.6 us
  waiting for transfers between devices  13.6 us (39%)
  starting transfers between devices  13.2 us (38%)
  Pallas kernels  7.61 us (22%)
    ppermute x10, waiting for transfers between devices, swapped(): lax.ppermute(value, axis, [(source, source ^ step) for source in range(co...  12.6 us
    ppermute x10, starting transfers between devices, swapped(): lax.ppermute(value, axis, [(source, source ^ step) for source in range(co...  9.95 us
    ppermute x2, starting transfers between devices, on_device(): far.append(((offset, first), at, lax.ppermute(message, 'group', pairs)))  3.21 us
    pallas_call x1, Pallas kernels, on_device(): pl.pallas_call(functools.partial(near_kernel, group=group, head_total=hea...  2.97 us
    pallas_call x2, Pallas kernels, on_device(): pl.pallas_call(functools.partial(far_kernel, group=group, halo=halo, at=a...  2.24 us
    pallas_call x1, Pallas kernels, on_device(): pl.pallas_call(pack_kernel, out_shape=[shape((3 * rows + EXTRA, HD), bf16...  1.21 us
    pallas_call x1, Pallas kernels, on_device(): pl.pallas_call(functools.partial(project_kernel, group=group, head_total=...  1.19 us
    ppermute x2, waiting for transfers between devices, on_device(): far.append(((offset, first), at, lax.ppermute(message, 'group', pairs)))  1.03 us
  transfers between devices with their start and end apart: 12, of which 8 were waited for; matrix products, arithmetic and copies ran while one was open for 0% of the time, Pallas kernels for 12%

profile of v4, /device:TPU:0, one launch (start us, length us, event | category | flops | bytes accessed | tf_op | source)
XLA Modules:
  0.0 34.6 jit_solution(11263953985470980514)
XLA Ops:
  0.0 1.2 %pack.1 = (bf16[784,128]{1,0:T(8,128)(2,1)S(1)}, bf16[784,128]{1,0:T(8,128)(2,1)S(1)}, bf16[784,128]{1,0:T(8,128)(2,1)S(1)}, bf16[784,128]{1,0:T(8,128)(2,1)S(1)}) custom-call(bf16[256,512]{1,0:T(8,128)(2,1)} %query_ref.1, bf16[256,512]{1,0:T(8,128)(2,1)} %key_ref.1, bf16[256,512]{1,0:T(8,128)(2,1)} %value_ref.1, s32[2,2,4]{2,1,0:T(2,128)} %bitcast.8, ...), custom_call_target="tpu_custom_call" | custom-call | tf_op jit(solution)/shard_map/pack/pallas_call | solution.py:282
  1.2 3.0 %collective-permute-start = (bf16[784,128]{1,0:T(8,128)(2,1)S(1)}, bf16[784,128]{1,0:T(8,128)(2,1)S(1)}, u32[]{:S(2)}, u32[]{:S(2)}) collective-permute-start(bf16[784,128]{1,0:T(8,128)(2,1)S(1)} %get-tuple-element.31), channel_id=1, source_target_pairs={{0,2},{2,0},{4,6},{6,4},{1,3},{3,1},{5,7},{7,5},{8,10},{10,8},{12,... | collective-permute-start | bytes 602120 | tf_op jit(solution)/shard_map/ppermute | solution.py:268
  4.2 1.5 %collective-permute-start.1 = (bf16[784,128]{1,0:T(8,128)(2,1)S(1)}, bf16[784,128]{1,0:T(8,128)(2,1)S(1)}, u32[]{:S(2)}, u32[]{:S(2)}) collective-permute-start(bf16[784,128]{1,0:T(8,128)(2,1)S(1)} %get-tuple-element.33), channel_id=1, source_target_pairs={{0,4},{2,6},{4,0},{6,2},{1,5},{3,7},{5,1},{7,3},{8,12},{10,14},{12... | collective-permute-start | bytes 602120 | tf_op jit(solution)/shard_map/ppermute | solution.py:268
  5.7 3.5 %collective-permute-done.refs_1_ = bf16[784,128]{1,0:T(8,128)(2,1)S(1)} collective-permute-done((bf16[784,128]{1,0:T(8,128)(2,1)S(1)}, bf16[784,128]{1,0:T(8,128)(2,1)S(1)}, u32[]{:S(2)}, u32[]{:S(2)}) %collective-permute-start) | collective-permute-done | bytes 200736 | tf_op jit(solution)/shard_map/ppermute | solution.py:268
  9.2 1.5 %collective-permute-done.1.refs_2_ = bf16[784,128]{1,0:T(8,128)(2,1)S(1)} collective-permute-done((bf16[784,128]{1,0:T(8,128)(2,1)S(1)}, bf16[784,128]{1,0:T(8,128)(2,1)S(1)}, u32[]{:S(2)}, u32[]{:S(2)}) %collective-permute-start.1) | collective-permute-done | bytes 200736 | tf_op jit(solution)/shard_map/ppermute | solution.py:268
  10.7 1.6 %collective-permute-start.2 = (bf16[784,128]{1,0:T(8,128)(2,1)S(1)}, bf16[784,128]{1,0:T(8,128)(2,1)S(1)}, u32[]{:S(2)}, u32[]{:S(2)}) collective-permute-start(bf16[784,128]{1,0:T(8,128)(2,1)S(1)} %get-tuple-element.35), channel_id=1, source_target_pairs={{0,6},{2,4},{4,2},{6,0},{1,7},{3,5},{5,3},{7,1},{8,14},{10,12},{12... | collective-permute-start | bytes 602120 | tf_op jit(solution)/shard_map/ppermute | solution.py:268
  12.3 1.6 %collective-permute-start.3 = (bf16[2,512,128]{2,1,0:T(8,128)(2,1)S(1)}, bf16[2,512,128]{2,1,0:T(8,128)(2,1)S(1)}, u32[]{:S(2)}, u32[]{:S(2)}) collective-permute-start(bf16[2,512,128]{2,1,0:T(8,128)(2,1)S(1)} %pad_maximum_fusion), channel_id=1, source_target_pairs={{0,8},{8,16},{16,24},{24,0},{1,9},{9,17},{17,25},{25,1},{2,10},{10... | collective-permute-start | bytes 786440 | tf_op jit(solution)/shard_map/ppermute | solution.py:337
  13.9 3.5 %collective-permute-done.2.refs_3_ = bf16[784,128]{1,0:T(8,128)(2,1)S(1)} collective-permute-done((bf16[784,128]{1,0:T(8,128)(2,1)S(1)}, bf16[784,128]{1,0:T(8,128)(2,1)S(1)}, u32[]{:S(2)}, u32[]{:S(2)}) %collective-permute-start.2) | collective-permute-done | bytes 200736 | tf_op jit(solution)/shard_map/ppermute | solution.py:268
  17.4 1.6 %collective-permute-start.4 = (bf16[1,512,128]{2,1,0:T(8,128)(2,1)S(1)}, bf16[1,512,128]{2,1,0:T(8,128)(2,1)S(1)}, u32[]{:S(2)}, u32[]{:S(2)}) collective-permute-start(bf16[1,512,128]{2,1,0:T(8,128)(2,1)S(1)} %fusion.1), channel_id=1, source_target_pairs={{0,8},{8,16},{16,24},{24,0},{1,9},{9,17},{17,25},{25,1},{2,10},{10... | collective-permute-start | bytes 393224 | tf_op jit(solution)/shard_map/ppermute | solution.py:337
  19.1 3.0 %near.1 = (bf16[4,272,128]{2,1,0:T(8,128)(2,1)S(1)}, f32[4,128,256]{2,1,0:T(8,128)S(1)}, f32[4,8,256]{2,1,0:T(8,128)S(1)}, bf16[2,512,512]{2,1,0:T(8,128)(2,1)S(1)}) custom-call(bf16[784,128]{1,0:T(8,128)(2,1)S(1)} %get-tuple-element.39.refs_0_, bf16[784,128]{1,0:T(8,128)(2,1)S(1)} %collective-permute-done.refs_1_, ...), custom_call_target="tpu_custom_call" | custom-call | flops 1 | bytes 1 | tf_op jit(solution)/shard_map/near/pallas_call | solution.py:339
  22.1 0.0 collective-permute-done.3.refs_3_
  22.1 1.2 %far.2 = (f32[4,128,256]{2,1,0:T(8,128)S(1)}, f32[4,8,256]{2,1,0:T(8,128)S(1)}) custom-call(bf16[4,272,128]{2,1,0:T(8,128)(2,1)S(1)} %get-tuple-element.44.refs_0_, f32[4,128,256]{2,1,0:T(8,128)S(1)} %get-tuple-element.45.refs_1_, f32[4,8,256]{2,1,0:T(8,128)S(1)} %get-tuple-element.46.refs_2_, bf16[2,512,128]{2,1,0:T(8,128)(2,1)S(1)} %collective-permute-done.3.refs_3_), custom_call_target="tpu_custom_call" | custom-call | flops 1000000000 | bytes 1 | tf_op jit(solution)/shard_map/far/pallas_call | solution.py:362
  23.2 1.0 %collective-permute-done.4.refs_3_ = bf16[1,512,128]{2,1,0:T(8,128)(2,1)S(1)} collective-permute-done((bf16[1,512,128]{2,1,0:T(8,128)(2,1)S(1)}, bf16[1,512,128]{2,1,0:T(8,128)(2,1)S(1)}, u32[]{:S(2)}, u32[]{:S(2)}) %collective-permute-start.4) | collective-permute-done | bytes 131104 | tf_op jit(solution)/shard_map/ppermute | solution.py:337
  24.3 1.1 %far.3 = (bf16[128,256]{1,0:T(8,128)(2,1)S(1)}, bf16[128,256]{1,0:T(8,128)(2,1)S(1)}, bf16[128,256]{1,0:T(8,128)(2,1)S(1)}, bf16[128,256]{1,0:T(8,128)(2,1)S(1)}) custom-call(bf16[4,272,128]{2,1,0:T(8,128)(2,1)S(1)} %get-tuple-element.44.refs_0_, f32[4,128,256]{2,1,0:T(8,128)S(1)} %get-tuple-element.48.refs_1_, f32[4,8,256]{2,1,0:T(8,128)S(1)} %get-tuple-element.49.refs_2_, ...), custom_call_target="tpu_custom_call" | custom-call | flops 1000000000 | bytes 1 | tf_op jit(solution)/shard_map/far/pallas_call | solution.py:362
  25.3 1.0 %collective-permute-start.5 = (bf16[128,256]{1,0:T(8,128)(2,1)S(1)}, bf16[128,256]{1,0:T(8,128)(2,1)S(1)}, u32[]{:S(2)}, u32[]{:S(2)}) collective-permute-start(bf16[128,256]{1,0:T(8,128)(2,1)S(1)} %get-tuple-element.52), channel_id=1, source_target_pairs={{0,6},{2,4},{4,2},{6,0},{1,7},{3,5},{5,3},{7,1},{8,14},{10,12},{12... | collective-permute-start | bytes 196616 | tf_op jit(solution)/shard_map/ppermute | solution.py:268
  26.4 1.5 %collective-permute-start.6 = (bf16[128,256]{1,0:T(8,128)(2,1)S(1)}, bf16[128,256]{1,0:T(8,128)(2,1)S(1)}, u32[]{:S(2)}, u32[]{:S(2)}) collective-permute-start(bf16[128,256]{1,0:T(8,128)(2,1)S(1)} %get-tuple-element.53), channel_id=1, source_target_pairs={{0,2},{2,0},{4,6},{6,4},{1,3},{3,1},{5,7},{7,5},{8,10},{10,8},{12,... | collective-permute-start | bytes 196616 | tf_op jit(solution)/shard_map/ppermute | solution.py:268
  27.8 1.1 %collective-permute-start.7 = (bf16[128,256]{1,0:T(8,128)(2,1)S(1)}, bf16[128,256]{1,0:T(8,128)(2,1)S(1)}, u32[]{:S(2)}, u32[]{:S(2)}) collective-permute-start(bf16[128,256]{1,0:T(8,128)(2,1)S(1)} %get-tuple-element.54), channel_id=1, source_target_pairs={{0,4},{2,6},{4,0},{6,2},{1,5},{3,7},{5,1},{7,3},{8,12},{10,14},{12... | collective-permute-start | bytes 196616 | tf_op jit(solution)/shard_map/ppermute | solution.py:268
  28.9 0.0 collective-permute-start.8
  28.9 1.7 %collective-permute-done.5.refs_1_ = bf16[128,256]{1,0:T(8,128)(2,1)S(1)} collective-permute-done((bf16[128,256]{1,0:T(8,128)(2,1)S(1)}, bf16[128,256]{1,0:T(8,128)(2,1)S(1)}, u32[]{:S(2)}, u32[]{:S(2)}) %collective-permute-start.5) | collective-permute-done | bytes 65568 | tf_op jit(solution)/shard_map/ppermute | solution.py:268
  30.6 0.0 collective-permute-start.9
  30.6 0.2 collective-permute-done.6.refs_2_
  30.8 0.3 collective-permute-start.10
  31.1 1.0 %collective-permute-done.7.refs_3_ = bf16[128,256]{1,0:T(8,128)(2,1)S(1)} collective-permute-done((bf16[128,256]{1,0:T(8,128)(2,1)S(1)}, bf16[128,256]{1,0:T(8,128)(2,1)S(1)}, u32[]{:S(2)}, u32[]{:S(2)}) %collective-permute-start.7) | collective-permute-done | bytes 65568 | tf_op jit(solution)/shard_map/ppermute | solution.py:268
  32.1 0.0 collective-permute-start.11
  32.1 0.0 collective-permute-done.8.refs_4_
  32.1 0.0 collective-permute-done.9.refs_5_
  32.1 0.0 collective-permute-done.10.refs_6_
  32.1 1.2 %collective-permute-done.11.refs_7_ = bf16[128,256]{1,0:T(8,128)(2,1)S(1)} collective-permute-done((bf16[128,256]{1,0:T(8,128)(2,1)S(1)}, bf16[128,256]{1,0:T(8,128)(2,1)S(1)}, u32[]{:S(2)}, u32[]{:S(2)}) %collective-permute-start.11) | collective-permute-done | bytes 65568 | tf_op jit(solution)/shard_map/ppermute | solution.py:268
  33.4 1.2 %project.1 = bf16[512,256]{1,0:T(8,128)(2,1)} custom-call(bf16[2,512,512]{2,1,0:T(8,128)(2,1)S(1)} %get-tuple-element.43.turned_ref, bf16[128,256]{1,0:T(8,128)(2,1)S(1)} %get-tuple-element.51.refs_0_, bf16[128,256]{1,0:T(8,128)(2,1)S(1)} %collective-permute-done.5.refs_1_, bf16[128,256]{1,0:T(8,128)(2,1)S(1)} %collective-permute-done.6.refs_2_, ...), custom_call_target="tpu_custom_call" | custom-call | tf_op jit(solution)/shard_map/project/pallas_call | solution.py:387
  (3 shorter events, 0.1 us)
Async XLA Ops:
  1.2 8.0 %collective-permute-start = (bf16[784,128]{1,0:T(8,128)(2,1)S(1)}, bf16[784,128]{1,0:T(8,128)(2,1)S(1)}, u32[]{:S(2)}, u32[]{:S(2)}) collective-permute-start(bf16[784,128]{1,0:T(8,128)(2,1)S(1)} %get-tuple-element.31), channel_id=1, source_target_pairs={{0,2},{2,0},{4,6},{6,4},{1,3},{3,1},{5,7},{7,5},{8,10},{10,8},{12,... | collective-permute-start | bytes 602120 | tf_op jit(solution)/shard_map/ppermute | solution.py:268
  4.2 6.4 %collective-permute-start.1 = (bf16[784,128]{1,0:T(8,128)(2,1)S(1)}, bf16[784,128]{1,0:T(8,128)(2,1)S(1)}, u32[]{:S(2)}, u32[]{:S(2)}) collective-permute-start(bf16[784,128]{1,0:T(8,128)(2,1)S(1)} %get-tuple-element.33), channel_id=1, source_target_pairs={{0,4},{2,6},{4,0},{6,2},{1,5},{3,7},{5,1},{7,3},{8,12},{10,14},{12... | collective-permute-start | bytes 602120 | tf_op jit(solution)/shard_map/ppermute | solution.py:268
  10.7 6.7 %collective-permute-start.2 = (bf16[784,128]{1,0:T(8,128)(2,1)S(1)}, bf16[784,128]{1,0:T(8,128)(2,1)S(1)}, u32[]{:S(2)}, u32[]{:S(2)}) collective-permute-start(bf16[784,128]{1,0:T(8,128)(2,1)S(1)} %get-tuple-element.35), channel_id=1, source_target_pairs={{0,6},{2,4},{4,2},{6,0},{1,7},{3,5},{5,3},{7,1},{8,14},{10,12},{12... | collective-permute-start | bytes 602120 | tf_op jit(solution)/shard_map/ppermute | solution.py:268
  12.3 9.8 %collective-permute-start.3 = (bf16[2,512,128]{2,1,0:T(8,128)(2,1)S(1)}, bf16[2,512,128]{2,1,0:T(8,128)(2,1)S(1)}, u32[]{:S(2)}, u32[]{:S(2)}) collective-permute-start(bf16[2,512,128]{2,1,0:T(8,128)(2,1)S(1)} %pad_maximum_fusion), channel_id=1, source_target_pairs={{0,8},{8,16},{16,24},{24,0},{1,9},{9,17},{17,25},{25,1},{2,10},{10... | collective-permute-start | bytes 786440 | tf_op jit(solution)/shard_map/ppermute | solution.py:337
  17.4 6.8 %collective-permute-start.4 = (bf16[1,512,128]{2,1,0:T(8,128)(2,1)S(1)}, bf16[1,512,128]{2,1,0:T(8,128)(2,1)S(1)}, u32[]{:S(2)}, u32[]{:S(2)}) collective-permute-start(bf16[1,512,128]{2,1,0:T(8,128)(2,1)S(1)} %fusion.1), channel_id=1, source_target_pairs={{0,8},{8,16},{16,24},{24,0},{1,9},{9,17},{17,25},{25,1},{2,10},{10... | collective-permute-start | bytes 393224 | tf_op jit(solution)/shard_map/ppermute | solution.py:337
  25.3 5.2 %collective-permute-start.5 = (bf16[128,256]{1,0:T(8,128)(2,1)S(1)}, bf16[128,256]{1,0:T(8,128)(2,1)S(1)}, u32[]{:S(2)}, u32[]{:S(2)}) collective-permute-start(bf16[128,256]{1,0:T(8,128)(2,1)S(1)} %get-tuple-element.52), channel_id=1, source_target_pairs={{0,6},{2,4},{4,2},{6,0},{1,7},{3,5},{5,3},{7,1},{8,14},{10,12},{12... | collective-permute-start | bytes 196616 | tf_op jit(solution)/shard_map/ppermute | solution.py:268
  26.4 4.4 %collective-permute-start.6 = (bf16[128,256]{1,0:T(8,128)(2,1)S(1)}, bf16[128,256]{1,0:T(8,128)(2,1)S(1)}, u32[]{:S(2)}, u32[]{:S(2)}) collective-permute-start(bf16[128,256]{1,0:T(8,128)(2,1)S(1)} %get-tuple-element.53), channel_id=1, source_target_pairs={{0,2},{2,0},{4,6},{6,4},{1,3},{3,1},{5,7},{7,5},{8,10},{10,8},{12,... | collective-permute-start | bytes 196616 | tf_op jit(solution)/shard_map/ppermute | solution.py:268
  27.8 4.3 %collective-permute-start.7 = (bf16[128,256]{1,0:T(8,128)(2,1)S(1)}, bf16[128,256]{1,0:T(8,128)(2,1)S(1)}, u32[]{:S(2)}, u32[]{:S(2)}) collective-permute-start(bf16[128,256]{1,0:T(8,128)(2,1)S(1)} %get-tuple-element.54), channel_id=1, source_target_pairs={{0,4},{2,6},{4,0},{6,2},{1,5},{3,7},{5,1},{7,3},{8,12},{10,14},{12... | collective-permute-start | bytes 196616 | tf_op jit(solution)/shard_map/ppermute | solution.py:268
  28.9 3.2 %collective-permute-start.8 = (bf16[128,256]{1,0:T(8,128)(2,1)S(1)}, bf16[128,256]{1,0:T(8,128)(2,1)S(1)}, u32[]{:S(2)}, u32[]{:S(2)}) collective-permute-start(bf16[128,256]{1,0:T(8,128)(2,1)S(1)} %get-tuple-element.51.refs_0_), channel_id=1, source_target_pairs={{0,1},{1,0},{2,3},{3,2},{4,5},{5,4},{6,7},{7,6},{8,9},{9,8},{10,11... | collective-permute-start | bytes 196616 | tf_op jit(solution)/shard_map/ppermute | solution.py:268
  30.6 1.5 %collective-permute-start.9 = (bf16[128,256]{1,0:T(8,128)(2,1)S(1)}, bf16[128,256]{1,0:T(8,128)(2,1)S(1)}, u32[]{:S(2)}, u32[]{:S(2)}) collective-permute-start(bf16[128,256]{1,0:T(8,128)(2,1)S(1)} %collective-permute-done.5.refs_1_), channel_id=1, source_target_pairs={{0,1},{1,0},{2,3},{3,2},{4,5},{5,4},{6,7},{7,6},{8,9},{9,8},{10,11... | collective-permute-start | bytes 196616 | tf_op jit(solution)/shard_map/ppermute | solution.py:268
  30.8 1.3 %collective-permute-start.10 = (bf16[128,256]{1,0:T(8,128)(2,1)S(1)}, bf16[128,256]{1,0:T(8,128)(2,1)S(1)}, u32[]{:S(2)}, u32[]{:S(2)}) collective-permute-start(bf16[128,256]{1,0:T(8,128)(2,1)S(1)} %collective-permute-done.6.refs_2_), channel_id=1, source_target_pairs={{0,1},{1,0},{2,3},{3,2},{4,5},{5,4},{6,7},{7,6},{8,9},{9,8},{10,11... | collective-permute-start | bytes 196616 | tf_op jit(solution)/shard_map/ppermute | solution.py:268
  32.1 1.3 %collective-permute-start.11 = (bf16[128,256]{1,0:T(8,128)(2,1)S(1)}, bf16[128,256]{1,0:T(8,128)(2,1)S(1)}, u32[]{:S(2)}, u32[]{:S(2)}) collective-permute-start(bf16[128,256]{1,0:T(8,128)(2,1)S(1)} %collective-permute-done.7.refs_3_), channel_id=1, source_target_pairs={{0,1},{1,0},{2,3},{3,2},{4,5},{5,4},{6,7},{7,6},{8,9},{9,8},{10,11... | collective-permute-start | bytes 196616 | tf_op jit(solution)/shard_map/ppermute | solution.py:268

commit v5 on v2

v5 whole, which is shorter than its diff:
```python
import functools

import jax
import jax.numpy as jnp
from jax import lax
from jax.experimental import pallas as pl
from jax.experimental.pallas import tpu as pltpu
from jax.sharding import Mesh, PartitionSpec as P

HEADS = 8
HD = 128
TILE = 128
SLOTS = 2
STEPS = 4
LOG2E = 1.4426950408889634
SCALE = LOG2E * HD ** (-0.5)
MASKED = -1e30
EXTRA = 16
NEAR = 10**9
MORE = 1
FAR = 10**9
VMEM = pl.BlockSpec(memory_space=pltpu.VMEM)
HBM = pl.BlockSpec(memory_space=pltpu.HBM)
PARAMS = pltpu.CompilerParams(vmem_limit_bytes=48 * 1024 * 1024)


def use_rows(index_ref, count_ref, tiles):
    row = lax.broadcasted_iota(jnp.int32, (EXTRA, HD), 0)
    uses = jnp.zeros((EXTRA, HD), jnp.float32)
    for turn in range(STEPS):
        for dest in range(tiles):
            for source in range(tiles):
                times = jnp.float32(0)
                for slot in range(SLOTS):
                    used = (slot < count_ref[dest, turn]) & (index_ref[dest, slot, turn] == source)
                    times += jnp.where(used, 1.0, 0.0)
                uses = jnp.where(row == (turn * tiles + dest) * tiles + source, times, uses)
    return uses


def pack_kernel(query_ref, key_ref, value_ref, index_ref, count_ref, *refs):
    out_refs, (values, index, count, sem) = refs[:-4], refs[-4:]
    rows, width = query_ref.shape
    group = width // HD
    tiles = rows // TILE
    place = lax.axis_index("place")
    value_copy = pltpu.make_async_copy(value_ref, values, sem.at[0])
    value_copy.start()
    table_copies = [
        pltpu.make_async_copy(index_ref, index, sem.at[1]),
        pltpu.make_async_copy(count_ref, count, sem.at[2]),
    ]
    for copy in table_copies:
        copy.start()
    copies = []
    for step in range(group):
        cols = pl.ds(pl.multiple_of(jnp.bitwise_xor(place, step) * HD, HD), HD)
        out = out_refs[step]
        copies += [
            pltpu.make_async_copy(
                key_ref.at[:, cols], out.at[pl.ds(0, rows)], sem.at[3 + 2 * step]
            ),
            pltpu.make_async_copy(
                query_ref.at[:, cols], out.at[pl.ds(2 * rows, rows)], sem.at[4 + 2 * step]
            ),
        ]
    for copy in copies:
        copy.start()
    for copy in table_copies:
        copy.wait()
    uses = use_rows(index, count, tiles).astype(jnp.bfloat16)
    value_copy.wait()
    for step in range(group):
        cols = pl.ds(pl.multiple_of(jnp.bitwise_xor(place, step) * HD, HD), HD)
        out = out_refs[step]
        out[3 * rows :] = uses
        for at in range(0, rows, TILE):
            out[rows + at : rows + at + TILE] = values[at : at + TILE, cols].T
    for copy in copies:
        copy.wait()


def use_bias(block_ref, rows, turn):
    tiles = rows // TILE
    uses = block_ref[3 * rows :].astype(jnp.float32)
    per_turn = tiles * tiles
    times = uses[:per_turn]
    for other in range(1, STEPS):
        times = jnp.where(turn == other, uses[other * per_turn : (other + 1) * per_turn], times)
    return jnp.where(times > 0.5, times - 1.0, MASKED)


def pair_scores(keys, block_ref, rows, turn):
    tiles = rows // TILE
    raw = (
        lax.dot_general(
            keys,
            block_ref[2 * rows : 3 * rows],
            (((1,), (1,)), ((), ())),
            preferred_element_type=jnp.float32,
        )
        * SCALE
    )
    bias = use_bias(block_ref, rows, turn)
    parts = []
    for source in range(tiles):
        line = jnp.concatenate(
            [bias[tile * tiles + source : tile * tiles + source + 1] for tile in range(tiles)],
            axis=1,
        )
        parts.append(raw[source * TILE : (source + 1) * TILE] + line)
    return raw, jnp.concatenate(parts, axis=0)


def add_source(score, values, top, total, mixed):
    weights = jnp.exp2(score - top)
    total = total + jnp.sum(weights, axis=0, keepdims=True)
    mixed = mixed + jnp.dot(
        values, weights.astype(jnp.bfloat16), preferred_element_type=jnp.float32
    )
    return total, mixed


def turned_values(source_ref, rows):
    return jnp.concatenate(
        [source_ref[rows + at : rows + at + TILE] for at in range(0, rows, TILE)], axis=1
    )


def start_slab(block_ref, step, mixed_ref, state_ref):
    rows = mixed_ref.shape[2]
    raw, score = pair_scores(block_ref[:rows], block_ref, rows, 0)
    eye = lax.broadcasted_iota(jnp.int32, (TILE, TILE), 0) == lax.broadcasted_iota(
        jnp.int32, (TILE, TILE), 1
    )
    own = jnp.concatenate(
        [
            jnp.sum(
                jnp.where(eye, raw[at : at + TILE, at : at + TILE], 0.0), axis=0, keepdims=True
            )
            for at in range(0, rows, TILE)
        ],
        axis=1,
    )
    top = jnp.maximum(own, jnp.max(score, axis=0, keepdims=True))
    weight = jnp.exp2(own - top)
    values = turned_values(block_ref, rows)
    total, mixed = add_source(score, values, top, weight, weight * values.astype(jnp.float32))
    mixed_ref[step] = mixed
    state_ref[step, 0:1] = top
    state_ref[step, 1:2] = total


def add_slab(block_ref, source_ref, turn, step, mixed_ref, state_ref):
    rows = mixed_ref.shape[2]
    score = pair_scores(source_ref[:rows], block_ref, rows, turn)[1]
    before = state_ref[step, 0:1]
    top = jnp.maximum(before, jnp.max(score, axis=0, keepdims=True))
    factor = jnp.exp2(before - top)
    total, mixed = add_source(
        score,
        turned_values(source_ref, rows),
        top,
        state_ref[step, 1:2] * factor,
        mixed_ref[step] * factor,
    )
    mixed_ref[step] = mixed
    state_ref[step, 0:1] = top
    state_ref[step, 1:2] = total


def add_pairs(place, steps, fresh, blocks, mixed_ref, state_ref):
    for step in fresh:
        start_slab(blocks[step], step, mixed_ref, state_ref)
    for one in steps:
        for two in fresh:
            if two in steps[: steps.index(one) + 1]:
                continue
            ahead = jnp.bitwise_xor(place, one) - jnp.bitwise_xor(place, two)

            @pl.when(ahead > 0)
            def _(one=one, two=two, ahead=ahead):
                add_slab(blocks[one], blocks[two], ahead, one, mixed_ref, state_ref)

            @pl.when(ahead < 0)
            def _(one=one, two=two, ahead=ahead):
                add_slab(blocks[two], blocks[one], -ahead, two, mixed_ref, state_ref)


def near_kernel(*refs, steps, head_total):
    blocks, weight_ref = refs[: len(steps)], refs[len(steps)]
    mixed_ref, state_ref, turned_ref, held, sem = refs[len(steps) + 1 :]
    me = lax.axis_index("head")
    depth = weight_ref.shape[0] // head_total
    features = weight_ref.shape[1] // head_total
    copies = []
    for other in range(head_total):
        start = pl.multiple_of(jnp.bitwise_xor(me, other) * depth, depth)
        cols = pl.ds(pl.multiple_of(me * features, features), features)
        copies.append(
            pltpu.make_async_copy(
                weight_ref.at[pl.ds(start, depth), cols], held.at[other], sem.at[other]
            )
        )
        copies[-1].start()
    add_pairs(lax.axis_index("place"), steps, steps, blocks, mixed_ref, state_ref)
    for other in range(head_total):
        copies[other].wait()
        turned_ref[other] = held[other].T


def more_kernel(*refs, group, fresh):
    blocks, (mixed_ref, state_ref, mixed_out, state_out) = refs[:group], refs[group:]
    for step in range(group):
        if step not in fresh:
            mixed_out[step] = mixed_ref[step]
            state_out[step] = state_ref[step]
    steps = list(range(group))
    add_pairs(lax.axis_index("place"), steps, fresh, blocks, mixed_out, state_out)


def far_kernel(*refs, group, halo, ready, last):
    blocks, (mixed_ref, state_ref) = refs[:group], refs[group : group + 2]
    pieces = refs[group + 2 : group + 2 + len(halo)]
    outs = refs[group + 2 + len(halo) :]
    out_refs, (mixed_out, state_out) = outs[: len(ready)], outs[len(ready) :]
    place = lax.axis_index("place")
    mixed_out[...] = mixed_ref[...]
    state_out[...] = state_ref[...]
    for piece_ref, (offset, choices) in zip(pieces, halo):
        for low in range(piece_ref.shape[0]):
            slabs = [choice[low] ^ at if choice else group for at, choice in enumerate(choices)]
            ahead = offset * group - pick(place, slabs)
            for step in range(group):
                turn = jnp.bitwise_xor(place, step) + ahead
                used = (turn < STEPS) & (turn > 0)

                @pl.when(used & (ahead > (offset - 1) * group))
                def _(low=low, step=step, turn=turn, piece_ref=piece_ref):
                    add_slab(
                        blocks[step], piece_ref.at[low], turn, step, mixed_out, state_out
                    )

    for step, out_ref in zip(ready, out_refs):
        out_ref[...] = (mixed_out[step] / state_out[step, 1:2]).astype(out_ref.dtype)


def hops(step):
    return step.bit_count()


def sending_order(group):
    return sorted(range(group), key=lambda step: (step > 0, -hops(step), step))


def halo_messages(group):
    messages = []
    for offset in range(1, -(-(STEPS - 1) // group) + 1):
        first = max(0, offset * group - STEPS + 1)
        early, late = [], []
        for place in range(group):
            needed = [step for step in range(group) if place ^ step >= first]
            early.append([step for step in needed if hops(step) < 2])
            late.append([step for step in needed if hops(step) > 1])
        common = min(len(steps) for steps in early)
        parts = [(False, [steps[:common] for steps in early])]
        parts += [(False, [steps[common:] for steps in early]), (True, late)]
        messages += [(is_late, offset, choices) for is_late, choices in parts if any(choices)]
    return messages


def pick(place, choices):
    result = jnp.int32(choices[-1])
    for at, choice in enumerate(choices[:-1]):
        result = jnp.where(place == at, jnp.int32(choice), result)
    return result


def project_kernel(turned_ref, *refs, group, head_total):
    mix_refs, out_ref, mix = refs[:-2], refs[-2], refs[-1]
    place = lax.axis_index("place")
    for other in range(head_total):
        for at, step in enumerate(sending_order(group)):
            mix[other, jnp.bitwise_xor(place, step)] = mix_refs[other * group + at][...]
    result = None
    for other in range(head_total):
        part = jnp.dot(
            turned_ref[other],
            mix[other].reshape(turned_ref.shape[2], out_ref.shape[1]),
            preferred_element_type=jnp.float32,
        )
        result = part if result is None else result + part
    out_ref[...] = result.astype(out_ref.dtype)


def swapped(value, axis, step):
    count = lax.axis_size(axis)
    return lax.ppermute(value, axis, [(source, source ^ step) for source in range(count)])


def halo_message(got, place, choices, rows):
    length = max(len(steps) for steps in choices)
    parts = []
    for low in range(length):
        steps = [choice[low] if choice else None for choice in choices]
        known = [step for step in steps if step is not None]
        piece = got[known[-1]][: 2 * rows]
        for at, step in enumerate(steps):
            if step is not None and step != known[-1]:
                piece = jnp.where(place == at, got[step][: 2 * rows], piece)
        parts.append(piece)
    return jnp.stack(parts)


def on_device(node_queries, node_keys, node_values, tile_index, tile_count, out_weight):
    rows, width = node_queries.shape
    group = width // HD
    groups = lax.axis_size("group")
    head_total = lax.axis_size("head")
    depth, feature_total = out_weight.shape
    features = feature_total // head_total
    bf16, f32 = jnp.bfloat16, jnp.float32
    shape = jax.ShapeDtypeStruct
    place = lax.axis_index("place")

    packed = pl.pallas_call(
        pack_kernel,
        out_shape=[shape((3 * rows + EXTRA, HD), bf16)] * group,
        in_specs=[HBM] * 5,
        out_specs=[VMEM] * group,
        scratch_shapes=[
            pltpu.VMEM((rows, width), bf16),
            pltpu.SMEM((rows // TILE, SLOTS, STEPS), jnp.int32),
            pltpu.SMEM((rows // TILE, STEPS), jnp.int32),
            pltpu.SemaphoreType.DMA((3 + 2 * group,)),
        ],
        compiler_params=PARAMS,
        name="pack",
    )(
        *[
            pltpu.with_memory_space_constraint(array, pltpu.HBM)
            for array in (
                node_queries,
                node_keys,
                node_values,
                jnp.transpose(tile_index, (1, 2, 0)),
                jnp.transpose(tile_count, (1, 0)),
            )
        ],
    )

    state_shapes = [shape((group, HD, rows), f32), shape((group, 8, rows), f32)]
    first_steps = [step for step in range(group) if hops(step) < 2]
    rest = [step for step in range(group) if hops(step) > 1]
    got = [packed[0]]
    messages = halo_messages(group)
    sent = {False: [], True: []}
    for step in range(group):
        if step:
            block = packed[step]
            if hops(step) > 1:
                block, got[1] = lax.optimization_barrier((block, got[1]))
            got.append(swapped(block, "place", step))
        for late, offset, choices in messages:
            if step != max(max(steps, default=0) for steps in choices):
                continue
            pairs = [
                (at * group + p, (at + offset) % groups * group + p)
                for at in range(groups)
                for p in range(group)
                if choices[p]
            ]
            message = halo_message(got, place, choices, rows)
            if late:
                message, state = lax.optimization_barrier((message, state))
            message, *got = lax.optimization_barrier([message, *got])
            arrived = lax.ppermute(message, ("group", "place"), pairs)
            sent[late].append(((offset, choices), arrived))
        if step == first_steps[-1]:
            mixed, state, turned = pl.pallas_call(
                functools.partial(near_kernel, steps=first_steps, head_total=head_total),
                out_shape=[*state_shapes, shape((head_total, features, depth // head_total), bf16)],
                in_specs=[VMEM] * len(first_steps) + [HBM],
                out_specs=[VMEM] * 3,
                scratch_shapes=[
                    pltpu.VMEM((head_total, depth // head_total, features), bf16),
                    pltpu.SemaphoreType.DMA((head_total,)),
                ],
                compiler_params=PARAMS,
                cost_estimate=pl.CostEstimate(flops=NEAR, transcendentals=1, bytes_accessed=1),
                name="near",
            )(
                *[got[step] for step in first_steps],
                pltpu.with_memory_space_constraint(out_weight, pltpu.HBM),
            )

    if rest:
        mixed, state = pl.pallas_call(
            functools.partial(more_kernel, group=group, fresh=rest),
            out_shape=state_shapes,
            in_specs=[VMEM] * (group + 2),
            out_specs=[VMEM] * 2,
            compiler_params=PARAMS,
            cost_estimate=pl.CostEstimate(flops=MORE, transcendentals=1, bytes_accessed=1),
            name="more",
        )(*got, mixed, state)

    mix = {}
    for late in (False, True):
        if late and not sent[late]:
            continue
        last = late or not sent[True]
        ready = [s for s in range(group) if s not in mix and (last or hops(s) > 1)]
        state_out = [] if last else state_shapes
        outs = pl.pallas_call(
            functools.partial(
                far_kernel,
                group=group,
                halo=[entry[0] for entry in sent[late]],
                ready=ready,
                last=last,
            ),
            out_shape=[shape((HD, rows), bf16)] * len(ready) + state_out,
            in_specs=[VMEM] * (group + 2 + len(sent[late])),
            out_specs=[VMEM] * (len(ready) + len(state_out)),
            scratch_shapes=[pltpu.VMEM(s.shape, f32) for s in state_shapes] if last else [],
            compiler_params=PARAMS,
            cost_estimate=pl.CostEstimate(flops=FAR, transcendentals=1, bytes_accessed=1),
            name="far",
        )(*got, mixed, state, *[entry[1] for entry in sent[late]])
        mix.update(zip(ready, outs))
        for step in ready:
            if step:
                mix[step] = swapped(mix[step], "place", step)
        if not last:
            mixed, state = outs[len(ready) :]

    mixes = [mix[step] for step in sending_order(group)]
    for other in range(1, head_total):
        mixes += [swapped(entry, "head", other) for entry in mixes[:group]]
    return pl.pallas_call(
        functools.partial(project_kernel, group=group, head_total=head_total),
        out_shape=shape((features, rows), bf16),
        in_specs=[VMEM] * (1 + head_total * group),
        out_specs=VMEM,
        scratch_shapes=[pltpu.VMEM((head_total, group, HD, rows), bf16)],
        compiler_params=PARAMS,
        name="project",
    )(turned, *mixes)


def solution(mesh):
    nodes, heads = mesh.devices.shape
    place = HEADS // heads
    split = Mesh(
        mesh.devices.reshape(nodes // place, place, heads), ("group", "place", "head")
    )
    node = ("group", "place")
    return jax.shard_map(
        on_device,
        mesh=split,
        in_specs=(
            P(node, "head"),
            P(node, "head"),
            P(node, "head"),
            P(None, node, None),
            P(None, node),
            P(),
        ),
        out_specs=P("head", node),
        check_vma=False,
    )
```

time: 40.1 us -> 38 us (0.948)
  waiting for transfers between devices: 21.2 us -> 9.7 us
  starting transfers between devices: 11.4 us -> 18.4 us
  Pallas kernels: 5.69 us -> 9.56 us
  local copies, waits for them, and re-layouts: 1.59 us -> 0.02 us
    ppermute x3, waiting for transfers between devices: 7.09 us -> 0.01 us  [on_device(): arrived = lax.ppermute(message, ('group', 'place'), pairs)]
    ppermute x10, starting transfers between devices: 8.11 us -> 12.6 us  [swapped(): lax.ppermute(value, axis, [(source, source ^ step) for source in range(co...]
    ppermute x10, waiting for transfers between devices: 14.1 us -> 9.69 us  [swapped(): lax.ppermute(value, axis, [(source, source ^ step) for source in range(co...]
    pallas_call x2 -> x4, Pallas kernels: 3.29 us -> 7.16 us  [the longest x2 2.72 us: on_device(): pl.pallas_call(functools.partial(far_kernel, group=group, halo=[entry[0]...]
    ppermute x3, starting transfers between devices: 3.26 us -> 5.77 us  [on_device(): arrived = lax.ppermute(message, ('group', 'place'), pairs)]
    unnamed x2 -> x0, local copies, waits for them, and re-layouts: 1.59 us -> none
  transfers between devices with their start and end apart: 13 -> 13, of which waited for: 8 -> 8; matrix products, arithmetic and copies ran while one was open for 0% -> 0% of each run, Pallas kernels for 6% -> 19%
where the time goes in v5:
time: 38 us; the launch traced here: 37.9 us
  starting transfers between devices  18.4 us (48%)
  waiting for transfers between devices  9.7 us (26%)
  Pallas kernels  9.56 us (25%)
    ppermute x10, starting transfers between devices, swapped(): lax.ppermute(value, axis, [(source, source ^ step) for source in range(co...  12.6 us
    ppermute x10, waiting for transfers between devices, swapped(): lax.ppermute(value, axis, [(source, source ^ step) for source in range(co...  9.69 us
    ppermute x3, starting transfers between devices, on_device(): arrived = lax.ppermute(message, ('group', 'place'), pairs)  5.77 us
    pallas_call x2, Pallas kernels, on_device(): pl.pallas_call(functools.partial(far_kernel, group=group, halo=[entry[0]...  2.72 us
    pallas_call x1, Pallas kernels, on_device(): pl.pallas_call(functools.partial(near_kernel, steps=first_steps, head_tot...  2.69 us
    pallas_call x1, Pallas kernels, on_device(): pl.pallas_call(functools.partial(more_kernel, group=group, fresh=rest), o...  1.74 us
    pallas_call x1, Pallas kernels, on_device(): pl.pallas_call(pack_kernel, out_shape=[shape((3 * rows + EXTRA, HD), bf16...  1.21 us
    pallas_call x1, Pallas kernels, on_device(): pl.pallas_call(functools.partial(project_kernel, group=group, head_total=...  1.19 us
  transfers between devices with their start and end apart: 13, of which 8 were waited for; matrix products, arithmetic and copies ran while one was open for 0% of the time, Pallas kernels for 19%

profile of v5, /device:TPU:0, one launch (start us, length us, event | category | flops | bytes accessed | tf_op | source)
XLA Modules:
  0.0 37.9 jit_solution(1875198791096953488)
XLA Ops:
  0.0 1.2 %pack.1 = (bf16[784,128]{1,0:T(8,128)(2,1)S(1)}, bf16[784,128]{1,0:T(8,128)(2,1)S(1)}, bf16[784,128]{1,0:T(8,128)(2,1)S(1)}, bf16[784,128]{1,0:T(8,128)(2,1)S(1)}) custom-call(bf16[256,512]{1,0:T(8,128)(2,1)} %query_ref.1, bf16[256,512]{1,0:T(8,128)(2,1)} %key_ref.1, bf16[256,512]{1,0:T(8,128)(2,1)} %value_ref.1, s32[2,2,4]{2,1,0:T(2,128)} %bitcast.10, ...), custom_call_target="tpu_custom_call" | custom-call | tf_op jit(solution)/shard_map/pack/pallas_call | solution.py:326
  1.2 3.0 %collective-permute-start = (bf16[784,128]{1,0:T(8,128)(2,1)S(1)}, bf16[784,128]{1,0:T(8,128)(2,1)S(1)}, u32[]{:S(2)}, u32[]{:S(2)}) collective-permute-start(bf16[784,128]{1,0:T(8,128)(2,1)S(1)} %get-tuple-element.37), channel_id=1, source_target_pairs={{0,2},{2,0},{4,6},{6,4},{1,3},{3,1},{5,7},{7,5},{8,10},{10,8},{12,... | collective-permute-start | bytes 602120 | tf_op jit(solution)/shard_map/ppermute | solution.py:298
  4.2 1.5 %collective-permute-start.1 = (bf16[784,128]{1,0:T(8,128)(2,1)S(1)}, bf16[784,128]{1,0:T(8,128)(2,1)S(1)}, u32[]{:S(2)}, u32[]{:S(2)}) collective-permute-start(bf16[784,128]{1,0:T(8,128)(2,1)S(1)} %get-tuple-element.39), channel_id=1, source_target_pairs={{0,4},{2,6},{4,0},{6,2},{1,5},{3,7},{5,1},{7,3},{8,12},{10,14},{12... | collective-permute-start | bytes 602120 | tf_op jit(solution)/shard_map/ppermute | solution.py:298
  5.7 3.5 %collective-permute-done.refs_1_ = bf16[784,128]{1,0:T(8,128)(2,1)S(1)} collective-permute-done((bf16[784,128]{1,0:T(8,128)(2,1)S(1)}, bf16[784,128]{1,0:T(8,128)(2,1)S(1)}, u32[]{:S(2)}, u32[]{:S(2)}) %collective-permute-start) | collective-permute-done | bytes 200736 | tf_op jit(solution)/shard_map/ppermute | solution.py:298
  9.2 1.5 %collective-permute-done.1.refs_2_ = bf16[784,128]{1,0:T(8,128)(2,1)S(1)} collective-permute-done((bf16[784,128]{1,0:T(8,128)(2,1)S(1)}, bf16[784,128]{1,0:T(8,128)(2,1)S(1)}, u32[]{:S(2)}, u32[]{:S(2)}) %collective-permute-start.1) | collective-permute-done | bytes 200736 | tf_op jit(solution)/shard_map/ppermute | solution.py:298
  10.8 1.6 %collective-permute-start.2 = (bf16[784,128]{1,0:T(8,128)(2,1)S(1)}, bf16[784,128]{1,0:T(8,128)(2,1)S(1)}, u32[]{:S(2)}, u32[]{:S(2)}) collective-permute-start(bf16[784,128]{1,0:T(8,128)(2,1)S(1)} %get-tuple-element.48), channel_id=1, source_target_pairs={{0,6},{2,4},{4,2},{6,0},{1,7},{3,5},{5,3},{7,1},{8,14},{10,12},{12... | collective-permute-start | bytes 602120 | tf_op jit(solution)/shard_map/ppermute | solution.py:298
  12.3 0.7 %collective-permute-start.4 = (bf16[1,512,128]{2,1,0:T(8,128)(2,1)S(1)}, bf16[1,512,128]{2,1,0:T(8,128)(2,1)S(1)}, u32[]{:S(2)}, u32[]{:S(2)}) collective-permute-start(bf16[1,512,128]{2,1,0:T(8,128)(2,1)S(1)} %slice_bitcast_fusion.1), channel_id=1, source_target_pairs={{6,14},{14,22},{22,30},{30,6},{7,15},{15,23},{23,31},{31,7}} | collective-permute-start | bytes 393224 | tf_op jit(solution)/shard_map/ppermute | solution.py:377
  13.0 1.6 %collective-permute-start.3 = (bf16[2,512,128]{2,1,0:T(8,128)(2,1)S(1)}, bf16[2,512,128]{2,1,0:T(8,128)(2,1)S(1)}, u32[]{:S(2)}, u32[]{:S(2)}) collective-permute-start(bf16[2,512,128]{2,1,0:T(8,128)(2,1)S(1)} %pad_maximum_fusion), channel_id=1, source_target_pairs={{0,8},{2,10},{4,12},{6,14},{8,16},{10,18},{12,20},{14,22},{16,24},... | collective-permute-start | bytes 786440 | tf_op jit(solution)/shard_map/ppermute | solution.py:377
  14.6 2.7 %near.1 = (f32[4,128,256]{2,1,0:T(8,128)S(1)}, f32[4,8,256]{2,1,0:T(8,128)S(1)}, bf16[2,512,512]{2,1,0:T(8,128)(2,1)S(1)}) custom-call(bf16[784,128]{1,0:T(8,128)(2,1)S(1)} %get-tuple-element.52.refs_0_, bf16[784,128]{1,0:T(8,128)(2,1)S(1)} %collective-permute-done.refs_1_, bf16[784,128]{1,0:T(8,128)(2,1)S(1)} %collective-permute-done.1.refs_2_, ...), custom_call_target="tpu_custom_call" | custom-call | flops 1000000000 | bytes 1 | tf_op jit(solution)/shard_map/near/pallas_call | solution.py:380
  17.3 0.1 collective-permute-done.2.refs_3_
  17.4 3.5 %collective-permute-start.5 = (bf16[1,512,128]{2,1,0:T(8,128)(2,1)S(1)}, bf16[1,512,128]{2,1,0:T(8,128)(2,1)S(1)}, u32[]{:S(2)}, u32[]{:S(2)}) collective-permute-start(bf16[1,512,128]{2,1,0:T(8,128)(2,1)S(1)} %slice_bitcast_fusion), channel_id=1, source_target_pairs={{0,8},{2,10},{4,12},{8,16},{10,18},{12,20},{16,24},{18,26},{20,28}... | collective-permute-start | bytes 393224 | tf_op jit(solution)/shard_map/ppermute | solution.py:377
  20.9 1.7 %more.1 = (f32[4,128,256]{2,1,0:T(8,128)S(1)}, f32[4,8,256]{2,1,0:T(8,128)S(1)}) custom-call(bf16[784,128]{1,0:T(8,128)(2,1)S(1)} %get-tuple-element.52.refs_0_, bf16[784,128]{1,0:T(8,128)(2,1)S(1)} %collective-permute-done.refs_1_, bf16[784,128]{1,0:T(8,128)(2,1)S(1)} %collective-permute-done.1.refs_2_, ...), custom_call_target="tpu_custom_call" | custom-call | flops 1 | bytes 1 | tf_op jit(solution)/shard_map/more/pallas_call | solution.py:398
  22.7 0.0 collective-permute-done.4.refs_7_
  22.7 0.0 collective-permute-done.3.refs_6_
  22.7 1.4 %far.2 = (bf16[128,256]{1,0:T(8,128)(2,1)S(1)}, f32[4,128,256]{2,1,0:T(8,128)S(1)}, f32[4,8,256]{2,1,0:T(8,128)S(1)}) custom-call(bf16[784,128]{1,0:T(8,128)(2,1)S(1)} %get-tuple-element.52.refs_0_, bf16[784,128]{1,0:T(8,128)(2,1)S(1)} %collective-permute-done.refs_1_, bf16[784,128]{1,0:T(8,128)(2,1)S(1)} %collective-permute-done.1.refs_2_, ...), custom_call_target="tpu_custom_call" | custom-call | flops 1000000000 | bytes 1 | tf_op jit(solution)/shard_map/far/pallas_call | solution.py:415
  24.1 5.5 %collective-permute-start.6 = (bf16[128,256]{1,0:T(8,128)(2,1)S(1)}, bf16[128,256]{1,0:T(8,128)(2,1)S(1)}, u32[]{:S(2)}, u32[]{:S(2)}) collective-permute-start(bf16[128,256]{1,0:T(8,128)(2,1)S(1)} %get-tuple-element.66), channel_id=1, source_target_pairs={{0,6},{2,4},{4,2},{6,0},{1,7},{3,5},{5,3},{7,1},{8,14},{10,12},{12... | collective-permute-start | bytes 196616 | tf_op jit(solution)/shard_map/ppermute | solution.py:298
  29.6 0.0 collective-permute-done.5.refs_6_
  29.6 1.3 %far.3 = (bf16[128,256]{1,0:T(8,128)(2,1)S(1)}, bf16[128,256]{1,0:T(8,128)(2,1)S(1)}, bf16[128,256]{1,0:T(8,128)(2,1)S(1)}) custom-call(bf16[784,128]{1,0:T(8,128)(2,1)S(1)} %get-tuple-element.52.refs_0_, bf16[784,128]{1,0:T(8,128)(2,1)S(1)} %collective-permute-done.refs_1_, bf16[784,128]{1,0:T(8,128)(2,1)S(1)} %collective-permute-done.1.refs_2_, ...), custom_call_target="tpu_custom_call" | custom-call | flops 1000000000 | bytes 1 | tf_op jit(solution)/shard_map/far/pallas_call | solution.py:415
  30.9 0.1 collective-permute-start.7
  31.0 0.1 collective-permute-start.8
  31.1 0.8 %collective-permute-done.6.refs_1_ = bf16[128,256]{1,0:T(8,128)(2,1)S(1)} collective-permute-done((bf16[128,256]{1,0:T(8,128)(2,1)S(1)}, bf16[128,256]{1,0:T(8,128)(2,1)S(1)}, u32[]{:S(2)}, u32[]{:S(2)}) %collective-permute-start.6) | collective-permute-done | bytes 65568 | tf_op jit(solution)/shard_map/ppermute | solution.py:298
  31.9 0.0 collective-permute-start.10
  31.9 0.5 %collective-permute-start.9 = (bf16[128,256]{1,0:T(8,128)(2,1)S(1)}, bf16[128,256]{1,0:T(8,128)(2,1)S(1)}, u32[]{:S(2)}, u32[]{:S(2)}) collective-permute-start(bf16[128,256]{1,0:T(8,128)(2,1)S(1)} %get-tuple-element.65.refs_0_), channel_id=1, source_target_pairs={{0,1},{1,0},{2,3},{3,2},{4,5},{5,4},{6,7},{7,6},{8,9},{9,8},{10,11... | collective-permute-start | bytes 196616 | tf_op jit(solution)/shard_map/ppermute | solution.py:298
  32.4 2.8 %collective-permute-done.7.refs_2_ = bf16[128,256]{1,0:T(8,128)(2,1)S(1)} collective-permute-done((bf16[128,256]{1,0:T(8,128)(2,1)S(1)}, bf16[128,256]{1,0:T(8,128)(2,1)S(1)}, u32[]{:S(2)}, u32[]{:S(2)}) %collective-permute-start.7) | collective-permute-done | bytes 65568 | tf_op jit(solution)/shard_map/ppermute | solution.py:298
  35.3 0.0 collective-permute-start.11
  35.3 0.1 collective-permute-done.8.refs_3_
  35.3 0.4 %collective-permute-start.12 = (bf16[128,256]{1,0:T(8,128)(2,1)S(1)}, bf16[128,256]{1,0:T(8,128)(2,1)S(1)}, u32[]{:S(2)}, u32[]{:S(2)}) collective-permute-start(bf16[128,256]{1,0:T(8,128)(2,1)S(1)} %collective-permute-done.8.refs_3_), channel_id=1, source_target_pairs={{0,1},{1,0},{2,3},{3,2},{4,5},{5,4},{6,7},{7,6},{8,9},{9,8},{10,11... | collective-permute-start | bytes 196616 | tf_op jit(solution)/shard_map/ppermute | solution.py:298
  35.8 0.0 collective-permute-done.10.refs_5_
  35.8 0.0 collective-permute-done.9.refs_4_
  35.8 0.7 %collective-permute-done.11.refs_6_ = bf16[128,256]{1,0:T(8,128)(2,1)S(1)} collective-permute-done((bf16[128,256]{1,0:T(8,128)(2,1)S(1)}, bf16[128,256]{1,0:T(8,128)(2,1)S(1)}, u32[]{:S(2)}, u32[]{:S(2)}) %collective-permute-start.11) | collective-permute-done | bytes 65568 | tf_op jit(solution)/shard_map/ppermute | solution.py:298
  36.5 0.2 collective-permute-done.12.refs_7_
  36.7 1.2 %project.1 = bf16[512,256]{1,0:T(8,128)(2,1)} custom-call(bf16[2,512,512]{2,1,0:T(8,128)(2,1)S(1)} %get-tuple-element.46.turned_ref, bf16[128,256]{1,0:T(8,128)(2,1)S(1)} %get-tuple-element.65.refs_0_, bf16[128,256]{1,0:T(8,128)(2,1)S(1)} %collective-permute-done.6.refs_1_, bf16[128,256]{1,0:T(8,128)(2,1)S(1)} %collective-permute-done.7.refs_2_, ...), custom_call_target="tpu_custom_call" | custom-call | tf_op jit(solution)/shard_map/project/pallas_call | solution.py:441
  (4 shorter events, 0.1 us)
Async XLA Ops:
  1.2 8.0 %collective-permute-start = (bf16[784,128]{1,0:T(8,128)(2,1)S(1)}, bf16[784,128]{1,0:T(8,128)(2,1)S(1)}, u32[]{:S(2)}, u32[]{:S(2)}) collective-permute-start(bf16[784,128]{1,0:T(8,128)(2,1)S(1)} %get-tuple-element.37), channel_id=1, source_target_pairs={{0,2},{2,0},{4,6},{6,4},{1,3},{3,1},{5,7},{7,5},{8,10},{10,8},{12,... | collective-permute-start | bytes 602120 | tf_op jit(solution)/shard_map/ppermute | solution.py:298
  4.2 6.4 %collective-permute-start.1 = (bf16[784,128]{1,0:T(8,128)(2,1)S(1)}, bf16[784,128]{1,0:T(8,128)(2,1)S(1)}, u32[]{:S(2)}, u32[]{:S(2)}) collective-permute-start(bf16[784,128]{1,0:T(8,128)(2,1)S(1)} %get-tuple-element.39), channel_id=1, source_target_pairs={{0,4},{2,6},{4,0},{6,2},{1,5},{3,7},{5,1},{7,3},{8,12},{10,14},{12... | collective-permute-start | bytes 602120 | tf_op jit(solution)/shard_map/ppermute | solution.py:298
  10.8 6.7 %collective-permute-start.2 = (bf16[784,128]{1,0:T(8,128)(2,1)S(1)}, bf16[784,128]{1,0:T(8,128)(2,1)S(1)}, u32[]{:S(2)}, u32[]{:S(2)}) collective-permute-start(bf16[784,128]{1,0:T(8,128)(2,1)S(1)} %get-tuple-element.48), channel_id=1, source_target_pairs={{0,6},{2,4},{4,2},{6,0},{1,7},{3,5},{5,3},{7,1},{8,14},{10,12},{12... | collective-permute-start | bytes 602120 | tf_op jit(solution)/shard_map/ppermute | solution.py:298
  12.3 10.4 %collective-permute-start.4 = (bf16[1,512,128]{2,1,0:T(8,128)(2,1)S(1)}, bf16[1,512,128]{2,1,0:T(8,128)(2,1)S(1)}, u32[]{:S(2)}, u32[]{:S(2)}) collective-permute-start(bf16[1,512,128]{2,1,0:T(8,128)(2,1)S(1)} %slice_bitcast_fusion.1), channel_id=1, source_target_pairs={{6,14},{14,22},{22,30},{30,6},{7,15},{15,23},{23,31},{31,7}} | collective-permute-start | bytes 393224 | tf_op jit(solution)/shard_map/ppermute | solution.py:377
  13.0 9.7 %collective-permute-start.3 = (bf16[2,512,128]{2,1,0:T(8,128)(2,1)S(1)}, bf16[2,512,128]{2,1,0:T(8,128)(2,1)S(1)}, u32[]{:S(2)}, u32[]{:S(2)}) collective-permute-start(bf16[2,512,128]{2,1,0:T(8,128)(2,1)S(1)} %pad_maximum_fusion), channel_id=1, source_target_pairs={{0,8},{2,10},{4,12},{6,14},{8,16},{10,18},{12,20},{14,22},{16,24},... | collective-permute-start | bytes 786440 | tf_op jit(solution)/shard_map/ppermute | solution.py:377
  17.4 12.1 %collective-permute-start.5 = (bf16[1,512,128]{2,1,0:T(8,128)(2,1)S(1)}, bf16[1,512,128]{2,1,0:T(8,128)(2,1)S(1)}, u32[]{:S(2)}, u32[]{:S(2)}) collective-permute-start(bf16[1,512,128]{2,1,0:T(8,128)(2,1)S(1)} %slice_bitcast_fusion), channel_id=1, source_target_pairs={{0,8},{2,10},{4,12},{8,16},{10,18},{12,20},{16,24},{18,26},{20,28}... | collective-permute-start | bytes 393224 | tf_op jit(solution)/shard_map/ppermute | solution.py:377
  24.1 7.8 %collective-permute-start.6 = (bf16[128,256]{1,0:T(8,128)(2,1)S(1)}, bf16[128,256]{1,0:T(8,128)(2,1)S(1)}, u32[]{:S(2)}, u32[]{:S(2)}) collective-permute-start(bf16[128,256]{1,0:T(8,128)(2,1)S(1)} %get-tuple-element.66), channel_id=1, source_target_pairs={{0,6},{2,4},{4,2},{6,0},{1,7},{3,5},{5,3},{7,1},{8,14},{10,12},{12... | collective-permute-start | bytes 196616 | tf_op jit(solution)/shard_map/ppermute | solution.py:298
  30.9 4.3 %collective-permute-start.7 = (bf16[128,256]{1,0:T(8,128)(2,1)S(1)}, bf16[128,256]{1,0:T(8,128)(2,1)S(1)}, u32[]{:S(2)}, u32[]{:S(2)}) collective-permute-start(bf16[128,256]{1,0:T(8,128)(2,1)S(1)} %get-tuple-element.67), channel_id=1, source_target_pairs={{0,2},{2,0},{4,6},{6,4},{1,3},{3,1},{5,7},{7,5},{8,10},{10,8},{12,... | collective-permute-start | bytes 196616 | tf_op jit(solution)/shard_map/ppermute | solution.py:298
  31.0 4.3 %collective-permute-start.8 = (bf16[128,256]{1,0:T(8,128)(2,1)S(1)}, bf16[128,256]{1,0:T(8,128)(2,1)S(1)}, u32[]{:S(2)}, u32[]{:S(2)}) collective-permute-start(bf16[128,256]{1,0:T(8,128)(2,1)S(1)} %get-tuple-element.68), channel_id=1, source_target_pairs={{0,4},{2,6},{4,0},{6,2},{1,5},{3,7},{5,1},{7,3},{8,12},{10,14},{12... | collective-permute-start | bytes 196616 | tf_op jit(solution)/shard_map/ppermute | solution.py:298
  31.9 3.9 %collective-permute-start.10 = (bf16[128,256]{1,0:T(8,128)(2,1)S(1)}, bf16[128,256]{1,0:T(8,128)(2,1)S(1)}, u32[]{:S(2)}, u32[]{:S(2)}) collective-permute-start(bf16[128,256]{1,0:T(8,128)(2,1)S(1)} %collective-permute-done.6.refs_1_), channel_id=1, source_target_pairs={{0,1},{1,0},{2,3},{3,2},{4,5},{5,4},{6,7},{7,6},{8,9},{9,8},{10,11... | collective-permute-start | bytes 196616 | tf_op jit(solution)/shard_map/ppermute | solution.py:298
  31.9 3.9 %collective-permute-start.9 = (bf16[128,256]{1,0:T(8,128)(2,1)S(1)}, bf16[128,256]{1,0:T(8,128)(2,1)S(1)}, u32[]{:S(2)}, u32[]{:S(2)}) collective-permute-start(bf16[128,256]{1,0:T(8,128)(2,1)S(1)} %get-tuple-element.65.refs_0_), channel_id=1, source_target_pairs={{0,1},{1,0},{2,3},{3,2},{4,5},{5,4},{6,7},{7,6},{8,9},{9,8},{10,11... | collective-permute-start | bytes 196616 | tf_op jit(solution)/shard_map/ppermute | solution.py:298
  35.3 1.3 %collective-permute-start.11 = (bf16[128,256]{1,0:T(8,128)(2,1)S(1)}, bf16[128,256]{1,0:T(8,128)(2,1)S(1)}, u32[]{:S(2)}, u32[]{:S(2)}) collective-permute-start(bf16[128,256]{1,0:T(8,128)(2,1)S(1)} %collective-permute-done.7.refs_2_), channel_id=1, source_target_pairs={{0,1},{1,0},{2,3},{3,2},{4,5},{5,4},{6,7},{7,6},{8,9},{9,8},{10,11... | collective-permute-start | bytes 196616 | tf_op jit(solution)/shard_map/ppermute | solution.py:298
  35.3 1.3 %collective-permute-start.12 = (bf16[128,256]{1,0:T(8,128)(2,1)S(1)}, bf16[128,256]{1,0:T(8,128)(2,1)S(1)}, u32[]{:S(2)}, u32[]{:S(2)}) collective-permute-start(bf16[128,256]{1,0:T(8,128)(2,1)S(1)} %collective-permute-done.8.refs_3_), channel_id=1, source_target_pairs={{0,1},{1,0},{2,3},{3,2},{4,5},{5,4},{6,7},{7,6},{8,9},{9,8},{10,11... | collective-permute-start | bytes 196616 | tf_op jit(solution)/shard_map/ppermute | solution.py:298

commit v6 on v5

--- a/solution.py
+++ b/solution.py
@@ -16,6 +16,7 @@
 SCALE = LOG2E * HD ** (-0.5)
 MASKED = -1e30
 EXTRA = 16
+OWN = 10**9
 NEAR = 10**9
 MORE = 1
 FAR = 10**9
@@ -187,9 +188,7 @@
                 add_slab(blocks[two], blocks[one], -ahead, two, mixed_ref, state_ref)
 
 
-def near_kernel(*refs, steps, head_total):
-    blocks, weight_ref = refs[: len(steps)], refs[len(steps)]
-    mixed_ref, state_ref, turned_ref, held, sem = refs[len(steps) + 1 :]
+def own_kernel(block_ref, weight_ref, mixed_ref, state_ref, turned_ref, held, sem, *, head_total):
     me = lax.axis_index("head")
     depth = weight_ref.shape[0] // head_total
     features = weight_ref.shape[1] // head_total
@@ -203,46 +202,45 @@
             )
         )
         copies[-1].start()
-    add_pairs(lax.axis_index("place"), steps, steps, blocks, mixed_ref, state_ref)
+    start_slab(block_ref, 0, mixed_ref, state_ref)
     for other in range(head_total):
         copies[other].wait()
         turned_ref[other] = held[other].T
 
 
-def more_kernel(*refs, group, fresh):
-    blocks, (mixed_ref, state_ref, mixed_out, state_out) = refs[:group], refs[group:]
-    for step in range(group):
+def near_kernel(*refs, steps, fresh):
+    blocks, (mixed_ref, state_ref, mixed_out, state_out) = refs[: len(steps)], refs[len(steps) :]
+    for step in steps:
         if step not in fresh:
             mixed_out[step] = mixed_ref[step]
             state_out[step] = state_ref[step]
-    steps = list(range(group))
     add_pairs(lax.axis_index("place"), steps, fresh, blocks, mixed_out, state_out)
 
 
-def far_kernel(*refs, group, halo, ready, last):
+def far_kernel(*refs, group, halo, last):
     blocks, (mixed_ref, state_ref) = refs[:group], refs[group : group + 2]
     pieces = refs[group + 2 : group + 2 + len(halo)]
     outs = refs[group + 2 + len(halo) :]
-    out_refs, (mixed_out, state_out) = outs[: len(ready)], outs[len(ready) :]
+    out_refs, (mixed_out, state_out) = outs[:-2], outs[-2:]
     place = lax.axis_index("place")
     mixed_out[...] = mixed_ref[...]
     state_out[...] = state_ref[...]
     for piece_ref, (offset, choices) in zip(pieces, halo):
         for low in range(piece_ref.shape[0]):
-            slabs = [choice[low] ^ at if choice else group for at, choice in enumerate(choices)]
+            slabs = [choice[low] ^ at for at, choice in enumerate(choices)]
             ahead = offset * group - pick(place, slabs)
             for step in range(group):
                 turn = jnp.bitwise_xor(place, step) + ahead
-                used = (turn < STEPS) & (turn > 0)
-
-                @pl.when(used & (ahead > (offset - 1) * group))
+
+                @pl.when(turn < STEPS)
                 def _(low=low, step=step, turn=turn, piece_ref=piece_ref):
                     add_slab(
                         blocks[step], piece_ref.at[low], turn, step, mixed_out, state_out
                     )
 
-    for step, out_ref in zip(ready, out_refs):
-        out_ref[...] = (mixed_out[step] / state_out[step, 1:2]).astype(out_ref.dtype)
+    if last:
+        for step, out_ref in zip(sending_order(group), out_refs):
+            out_ref[...] = (mixed_out[step] / state_out[step, 1:2]).astype(out_ref.dtype)
 
 
 def hops(step):
@@ -257,15 +255,11 @@
     messages = []
     for offset in range(1, -(-(STEPS - 1) // group) + 1):
         first = max(0, offset * group - STEPS + 1)
-        early, late = [], []
-        for place in range(group):
-            needed = [step for step in range(group) if place ^ step >= first]
-            early.append([step for step in needed if hops(step) < 2])
-            late.append([step for step in needed if hops(step) > 1])
-        common = min(len(steps) for steps in early)
-        parts = [(False, [steps[:common] for steps in early])]
-        parts += [(False, [steps[common:] for steps in early]), (True, late)]
-        messages += [(is_late, offset, choices) for is_late, choices in parts if any(choices)]
+        needed = [[step for step in range(group) if place ^ step >= first] for place in range(group)]
+        early = min(len([step for step in steps if hops(step) < 2]) for steps in needed)
+        messages.append((False, offset, [steps[:early] for steps in needed]))
+        if early < group - first:
+            messages.append((True, offset, [steps[early:] for steps in needed]))
     return messages
 
 
@@ -299,14 +293,11 @@
 
 
 def halo_message(got, place, choices, rows):
-    length = max(len(steps) for steps in choices)
     parts = []
-    for low in range(length):
-        steps = [choice[low] if choice else None for choice in choices]
-        known = [step for step in steps if step is not None]
-        piece = got[known[-1]][: 2 * rows]
+    for steps in zip(*choices):
+        piece = got[steps[-1]][: 2 * rows]
         for at, step in enumerate(steps):
-            if step is not None and step != known[-1]:
+            if step != steps[-1]:
                 piece = jnp.where(place == at, got[step][: 2 * rows], piece)
         parts.append(piece)
     return jnp.stack(parts)
@@ -349,7 +340,34 @@
         ],
     )
 
-    state_shapes = [shape((group, HD, rows), f32), shape((group, 8, rows), f32)]
+    def state_shapes(count):
+        return [shape((count, HD, rows), f32), shape((count, 8, rows), f32)]
+
+    def near(steps, fresh, mixed, state, cost):
+        return pl.pallas_call(
+            functools.partial(near_kernel, steps=steps, fresh=fresh),
+            out_shape=state_shapes(len(steps)),
+            in_specs=[VMEM] * (len(steps) + 2),
+            out_specs=[VMEM] * 2,
+            compiler_params=PARAMS,
+            cost_estimate=pl.CostEstimate(flops=cost, transcendentals=1, bytes_accessed=1),
+            name="near",
+        )(*[got[step] for step in steps], mixed, state)
+
+    mixed, state, turned = pl.pallas_call(
+        functools.partial(own_kernel, head_total=head_total),
+        out_shape=[*state_shapes(1), shape((head_total, features, depth // head_total), bf16)],
+        in_specs=[VMEM, HBM],
+        out_specs=[VMEM] * 3,
+        scratch_shapes=[
+            pltpu.VMEM((head_total, depth // head_total, features), bf16),
+            pltpu.SemaphoreType.DMA((head_total,)),
+        ],
+        compiler_params=PARAMS,
+        cost_estimate=pl.CostEstimate(flops=OWN, transcendentals=1, bytes_accessed=1),
+        name="own",
+    )(packed[0], pltpu.with_memory_space_constraint(out_weight, pltpu.HBM))
+
     first_steps = [step for step in range(group) if hops(step) < 2]
     rest = [step for step in range(group) if hops(step) > 1]
     got = [packed[0]]
@@ -359,83 +377,43 @@
         if step:
             block = packed[step]
             if hops(step) > 1:
-                block, got[1] = lax.optimization_barrier((block, got[1]))
+                block, turned = lax.optimization_barrier((block, turned))
             got.append(swapped(block, "place", step))
         for late, offset, choices in messages:
-            if step != max(max(steps, default=0) for steps in choices):
+            if step != max(max(steps) for steps in choices):
                 continue
-            pairs = [
-                (at * group + p, (at + offset) % groups * group + p)
-                for at in range(groups)
-                for p in range(group)
-                if choices[p]
-            ]
+            pairs = [(source, (source + offset) % groups) for source in range(groups)]
             message = halo_message(got, place, choices, rows)
             if late:
                 message, state = lax.optimization_barrier((message, state))
             message, *got = lax.optimization_barrier([message, *got])
-            arrived = lax.ppermute(message, ("group", "place"), pairs)
-            sent[late].append(((offset, choices), arrived))
+            sent[late].append(((offset, choices), lax.ppermute(message, "group", pairs)))
         if step == first_steps[-1]:
-            mixed, state, turned = pl.pallas_call(
-                functools.partial(near_kernel, steps=first_steps, head_total=head_total),
-                out_shape=[*state_shapes, shape((head_total, features, depth // head_total), bf16)],
-                in_specs=[VMEM] * len(first_steps) + [HBM],
-                out_specs=[VMEM] * 3,
-                scratch_shapes=[
-                    pltpu.VMEM((head_total, depth // head_total, features), bf16),
-                    pltpu.SemaphoreType.DMA((head_total,)),
-                ],
-                compiler_params=PARAMS,
-                cost_estimate=pl.CostEstimate(flops=NEAR, transcendentals=1, bytes_accessed=1),
-                name="near",
-            )(
-                *[got[step] for step in first_steps],
-                pltpu.with_memory_space_constraint(out_weight, pltpu.HBM),
-            )
-
+            mixed, state = near(first_steps, first_steps[1:], mixed, state, NEAR)
     if rest:
-        mixed, state = pl.pallas_call(
-            functools.partial(more_kernel, group=group, fresh=rest),
-            out_shape=state_shapes,
-            in_specs=[VMEM] * (group + 2),
-            out_specs=[VMEM] * 2,
-            compiler_params=PARAMS,
-            cost_estimate=pl.CostEstimate(flops=MORE, transcendentals=1, bytes_accessed=1),
-            name="more",
-        )(*got, mixed, state)
-
-    mix = {}
+        mixed, state = near(list(range(group)), rest, mixed, state, MORE)
+
     for late in (False, True):
-        if late and not sent[late]:
+        if not sent[late]:
             continue
         last = late or not sent[True]
-        ready = [s for s in range(group) if s not in mix and (last or hops(s) > 1)]
-        state_out = [] if last else state_shapes
         outs = pl.pallas_call(
             functools.partial(
-                far_kernel,
-                group=group,
-                halo=[entry[0] for entry in sent[late]],
-                ready=ready,
-                last=last,
+                far_kernel, group=group, halo=[entry[0] for entry in sent[late]], last=last
             ),
-            out_shape=[shape((HD, rows), bf16)] * len(ready) + state_out,
+            out_shape=[shape((HD, rows), bf16)] * group if last else state_shapes(group),
             in_specs=[VMEM] * (group + 2 + len(sent[late])),
-            out_specs=[VMEM] * (len(ready) + len(state_out)),
-            scratch_shapes=[pltpu.VMEM(s.shape, f32) for s in state_shapes] if last else [],
+            out_specs=[VMEM] * (group if last else 2),
+            scratch_shapes=[pltpu.VMEM(s.shape, f32) for s in state_shapes(group)] if last else [],
             compiler_params=PARAMS,
             cost_estimate=pl.CostEstimate(flops=FAR, transcendentals=1, bytes_accessed=1),
             name="far",
         )(*got, mixed, state, *[entry[1] for entry in sent[late]])
-        mix.update(zip(ready, outs))
-        for step in ready:
-            if step:
-                mix[step] = swapped(mix[step], "place", step)
         if not last:
-            mixed, state = outs[len(ready) :]
-
-    mixes = [mix[step] for step in sending_order(group)]
+            mixed, state = outs
+
+    order = sending_order(group)
+    mixes = [outs[0]] + [swapped(out, "place", step) for step, out in zip(order[1:], outs[1:])]
     for other in range(1, head_total):
         mixes += [swapped(entry, "head", other) for entry in mixes[:group]]
     return pl.pallas_call(

time: 38 us -> 36 us (0.947)
  starting transfers between devices: 18.4 us -> 11.9 us
  waiting for transfers between devices: 9.7 us -> 13.3 us
  Pallas kernels: 9.56 us -> 10.4 us
    ppermute x10, starting transfers between devices: 12.6 us -> 8.68 us  [swapped(): lax.ppermute(value, axis, [(source, source ^ step) for source in range(co...]
    ppermute x3 -> x2, starting transfers between devices: 5.77 us -> 3.26 us  [on_device(): lax.ppermute(message, 'group', pairs)]
    ppermute x3 -> x2, waiting for transfers between devices: 0.01 us -> 2.09 us  [on_device(): lax.ppermute(message, 'group', pairs)]
    ppermute x10, waiting for transfers between devices: 9.69 us -> 11.2 us  [swapped(): lax.ppermute(value, axis, [(source, source ^ step) for source in range(co...]
    pallas_call x2 -> x3, Pallas kernels: 4.43 us -> 5.33 us  [the longest x2 3.75 us: near(): pl.pallas_call(functools.partial(near_kernel, steps=steps, fresh=fresh),...]
  transfers between devices with their start and end apart: 13 -> 12, of which waited for: 8 -> 8; matrix products, arithmetic and copies ran while one was open for 0% -> 0% of each run, Pallas kernels for 19% -> 19%
where the time goes in v6:
time: 36 us; the launch traced here: 35.8 us
  waiting for transfers between devices  13.3 us (37%)
  starting transfers between devices  11.9 us (33%)
  Pallas kernels  10.4 us (29%)
    ppermute x10, waiting for transfers between devices, swapped(): lax.ppermute(value, axis, [(source, source ^ step) for source in range(co...  11.2 us
    ppermute x10, starting transfers between devices, swapped(): lax.ppermute(value, axis, [(source, source ^ step) for source in range(co...  8.68 us
    pallas_call x2, Pallas kernels, near(): pl.pallas_call(functools.partial(near_kernel, steps=steps, fresh=fresh),...  3.75 us
    ppermute x2, starting transfers between devices, on_device(): lax.ppermute(message, 'group', pairs)  3.26 us
    pallas_call x2, Pallas kernels, on_device(): pl.pallas_call(functools.partial(far_kernel, group=group, halo=[entry[0]...  2.68 us
    ppermute x2, waiting for transfers between devices, on_device(): lax.ppermute(message, 'group', pairs)  2.09 us
    pallas_call x1, Pallas kernels, on_device(): pl.pallas_call(functools.partial(own_kernel, head_total=head_total), out_...  1.58 us
    pallas_call x1, Pallas kernels, on_device(): pl.pallas_call(pack_kernel, out_shape=[shape((3 * rows + EXTRA, HD), bf16...  1.21 us
  transfers between devices with their start and end apart: 12, of which 8 were waited for; matrix products, arithmetic and copies ran while one was open for 0% of the time, Pallas kernels for 19%

profile of v6, /device:TPU:0, one launch (start us, length us, event | category | flops | bytes accessed | tf_op | source)
XLA Modules:
  0.0 35.8 jit_solution(15831009966169049562)
XLA Ops:
  0.0 1.2 %pack.1 = (bf16[784,128]{1,0:T(8,128)(2,1)S(1)}, bf16[784,128]{1,0:T(8,128)(2,1)S(1)}, bf16[784,128]{1,0:T(8,128)(2,1)S(1)}, bf16[784,128]{1,0:T(8,128)(2,1)S(1)}) custom-call(bf16[256,512]{1,0:T(8,128)(2,1)} %query_ref.1, bf16[256,512]{1,0:T(8,128)(2,1)} %key_ref.1, bf16[256,512]{1,0:T(8,128)(2,1)} %value_ref.1, s32[2,2,4]{2,1,0:T(2,128)} %bitcast.8, ...), custom_call_target="tpu_custom_call" | custom-call | tf_op jit(solution)/shard_map/pack/pallas_call | solution.py:317
  1.2 3.0 %collective-permute-start.1 = (bf16[784,128]{1,0:T(8,128)(2,1)S(1)}, bf16[784,128]{1,0:T(8,128)(2,1)S(1)}, u32[]{:S(2)}, u32[]{:S(2)}) collective-permute-start(bf16[784,128]{1,0:T(8,128)(2,1)S(1)} %get-tuple-element.40), channel_id=1, source_target_pairs={{0,2},{2,0},{4,6},{6,4},{1,3},{3,1},{5,7},{7,5},{8,10},{10,8},{12,... | collective-permute-start | bytes 602120 | tf_op jit(solution)/shard_map/ppermute | solution.py:292
  4.2 1.5 %collective-permute-start.2 = (bf16[784,128]{1,0:T(8,128)(2,1)S(1)}, bf16[784,128]{1,0:T(8,128)(2,1)S(1)}, u32[]{:S(2)}, u32[]{:S(2)}) collective-permute-start(bf16[784,128]{1,0:T(8,128)(2,1)S(1)} %get-tuple-element.41), channel_id=1, source_target_pairs={{0,4},{2,6},{4,0},{6,2},{1,5},{3,7},{5,1},{7,3},{8,12},{10,14},{12... | collective-permute-start | bytes 602120 | tf_op jit(solution)/shard_map/ppermute | solution.py:292
  5.7 1.6 %own.1 = (f32[1,128,256]{2,1,0:T(8,128)S(1)}, f32[1,8,256]{2,1,0:T(8,128)S(1)}, bf16[2,512,512]{2,1,0:T(8,128)(2,1)S(1)}) custom-call(bf16[784,128]{1,0:T(8,128)(2,1)S(1)} %get-tuple-element.49.block_ref.refs_0_, bf16[1024,1024]{1,0:T(8,128)(2,1)} %weight_ref.1), custom_call_target="tpu_custom_call" | custom-call | flops 1000000000 | bytes 1 | tf_op jit(solution)/shard_map/own/pallas_call | solution.py:357
  7.3 0.1 collective-permute-start
  7.4 2.2 %collective-permute-done.1.refs_1_ = bf16[784,128]{1,0:T(8,128)(2,1)S(1)} collective-permute-done((bf16[784,128]{1,0:T(8,128)(2,1)S(1)}, bf16[784,128]{1,0:T(8,128)(2,1)S(1)}, u32[]{:S(2)}, u32[]{:S(2)}) %collective-permute-start.1) | collective-permute-done | bytes 200736 | tf_op jit(solution)/shard_map/ppermute | solution.py:292
  9.6 5.4 %collective-permute-done.2.refs_2_ = bf16[784,128]{1,0:T(8,128)(2,1)S(1)} collective-permute-done((bf16[784,128]{1,0:T(8,128)(2,1)S(1)}, bf16[784,128]{1,0:T(8,128)(2,1)S(1)}, u32[]{:S(2)}, u32[]{:S(2)}) %collective-permute-start.2) | collective-permute-done | bytes 200736 | tf_op jit(solution)/shard_map/ppermute | solution.py:292
  15.0 1.6 %collective-permute-start.3 = (bf16[2,512,128]{2,1,0:T(8,128)(2,1)S(1)}, bf16[2,512,128]{2,1,0:T(8,128)(2,1)S(1)}, u32[]{:S(2)}, u32[]{:S(2)}) collective-permute-start(bf16[2,512,128]{2,1,0:T(8,128)(2,1)S(1)} %pad_maximum_fusion), channel_id=1, source_target_pairs={{0,8},{8,16},{16,24},{24,0},{1,9},{9,17},{17,25},{25,1},{2,10},{10... | collective-permute-start | bytes 786440 | tf_op jit(solution)/shard_map/ppermute | solution.py:390
  16.7 2.0 %near.2 = (f32[3,128,256]{2,1,0:T(8,128)S(1)}, f32[3,8,256]{2,1,0:T(8,128)S(1)}) custom-call(bf16[784,128]{1,0:T(8,128)(2,1)S(1)} %get-tuple-element.49.block_ref.refs_0_, bf16[784,128]{1,0:T(8,128)(2,1)S(1)} %collective-permute-done.1.refs_1_, bf16[784,128]{1,0:T(8,128)(2,1)S(1)} %collective-permute-done.2.refs_2_, ...), custom_call_target="tpu_custom_call" | custom-call | flops 1000000000 | bytes 1 | tf_op jit(solution)/shard_map/near/pallas_call | solution.py:347
  18.7 0.0 collective-permute-done.refs_3_
  18.7 1.6 %collective-permute-start.4 = (bf16[1,512,128]{2,1,0:T(8,128)(2,1)S(1)}, bf16[1,512,128]{2,1,0:T(8,128)(2,1)S(1)}, u32[]{:S(2)}, u32[]{:S(2)}) collective-permute-start(bf16[1,512,128]{2,1,0:T(8,128)(2,1)S(1)} %fusion.1), channel_id=1, source_target_pairs={{0,8},{8,16},{16,24},{24,0},{1,9},{9,17},{17,25},{25,1},{2,10},{10... | collective-permute-start | bytes 393224 | tf_op jit(solution)/shard_map/ppermute | solution.py:390
  20.4 1.7 %near.3 = (f32[4,128,256]{2,1,0:T(8,128)S(1)}, f32[4,8,256]{2,1,0:T(8,128)S(1)}) custom-call(bf16[784,128]{1,0:T(8,128)(2,1)S(1)} %get-tuple-element.49.block_ref.refs_0_, bf16[784,128]{1,0:T(8,128)(2,1)S(1)} %collective-permute-done.1.refs_1_, bf16[784,128]{1,0:T(8,128)(2,1)S(1)} %collective-permute-done.2.refs_2_, ...), custom_call_target="tpu_custom_call" | custom-call | flops 1 | bytes 1 | tf_op jit(solution)/shard_map/near/pallas_call | solution.py:347
  22.1 1.2 %collective-permute-done.3.refs_6_ = bf16[2,512,128]{2,1,0:T(8,128)(2,1)S(1)} collective-permute-done((bf16[2,512,128]{2,1,0:T(8,128)(2,1)S(1)}, bf16[2,512,128]{2,1,0:T(8,128)(2,1)S(1)}, u32[]{:S(2)}, u32[]{:S(2)}) %collective-permute-start.3) | collective-permute-done | bytes 262176 | tf_op jit(solution)/shard_map/ppermute | solution.py:390
  23.3 1.3 %far.2 = (f32[4,128,256]{2,1,0:T(8,128)S(1)}, f32[4,8,256]{2,1,0:T(8,128)S(1)}) custom-call(bf16[784,128]{1,0:T(8,128)(2,1)S(1)} %get-tuple-element.49.block_ref.refs_0_, bf16[784,128]{1,0:T(8,128)(2,1)S(1)} %collective-permute-done.1.refs_1_, bf16[784,128]{1,0:T(8,128)(2,1)S(1)} %collective-permute-done.2.refs_2_, ...), custom_call_target="tpu_custom_call" | custom-call | flops 1000000000 | bytes 1 | tf_op jit(solution)/shard_map/far/pallas_call | solution.py:400
  24.6 0.9 %collective-permute-done.4.refs_6_ = bf16[1,512,128]{2,1,0:T(8,128)(2,1)S(1)} collective-permute-done((bf16[1,512,128]{2,1,0:T(8,128)(2,1)S(1)}, bf16[1,512,128]{2,1,0:T(8,128)(2,1)S(1)}, u32[]{:S(2)}, u32[]{:S(2)}) %collective-permute-start.4) | collective-permute-done | bytes 131104 | tf_op jit(solution)/shard_map/ppermute | solution.py:390
  25.5 1.3 %far.3 = (bf16[128,256]{1,0:T(8,128)(2,1)S(1)}, bf16[128,256]{1,0:T(8,128)(2,1)S(1)}, bf16[128,256]{1,0:T(8,128)(2,1)S(1)}, bf16[128,256]{1,0:T(8,128)(2,1)S(1)}) custom-call(bf16[784,128]{1,0:T(8,128)(2,1)S(1)} %get-tuple-element.49.block_ref.refs_0_, bf16[784,128]{1,0:T(8,128)(2,1)S(1)} %collective-permute-done.1.refs_1_, ...), custom_call_target="tpu_custom_call" | custom-call | flops 1000000000 | bytes 1 | tf_op jit(solution)/shard_map/far/pallas_call | solution.py:400
  26.9 0.7 %collective-permute-start.5 = (bf16[128,256]{1,0:T(8,128)(2,1)S(1)}, bf16[128,256]{1,0:T(8,128)(2,1)S(1)}, u32[]{:S(2)}, u32[]{:S(2)}) collective-permute-start(bf16[128,256]{1,0:T(8,128)(2,1)S(1)} %get-tuple-element.62), channel_id=1, source_target_pairs={{0,6},{2,4},{4,2},{6,0},{1,7},{3,5},{5,3},{7,1},{8,14},{10,12},{12... | collective-permute-start | bytes 196616 | tf_op jit(solution)/shard_map/ppermute | solution.py:292
  27.6 1.5 %collective-permute-start.6 = (bf16[128,256]{1,0:T(8,128)(2,1)S(1)}, bf16[128,256]{1,0:T(8,128)(2,1)S(1)}, u32[]{:S(2)}, u32[]{:S(2)}) collective-permute-start(bf16[128,256]{1,0:T(8,128)(2,1)S(1)} %get-tuple-element.63), channel_id=1, source_target_pairs={{0,2},{2,0},{4,6},{6,4},{1,3},{3,1},{5,7},{7,5},{8,10},{10,8},{12,... | collective-permute-start | bytes 196616 | tf_op jit(solution)/shard_map/ppermute | solution.py:292
  29.1 1.4 %collective-permute-start.7 = (bf16[128,256]{1,0:T(8,128)(2,1)S(1)}, bf16[128,256]{1,0:T(8,128)(2,1)S(1)}, u32[]{:S(2)}, u32[]{:S(2)}) collective-permute-start(bf16[128,256]{1,0:T(8,128)(2,1)S(1)} %get-tuple-element.64), channel_id=1, source_target_pairs={{0,4},{2,6},{4,0},{6,2},{1,5},{3,7},{5,1},{7,3},{8,12},{10,14},{12... | collective-permute-start | bytes 196616 | tf_op jit(solution)/shard_map/ppermute | solution.py:292
  30.5 0.0 collective-permute-start.8
  30.5 1.7 %collective-permute-done.5.refs_1_ = bf16[128,256]{1,0:T(8,128)(2,1)S(1)} collective-permute-done((bf16[128,256]{1,0:T(8,128)(2,1)S(1)}, bf16[128,256]{1,0:T(8,128)(2,1)S(1)}, u32[]{:S(2)}, u32[]{:S(2)}) %collective-permute-start.5) | collective-permute-done | bytes 65568 | tf_op jit(solution)/shard_map/ppermute | solution.py:292
  32.1 0.0 collective-permute-start.9
  32.1 0.0 collective-permute-done.6.refs_2_
  32.1 0.5 %collective-permute-start.10 = (bf16[128,256]{1,0:T(8,128)(2,1)S(1)}, bf16[128,256]{1,0:T(8,128)(2,1)S(1)}, u32[]{:S(2)}, u32[]{:S(2)}) collective-permute-start(bf16[128,256]{1,0:T(8,128)(2,1)S(1)} %collective-permute-done.6.refs_2_), channel_id=1, source_target_pairs={{0,1},{1,0},{2,3},{3,2},{4,5},{5,4},{6,7},{7,6},{8,9},{9,8},{10,11... | collective-permute-start | bytes 196616 | tf_op jit(solution)/shard_map/ppermute | solution.py:292
  32.6 0.7 %collective-permute-done.7.refs_3_ = bf16[128,256]{1,0:T(8,128)(2,1)S(1)} collective-permute-done((bf16[128,256]{1,0:T(8,128)(2,1)S(1)}, bf16[128,256]{1,0:T(8,128)(2,1)S(1)}, u32[]{:S(2)}, u32[]{:S(2)}) %collective-permute-start.7) | collective-permute-done | bytes 65568 | tf_op jit(solution)/shard_map/ppermute | solution.py:292
  33.4 0.0 collective-permute-start.11
  33.4 0.0 collective-permute-done.8.refs_4_
  33.4 0.0 collective-permute-done.9.refs_5_
  33.4 0.2 collective-permute-done.10.refs_6_
  33.5 1.1 %collective-permute-done.11.refs_7_ = bf16[128,256]{1,0:T(8,128)(2,1)S(1)} collective-permute-done((bf16[128,256]{1,0:T(8,128)(2,1)S(1)}, bf16[128,256]{1,0:T(8,128)(2,1)S(1)}, u32[]{:S(2)}, u32[]{:S(2)}) %collective-permute-start.11) | collective-permute-done | bytes 65568 | tf_op jit(solution)/shard_map/ppermute | solution.py:292
  34.6 1.2 %project.1 = bf16[512,256]{1,0:T(8,128)(2,1)} custom-call(bf16[2,512,512]{2,1,0:T(8,128)(2,1)S(1)} %get-tuple-element.38.turned_ref, bf16[128,256]{1,0:T(8,128)(2,1)S(1)} %get-tuple-element.61.refs_0_, bf16[128,256]{1,0:T(8,128)(2,1)S(1)} %collective-permute-done.5.refs_1_, bf16[128,256]{1,0:T(8,128)(2,1)S(1)} %collective-permute-done.6.refs_2_, ...), custom_call_target="tpu_custom_call" | custom-call | tf_op jit(solution)/shard_map/project/pallas_call | solution.py:419
  (3 shorter events, 0.1 us)
Async XLA Ops:
  1.2 8.4 %collective-permute-start.1 = (bf16[784,128]{1,0:T(8,128)(2,1)S(1)}, bf16[784,128]{1,0:T(8,128)(2,1)S(1)}, u32[]{:S(2)}, u32[]{:S(2)}) collective-permute-start(bf16[784,128]{1,0:T(8,128)(2,1)S(1)} %get-tuple-element.40), channel_id=1, source_target_pairs={{0,2},{2,0},{4,6},{6,4},{1,3},{3,1},{5,7},{7,5},{8,10},{10,8},{12,... | collective-permute-start | bytes 602120 | tf_op jit(solution)/shard_map/ppermute | solution.py:292
  4.2 10.8 %collective-permute-start.2 = (bf16[784,128]{1,0:T(8,128)(2,1)S(1)}, bf16[784,128]{1,0:T(8,128)(2,1)S(1)}, u32[]{:S(2)}, u32[]{:S(2)}) collective-permute-start(bf16[784,128]{1,0:T(8,128)(2,1)S(1)} %get-tuple-element.41), channel_id=1, source_target_pairs={{0,4},{2,6},{4,0},{6,2},{1,5},{3,7},{5,1},{7,3},{8,12},{10,14},{12... | collective-permute-start | bytes 602120 | tf_op jit(solution)/shard_map/ppermute | solution.py:292
  7.3 11.3 %collective-permute-start = (bf16[784,128]{1,0:T(8,128)(2,1)S(1)}, bf16[784,128]{1,0:T(8,128)(2,1)S(1)}, u32[]{:S(2)}, u32[]{:S(2)}) collective-permute-start(bf16[784,128]{1,0:T(8,128)(2,1)S(1)} %get-tuple-element.39), channel_id=1, source_target_pairs={{0,6},{2,4},{4,2},{6,0},{1,7},{3,5},{5,3},{7,1},{8,14},{10,12},{12... | collective-permute-start | bytes 602120 | tf_op jit(solution)/shard_map/ppermute | solution.py:292
  15.0 8.2 %collective-permute-start.3 = (bf16[2,512,128]{2,1,0:T(8,128)(2,1)S(1)}, bf16[2,512,128]{2,1,0:T(8,128)(2,1)S(1)}, u32[]{:S(2)}, u32[]{:S(2)}) collective-permute-start(bf16[2,512,128]{2,1,0:T(8,128)(2,1)S(1)} %pad_maximum_fusion), channel_id=1, source_target_pairs={{0,8},{8,16},{16,24},{24,0},{1,9},{9,17},{17,25},{25,1},{2,10},{10... | collective-permute-start | bytes 786440 | tf_op jit(solution)/shard_map/ppermute | solution.py:390
  18.7 6.8 %collective-permute-start.4 = (bf16[1,512,128]{2,1,0:T(8,128)(2,1)S(1)}, bf16[1,512,128]{2,1,0:T(8,128)(2,1)S(1)}, u32[]{:S(2)}, u32[]{:S(2)}) collective-permute-start(bf16[1,512,128]{2,1,0:T(8,128)(2,1)S(1)} %fusion.1), channel_id=1, source_target_pairs={{0,8},{8,16},{16,24},{24,0},{1,9},{9,17},{17,25},{25,1},{2,10},{10... | collective-permute-start | bytes 393224 | tf_op jit(solution)/shard_map/ppermute | solution.py:390
  26.9 5.2 %collective-permute-start.5 = (bf16[128,256]{1,0:T(8,128)(2,1)S(1)}, bf16[128,256]{1,0:T(8,128)(2,1)S(1)}, u32[]{:S(2)}, u32[]{:S(2)}) collective-permute-start(bf16[128,256]{1,0:T(8,128)(2,1)S(1)} %get-tuple-element.62), channel_id=1, source_target_pairs={{0,6},{2,4},{4,2},{6,0},{1,7},{3,5},{5,3},{7,1},{8,14},{10,12},{12... | collective-permute-start | bytes 196616 | tf_op jit(solution)/shard_map/ppermute | solution.py:292
  27.6 4.5 %collective-permute-start.6 = (bf16[128,256]{1,0:T(8,128)(2,1)S(1)}, bf16[128,256]{1,0:T(8,128)(2,1)S(1)}, u32[]{:S(2)}, u32[]{:S(2)}) collective-permute-start(bf16[128,256]{1,0:T(8,128)(2,1)S(1)} %get-tuple-element.63), channel_id=1, source_target_pairs={{0,2},{2,0},{4,6},{6,4},{1,3},{3,1},{5,7},{7,5},{8,10},{10,8},{12,... | collective-permute-start | bytes 196616 | tf_op jit(solution)/shard_map/ppermute | solution.py:292
  29.1 4.3 %collective-permute-start.7 = (bf16[128,256]{1,0:T(8,128)(2,1)S(1)}, bf16[128,256]{1,0:T(8,128)(2,1)S(1)}, u32[]{:S(2)}, u32[]{:S(2)}) collective-permute-start(bf16[128,256]{1,0:T(8,128)(2,1)S(1)} %get-tuple-element.64), channel_id=1, source_target_pairs={{0,4},{2,6},{4,0},{6,2},{1,5},{3,7},{5,1},{7,3},{8,12},{10,14},{12... | collective-permute-start | bytes 196616 | tf_op jit(solution)/shard_map/ppermute | solution.py:292
  30.5 2.9 %collective-permute-start.8 = (bf16[128,256]{1,0:T(8,128)(2,1)S(1)}, bf16[128,256]{1,0:T(8,128)(2,1)S(1)}, u32[]{:S(2)}, u32[]{:S(2)}) collective-permute-start(bf16[128,256]{1,0:T(8,128)(2,1)S(1)} %get-tuple-element.61.refs_0_), channel_id=1, source_target_pairs={{0,1},{1,0},{2,3},{3,2},{4,5},{5,4},{6,7},{7,6},{8,9},{9,8},{10,11... | collective-permute-start | bytes 196616 | tf_op jit(solution)/shard_map/ppermute | solution.py:292
  32.1 1.3 %collective-permute-start.9 = (bf16[128,256]{1,0:T(8,128)(2,1)S(1)}, bf16[128,256]{1,0:T(8,128)(2,1)S(1)}, u32[]{:S(2)}, u32[]{:S(2)}) collective-permute-start(bf16[128,256]{1,0:T(8,128)(2,1)S(1)} %collective-permute-done.5.refs_1_), channel_id=1, source_target_pairs={{0,1},{1,0},{2,3},{3,2},{4,5},{5,4},{6,7},{7,6},{8,9},{9,8},{10,11... | collective-permute-start | bytes 196616 | tf_op jit(solution)/shard_map/ppermute | solution.py:292
  32.1 1.4 %collective-permute-start.10 = (bf16[128,256]{1,0:T(8,128)(2,1)S(1)}, bf16[128,256]{1,0:T(8,128)(2,1)S(1)}, u32[]{:S(2)}, u32[]{:S(2)}) collective-permute-start(bf16[128,256]{1,0:T(8,128)(2,1)S(1)} %collective-permute-done.6.refs_2_), channel_id=1, source_target_pairs={{0,1},{1,0},{2,3},{3,2},{4,5},{5,4},{6,7},{7,6},{8,9},{9,8},{10,11... | collective-permute-start | bytes 196616 | tf_op jit(solution)/shard_map/ppermute | solution.py:292
  33.4 1.3 %collective-permute-start.11 = (bf16[128,256]{1,0:T(8,128)(2,1)S(1)}, bf16[128,256]{1,0:T(8,128)(2,1)S(1)}, u32[]{:S(2)}, u32[]{:S(2)}) collective-permute-start(bf16[128,256]{1,0:T(8,128)(2,1)S(1)} %collective-permute-done.7.refs_3_), channel_id=1, source_target_pairs={{0,1},{1,0},{2,3},{3,2},{4,5},{5,4},{6,7},{7,6},{8,9},{9,8},{10,11... | collective-permute-start | bytes 196616 | tf_op jit(solution)/shard_map/ppermute | solution.py:292

commit v7 on v4

--- a/solution.py
+++ b/solution.py
@@ -16,7 +16,9 @@
 SCALE = LOG2E * HD ** (-0.5)
 MASKED = -1e30
 EXTRA = 16
-COST = 10**9
+OWN = 10**9
+NEAR = 1
+FAR = 4 * 10**9
 VMEM = pl.BlockSpec(memory_space=pltpu.VMEM)
 HBM = pl.BlockSpec(memory_space=pltpu.HBM)
 PARAMS = pltpu.CompilerParams(vmem_limit_bytes=48 * 1024 * 1024)
@@ -36,10 +38,23 @@
     return uses
 
 
+def hops(step):
+    return step.bit_count()
+
+
+def query_places(refs, group, rows):
+    apart = iter(refs[group:])
+    return [
+        next(apart) if hops(step) > 1 else refs[step].at[pl.ds(2 * rows, rows + EXTRA)]
+        for step in range(group)
+    ]
+
+
 def pack_kernel(query_ref, key_ref, value_ref, index_ref, count_ref, *refs):
     out_refs, (values, index, count, sem) = refs[:-4], refs[-4:]
-    rows, width = query_ref.shape
-    group = width // HD
+    group = query_ref.shape[1] // HD
+    block_refs, query_refs = out_refs[:group], query_places(out_refs, group, query_ref.shape[0])
+    rows = query_ref.shape[0]
     tiles = rows // TILE
     place = lax.axis_index("place")
     value_copy = pltpu.make_async_copy(value_ref, values, sem.at[0])
@@ -53,13 +68,12 @@
     copies = []
     for step in range(group):
         cols = pl.ds(pl.multiple_of(jnp.bitwise_xor(place, step) * HD, HD), HD)
-        out = out_refs[step]
         copies += [
             pltpu.make_async_copy(
-                key_ref.at[:, cols], out.at[pl.ds(0, rows)], sem.at[3 + 2 * step]
+                key_ref.at[:, cols], block_refs[step].at[pl.ds(0, rows)], sem.at[3 + 2 * step]
             ),
             pltpu.make_async_copy(
-                query_ref.at[:, cols], out.at[pl.ds(2 * rows, rows)], sem.at[4 + 2 * step]
+                query_ref.at[:, cols], query_refs[step].at[pl.ds(0, rows)], sem.at[4 + 2 * step]
             ),
         ]
     for copy in copies:
@@ -70,8 +84,8 @@
     value_copy.wait()
     for step in range(group):
         cols = pl.ds(pl.multiple_of(jnp.bitwise_xor(place, step) * HD, HD), HD)
-        out = out_refs[step]
-        out[3 * rows :] = uses
+        out = block_refs[step]
+        query_refs[step][rows:] = uses
         for at in range(0, rows, TILE):
             out[rows + at : rows + at + TILE] = values[at : at + TILE, cols].T
     for copy in copies:
@@ -115,11 +129,7 @@
     return total, mixed
 
 
-def near_kernel(*refs, group, head_total):
-    got_refs, weight_ref = refs[:group], refs[group]
-    query_ref, mixed_ref, state_ref, turned_ref, kv, held, sem = refs[group + 1 :]
-    rows = mixed_ref.shape[2]
-    place = lax.axis_index("place")
+def turn_kernel(block_ref, weight_ref, turned_ref, held, sem, *, head_total):
     me = lax.axis_index("head")
     depth = weight_ref.shape[0] // head_total
     features = weight_ref.shape[1] // head_total
@@ -133,10 +143,20 @@
             )
         )
         copies[-1].start()
+    for other in range(head_total):
+        copies[other].wait()
+        turned_ref[other] = held[other].T
+
+
+def near_kernel(*refs, group):
+    got_refs, (query_ref, mixed_ref, state_ref, kv) = refs[:-4], refs[-4:]
+    rows = mixed_ref.shape[2]
+    place = lax.axis_index("place")
+    query_refs = query_places(got_refs, group, rows)
     for step in range(group):
         slab = jnp.bitwise_xor(place, step)
         kv[slab] = got_refs[step][: 2 * rows]
-        query_ref[slab] = got_refs[step][2 * rows :]
+        query_ref[slab] = query_refs[step][...]
     eye = lax.broadcasted_iota(jnp.int32, (TILE, TILE), 0) == lax.broadcasted_iota(
         jnp.int32, (TILE, TILE), 1
     )
@@ -172,17 +192,10 @@
         mixed_ref[dest] = mixed
         state_ref[dest, 0:1] = top
         state_ref[dest, 1:2] = total
-    for other in range(head_total):
-        copies[other].wait()
-        turned_ref[other] = held[other].T
 
 
 def halo_steps(group, first):
     return [[k for k in range(group) if place ^ k >= first] for place in range(group)]
-
-
-def hops(step):
-    return step.bit_count()
 
 
 def sending_order(group):
@@ -279,11 +292,16 @@
     shape = jax.ShapeDtypeStruct
     place = lax.axis_index("place")
 
+    apart = [step for step in range(group) if hops(step) > 1]
+    whole_block, query_block = shape((3 * rows + EXTRA, HD), bf16), shape((rows + EXTRA, HD), bf16)
     packed = pl.pallas_call(
         pack_kernel,
-        out_shape=[shape((3 * rows + EXTRA, HD), bf16)] * group,
+        out_shape=[
+            shape((2 * rows, HD), bf16) if step in apart else whole_block for step in range(group)
+        ]
+        + [query_block] * len(apart),
         in_specs=[HBM] * 5,
-        out_specs=[VMEM] * group,
+        out_specs=[VMEM] * (group + len(apart)),
         scratch_shapes=[
             pltpu.VMEM((rows, width), bf16),
             pltpu.SMEM((rows // TILE, SLOTS, STEPS), jnp.int32),
@@ -305,6 +323,20 @@
         ],
     )
 
+    turned = pl.pallas_call(
+        functools.partial(turn_kernel, head_total=head_total),
+        out_shape=shape((head_total, features, depth // head_total), bf16),
+        in_specs=[HBM, HBM],
+        out_specs=VMEM,
+        scratch_shapes=[
+            pltpu.VMEM((head_total, depth // head_total, features), bf16),
+            pltpu.SemaphoreType.DMA((head_total,)),
+        ],
+        compiler_params=PARAMS,
+        cost_estimate=pl.CostEstimate(flops=OWN, transcendentals=1, bytes_accessed=1),
+        name="turn",
+    )(packed[0], pltpu.with_memory_space_constraint(out_weight, pltpu.HBM))
+
     halos = []
     for offset in range(1, -(-(STEPS - 1) // group) + 1):
         halos.append((offset, max(0, offset * group - STEPS + 1)))
@@ -318,7 +350,7 @@
         if step:
             block = packed[step]
             if hops(step) > 1:
-                block, got[1] = lax.optimization_barrier((block, got[1]))
+                block, got[1], turned = lax.optimization_barrier((block, got[1], turned))
             got.append(swapped(block, "place", step))
         for (offset, first), (at, until), needed in waiting:
             if needed != step:
@@ -336,25 +368,24 @@
             message, *got = lax.optimization_barrier([message, *got])
             far.append(((offset, first), at, lax.ppermute(message, "group", pairs)))
 
-    queries, mixed, state, turned = pl.pallas_call(
-        functools.partial(near_kernel, group=group, head_total=head_total),
+    far_queries = [
+        swapped(block, "place", step) for step, block in zip(apart, packed[group:])
+    ]
+
+    queries, mixed, state = pl.pallas_call(
+        functools.partial(near_kernel, group=group),
         out_shape=(
             shape((group, rows + EXTRA, HD), bf16),
             shape((group, HD, rows), f32),
             shape((group, 8, rows), f32),
-            shape((head_total, features, depth // head_total), bf16),
         ),
-        in_specs=[VMEM] * group + [HBM],
-        out_specs=(VMEM, VMEM, VMEM, VMEM),
-        scratch_shapes=[
-            pltpu.VMEM((group, 2 * rows, HD), bf16),
-            pltpu.VMEM((head_total, depth // head_total, features), bf16),
-            pltpu.SemaphoreType.DMA((head_total,)),
-        ],
+        in_specs=[VMEM] * (group + len(apart)),
+        out_specs=(VMEM, VMEM, VMEM),
+        scratch_shapes=[pltpu.VMEM((group, 2 * rows, HD), bf16)],
         compiler_params=PARAMS,
-        cost_estimate=pl.CostEstimate(flops=1, transcendentals=1, bytes_accessed=1),
+        cost_estimate=pl.CostEstimate(flops=NEAR, transcendentals=1, bytes_accessed=1),
         name="near",
-    )(*got, pltpu.with_memory_space_constraint(out_weight, pltpu.HBM))
+    )(*got, *far_queries)
 
     for number, (halo, at, message) in enumerate(far):
         last = number == len(far) - 1
@@ -373,7 +404,7 @@
             else [],
             compiler_params=PARAMS,
             cost_estimate=pl.CostEstimate(
-                flops=COST, transcendentals=1, bytes_accessed=1
+                flops=FAR, transcendentals=1, bytes_accessed=1
             ),
             name="far",
         )(queries, mixed, state, message)

time: 34.7 us -> 34 us (0.980)
  waiting for transfers between devices: 13.6 us -> 11.1 us
  starting transfers between devices: 13.2 us -> 14.8 us
    ppermute x10 -> x11, waiting for transfers between devices: 12.6 us -> 8.82 us  [swapped(): lax.ppermute(value, axis, [(source, source ^ step) for source in range(co...]
    ppermute x10 -> x11, starting transfers between devices: 9.95 us -> 11.6 us  [swapped(): lax.ppermute(value, axis, [(source, source ^ step) for source in range(co...]
    ppermute x2, waiting for transfers between devices: 1.03 us -> 2.28 us  [on_device(): far.append(((offset, first), at, lax.ppermute(message, 'group', pairs)))]
    pallas_call x2 -> x3, Pallas kernels: 4.19 us -> 4.37 us  [the longest x1 1.72 us: on_device(): pl.pallas_call(functools.partial(near_kernel, group=group), out_shape=(sh...]
  transfers between devices with their start and end apart: 12 -> 13, of which waited for: 8 -> 10; matrix products, arithmetic and copies ran while one was open for 0% -> 0% of each run, Pallas kernels for 12% -> 13%
where the time goes in v7:
time: 34 us; the launch traced here: 33.8 us
  starting transfers between devices  14.8 us (44%)
  waiting for transfers between devices  11.1 us (33%)
  Pallas kernels  7.8 us (23%)
    ppermute x11, starting transfers between devices, swapped(): lax.ppermute(value, axis, [(source, source ^ step) for source in range(co...  11.6 us
    ppermute x11, waiting for transfers between devices, swapped(): lax.ppermute(value, axis, [(source, source ^ step) for source in range(co...  8.82 us
    ppermute x2, starting transfers between devices, on_device(): far.append(((offset, first), at, lax.ppermute(message, 'group', pairs)))  3.21 us
    ppermute x2, waiting for transfers between devices, on_device(): far.append(((offset, first), at, lax.ppermute(message, 'group', pairs)))  2.28 us
    pallas_call x2, Pallas kernels, on_device(): pl.pallas_call(functools.partial(far_kernel, group=group, halo=halo, at=a...  2.25 us
    pallas_call x1, Pallas kernels, on_device(): pl.pallas_call(functools.partial(near_kernel, group=group), out_shape=(sh...  1.72 us
    pallas_call x1, Pallas kernels, on_device(): pl.pallas_call(functools.partial(turn_kernel, head_total=head_total), out...  1.44 us
    pallas_call x1, Pallas kernels, on_device(): pl.pallas_call(pack_kernel, out_shape=[shape((2 * rows, HD), bf16) if ste...  1.21 us
  transfers between devices with their start and end apart: 13, of which 10 were waited for; matrix products, arithmetic and copies ran while one was open for 0% of the time, Pallas kernels for 13%

profile of v7, /device:TPU:0, one launch (start us, length us, event | category | flops | bytes accessed | tf_op | source)
XLA Modules:
  0.0 33.8 jit_solution(9375453668552444339)
XLA Ops:
  0.0 1.2 %pack.1 = (bf16[784,128]{1,0:T(8,128)(2,1)S(1)}, bf16[784,128]{1,0:T(8,128)(2,1)S(1)}, bf16[784,128]{1,0:T(8,128)(2,1)S(1)}, bf16[512,128]{1,0:T(8,128)(2,1)S(1)}, bf16[272,128]{1,0:T(8,128)(2,1)S(1)}) custom-call(bf16[256,512]{1,0:T(8,128)(2,1)} %query_ref.1, bf16[256,512]{1,0:T(8,128)(2,1)} %key_ref.1, bf16[256,512]{1,0:T(8,128)(2,1)} %value_ref.1, ...), custom_call_target="tpu_custom_call" | custom-call | tf_op jit(solution)/shard_map/pack/pallas_call | solution.py:297
  1.2 3.0 %collective-permute-start = (bf16[784,128]{1,0:T(8,128)(2,1)S(1)}, bf16[784,128]{1,0:T(8,128)(2,1)S(1)}, u32[]{:S(2)}, u32[]{:S(2)}) collective-permute-start(bf16[784,128]{1,0:T(8,128)(2,1)S(1)} %get-tuple-element.32), channel_id=1, source_target_pairs={{0,2},{2,0},{4,6},{6,4},{1,3},{3,1},{5,7},{7,5},{8,10},{10,8},{12,... | collective-permute-start | bytes 602120 | tf_op jit(solution)/shard_map/ppermute | solution.py:281
  4.2 1.5 %collective-permute-start.1 = (bf16[784,128]{1,0:T(8,128)(2,1)S(1)}, bf16[784,128]{1,0:T(8,128)(2,1)S(1)}, u32[]{:S(2)}, u32[]{:S(2)}) collective-permute-start(bf16[784,128]{1,0:T(8,128)(2,1)S(1)} %get-tuple-element.34), channel_id=1, source_target_pairs={{0,4},{2,6},{4,0},{6,2},{1,5},{3,7},{5,1},{7,3},{8,12},{10,14},{12... | collective-permute-start | bytes 602120 | tf_op jit(solution)/shard_map/ppermute | solution.py:281
  5.7 1.4 %turn.1.turned_ref = bf16[2,512,512]{2,1,0:T(8,128)(2,1)S(1)} custom-call(bf16[784,128]{1,0:T(8,128)(2,1)S(1)} %get-tuple-element.41.block_ref.refs_0_, bf16[1024,1024]{1,0:T(8,128)(2,1)} %weight_ref.1), custom_call_target="tpu_custom_call" | custom-call | flops 1000000000 | bytes 1 | tf_op jit(solution)/shard_map/turn/pallas_call | solution.py:326
  7.2 2.0 %collective-permute-done.refs_1_ = bf16[784,128]{1,0:T(8,128)(2,1)S(1)} collective-permute-done((bf16[784,128]{1,0:T(8,128)(2,1)S(1)}, bf16[784,128]{1,0:T(8,128)(2,1)S(1)}, u32[]{:S(2)}, u32[]{:S(2)}) %collective-permute-start) | collective-permute-done | bytes 200736 | tf_op jit(solution)/shard_map/ppermute | solution.py:281
  9.2 1.5 %collective-permute-done.1.refs_2_ = bf16[784,128]{1,0:T(8,128)(2,1)S(1)} collective-permute-done((bf16[784,128]{1,0:T(8,128)(2,1)S(1)}, bf16[784,128]{1,0:T(8,128)(2,1)S(1)}, u32[]{:S(2)}, u32[]{:S(2)}) %collective-permute-start.1) | collective-permute-done | bytes 200736 | tf_op jit(solution)/shard_map/ppermute | solution.py:281
  10.7 1.6 %collective-permute-start.2 = (bf16[512,128]{1,0:T(8,128)(2,1)S(1)}, bf16[512,128]{1,0:T(8,128)(2,1)S(1)}, u32[]{:S(2)}, u32[]{:S(2)}) collective-permute-start(bf16[512,128]{1,0:T(8,128)(2,1)S(1)} %get-tuple-element.37), channel_id=1, source_target_pairs={{0,6},{2,4},{4,2},{6,0},{1,7},{3,5},{5,3},{7,1},{8,14},{10,12},{12... | collective-permute-start | bytes 393224 | tf_op jit(solution)/shard_map/ppermute | solution.py:281
  12.3 1.6 %collective-permute-start.4 = (bf16[2,512,128]{2,1,0:T(8,128)(2,1)S(1)}, bf16[2,512,128]{2,1,0:T(8,128)(2,1)S(1)}, u32[]{:S(2)}, u32[]{:S(2)}) collective-permute-start(bf16[2,512,128]{2,1,0:T(8,128)(2,1)S(1)} %pad_maximum_fusion), channel_id=1, source_target_pairs={{0,8},{8,16},{16,24},{24,0},{1,9},{9,17},{17,25},{25,1},{2,10},{10... | collective-permute-start | bytes 786440 | tf_op jit(solution)/shard_map/ppermute | solution.py:369
  13.9 1.4 %collective-permute-start.3 = (bf16[272,128]{1,0:T(8,128)(2,1)S(1)}, bf16[272,128]{1,0:T(8,128)(2,1)S(1)}, u32[]{:S(2)}, u32[]{:S(2)}) collective-permute-start(bf16[272,128]{1,0:T(8,128)(2,1)S(1)} %get-tuple-element.45), channel_id=1, source_target_pairs={{0,6},{2,4},{4,2},{6,0},{1,7},{3,5},{5,3},{7,1},{8,14},{10,12},{12... | collective-permute-start | bytes 208904 | tf_op jit(solution)/shard_map/ppermute | solution.py:281
  15.3 2.1 %collective-permute-done.2.refs_3_ = bf16[512,128]{1,0:T(8,128)(2,1)S(1)} collective-permute-done((bf16[512,128]{1,0:T(8,128)(2,1)S(1)}, bf16[512,128]{1,0:T(8,128)(2,1)S(1)}, u32[]{:S(2)}, u32[]{:S(2)}) %collective-permute-start.2) | collective-permute-done | bytes 131104 | tf_op jit(solution)/shard_map/ppermute | solution.py:281
  17.4 1.6 %collective-permute-start.5 = (bf16[1,512,128]{2,1,0:T(8,128)(2,1)S(1)}, bf16[1,512,128]{2,1,0:T(8,128)(2,1)S(1)}, u32[]{:S(2)}, u32[]{:S(2)}) collective-permute-start(bf16[1,512,128]{2,1,0:T(8,128)(2,1)S(1)} %fusion.1), channel_id=1, source_target_pairs={{0,8},{8,16},{16,24},{24,0},{1,9},{9,17},{17,25},{25,1},{2,10},{10... | collective-permute-start | bytes 393224 | tf_op jit(solution)/shard_map/ppermute | solution.py:369
  19.1 0.0 collective-permute-done.3.refs_4_
  19.1 1.7 %near.1 = (bf16[4,272,128]{2,1,0:T(8,128)(2,1)S(1)}, f32[4,128,256]{2,1,0:T(8,128)S(1)}, f32[4,8,256]{2,1,0:T(8,128)S(1)}) custom-call(bf16[784,128]{1,0:T(8,128)(2,1)S(1)} %get-tuple-element.41.block_ref.refs_0_, bf16[784,128]{1,0:T(8,128)(2,1)S(1)} %collective-permute-done.refs_1_, bf16[784,128]{1,0:T(8,128)(2,1)S(1)} %collective-permute-done.1.refs_2_, ...), custom_call_target="tpu_custom_call" | custom-call | flops 1 | bytes 1 | tf_op jit(solution)/shard_map/near/pallas_call | solution.py:375
  20.8 1.4 %collective-permute-done.4.refs_3_ = bf16[2,512,128]{2,1,0:T(8,128)(2,1)S(1)} collective-permute-done((bf16[2,512,128]{2,1,0:T(8,128)(2,1)S(1)}, bf16[2,512,128]{2,1,0:T(8,128)(2,1)S(1)}, u32[]{:S(2)}, u32[]{:S(2)}) %collective-permute-start.4) | collective-permute-done | bytes 262176 | tf_op jit(solution)/shard_map/ppermute | solution.py:369
  22.2 1.2 %far.2 = (f32[4,128,256]{2,1,0:T(8,128)S(1)}, f32[4,8,256]{2,1,0:T(8,128)S(1)}) custom-call(bf16[4,272,128]{2,1,0:T(8,128)(2,1)S(1)} %get-tuple-element.46.refs_0_, f32[4,128,256]{2,1,0:T(8,128)S(1)} %get-tuple-element.47.refs_1_, f32[4,8,256]{2,1,0:T(8,128)S(1)} %get-tuple-element.48.refs_2_, bf16[2,512,128]{2,1,0:T(8,128)(2,1)S(1)} %collective-permute-done.4.refs_3_), custom_call_target="tpu_custom_call" | custom-call | flops 4000000000 | bytes 1 | tf_op jit(solution)/shard_map/far/pallas_call | solution.py:393
  23.4 0.9 %collective-permute-done.5.refs_3_ = bf16[1,512,128]{2,1,0:T(8,128)(2,1)S(1)} collective-permute-done((bf16[1,512,128]{2,1,0:T(8,128)(2,1)S(1)}, bf16[1,512,128]{2,1,0:T(8,128)(2,1)S(1)}, u32[]{:S(2)}, u32[]{:S(2)}) %collective-permute-start.5) | collective-permute-done | bytes 131104 | tf_op jit(solution)/shard_map/ppermute | solution.py:369
  24.3 1.1 %far.3 = (bf16[128,256]{1,0:T(8,128)(2,1)S(1)}, bf16[128,256]{1,0:T(8,128)(2,1)S(1)}, bf16[128,256]{1,0:T(8,128)(2,1)S(1)}, bf16[128,256]{1,0:T(8,128)(2,1)S(1)}) custom-call(bf16[4,272,128]{2,1,0:T(8,128)(2,1)S(1)} %get-tuple-element.46.refs_0_, f32[4,128,256]{2,1,0:T(8,128)S(1)} %get-tuple-element.50.refs_1_, f32[4,8,256]{2,1,0:T(8,128)S(1)} %get-tuple-element.51.refs_2_, ...), custom_call_target="tpu_custom_call" | custom-call | flops 4000000000 | bytes 1 | tf_op jit(solution)/shard_map/far/pallas_call | solution.py:393
  25.3 1.0 %collective-permute-start.6 = (bf16[128,256]{1,0:T(8,128)(2,1)S(1)}, bf16[128,256]{1,0:T(8,128)(2,1)S(1)}, u32[]{:S(2)}, u32[]{:S(2)}) collective-permute-start(bf16[128,256]{1,0:T(8,128)(2,1)S(1)} %get-tuple-element.54), channel_id=1, source_target_pairs={{0,6},{2,4},{4,2},{6,0},{1,7},{3,5},{5,3},{7,1},{8,14},{10,12},{12... | collective-permute-start | bytes 196616 | tf_op jit(solution)/shard_map/ppermute | solution.py:281
  26.3 0.7 %collective-permute-start.7 = (bf16[128,256]{1,0:T(8,128)(2,1)S(1)}, bf16[128,256]{1,0:T(8,128)(2,1)S(1)}, u32[]{:S(2)}, u32[]{:S(2)}) collective-permute-start(bf16[128,256]{1,0:T(8,128)(2,1)S(1)} %get-tuple-element.55), channel_id=1, source_target_pairs={{0,2},{2,0},{4,6},{6,4},{1,3},{3,1},{5,7},{7,5},{8,10},{10,8},{12,... | collective-permute-start | bytes 196616 | tf_op jit(solution)/shard_map/ppermute | solution.py:281
  27.1 1.8 %collective-permute-start.8 = (bf16[128,256]{1,0:T(8,128)(2,1)S(1)}, bf16[128,256]{1,0:T(8,128)(2,1)S(1)}, u32[]{:S(2)}, u32[]{:S(2)}) collective-permute-start(bf16[128,256]{1,0:T(8,128)(2,1)S(1)} %get-tuple-element.56), channel_id=1, source_target_pairs={{0,4},{2,6},{4,0},{6,2},{1,5},{3,7},{5,1},{7,3},{8,12},{10,14},{12... | collective-permute-start | bytes 196616 | tf_op jit(solution)/shard_map/ppermute | solution.py:281
  28.9 0.0 collective-permute-start.9
  28.9 1.7 %collective-permute-done.6.refs_1_ = bf16[128,256]{1,0:T(8,128)(2,1)S(1)} collective-permute-done((bf16[128,256]{1,0:T(8,128)(2,1)S(1)}, bf16[128,256]{1,0:T(8,128)(2,1)S(1)}, u32[]{:S(2)}, u32[]{:S(2)}) %collective-permute-start.6) | collective-permute-done | bytes 65568 | tf_op jit(solution)/shard_map/ppermute | solution.py:281
  30.6 0.0 collective-permute-start.10
  30.6 0.0 collective-permute-done.7.refs_2_
  30.6 0.5 %collective-permute-start.11 = (bf16[128,256]{1,0:T(8,128)(2,1)S(1)}, bf16[128,256]{1,0:T(8,128)(2,1)S(1)}, u32[]{:S(2)}, u32[]{:S(2)}) collective-permute-start(bf16[128,256]{1,0:T(8,128)(2,1)S(1)} %collective-permute-done.7.refs_2_), channel_id=1, source_target_pairs={{0,1},{1,0},{2,3},{3,2},{4,5},{5,4},{6,7},{7,6},{8,9},{9,8},{10,11... | collective-permute-start | bytes 196616 | tf_op jit(solution)/shard_map/ppermute | solution.py:281
  31.1 0.3 collective-permute-done.8.refs_3_
  31.4 0.0 collective-permute-start.12
  31.4 0.0 collective-permute-done.9.refs_4_
  31.4 0.5 %collective-permute-done.10.refs_5_ = bf16[128,256]{1,0:T(8,128)(2,1)S(1)} collective-permute-done((bf16[128,256]{1,0:T(8,128)(2,1)S(1)}, bf16[128,256]{1,0:T(8,128)(2,1)S(1)}, u32[]{:S(2)}, u32[]{:S(2)}) %collective-permute-start.10) | collective-permute-done | bytes 65568 | tf_op jit(solution)/shard_map/ppermute | solution.py:281
  31.8 0.2 collective-permute-done.11.refs_6_
  32.0 0.6 %collective-permute-done.12.refs_7_ = bf16[128,256]{1,0:T(8,128)(2,1)S(1)} collective-permute-done((bf16[128,256]{1,0:T(8,128)(2,1)S(1)}, bf16[128,256]{1,0:T(8,128)(2,1)S(1)}, u32[]{:S(2)}, u32[]{:S(2)}) %collective-permute-start.12) | collective-permute-done | bytes 65568 | tf_op jit(solution)/shard_map/ppermute | solution.py:281
  32.6 1.2 %project.1 = bf16[512,256]{1,0:T(8,128)(2,1)} custom-call(bf16[2,512,512]{2,1,0:T(8,128)(2,1)S(1)} %turn.1.turned_ref, bf16[128,256]{1,0:T(8,128)(2,1)S(1)} %get-tuple-element.53.refs_0_, bf16[128,256]{1,0:T(8,128)(2,1)S(1)} %collective-permute-done.6.refs_1_, bf16[128,256]{1,0:T(8,128)(2,1)S(1)} %collective-permute-done.7.refs_2_, ...), custom_call_target="tpu_custom_call" | custom-call | tf_op jit(solution)/shard_map/project/pallas_call | solution.py:418
  (3 shorter events, 0.1 us)
Async XLA Ops:
  1.2 8.0 %collective-permute-start = (bf16[784,128]{1,0:T(8,128)(2,1)S(1)}, bf16[784,128]{1,0:T(8,128)(2,1)S(1)}, u32[]{:S(2)}, u32[]{:S(2)}) collective-permute-start(bf16[784,128]{1,0:T(8,128)(2,1)S(1)} %get-tuple-element.32), channel_id=1, source_target_pairs={{0,2},{2,0},{4,6},{6,4},{1,3},{3,1},{5,7},{7,5},{8,10},{10,8},{12,... | collective-permute-start | bytes 602120 | tf_op jit(solution)/shard_map/ppermute | solution.py:281
  4.2 6.4 %collective-permute-start.1 = (bf16[784,128]{1,0:T(8,128)(2,1)S(1)}, bf16[784,128]{1,0:T(8,128)(2,1)S(1)}, u32[]{:S(2)}, u32[]{:S(2)}) collective-permute-start(bf16[784,128]{1,0:T(8,128)(2,1)S(1)} %get-tuple-element.34), channel_id=1, source_target_pairs={{0,4},{2,6},{4,0},{6,2},{1,5},{3,7},{5,1},{7,3},{8,12},{10,14},{12... | collective-permute-start | bytes 602120 | tf_op jit(solution)/shard_map/ppermute | solution.py:281
  10.7 6.7 %collective-permute-start.2 = (bf16[512,128]{1,0:T(8,128)(2,1)S(1)}, bf16[512,128]{1,0:T(8,128)(2,1)S(1)}, u32[]{:S(2)}, u32[]{:S(2)}) collective-permute-start(bf16[512,128]{1,0:T(8,128)(2,1)S(1)} %get-tuple-element.37), channel_id=1, source_target_pairs={{0,6},{2,4},{4,2},{6,0},{1,7},{3,5},{5,3},{7,1},{8,14},{10,12},{12... | collective-permute-start | bytes 393224 | tf_op jit(solution)/shard_map/ppermute | solution.py:281
  12.3 9.9 %collective-permute-start.4 = (bf16[2,512,128]{2,1,0:T(8,128)(2,1)S(1)}, bf16[2,512,128]{2,1,0:T(8,128)(2,1)S(1)}, u32[]{:S(2)}, u32[]{:S(2)}) collective-permute-start(bf16[2,512,128]{2,1,0:T(8,128)(2,1)S(1)} %pad_maximum_fusion), channel_id=1, source_target_pairs={{0,8},{8,16},{16,24},{24,0},{1,9},{9,17},{17,25},{25,1},{2,10},{10... | collective-permute-start | bytes 786440 | tf_op jit(solution)/shard_map/ppermute | solution.py:369
  13.9 5.2 %collective-permute-start.3 = (bf16[272,128]{1,0:T(8,128)(2,1)S(1)}, bf16[272,128]{1,0:T(8,128)(2,1)S(1)}, u32[]{:S(2)}, u32[]{:S(2)}) collective-permute-start(bf16[272,128]{1,0:T(8,128)(2,1)S(1)} %get-tuple-element.45), channel_id=1, source_target_pairs={{0,6},{2,4},{4,2},{6,0},{1,7},{3,5},{5,3},{7,1},{8,14},{10,12},{12... | collective-permute-start | bytes 208904 | tf_op jit(solution)/shard_map/ppermute | solution.py:281
  17.4 6.8 %collective-permute-start.5 = (bf16[1,512,128]{2,1,0:T(8,128)(2,1)S(1)}, bf16[1,512,128]{2,1,0:T(8,128)(2,1)S(1)}, u32[]{:S(2)}, u32[]{:S(2)}) collective-permute-start(bf16[1,512,128]{2,1,0:T(8,128)(2,1)S(1)} %fusion.1), channel_id=1, source_target_pairs={{0,8},{8,16},{16,24},{24,0},{1,9},{9,17},{17,25},{25,1},{2,10},{10... | collective-permute-start | bytes 393224 | tf_op jit(solution)/shard_map/ppermute | solution.py:369
  25.3 5.2 %collective-permute-start.6 = (bf16[128,256]{1,0:T(8,128)(2,1)S(1)}, bf16[128,256]{1,0:T(8,128)(2,1)S(1)}, u32[]{:S(2)}, u32[]{:S(2)}) collective-permute-start(bf16[128,256]{1,0:T(8,128)(2,1)S(1)} %get-tuple-element.54), channel_id=1, source_target_pairs={{0,6},{2,4},{4,2},{6,0},{1,7},{3,5},{5,3},{7,1},{8,14},{10,12},{12... | collective-permute-start | bytes 196616 | tf_op jit(solution)/shard_map/ppermute | solution.py:281
  26.3 4.3 %collective-permute-start.7 = (bf16[128,256]{1,0:T(8,128)(2,1)S(1)}, bf16[128,256]{1,0:T(8,128)(2,1)S(1)}, u32[]{:S(2)}, u32[]{:S(2)}) collective-permute-start(bf16[128,256]{1,0:T(8,128)(2,1)S(1)} %get-tuple-element.55), channel_id=1, source_target_pairs={{0,2},{2,0},{4,6},{6,4},{1,3},{3,1},{5,7},{7,5},{8,10},{10,8},{12,... | collective-permute-start | bytes 196616 | tf_op jit(solution)/shard_map/ppermute | solution.py:281
  27.1 4.3 %collective-permute-start.8 = (bf16[128,256]{1,0:T(8,128)(2,1)S(1)}, bf16[128,256]{1,0:T(8,128)(2,1)S(1)}, u32[]{:S(2)}, u32[]{:S(2)}) collective-permute-start(bf16[128,256]{1,0:T(8,128)(2,1)S(1)} %get-tuple-element.56), channel_id=1, source_target_pairs={{0,4},{2,6},{4,0},{6,2},{1,5},{3,7},{5,1},{7,3},{8,12},{10,14},{12... | collective-permute-start | bytes 196616 | tf_op jit(solution)/shard_map/ppermute | solution.py:281
  28.9 2.5 %collective-permute-start.9 = (bf16[128,256]{1,0:T(8,128)(2,1)S(1)}, bf16[128,256]{1,0:T(8,128)(2,1)S(1)}, u32[]{:S(2)}, u32[]{:S(2)}) collective-permute-start(bf16[128,256]{1,0:T(8,128)(2,1)S(1)} %get-tuple-element.53.refs_0_), channel_id=1, source_target_pairs={{0,1},{1,0},{2,3},{3,2},{4,5},{5,4},{6,7},{7,6},{8,9},{9,8},{10,11... | collective-permute-start | bytes 196616 | tf_op jit(solution)/shard_map/ppermute | solution.py:281
  30.6 1.3 %collective-permute-start.10 = (bf16[128,256]{1,0:T(8,128)(2,1)S(1)}, bf16[128,256]{1,0:T(8,128)(2,1)S(1)}, u32[]{:S(2)}, u32[]{:S(2)}) collective-permute-start(bf16[128,256]{1,0:T(8,128)(2,1)S(1)} %collective-permute-done.6.refs_1_), channel_id=1, source_target_pairs={{0,1},{1,0},{2,3},{3,2},{4,5},{5,4},{6,7},{7,6},{8,9},{9,8},{10,11... | collective-permute-start | bytes 196616 | tf_op jit(solution)/shard_map/ppermute | solution.py:281
  30.6 1.4 %collective-permute-start.11 = (bf16[128,256]{1,0:T(8,128)(2,1)S(1)}, bf16[128,256]{1,0:T(8,128)(2,1)S(1)}, u32[]{:S(2)}, u32[]{:S(2)}) collective-permute-start(bf16[128,256]{1,0:T(8,128)(2,1)S(1)} %collective-permute-done.7.refs_2_), channel_id=1, source_target_pairs={{0,1},{1,0},{2,3},{3,2},{4,5},{5,4},{6,7},{7,6},{8,9},{9,8},{10,11... | collective-permute-start | bytes 196616 | tf_op jit(solution)/shard_map/ppermute | solution.py:281
  31.4 1.3 %collective-permute-start.12 = (bf16[128,256]{1,0:T(8,128)(2,1)S(1)}, bf16[128,256]{1,0:T(8,128)(2,1)S(1)}, u32[]{:S(2)}, u32[]{:S(2)}) collective-permute-start(bf16[128,256]{1,0:T(8,128)(2,1)S(1)} %collective-permute-done.8.refs_3_), channel_id=1, source_target_pairs={{0,1},{1,0},{2,3},{3,2},{4,5},{5,4},{6,7},{7,6},{8,9},{9,8},{10,11... | collective-permute-start | bytes 196616 | tf_op jit(solution)/shard_map/ppermute | solution.py:281

commit v8 on v7

v8 whole, which is shorter than its diff:
```python
import functools

import jax
import jax.numpy as jnp
from jax import lax
from jax.experimental import pallas as pl
from jax.experimental.pallas import tpu as pltpu
from jax.sharding import Mesh, PartitionSpec as P

HEADS = 8
HD = 128
TILE = 128
SLOTS = 2
STEPS = 4
LOG2E = 1.4426950408889634
SCALE = LOG2E * HD ** (-0.5)
MASKED = -1e30
EXTRA = 16
OWN = 10**9
NEAR = 1000000000
MORE = 1000000000
FAR = 1
VMEM = pl.BlockSpec(memory_space=pltpu.VMEM)
HBM = pl.BlockSpec(memory_space=pltpu.HBM)
PARAMS = pltpu.CompilerParams(vmem_limit_bytes=48 * 1024 * 1024)


def use_rows(index_ref, count_ref, tiles):
    row = lax.broadcasted_iota(jnp.int32, (EXTRA, HD), 0)
    uses = jnp.zeros((EXTRA, HD), jnp.float32)
    for turn in range(STEPS):
        for dest in range(tiles):
            for source in range(tiles):
                times = jnp.float32(0)
                for slot in range(SLOTS):
                    used = (slot < count_ref[dest, turn]) & (index_ref[dest, slot, turn] == source)
                    times += jnp.where(used, 1.0, 0.0)
                uses = jnp.where(row == (turn * tiles + dest) * tiles + source, times, uses)
    return uses


def hops(step):
    return step.bit_count()


def query_places(refs, group, rows):
    apart = iter(refs[group:])
    return [
        next(apart) if hops(step) > 1 else refs[step].at[pl.ds(2 * rows, rows + EXTRA)]
        for step in range(group)
    ]


def pack_kernel(query_ref, key_ref, value_ref, index_ref, count_ref, *refs):
    out_refs, (values, index, count, sem) = refs[:-4], refs[-4:]
    group = query_ref.shape[1] // HD
    block_refs, query_refs = out_refs[:group], query_places(out_refs, group, query_ref.shape[0])
    rows = query_ref.shape[0]
    tiles = rows // TILE
    place = lax.axis_index("place")
    value_copy = pltpu.make_async_copy(value_ref, values, sem.at[0])
    value_copy.start()
    table_copies = [
        pltpu.make_async_copy(index_ref, index, sem.at[1]),
        pltpu.make_async_copy(count_ref, count, sem.at[2]),
    ]
    for copy in table_copies:
        copy.start()
    copies = []
    for step in range(group):
        cols = pl.ds(pl.multiple_of(jnp.bitwise_xor(place, step) * HD, HD), HD)
        copies += [
            pltpu.make_async_copy(
                key_ref.at[:, cols], block_refs[step].at[pl.ds(0, rows)], sem.at[3 + 2 * step]
            ),
            pltpu.make_async_copy(
                query_ref.at[:, cols], query_refs[step].at[pl.ds(0, rows)], sem.at[4 + 2 * step]
            ),
        ]
    for copy in copies:
        copy.start()
    for copy in table_copies:
        copy.wait()
    uses = use_rows(index, count, tiles).astype(jnp.bfloat16)
    value_copy.wait()
    for step in range(group):
        cols = pl.ds(pl.multiple_of(jnp.bitwise_xor(place, step) * HD, HD), HD)
        out = block_refs[step]
        query_refs[step][rows:] = uses
        for at in range(0, rows, TILE):
            out[rows + at : rows + at + TILE] = values[at : at + TILE, cols].T
    for copy in copies:
        copy.wait()


def pair_scores(keys, query_ref, turn):
    rows = keys.shape[0]
    tiles = rows // TILE
    raw = (
        lax.dot_general(
            keys, query_ref[:rows], (((1,), (1,)), ((), ())), preferred_element_type=jnp.float32
        )
        * SCALE
    )
    uses = query_ref[rows:].astype(jnp.float32)
    parts = []
    for source in range(tiles):
        bias = []
        for tile in range(tiles):
            at = (turn * tiles + tile) * tiles + source
            times = uses[at : at + 1]
            bias.append(jnp.where(times > 0.5, times - 1.0, MASKED))
        parts.append(
            raw[source * TILE : (source + 1) * TILE] + jnp.concatenate(bias, axis=1)
        )
    return raw, jnp.concatenate(parts, axis=0)


def own_scores(raw):
    eye = lax.broadcasted_iota(jnp.int32, (TILE, TILE), 0) == lax.broadcasted_iota(
        jnp.int32, (TILE, TILE), 1
    )
    return jnp.concatenate(
        [
            jnp.sum(
                jnp.where(eye, raw[at : at + TILE, at : at + TILE], 0.0), axis=0, keepdims=True
            )
            for at in range(0, raw.shape[0], TILE)
        ],
        axis=1,
    )


def turned_values(source_ref, rows):
    return jnp.concatenate(
        [source_ref[rows + at : rows + at + TILE] for at in range(0, rows, TILE)], axis=1
    )


def attend(query_ref, sources, before):
    rows = query_ref.shape[0] - EXTRA
    scores = []
    for source_ref, turn in sources:
        raw, score = pair_scores(source_ref[:rows], query_ref, turn)
        scores.append(score)
        if turn == 0:
            own = own_scores(raw)
    top = own if before is None else before[0]
    for score in scores:
        top = jnp.maximum(top, jnp.max(score, axis=0, keepdims=True))
    if before is None:
        total = jnp.exp2(own - top)
        own_ref = next(source_ref for source_ref, turn in sources if turn == 0)
        mixed = total * turned_values(own_ref, rows).astype(jnp.float32)
    else:
        factor = jnp.exp2(before[0] - top)
        total, mixed = before[1] * factor, before[2] * factor
    for score, (source_ref, _) in zip(scores, sources):
        weights = jnp.exp2(score - top)
        total = total + jnp.sum(weights, axis=0, keepdims=True)
        mixed = mixed + jnp.dot(
            turned_values(source_ref, rows),
            weights.astype(jnp.bfloat16),
            preferred_element_type=jnp.float32,
        )
    return top, total, mixed


def sources_of(group, place, step):
    result = []
    for turn in range(STEPS):
        slab = (place ^ step) - turn
        result.append(((-(slab // group), place ^ (slab % group)), turn))
    return result


def stage_plan(group):
    steps = list(range(group))
    near = [step for step in steps if hops(step) < 2]
    stages = [(near, lambda offset, step: hops(step) < 2 and (offset == 0 or step == 0))]
    if len(near) < group:
        stages.append((steps, lambda offset, step: offset == 0 or step == 0))
    stages.append((steps, lambda offset, step: offset == 0 or hops(step) < 2))
    if len(near) < group:
        stages.append((steps, lambda offset, step: True))
    plan, taken = [], set()
    for dests, there in stages:
        work = []
        for place in range(group):
            table = {}
            for dest in dests:
                todo = [
                    (key, turn)
                    for key, turn in sources_of(group, place, dest)
                    if there(*key) and (place, dest, turn) not in taken
                ]
                taken.update((place, dest, turn) for _, turn in todo)
                if todo:
                    table[dest] = todo
            work.append(table)
        plan.append(work)
    return plan


def attend_kernel(*refs, names, work, started, active, ready, rows):
    named = dict(zip(names, refs))
    outs = refs[len(names) :]
    out_refs, state_refs = dict(zip(ready, outs)), outs[len(ready) :]
    group = len(work)

    def block(offset, step):
        for name in named:
            if name[0] == "halo" and name[1] == offset and step in name[2]:
                return named[name].at[name[2].index(step)]
        return named.get(("block", step), named.get(("kv", step)))

    def queries(step):
        if ("q", step) in named:
            return named["q", step]
        return named["block", step].at[pl.ds(2 * rows, rows + EXTRA)]

    here = lax.axis_index("place")
    for place in range(group):

        @pl.when(here == place)
        def _(place=place):
            for step in active:
                before = None
                if step in started:
                    mixed_ref, state_ref = named["mixed",], named["state",]
                    before = (state_ref[step, 0:1], state_ref[step, 1:2], mixed_ref[step])
                todo = [(block(*key), turn) for key, turn in work[place].get(step, [])]
                top, total, mixed = attend(queries(step), todo, before) if todo else before
                if step in ready:
                    out_refs[step][...] = (mixed / total).astype(out_refs[step].dtype)
                else:
                    state_refs[0][step] = mixed
                    state_refs[1][step, 0:1] = top
                    state_refs[1][step, 1:2] = total


def turn_kernel(block_ref, weight_ref, turned_ref, held, sem, *, head_total):
    me = lax.axis_index("head")
    depth = weight_ref.shape[0] // head_total
    features = weight_ref.shape[1] // head_total
    copies = []
    for other in range(head_total):
        start = pl.multiple_of(jnp.bitwise_xor(me, other) * depth, depth)
        cols = pl.ds(pl.multiple_of(me * features, features), features)
        copies.append(
            pltpu.make_async_copy(
                weight_ref.at[pl.ds(start, depth), cols], held.at[other], sem.at[other]
            )
        )
        copies[-1].start()
    for other in range(head_total):
        copies[other].wait()
        turned_ref[other] = held[other].T


def sending_order(group):
    return sorted(range(group), key=lambda step: (step > 0, -hops(step), step))


def project_kernel(turned_ref, *refs, group, head_total):
    mix_refs, out_ref, mix = refs[:-2], refs[-2], refs[-1]
    place = lax.axis_index("place")
    for other in range(head_total):
        for at, step in enumerate(sending_order(group)):
            mix[other, jnp.bitwise_xor(place, step)] = mix_refs[other * group + at][...]
    result = None
    for other in range(head_total):
        part = jnp.dot(
            turned_ref[other],
            mix[other].reshape(turned_ref.shape[2], out_ref.shape[1]),
            preferred_element_type=jnp.float32,
        )
        result = part if result is None else result + part
    out_ref[...] = result.astype(out_ref.dtype)


def swapped(value, axis, step):
    count = lax.axis_size(axis)
    return lax.ppermute(value, axis, [(source, source ^ step) for source in range(count)])


def on_device(node_queries, node_keys, node_values, tile_index, tile_count, out_weight):
    rows, width = node_queries.shape
    group = width // HD
    groups = lax.axis_size("group")
    head_total = lax.axis_size("head")
    depth, feature_total = out_weight.shape
    features = feature_total // head_total
    bf16, f32 = jnp.bfloat16, jnp.float32
    shape = jax.ShapeDtypeStruct

    apart = [step for step in range(group) if hops(step) > 1]
    whole_block, query_block = shape((3 * rows + EXTRA, HD), bf16), shape((rows + EXTRA, HD), bf16)
    packed = pl.pallas_call(
        pack_kernel,
        out_shape=[
            shape((2 * rows, HD), bf16) if step in apart else whole_block for step in range(group)
        ]
        + [query_block] * len(apart),
        in_specs=[HBM] * 5,
        out_specs=[VMEM] * (group + len(apart)),
        scratch_shapes=[
            pltpu.VMEM((rows, width), bf16),
            pltpu.SMEM((rows // TILE, SLOTS, STEPS), jnp.int32),
            pltpu.SMEM((rows // TILE, STEPS), jnp.int32),
            pltpu.SemaphoreType.DMA((3 + 2 * group,)),
        ],
        compiler_params=PARAMS,
        name="pack",
    )(
        *[
            pltpu.with_memory_space_constraint(array, pltpu.HBM)
            for array in (
                node_queries,
                node_keys,
                node_values,
                jnp.transpose(tile_index, (1, 2, 0)),
                jnp.transpose(tile_count, (1, 0)),
            )
        ],
    )

    turned = pl.pallas_call(
        functools.partial(turn_kernel, head_total=head_total),
        out_shape=shape((head_total, features, depth // head_total), bf16),
        in_specs=[HBM, HBM],
        out_specs=VMEM,
        scratch_shapes=[
            pltpu.VMEM((head_total, depth // head_total, features), bf16),
            pltpu.SemaphoreType.DMA((head_total,)),
        ],
        compiler_params=PARAMS,
        cost_estimate=pl.CostEstimate(flops=OWN, transcendentals=1, bytes_accessed=1),
        name="turn",
    )(packed[0], pltpu.with_memory_space_constraint(out_weight, pltpu.HBM))

    offsets = list(range(1, -(-(STEPS - 1) // group) + 1))
    plan = stage_plan(group)
    finish = [
        max(at for at, work in enumerate(plan) for table in work if step in table)
        for step in range(group)
    ]
    arrays = {("block", 0): packed[0]}
    near = [step for step in range(1, group) if hops(step) < 2]
    first = ("halo", 1, (0,))

    def send_on(steps):
        blocks = [arrays.get(("block", step), arrays.get(("kv", step))) for step in steps]
        message = jnp.stack([block[: 2 * rows] for block in blocks])
        if steps == near:
            message, arrays[first] = lax.optimization_barrier((message, arrays[first]))
        if steps[0] in apart:
            message, arrays["state",] = lax.optimization_barrier((message, arrays["state",]))
        for offset in offsets:
            pairs = [(source, (source + offset) % groups) for source in range(groups)]
            arrays["halo", offset, tuple(steps)] = lax.ppermute(message, "group", pairs)

    def stage(at, cost):
        work = plan[at]
        started = [
            step
            for step in range(group)
            if finish[step] >= at and any(step in table for work in plan[:at] for table in work)
        ]
        active = sorted(set(started) | {step for table in work for step in table})
        ready = [step for step in active if finish[step] == at]
        keys = {key for table in work for todo in table.values() for key, _ in todo}
        dests = {step for table in work for step in table}
        names = []
        for name in arrays:
            if name[0] == "halo":
                used = any((name[1], step) in keys for step in name[2])
            elif name[0] in ("block", "kv"):
                used = (0, name[1]) in keys or (name[0] == "block" and name[1] in dests)
            elif name[0] == "q":
                used = name[1] in dests
            else:
                used = bool(started)
            if used:
                names.append(name)
        states = [shape((group, HD, rows), f32), shape((group, 8, rows), f32)]
        if len(ready) == len(active):
            states = []
        outs = pl.pallas_call(
            functools.partial(
                attend_kernel,
                names=names,
                work=work,
                started=started,
                active=active,
                ready=ready,
                rows=rows,
            ),
            out_shape=[shape((HD, rows), bf16)] * len(ready) + states,
            in_specs=[VMEM] * len(names),
            out_specs=[VMEM] * (len(ready) + len(states)),
            compiler_params=PARAMS,
            cost_estimate=pl.CostEstimate(flops=cost, transcendentals=1, bytes_accessed=1),
            name="attend",
        )(*[arrays[name] for name in names])
        if states:
            arrays["mixed",], arrays["state",] = outs[len(ready) :]
        return dict(zip(ready, outs))

    for step in near:
        arrays["block", step] = swapped(packed[step], "place", step)
    arrays["block", 0], turned = lax.optimization_barrier((packed[0], turned))
    send_on([0])
    mix = {}
    held = packed[near[-1] + 1 :] if apart else []
    if apart:
        tied = lax.optimization_barrier((list(held), turned, arrays["block", 1]))
        held, turned, arrays["block", 1] = tied
    if near:
        send_on(near)
    for step, block in zip(apart, held):
        arrays["kv", step] = swapped(block, "place", step)
    mix.update(stage(0, NEAR))
    if apart:
        send_on(apart)
        for step, block in zip(apart, held[len(apart) :]):
            arrays["q", step] = swapped(block, "place", step)
    for at in range(1, len(plan)):
        done = stage(at, MORE if at == 1 and apart else FAR)
        order = [step for step in sending_order(group) if step in done]
        mix.update((step, swapped(done[step], "place", step) if step else done[0]) for step in order)

    mixes = [mix[step] for step in sending_order(group)]
    for other in range(1, head_total):
        mixes += [swapped(entry, "head", other) for entry in mixes[:group]]
    return pl.pallas_call(
        functools.partial(project_kernel, group=group, head_total=head_total),
        out_shape=shape((features, rows), bf16),
        in_specs=[VMEM] * (1 + head_total * group),
        out_specs=VMEM,
        scratch_shapes=[pltpu.VMEM((head_total, group, HD, rows), bf16)],
        compiler_params=PARAMS,
        name="project",
    )(turned, *mixes)


def solution(mesh):
    nodes, heads = mesh.devices.shape
    place = HEADS // heads
    split = Mesh(
        mesh.devices.reshape(nodes // place, place, heads), ("group", "place", "head")
    )
    node = ("group", "place")
    return jax.shard_map(
        on_device,
        mesh=split,
        in_specs=(
            P(node, "head"),
            P(node, "head"),
            P(node, "head"),
            P(None, node, None),
            P(None, node),
            P(),
        ),
        out_specs=P("head", node),
        check_vma=False,
    )
```

time: 34 us -> 35.8 us (1.053)
  waiting for transfers between devices: 11.1 us -> 15.1 us
  starting transfers between devices: 14.8 us -> 13 us
  Pallas kernels: 7.8 us -> 7.37 us
    ppermute x2 -> x3, waiting for transfers between devices: 2.28 us -> 5.39 us  [send_on(): arrays['halo', offset, tuple(steps)] = lax.ppermute(message, 'group', pairs)]
    ppermute x2 -> x3, starting transfers between devices: 3.21 us -> 1.63 us  [send_on(): arrays['halo', offset, tuple(steps)] = lax.ppermute(message, 'group', pairs)]
    ppermute x11, waiting for transfers between devices: 8.82 us -> 9.72 us  [swapped(): lax.ppermute(value, axis, [(source, source ^ step) for source in range(co...]
    pallas_call x3 -> x4, Pallas kernels: 3.96 us -> 3.53 us  [stage(): pl.pallas_call(functools.partial(attend_kernel, names=names, work=work, s...]
  transfers between devices with their start and end apart: 13 -> 14, of which waited for: 10 -> 11; matrix products, arithmetic and copies ran while one was open for 0% -> 0% of each run, Pallas kernels for 13% -> 14%
where the time goes in v8:
time: 35.8 us; the launch traced here: 35.6 us
  waiting for transfers between devices  15.1 us (42%)
  starting transfers between devices  13 us (36%)
  Pallas kernels  7.37 us (21%)
    ppermute x11, starting transfers between devices, swapped(): lax.ppermute(value, axis, [(source, source ^ step) for source in range(co...  11.4 us
    ppermute x11, waiting for transfers between devices, swapped(): lax.ppermute(value, axis, [(source, source ^ step) for source in range(co...  9.72 us
    ppermute x3, waiting for transfers between devices, send_on(): arrays['halo', offset, tuple(steps)] = lax.ppermute(message, 'group', pairs)  5.39 us
    pallas_call x4, Pallas kernels, stage(): pl.pallas_call(functools.partial(attend_kernel, names=names, work=work, s...  3.53 us
    ppermute x3, starting transfers between devices, send_on(): arrays['halo', offset, tuple(steps)] = lax.ppermute(message, 'group', pairs)  1.63 us
    pallas_call x1, Pallas kernels, on_device(): pl.pallas_call(functools.partial(turn_kernel, head_total=head_total), out...  1.44 us
    pallas_call x1, Pallas kernels, on_device(): pl.pallas_call(pack_kernel, out_shape=[shape((2 * rows, HD), bf16) if ste...  1.21 us
    pallas_call x1, Pallas kernels, on_device(): pl.pallas_call(functools.partial(project_kernel, group=group, head_total=...  1.19 us
  transfers between devices with their start and end apart: 14, of which 11 were waited for; matrix products, arithmetic and copies ran while one was open for 0% of the time, Pallas kernels for 14%

profile of v8, /device:TPU:0, one launch (start us, length us, event | category | flops | bytes accessed | tf_op | source)
XLA Modules:
  0.0 35.6 jit_solution(8103321669632599884)
XLA Ops:
  0.0 1.2 %pack.1 = (bf16[784,128]{1,0:T(8,128)(2,1)S(1)}, bf16[784,128]{1,0:T(8,128)(2,1)S(1)}, bf16[784,128]{1,0:T(8,128)(2,1)S(1)}, bf16[512,128]{1,0:T(8,128)(2,1)S(1)}, bf16[272,128]{1,0:T(8,128)(2,1)S(1)}) custom-call(bf16[256,512]{1,0:T(8,128)(2,1)} %query_ref.1, bf16[256,512]{1,0:T(8,128)(2,1)} %key_ref.1, bf16[256,512]{1,0:T(8,128)(2,1)} %value_ref.1, ...), custom_call_target="tpu_custom_call" | custom-call | tf_op jit(solution)/shard_map/pack/pallas_call | solution.py:299
  1.2 3.0 %collective-permute-start = (bf16[784,128]{1,0:T(8,128)(2,1)S(1)}, bf16[784,128]{1,0:T(8,128)(2,1)S(1)}, u32[]{:S(2)}, u32[]{:S(2)}) collective-permute-start(bf16[784,128]{1,0:T(8,128)(2,1)S(1)} %get-tuple-element.34), channel_id=1, source_target_pairs={{0,2},{2,0},{4,6},{6,4},{1,3},{3,1},{5,7},{7,5},{8,10},{10,8},{12,... | collective-permute-start | bytes 602120 | tf_op jit(solution)/shard_map/ppermute | solution.py:284
  4.2 1.5 %collective-permute-start.1 = (bf16[784,128]{1,0:T(8,128)(2,1)S(1)}, bf16[784,128]{1,0:T(8,128)(2,1)S(1)}, u32[]{:S(2)}, u32[]{:S(2)}) collective-permute-start(bf16[784,128]{1,0:T(8,128)(2,1)S(1)} %get-tuple-element.38), channel_id=1, source_target_pairs={{0,4},{2,6},{4,0},{6,2},{1,5},{3,7},{5,1},{7,3},{8,12},{10,14},{12... | collective-permute-start | bytes 602120 | tf_op jit(solution)/shard_map/ppermute | solution.py:284
  5.7 1.4 %turn.1.turned_ref = bf16[2,512,512]{2,1,0:T(8,128)(2,1)S(1)} custom-call(bf16[784,128]{1,0:T(8,128)(2,1)S(1)} %get-tuple-element.36.block_ref.refs_0_, bf16[1024,1024]{1,0:T(8,128)(2,1)} %weight_ref.1), custom_call_target="tpu_custom_call" | custom-call | flops 1000000000 | bytes 1 | tf_op jit(solution)/shard_map/turn/pallas_call | solution.py:328
  7.2 1.6 %collective-permute-start.2 = (bf16[1,512,128]{2,1,0:T(8,128)(2,1)S(1)}, bf16[1,512,128]{2,1,0:T(8,128)(2,1)S(1)}, u32[]{:S(2)}, u32[]{:S(2)}) collective-permute-start(bf16[1,512,128]{2,1,0:T(8,128)(2,1)S(1)} %slice_bitcast_fusion.1), channel_id=1, source_target_pairs={{0,8},{8,16},{16,24},{24,0},{1,9},{9,17},{17,25},{25,1},{2,10},{10... | collective-permute-start | bytes 393224 | tf_op jit(solution)/shard_map/ppermute | solution.py:361
  8.8 0.4 %collective-permute-done.refs_1_ = bf16[784,128]{1,0:T(8,128)(2,1)S(1)} collective-permute-done((bf16[784,128]{1,0:T(8,128)(2,1)S(1)}, bf16[784,128]{1,0:T(8,128)(2,1)S(1)}, u32[]{:S(2)}, u32[]{:S(2)}) %collective-permute-start) | collective-permute-done | bytes 200736 | tf_op jit(solution)/shard_map/ppermute | solution.py:284
  9.2 1.4 %collective-permute-done.1.refs_2_ = bf16[784,128]{1,0:T(8,128)(2,1)S(1)} collective-permute-done((bf16[784,128]{1,0:T(8,128)(2,1)S(1)}, bf16[784,128]{1,0:T(8,128)(2,1)S(1)}, u32[]{:S(2)}, u32[]{:S(2)}) %collective-permute-start.1) | collective-permute-done | bytes 200736 | tf_op jit(solution)/shard_map/ppermute | solution.py:284
  10.7 3.3 %collective-permute-done.2.refs_3_ = bf16[1,512,128]{2,1,0:T(8,128)(2,1)S(1)} collective-permute-done((bf16[1,512,128]{2,1,0:T(8,128)(2,1)S(1)}, bf16[1,512,128]{2,1,0:T(8,128)(2,1)S(1)}, u32[]{:S(2)}, u32[]{:S(2)}) %collective-permute-start.2) | collective-permute-done | bytes 131104 | tf_op jit(solution)/shard_map/ppermute | solution.py:361
  14.0 0.3 collective-permute-start.4
  14.3 0.0 collective-permute-start.3
  14.3 2.7 %collective-permute-start.5 = (bf16[272,128]{1,0:T(8,128)(2,1)S(1)}, bf16[272,128]{1,0:T(8,128)(2,1)S(1)}, u32[]{:S(2)}, u32[]{:S(2)}) collective-permute-start(bf16[272,128]{1,0:T(8,128)(2,1)S(1)} %get-tuple-element.45), channel_id=1, source_target_pairs={{0,6},{2,4},{4,2},{6,0},{1,7},{3,5},{5,3},{7,1},{8,14},{10,12},{12... | collective-permute-start | bytes 208904 | tf_op jit(solution)/shard_map/ppermute | solution.py:284
  17.0 1.2 %attend.4 = (f32[4,128,256]{2,1,0:T(8,128)S(1)}, f32[4,8,256]{2,1,0:T(8,128)S(1)}) custom-call(bf16[784,128]{1,0:T(8,128)(2,1)S(1)} %get-tuple-element.36.block_ref.refs_0_, bf16[784,128]{1,0:T(8,128)(2,1)S(1)} %collective-permute-done.refs_1_, bf16[784,128]{1,0:T(8,128)(2,1)S(1)} %collective-permute-done.1.refs_2_, ...), custom_call_target="tpu_custom_call" | custom-call | flops 1000000000 | bytes 1 | tf_op jit(solution)/shard_map/attend/pallas_call | solution.py:389
  18.2 1.7 %collective-permute-done.4.refs_4_ = bf16[512,128]{1,0:T(8,128)(2,1)S(1)} collective-permute-done((bf16[512,128]{1,0:T(8,128)(2,1)S(1)}, bf16[512,128]{1,0:T(8,128)(2,1)S(1)}, u32[]{:S(2)}, u32[]{:S(2)}) %collective-permute-start.4) | collective-permute-done | bytes 131104 | tf_op jit(solution)/shard_map/ppermute | solution.py:284
  19.9 0.0 collective-permute-start.6
  19.9 0.7 %collective-permute-done.5.refs_7_.refs_6_ = bf16[272,128]{1,0:T(8,128)(2,1)S(1)} collective-permute-done((bf16[272,128]{1,0:T(8,128)(2,1)S(1)}, bf16[272,128]{1,0:T(8,128)(2,1)S(1)}, u32[]{:S(2)}, u32[]{:S(2)}) %collective-permute-start.5) | collective-permute-done | bytes 69664 | tf_op jit(solution)/shard_map/ppermute | solution.py:284
  20.6 0.8 %attend.5 = (f32[4,128,256]{2,1,0:T(8,128)S(1)}, f32[4,8,256]{2,1,0:T(8,128)S(1)}) custom-call(bf16[784,128]{1,0:T(8,128)(2,1)S(1)} %get-tuple-element.36.block_ref.refs_0_, bf16[784,128]{1,0:T(8,128)(2,1)S(1)} %collective-permute-done.refs_1_, bf16[784,128]{1,0:T(8,128)(2,1)S(1)} %collective-permute-done.1.refs_2_, ...), custom_call_target="tpu_custom_call" | custom-call | flops 1000000000 | bytes 1 | tf_op jit(solution)/shard_map/attend/pallas_call | solution.py:389
  21.4 2.1 %collective-permute-done.3.refs_3_ = bf16[2,512,128]{2,1,0:T(8,128)(2,1)S(1)} collective-permute-done((bf16[2,512,128]{2,1,0:T(8,128)(2,1)S(1)}, bf16[2,512,128]{2,1,0:T(8,128)(2,1)S(1)}, u32[]{:S(2)}, u32[]{:S(2)}) %collective-permute-start.3) | collective-permute-done | bytes 262176 | tf_op jit(solution)/shard_map/ppermute | solution.py:361
  23.5 0.6 %attend.6 = (bf16[128,256]{1,0:T(8,128)(2,1)S(1)}, f32[4,128,256]{2,1,0:T(8,128)S(1)}, f32[4,8,256]{2,1,0:T(8,128)S(1)}) custom-call(bf16[784,128]{1,0:T(8,128)(2,1)S(1)} %get-tuple-element.36.block_ref.refs_0_, bf16[784,128]{1,0:T(8,128)(2,1)S(1)} %collective-permute-done.refs_1_, bf16[784,128]{1,0:T(8,128)(2,1)S(1)} %collective-permute-done.1.refs_2_, ...), custom_call_target="tpu_custom_call" | custom-call | flops 1 | bytes 1 | tf_op jit(solution)/shard_map/attend/pallas_call | solution.py:389
  24.1 3.0 %collective-permute-start.7 = (bf16[128,256]{1,0:T(8,128)(2,1)S(1)}, bf16[128,256]{1,0:T(8,128)(2,1)S(1)}, u32[]{:S(2)}, u32[]{:S(2)}) collective-permute-start(bf16[128,256]{1,0:T(8,128)(2,1)S(1)} %get-tuple-element.52), channel_id=1, source_target_pairs={{0,6},{2,4},{4,2},{6,0},{1,7},{3,5},{5,3},{7,1},{8,14},{10,12},{12... | collective-permute-start | bytes 196616 | tf_op jit(solution)/shard_map/ppermute | solution.py:284
  27.1 0.0 collective-permute-done.6.refs_5_
  27.1 1.0 %attend.7 = (bf16[128,256]{1,0:T(8,128)(2,1)S(1)}, bf16[128,256]{1,0:T(8,128)(2,1)S(1)}, bf16[128,256]{1,0:T(8,128)(2,1)S(1)}) custom-call(bf16[784,128]{1,0:T(8,128)(2,1)S(1)} %get-tuple-element.36.block_ref.refs_0_, bf16[784,128]{1,0:T(8,128)(2,1)S(1)} %collective-permute-done.refs_1_, bf16[784,128]{1,0:T(8,128)(2,1)S(1)} %collective-permute-done.1.refs_2_, ...), custom_call_target="tpu_custom_call" | custom-call | flops 1 | bytes 1 | tf_op jit(solution)/shard_map/attend/pallas_call | solution.py:389
  28.1 0.8 %collective-permute-start.8 = (bf16[128,256]{1,0:T(8,128)(2,1)S(1)}, bf16[128,256]{1,0:T(8,128)(2,1)S(1)}, u32[]{:S(2)}, u32[]{:S(2)}) collective-permute-start(bf16[128,256]{1,0:T(8,128)(2,1)S(1)} %get-tuple-element.53), channel_id=1, source_target_pairs={{0,2},{2,0},{4,6},{6,4},{1,3},{3,1},{5,7},{7,5},{8,10},{10,8},{12,... | collective-permute-start | bytes 196616 | tf_op jit(solution)/shard_map/ppermute | solution.py:284
  28.9 0.0 collective-permute-start.9
  28.9 0.0 collective-permute-start.10
  28.9 0.4 %collective-permute-done.7.refs_1_ = bf16[128,256]{1,0:T(8,128)(2,1)S(1)} collective-permute-done((bf16[128,256]{1,0:T(8,128)(2,1)S(1)}, bf16[128,256]{1,0:T(8,128)(2,1)S(1)}, u32[]{:S(2)}, u32[]{:S(2)}) %collective-permute-start.7) | collective-permute-done | bytes 65568 | tf_op jit(solution)/shard_map/ppermute | solution.py:284
  29.3 0.1 collective-permute-start.11
  29.4 3.0 %collective-permute-done.8.refs_2_ = bf16[128,256]{1,0:T(8,128)(2,1)S(1)} collective-permute-done((bf16[128,256]{1,0:T(8,128)(2,1)S(1)}, bf16[128,256]{1,0:T(8,128)(2,1)S(1)}, u32[]{:S(2)}, u32[]{:S(2)}) %collective-permute-start.8) | collective-permute-done | bytes 65568 | tf_op jit(solution)/shard_map/ppermute | solution.py:284
  32.4 0.0 collective-permute-start.12
  32.4 0.7 %collective-permute-done.9.refs_3_ = bf16[128,256]{1,0:T(8,128)(2,1)S(1)} collective-permute-done((bf16[128,256]{1,0:T(8,128)(2,1)S(1)}, bf16[128,256]{1,0:T(8,128)(2,1)S(1)}, u32[]{:S(2)}, u32[]{:S(2)}) %collective-permute-start.9) | collective-permute-done | bytes 65568 | tf_op jit(solution)/shard_map/ppermute | solution.py:284
  33.2 0.0 collective-permute-start.13
  33.2 0.0 collective-permute-done.10.refs_4_
  33.2 0.0 collective-permute-done.11.refs_5_
  33.2 0.5 %collective-permute-done.12.refs_6_ = bf16[128,256]{1,0:T(8,128)(2,1)S(1)} collective-permute-done((bf16[128,256]{1,0:T(8,128)(2,1)S(1)}, bf16[128,256]{1,0:T(8,128)(2,1)S(1)}, u32[]{:S(2)}, u32[]{:S(2)}) %collective-permute-start.12) | collective-permute-done | bytes 65568 | tf_op jit(solution)/shard_map/ppermute | solution.py:284
  33.7 0.7 %collective-permute-done.13.refs_7_ = bf16[128,256]{1,0:T(8,128)(2,1)S(1)} collective-permute-done((bf16[128,256]{1,0:T(8,128)(2,1)S(1)}, bf16[128,256]{1,0:T(8,128)(2,1)S(1)}, u32[]{:S(2)}, u32[]{:S(2)}) %collective-permute-start.13) | collective-permute-done | bytes 65568 | tf_op jit(solution)/shard_map/ppermute | solution.py:284
  34.4 1.2 %project.1 = bf16[512,256]{1,0:T(8,128)(2,1)} custom-call(bf16[2,512,512]{2,1,0:T(8,128)(2,1)S(1)} %turn.1.turned_ref, bf16[128,256]{1,0:T(8,128)(2,1)S(1)} %get-tuple-element.51.refs_0_, bf16[128,256]{1,0:T(8,128)(2,1)S(1)} %collective-permute-done.7.refs_1_, bf16[128,256]{1,0:T(8,128)(2,1)S(1)} %collective-permute-done.8.refs_2_, ...), custom_call_target="tpu_custom_call" | custom-call | tf_op jit(solution)/shard_map/project/pallas_call | solution.py:436
  (4 shorter events, 0.1 us)
Async XLA Ops:
  1.2 8.0 %collective-permute-start = (bf16[784,128]{1,0:T(8,128)(2,1)S(1)}, bf16[784,128]{1,0:T(8,128)(2,1)S(1)}, u32[]{:S(2)}, u32[]{:S(2)}) collective-permute-start(bf16[784,128]{1,0:T(8,128)(2,1)S(1)} %get-tuple-element.34), channel_id=1, source_target_pairs={{0,2},{2,0},{4,6},{6,4},{1,3},{3,1},{5,7},{7,5},{8,10},{10,8},{12,... | collective-permute-start | bytes 602120 | tf_op jit(solution)/shard_map/ppermute | solution.py:284
  4.2 6.4 %collective-permute-start.1 = (bf16[784,128]{1,0:T(8,128)(2,1)S(1)}, bf16[784,128]{1,0:T(8,128)(2,1)S(1)}, u32[]{:S(2)}, u32[]{:S(2)}) collective-permute-start(bf16[784,128]{1,0:T(8,128)(2,1)S(1)} %get-tuple-element.38), channel_id=1, source_target_pairs={{0,4},{2,6},{4,0},{6,2},{1,5},{3,7},{5,1},{7,3},{8,12},{10,14},{12... | collective-permute-start | bytes 602120 | tf_op jit(solution)/shard_map/ppermute | solution.py:284
  7.2 6.8 %collective-permute-start.2 = (bf16[1,512,128]{2,1,0:T(8,128)(2,1)S(1)}, bf16[1,512,128]{2,1,0:T(8,128)(2,1)S(1)}, u32[]{:S(2)}, u32[]{:S(2)}) collective-permute-start(bf16[1,512,128]{2,1,0:T(8,128)(2,1)S(1)} %slice_bitcast_fusion.1), channel_id=1, source_target_pairs={{0,8},{8,16},{16,24},{24,0},{1,9},{9,17},{17,25},{25,1},{2,10},{10... | collective-permute-start | bytes 393224 | tf_op jit(solution)/shard_map/ppermute | solution.py:361
  14.0 5.9 %collective-permute-start.4 = (bf16[512,128]{1,0:T(8,128)(2,1)S(1)}, bf16[512,128]{1,0:T(8,128)(2,1)S(1)}, u32[]{:S(2)}, u32[]{:S(2)}) collective-permute-start(bf16[512,128]{1,0:T(8,128)(2,1)S(1)} %get-tuple-element.41), channel_id=1, source_target_pairs={{0,6},{2,4},{4,2},{6,0},{1,7},{3,5},{5,3},{7,1},{8,14},{10,12},{12... | collective-permute-start | bytes 393224 | tf_op jit(solution)/shard_map/ppermute | solution.py:284
  14.3 9.2 %collective-permute-start.3 = (bf16[2,512,128]{2,1,0:T(8,128)(2,1)S(1)}, bf16[2,512,128]{2,1,0:T(8,128)(2,1)S(1)}, u32[]{:S(2)}, u32[]{:S(2)}) collective-permute-start(bf16[2,512,128]{2,1,0:T(8,128)(2,1)S(1)} %pad_maximum_fusion), channel_id=1, source_target_pairs={{0,8},{8,16},{16,24},{24,0},{1,9},{9,17},{17,25},{25,1},{2,10},{10... | collective-permute-start | bytes 786440 | tf_op jit(solution)/shard_map/ppermute | solution.py:361
  14.3 6.3 %collective-permute-start.5 = (bf16[272,128]{1,0:T(8,128)(2,1)S(1)}, bf16[272,128]{1,0:T(8,128)(2,1)S(1)}, u32[]{:S(2)}, u32[]{:S(2)}) collective-permute-start(bf16[272,128]{1,0:T(8,128)(2,1)S(1)} %get-tuple-element.45), channel_id=1, source_target_pairs={{0,6},{2,4},{4,2},{6,0},{1,7},{3,5},{5,3},{7,1},{8,14},{10,12},{12... | collective-permute-start | bytes 208904 | tf_op jit(solution)/shard_map/ppermute | solution.py:284
  19.9 7.2 %collective-permute-start.6 = (bf16[1,512,128]{2,1,0:T(8,128)(2,1)S(1)}, bf16[1,512,128]{2,1,0:T(8,128)(2,1)S(1)}, u32[]{:S(2)}, u32[]{:S(2)}) collective-permute-start(bf16[1,512,128]{2,1,0:T(8,128)(2,1)S(1)} %bitcast.9), channel_id=1, source_target_pairs={{0,8},{8,16},{16,24},{24,0},{1,9},{9,17},{17,25},{25,1},{2,10},{10... | collective-permute-start | bytes 393224 | tf_op jit(solution)/shard_map/ppermute | solution.py:361
  24.1 5.3 %collective-permute-start.7 = (bf16[128,256]{1,0:T(8,128)(2,1)S(1)}, bf16[128,256]{1,0:T(8,128)(2,1)S(1)}, u32[]{:S(2)}, u32[]{:S(2)}) collective-permute-start(bf16[128,256]{1,0:T(8,128)(2,1)S(1)} %get-tuple-element.52), channel_id=1, source_target_pairs={{0,6},{2,4},{4,2},{6,0},{1,7},{3,5},{5,3},{7,1},{8,14},{10,12},{12... | collective-permute-start | bytes 196616 | tf_op jit(solution)/shard_map/ppermute | solution.py:284
  28.1 4.3 %collective-permute-start.8 = (bf16[128,256]{1,0:T(8,128)(2,1)S(1)}, bf16[128,256]{1,0:T(8,128)(2,1)S(1)}, u32[]{:S(2)}, u32[]{:S(2)}) collective-permute-start(bf16[128,256]{1,0:T(8,128)(2,1)S(1)} %get-tuple-element.53), channel_id=1, source_target_pairs={{0,2},{2,0},{4,6},{6,4},{1,3},{3,1},{5,7},{7,5},{8,10},{10,8},{12,... | collective-permute-start | bytes 196616 | tf_op jit(solution)/shard_map/ppermute | solution.py:284
  28.9 4.3 %collective-permute-start.9 = (bf16[128,256]{1,0:T(8,128)(2,1)S(1)}, bf16[128,256]{1,0:T(8,128)(2,1)S(1)}, u32[]{:S(2)}, u32[]{:S(2)}) collective-permute-start(bf16[128,256]{1,0:T(8,128)(2,1)S(1)} %get-tuple-element.54), channel_id=1, source_target_pairs={{0,4},{2,6},{4,0},{6,2},{1,5},{3,7},{5,1},{7,3},{8,12},{10,14},{12... | collective-permute-start | bytes 196616 | tf_op jit(solution)/shard_map/ppermute | solution.py:284
  28.9 4.3 %collective-permute-start.10 = (bf16[128,256]{1,0:T(8,128)(2,1)S(1)}, bf16[128,256]{1,0:T(8,128)(2,1)S(1)}, u32[]{:S(2)}, u32[]{:S(2)}) collective-permute-start(bf16[128,256]{1,0:T(8,128)(2,1)S(1)} %get-tuple-element.51.refs_0_), channel_id=1, source_target_pairs={{0,1},{1,0},{2,3},{3,2},{4,5},{5,4},{6,7},{7,6},{8,9},{9,8},{10,11... | collective-permute-start | bytes 196616 | tf_op jit(solution)/shard_map/ppermute | solution.py:284
  29.3 3.8 %collective-permute-start.11 = (bf16[128,256]{1,0:T(8,128)(2,1)S(1)}, bf16[128,256]{1,0:T(8,128)(2,1)S(1)}, u32[]{:S(2)}, u32[]{:S(2)}) collective-permute-start(bf16[128,256]{1,0:T(8,128)(2,1)S(1)} %collective-permute-done.7.refs_1_), channel_id=1, source_target_pairs={{0,1},{1,0},{2,3},{3,2},{4,5},{5,4},{6,7},{7,6},{8,9},{9,8},{10,11... | collective-permute-start | bytes 196616 | tf_op jit(solution)/shard_map/ppermute | solution.py:284
  32.4 1.3 %collective-permute-start.12 = (bf16[128,256]{1,0:T(8,128)(2,1)S(1)}, bf16[128,256]{1,0:T(8,128)(2,1)S(1)}, u32[]{:S(2)}, u32[]{:S(2)}) collective-permute-start(bf16[128,256]{1,0:T(8,128)(2,1)S(1)} %collective-permute-done.8.refs_2_), channel_id=1, source_target_pairs={{0,1},{1,0},{2,3},{3,2},{4,5},{5,4},{6,7},{7,6},{8,9},{9,8},{10,11... | collective-permute-start | bytes 196616 | tf_op jit(solution)/shard_map/ppermute | solution.py:284
  33.2 1.3 %collective-permute-start.13 = (bf16[128,256]{1,0:T(8,128)(2,1)S(1)}, bf16[128,256]{1,0:T(8,128)(2,1)S(1)}, u32[]{:S(2)}, u32[]{:S(2)}) collective-permute-start(bf16[128,256]{1,0:T(8,128)(2,1)S(1)} %collective-permute-done.9.refs_3_), channel_id=1, source_target_pairs={{0,1},{1,0},{2,3},{3,2},{4,5},{5,4},{6,7},{7,6},{8,9},{9,8},{10,11... | collective-permute-start | bytes 196616 | tf_op jit(solution)/shard_map/ppermute | solution.py:284

commit v9 on v8

--- a/solution.py
+++ b/solution.py
@@ -18,8 +18,8 @@
 EXTRA = 16
 OWN = 10**9
 NEAR = 1000000000
-MORE = 1000000000
-FAR = 1
+MORE = 1
+FAR = 1000000000
 VMEM = pl.BlockSpec(memory_space=pltpu.VMEM)
 HBM = pl.BlockSpec(memory_space=pltpu.HBM)
 PARAMS = pltpu.CompilerParams(vmem_limit_bytes=48 * 1024 * 1024)
@@ -352,10 +352,6 @@
     def send_on(steps):
         blocks = [arrays.get(("block", step), arrays.get(("kv", step))) for step in steps]
         message = jnp.stack([block[: 2 * rows] for block in blocks])
-        if steps == near:
-            message, arrays[first] = lax.optimization_barrier((message, arrays[first]))
-        if steps[0] in apart:
-            message, arrays["state",] = lax.optimization_barrier((message, arrays["state",]))
         for offset in offsets:
             pairs = [(source, (source + offset) % groups) for source in range(groups)]
             arrays["halo", offset, tuple(steps)] = lax.ppermute(message, "group", pairs)
@@ -409,21 +405,22 @@
 
     for step in near:
         arrays["block", step] = swapped(packed[step], "place", step)
-    arrays["block", 0], turned = lax.optimization_barrier((packed[0], turned))
     send_on([0])
     mix = {}
     held = packed[near[-1] + 1 :] if apart else []
     if apart:
-        tied = lax.optimization_barrier((list(held), turned, arrays["block", 1]))
-        held, turned, arrays["block", 1] = tied
-    if near:
-        send_on(near)
+        tied = lax.optimization_barrier((list(held), turned, [arrays["block", step] for step in near]))
+        held, turned, blocks = tied
+        arrays.update((("block", step), block) for step, block in zip(near, blocks))
+    for step in near:
+        send_on([step])
     for step, block in zip(apart, held):
         arrays["kv", step] = swapped(block, "place", step)
     mix.update(stage(0, NEAR))
     if apart:
         send_on(apart)
         for step, block in zip(apart, held[len(apart) :]):
+            block, arrays[first] = lax.optimization_barrier((block, arrays[first]))
             arrays["q", step] = swapped(block, "place", step)
     for at in range(1, len(plan)):
         done = stage(at, MORE if at == 1 and apart else FAR)

time: 35.8 us -> 32.8 us (0.916)
  waiting for transfers between devices: 15.1 us -> 7.78 us
  starting transfers between devices: 13 us -> 17.4 us
    ppermute x3 -> x4, starting transfers between devices: 1.63 us -> 6.46 us  [send_on(): arrays['halo', offset, tuple(steps)] = lax.ppermute(message, 'group', pairs)]
    ppermute x3 -> x4, waiting for transfers between devices: 5.39 us -> 0.67 us  [send_on(): arrays['halo', offset, tuple(steps)] = lax.ppermute(message, 'group', pairs)]
    ppermute x11, waiting for transfers between devices: 9.72 us -> 7.11 us  [swapped(): lax.ppermute(value, axis, [(source, source ^ step) for source in range(co...]
    ppermute x11, starting transfers between devices: 11.4 us -> 10.9 us  [swapped(): lax.ppermute(value, axis, [(source, source ^ step) for source in range(co...]
  transfers between devices with their start and end apart: 14 -> 15, of which waited for: 11 -> 9; matrix products, arithmetic and copies ran while one was open for 0% -> 0% of each run, Pallas kernels for 14% -> 15%
where the time goes in v9:
time: 32.8 us; the launch traced here: 32.7 us
  starting transfers between devices  17.4 us (53%)
  waiting for transfers between devices  7.78 us (24%)
  Pallas kernels  7.37 us (22%)
    ppermute x11, starting transfers between devices, swapped(): lax.ppermute(value, axis, [(source, source ^ step) for source in range(co...  10.9 us
    ppermute x11, waiting for transfers between devices, swapped(): lax.ppermute(value, axis, [(source, source ^ step) for source in range(co...  7.11 us
    ppermute x4, starting transfers between devices, send_on(): arrays['halo', offset, tuple(steps)] = lax.ppermute(message, 'group', pairs)  6.46 us
    pallas_call x4, Pallas kernels, stage(): pl.pallas_call(functools.partial(attend_kernel, names=names, work=work, s...  3.53 us
    pallas_call x1, Pallas kernels, on_device(): pl.pallas_call(functools.partial(turn_kernel, head_total=head_total), out...  1.44 us
    pallas_call x1, Pallas kernels, on_device(): pl.pallas_call(pack_kernel, out_shape=[shape((2 * rows, HD), bf16) if ste...  1.21 us
    pallas_call x1, Pallas kernels, on_device(): pl.pallas_call(functools.partial(project_kernel, group=group, head_total=...  1.19 us
    ppermute x4, waiting for transfers between devices, send_on(): arrays['halo', offset, tuple(steps)] = lax.ppermute(message, 'group', pairs)  0.67 us
  transfers between devices with their start and end apart: 15, of which 9 were waited for; matrix products, arithmetic and copies ran while one was open for 0% of the time, Pallas kernels for 15%

profile of v9, /device:TPU:0, one launch (start us, length us, event | category | flops | bytes accessed | tf_op | source)
XLA Modules:
  0.0 32.7 jit_solution(12094520698564296973)
XLA Ops:
  0.0 1.2 %pack.1 = (bf16[784,128]{1,0:T(8,128)(2,1)S(1)}, bf16[784,128]{1,0:T(8,128)(2,1)S(1)}, bf16[784,128]{1,0:T(8,128)(2,1)S(1)}, bf16[512,128]{1,0:T(8,128)(2,1)S(1)}, bf16[272,128]{1,0:T(8,128)(2,1)S(1)}) custom-call(bf16[256,512]{1,0:T(8,128)(2,1)} %query_ref.1, bf16[256,512]{1,0:T(8,128)(2,1)} %key_ref.1, bf16[256,512]{1,0:T(8,128)(2,1)} %value_ref.1, ...), custom_call_target="tpu_custom_call" | custom-call | tf_op jit(solution)/shard_map/pack/pallas_call | solution.py:299
  1.2 3.0 %collective-permute-start = (bf16[784,128]{1,0:T(8,128)(2,1)S(1)}, bf16[784,128]{1,0:T(8,128)(2,1)S(1)}, u32[]{:S(2)}, u32[]{:S(2)}) collective-permute-start(bf16[784,128]{1,0:T(8,128)(2,1)S(1)} %get-tuple-element.30), channel_id=1, source_target_pairs={{0,2},{2,0},{4,6},{6,4},{1,3},{3,1},{5,7},{7,5},{8,10},{10,8},{12,... | collective-permute-start | bytes 602120 | tf_op jit(solution)/shard_map/ppermute | solution.py:284
  4.2 1.5 %collective-permute-start.1 = (bf16[784,128]{1,0:T(8,128)(2,1)S(1)}, bf16[784,128]{1,0:T(8,128)(2,1)S(1)}, u32[]{:S(2)}, u32[]{:S(2)}) collective-permute-start(bf16[784,128]{1,0:T(8,128)(2,1)S(1)} %get-tuple-element.31), channel_id=1, source_target_pairs={{0,4},{2,6},{4,0},{6,2},{1,5},{3,7},{5,1},{7,3},{8,12},{10,14},{12... | collective-permute-start | bytes 602120 | tf_op jit(solution)/shard_map/ppermute | solution.py:284
  5.8 1.6 %collective-permute-start.4 = (bf16[1,512,128]{2,1,0:T(8,128)(2,1)S(1)}, bf16[1,512,128]{2,1,0:T(8,128)(2,1)S(1)}, u32[]{:S(2)}, u32[]{:S(2)}) collective-permute-start(bf16[1,512,128]{2,1,0:T(8,128)(2,1)S(1)} %slice_bitcast_fusion), channel_id=1, source_target_pairs={{0,8},{8,16},{16,24},{24,0},{1,9},{9,17},{17,25},{25,1},{2,10},{10... | collective-permute-start | bytes 393224 | tf_op jit(solution)/shard_map/ppermute | solution.py:357
  7.4 1.4 %turn.1.turned_ref = bf16[2,512,512]{2,1,0:T(8,128)(2,1)S(1)} custom-call(bf16[784,128]{1,0:T(8,128)(2,1)S(1)} %get-tuple-element.29.block_ref.refs_0_, bf16[1024,1024]{1,0:T(8,128)(2,1)} %weight_ref.1), custom_call_target="tpu_custom_call" | custom-call | flops 1000000000 | bytes 1 | tf_op jit(solution)/shard_map/turn/pallas_call | solution.py:328
  8.8 0.4 %collective-permute-done.refs_1_ = bf16[784,128]{1,0:T(8,128)(2,1)S(1)} collective-permute-done((bf16[784,128]{1,0:T(8,128)(2,1)S(1)}, bf16[784,128]{1,0:T(8,128)(2,1)S(1)}, u32[]{:S(2)}, u32[]{:S(2)}) %collective-permute-start) | collective-permute-done | bytes 200736 | tf_op jit(solution)/shard_map/ppermute | solution.py:284
  9.2 1.5 %collective-permute-done.1.refs_2_ = bf16[784,128]{1,0:T(8,128)(2,1)S(1)} collective-permute-done((bf16[784,128]{1,0:T(8,128)(2,1)S(1)}, bf16[784,128]{1,0:T(8,128)(2,1)S(1)}, u32[]{:S(2)}, u32[]{:S(2)}) %collective-permute-start.1) | collective-permute-done | bytes 200736 | tf_op jit(solution)/shard_map/ppermute | solution.py:284
  10.7 1.5 %collective-permute-start.5 = (bf16[512,128]{1,0:T(8,128)(2,1)S(1)}, bf16[512,128]{1,0:T(8,128)(2,1)S(1)}, u32[]{:S(2)}, u32[]{:S(2)}) collective-permute-start(bf16[512,128]{1,0:T(8,128)(2,1)S(1)} %get-tuple-element.37), channel_id=1, source_target_pairs={{0,6},{2,4},{4,2},{6,0},{1,7},{3,5},{5,3},{7,1},{8,14},{10,12},{12... | collective-permute-start | bytes 393224 | tf_op jit(solution)/shard_map/ppermute | solution.py:284
  12.2 1.6 %collective-permute-start.2 = (bf16[1,512,128]{2,1,0:T(8,128)(2,1)S(1)}, bf16[1,512,128]{2,1,0:T(8,128)(2,1)S(1)}, u32[]{:S(2)}, u32[]{:S(2)}) collective-permute-start(bf16[1,512,128]{2,1,0:T(8,128)(2,1)S(1)} %slice_bitcast_fusion.2), channel_id=1, source_target_pairs={{0,8},{8,16},{16,24},{24,0},{1,9},{9,17},{17,25},{25,1},{2,10},{10... | collective-permute-start | bytes 393224 | tf_op jit(solution)/shard_map/ppermute | solution.py:357
  13.8 1.6 %collective-permute-start.3 = (bf16[1,512,128]{2,1,0:T(8,128)(2,1)S(1)}, bf16[1,512,128]{2,1,0:T(8,128)(2,1)S(1)}, u32[]{:S(2)}, u32[]{:S(2)}) collective-permute-start(bf16[1,512,128]{2,1,0:T(8,128)(2,1)S(1)} %slice_bitcast_fusion.1), channel_id=1, source_target_pairs={{0,8},{8,16},{16,24},{24,0},{1,9},{9,17},{17,25},{25,1},{2,10},{10... | collective-permute-start | bytes 393224 | tf_op jit(solution)/shard_map/ppermute | solution.py:357
  15.4 0.0 collective-permute-done.4.refs_3_
  15.5 1.4 %collective-permute-start.6 = (bf16[272,128]{1,0:T(8,128)(2,1)S(1)}, bf16[272,128]{1,0:T(8,128)(2,1)S(1)}, u32[]{:S(2)}, u32[]{:S(2)}) collective-permute-start(bf16[272,128]{1,0:T(8,128)(2,1)S(1)} %get-tuple-element.40), channel_id=1, source_target_pairs={{0,6},{2,4},{4,2},{6,0},{1,7},{3,5},{5,3},{7,1},{8,14},{10,12},{12... | collective-permute-start | bytes 208904 | tf_op jit(solution)/shard_map/ppermute | solution.py:284
  16.9 0.0 collective-permute-done.5.refs_4_
  16.9 1.6 %collective-permute-start.7 = (bf16[1,512,128]{2,1,0:T(8,128)(2,1)S(1)}, bf16[1,512,128]{2,1,0:T(8,128)(2,1)S(1)}, u32[]{:S(2)}, u32[]{:S(2)}) collective-permute-start(bf16[1,512,128]{2,1,0:T(8,128)(2,1)S(1)} %bitcast.9), channel_id=1, source_target_pairs={{0,8},{8,16},{16,24},{24,0},{1,9},{9,17},{17,25},{25,1},{2,10},{10... | collective-permute-start | bytes 393224 | tf_op jit(solution)/shard_map/ppermute | solution.py:357
  18.5 1.2 %attend.4 = (f32[4,128,256]{2,1,0:T(8,128)S(1)}, f32[4,8,256]{2,1,0:T(8,128)S(1)}) custom-call(bf16[784,128]{1,0:T(8,128)(2,1)S(1)} %get-tuple-element.29.block_ref.refs_0_, bf16[784,128]{1,0:T(8,128)(2,1)S(1)} %collective-permute-done.refs_1_, bf16[784,128]{1,0:T(8,128)(2,1)S(1)} %collective-permute-done.1.refs_2_, ...), custom_call_target="tpu_custom_call" | custom-call | flops 1000000000 | bytes 1 | tf_op jit(solution)/shard_map/attend/pallas_call | solution.py:385
  19.7 1.0 %collective-permute-done.6.refs_7_ = bf16[272,128]{1,0:T(8,128)(2,1)S(1)} collective-permute-done((bf16[272,128]{1,0:T(8,128)(2,1)S(1)}, bf16[272,128]{1,0:T(8,128)(2,1)S(1)}, u32[]{:S(2)}, u32[]{:S(2)}) %collective-permute-start.6) | collective-permute-done | bytes 69664 | tf_op jit(solution)/shard_map/ppermute | solution.py:284
  20.7 0.8 %attend.5 = (f32[4,128,256]{2,1,0:T(8,128)S(1)}, f32[4,8,256]{2,1,0:T(8,128)S(1)}) custom-call(bf16[784,128]{1,0:T(8,128)(2,1)S(1)} %get-tuple-element.29.block_ref.refs_0_, bf16[784,128]{1,0:T(8,128)(2,1)S(1)} %collective-permute-done.refs_1_, bf16[784,128]{1,0:T(8,128)(2,1)S(1)} %collective-permute-done.1.refs_2_, ...), custom_call_target="tpu_custom_call" | custom-call | flops 1 | bytes 1 | tf_op jit(solution)/shard_map/attend/pallas_call | solution.py:385
  21.5 0.0 collective-permute-done.2.refs_3_
  21.5 0.7 %collective-permute-done.3.refs_4_ = bf16[1,512,128]{2,1,0:T(8,128)(2,1)S(1)} collective-permute-done((bf16[1,512,128]{2,1,0:T(8,128)(2,1)S(1)}, bf16[1,512,128]{2,1,0:T(8,128)(2,1)S(1)}, u32[]{:S(2)}, u32[]{:S(2)}) %collective-permute-start.3) | collective-permute-done | bytes 131104 | tf_op jit(solution)/shard_map/ppermute | solution.py:357
  22.1 0.6 %attend.6 = (bf16[128,256]{1,0:T(8,128)(2,1)S(1)}, f32[4,128,256]{2,1,0:T(8,128)S(1)}, f32[4,8,256]{2,1,0:T(8,128)S(1)}) custom-call(bf16[784,128]{1,0:T(8,128)(2,1)S(1)} %get-tuple-element.29.block_ref.refs_0_, bf16[784,128]{1,0:T(8,128)(2,1)S(1)} %collective-permute-done.refs_1_, bf16[784,128]{1,0:T(8,128)(2,1)S(1)} %collective-permute-done.1.refs_2_, ...), custom_call_target="tpu_custom_call" | custom-call | flops 1000000000 | bytes 1 | tf_op jit(solution)/shard_map/attend/pallas_call | solution.py:385
  22.7 1.6 %collective-permute-start.8 = (bf16[128,256]{1,0:T(8,128)(2,1)S(1)}, bf16[128,256]{1,0:T(8,128)(2,1)S(1)}, u32[]{:S(2)}, u32[]{:S(2)}) collective-permute-start(bf16[128,256]{1,0:T(8,128)(2,1)S(1)} %get-tuple-element.46), channel_id=1, source_target_pairs={{0,6},{2,4},{4,2},{6,0},{1,7},{3,5},{5,3},{7,1},{8,14},{10,12},{12... | collective-permute-start | bytes 196616 | tf_op jit(solution)/shard_map/ppermute | solution.py:284
  24.3 0.0 collective-permute-done.7.refs_5_
  24.3 1.0 %attend.7 = (bf16[128,256]{1,0:T(8,128)(2,1)S(1)}, bf16[128,256]{1,0:T(8,128)(2,1)S(1)}, bf16[128,256]{1,0:T(8,128)(2,1)S(1)}) custom-call(bf16[784,128]{1,0:T(8,128)(2,1)S(1)} %get-tuple-element.29.block_ref.refs_0_, bf16[784,128]{1,0:T(8,128)(2,1)S(1)} %collective-permute-done.refs_1_, bf16[784,128]{1,0:T(8,128)(2,1)S(1)} %collective-permute-done.1.refs_2_, ...), custom_call_target="tpu_custom_call" | custom-call | flops 1000000000 | bytes 1 | tf_op jit(solution)/shard_map/attend/pallas_call | solution.py:385
  25.3 0.6 %collective-permute-start.9 = (bf16[128,256]{1,0:T(8,128)(2,1)S(1)}, bf16[128,256]{1,0:T(8,128)(2,1)S(1)}, u32[]{:S(2)}, u32[]{:S(2)}) collective-permute-start(bf16[128,256]{1,0:T(8,128)(2,1)S(1)} %get-tuple-element.47), channel_id=1, source_target_pairs={{0,2},{2,0},{4,6},{6,4},{1,3},{3,1},{5,7},{7,5},{8,10},{10,8},{12,... | collective-permute-start | bytes 196616 | tf_op jit(solution)/shard_map/ppermute | solution.py:284
  26.0 0.7 %collective-permute-start.10 = (bf16[128,256]{1,0:T(8,128)(2,1)S(1)}, bf16[128,256]{1,0:T(8,128)(2,1)S(1)}, u32[]{:S(2)}, u32[]{:S(2)}) collective-permute-start(bf16[128,256]{1,0:T(8,128)(2,1)S(1)} %get-tuple-element.48), channel_id=1, source_target_pairs={{0,4},{2,6},{4,0},{6,2},{1,5},{3,7},{5,1},{7,3},{8,12},{10,14},{12... | collective-permute-start | bytes 196616 | tf_op jit(solution)/shard_map/ppermute | solution.py:284
  26.7 1.2 %collective-permute-done.8.refs_1_ = bf16[128,256]{1,0:T(8,128)(2,1)S(1)} collective-permute-done((bf16[128,256]{1,0:T(8,128)(2,1)S(1)}, bf16[128,256]{1,0:T(8,128)(2,1)S(1)}, u32[]{:S(2)}, u32[]{:S(2)}) %collective-permute-start.8) | collective-permute-done | bytes 65568 | tf_op jit(solution)/shard_map/ppermute | solution.py:284
  27.9 0.0 collective-permute-start.12
  27.9 0.5 %collective-permute-start.11 = (bf16[128,256]{1,0:T(8,128)(2,1)S(1)}, bf16[128,256]{1,0:T(8,128)(2,1)S(1)}, u32[]{:S(2)}, u32[]{:S(2)}) collective-permute-start(bf16[128,256]{1,0:T(8,128)(2,1)S(1)} %get-tuple-element.45.refs_0_), channel_id=1, source_target_pairs={{0,1},{1,0},{2,3},{3,2},{4,5},{5,4},{6,7},{7,6},{8,9},{9,8},{10,11... | collective-permute-start | bytes 196616 | tf_op jit(solution)/shard_map/ppermute | solution.py:284
  28.4 1.2 %collective-permute-done.9.refs_2_ = bf16[128,256]{1,0:T(8,128)(2,1)S(1)} collective-permute-done((bf16[128,256]{1,0:T(8,128)(2,1)S(1)}, bf16[128,256]{1,0:T(8,128)(2,1)S(1)}, u32[]{:S(2)}, u32[]{:S(2)}) %collective-permute-start.9) | collective-permute-done | bytes 65568 | tf_op jit(solution)/shard_map/ppermute | solution.py:284
  29.7 0.0 collective-permute-start.13
  29.7 0.6 %collective-permute-done.10.refs_3_ = bf16[128,256]{1,0:T(8,128)(2,1)S(1)} collective-permute-done((bf16[128,256]{1,0:T(8,128)(2,1)S(1)}, bf16[128,256]{1,0:T(8,128)(2,1)S(1)}, u32[]{:S(2)}, u32[]{:S(2)}) %collective-permute-start.10) | collective-permute-done | bytes 65568 | tf_op jit(solution)/shard_map/ppermute | solution.py:284
  30.2 0.0 collective-permute-start.14
  30.2 0.0 collective-permute-done.12.refs_5_
  30.2 0.0 collective-permute-done.11.refs_4_
  30.2 0.7 %collective-permute-done.13.refs_6_ = bf16[128,256]{1,0:T(8,128)(2,1)S(1)} collective-permute-done((bf16[128,256]{1,0:T(8,128)(2,1)S(1)}, bf16[128,256]{1,0:T(8,128)(2,1)S(1)}, u32[]{:S(2)}, u32[]{:S(2)}) %collective-permute-start.13) | collective-permute-done | bytes 65568 | tf_op jit(solution)/shard_map/ppermute | solution.py:284
  30.9 0.6 %collective-permute-done.14.refs_7_ = bf16[128,256]{1,0:T(8,128)(2,1)S(1)} collective-permute-done((bf16[128,256]{1,0:T(8,128)(2,1)S(1)}, bf16[128,256]{1,0:T(8,128)(2,1)S(1)}, u32[]{:S(2)}, u32[]{:S(2)}) %collective-permute-start.14) | collective-permute-done | bytes 65568 | tf_op jit(solution)/shard_map/ppermute | solution.py:284
  31.5 1.2 %project.1 = bf16[512,256]{1,0:T(8,128)(2,1)} custom-call(bf16[2,512,512]{2,1,0:T(8,128)(2,1)S(1)} %turn.1.turned_ref, bf16[128,256]{1,0:T(8,128)(2,1)S(1)} %get-tuple-element.45.refs_0_, bf16[128,256]{1,0:T(8,128)(2,1)S(1)} %collective-permute-done.8.refs_1_, bf16[128,256]{1,0:T(8,128)(2,1)S(1)} %collective-permute-done.9.refs_2_, ...), custom_call_target="tpu_custom_call" | custom-call | tf_op jit(solution)/shard_map/project/pallas_call | solution.py:433
  (3 shorter events, 0.0 us)
Async XLA Ops:
  1.2 8.0 %collective-permute-start = (bf16[784,128]{1,0:T(8,128)(2,1)S(1)}, bf16[784,128]{1,0:T(8,128)(2,1)S(1)}, u32[]{:S(2)}, u32[]{:S(2)}) collective-permute-start(bf16[784,128]{1,0:T(8,128)(2,1)S(1)} %get-tuple-element.30), channel_id=1, source_target_pairs={{0,2},{2,0},{4,6},{6,4},{1,3},{3,1},{5,7},{7,5},{8,10},{10,8},{12,... | collective-permute-start | bytes 602120 | tf_op jit(solution)/shard_map/ppermute | solution.py:284
  4.2 6.4 %collective-permute-start.1 = (bf16[784,128]{1,0:T(8,128)(2,1)S(1)}, bf16[784,128]{1,0:T(8,128)(2,1)S(1)}, u32[]{:S(2)}, u32[]{:S(2)}) collective-permute-start(bf16[784,128]{1,0:T(8,128)(2,1)S(1)} %get-tuple-element.31), channel_id=1, source_target_pairs={{0,4},{2,6},{4,0},{6,2},{1,5},{3,7},{5,1},{7,3},{8,12},{10,14},{12... | collective-permute-start | bytes 602120 | tf_op jit(solution)/shard_map/ppermute | solution.py:284
  5.8 9.7 %collective-permute-start.4 = (bf16[1,512,128]{2,1,0:T(8,128)(2,1)S(1)}, bf16[1,512,128]{2,1,0:T(8,128)(2,1)S(1)}, u32[]{:S(2)}, u32[]{:S(2)}) collective-permute-start(bf16[1,512,128]{2,1,0:T(8,128)(2,1)S(1)} %slice_bitcast_fusion), channel_id=1, source_target_pairs={{0,8},{8,16},{16,24},{24,0},{1,9},{9,17},{17,25},{25,1},{2,10},{10... | collective-permute-start | bytes 393224 | tf_op jit(solution)/shard_map/ppermute | solution.py:357
  10.7 6.2 %collective-permute-start.5 = (bf16[512,128]{1,0:T(8,128)(2,1)S(1)}, bf16[512,128]{1,0:T(8,128)(2,1)S(1)}, u32[]{:S(2)}, u32[]{:S(2)}) collective-permute-start(bf16[512,128]{1,0:T(8,128)(2,1)S(1)} %get-tuple-element.37), channel_id=1, source_target_pairs={{0,6},{2,4},{4,2},{6,0},{1,7},{3,5},{5,3},{7,1},{8,14},{10,12},{12... | collective-permute-start | bytes 393224 | tf_op jit(solution)/shard_map/ppermute | solution.py:284
  12.2 9.3 %collective-permute-start.2 = (bf16[1,512,128]{2,1,0:T(8,128)(2,1)S(1)}, bf16[1,512,128]{2,1,0:T(8,128)(2,1)S(1)}, u32[]{:S(2)}, u32[]{:S(2)}) collective-permute-start(bf16[1,512,128]{2,1,0:T(8,128)(2,1)S(1)} %slice_bitcast_fusion.2), channel_id=1, source_target_pairs={{0,8},{8,16},{16,24},{24,0},{1,9},{9,17},{17,25},{25,1},{2,10},{10... | collective-permute-start | bytes 393224 | tf_op jit(solution)/shard_map/ppermute | solution.py:357
  13.8 8.3 %collective-permute-start.3 = (bf16[1,512,128]{2,1,0:T(8,128)(2,1)S(1)}, bf16[1,512,128]{2,1,0:T(8,128)(2,1)S(1)}, u32[]{:S(2)}, u32[]{:S(2)}) collective-permute-start(bf16[1,512,128]{2,1,0:T(8,128)(2,1)S(1)} %slice_bitcast_fusion.1), channel_id=1, source_target_pairs={{0,8},{8,16},{16,24},{24,0},{1,9},{9,17},{17,25},{25,1},{2,10},{10... | collective-permute-start | bytes 393224 | tf_op jit(solution)/shard_map/ppermute | solution.py:357
  15.5 5.2 %collective-permute-start.6 = (bf16[272,128]{1,0:T(8,128)(2,1)S(1)}, bf16[272,128]{1,0:T(8,128)(2,1)S(1)}, u32[]{:S(2)}, u32[]{:S(2)}) collective-permute-start(bf16[272,128]{1,0:T(8,128)(2,1)S(1)} %get-tuple-element.40), channel_id=1, source_target_pairs={{0,6},{2,4},{4,2},{6,0},{1,7},{3,5},{5,3},{7,1},{8,14},{10,12},{12... | collective-permute-start | bytes 208904 | tf_op jit(solution)/shard_map/ppermute | solution.py:284
  16.9 7.4 %collective-permute-start.7 = (bf16[1,512,128]{2,1,0:T(8,128)(2,1)S(1)}, bf16[1,512,128]{2,1,0:T(8,128)(2,1)S(1)}, u32[]{:S(2)}, u32[]{:S(2)}) collective-permute-start(bf16[1,512,128]{2,1,0:T(8,128)(2,1)S(1)} %bitcast.9), channel_id=1, source_target_pairs={{0,8},{8,16},{16,24},{24,0},{1,9},{9,17},{17,25},{25,1},{2,10},{10... | collective-permute-start | bytes 393224 | tf_op jit(solution)/shard_map/ppermute | solution.py:357
  22.7 5.2 %collective-permute-start.8 = (bf16[128,256]{1,0:T(8,128)(2,1)S(1)}, bf16[128,256]{1,0:T(8,128)(2,1)S(1)}, u32[]{:S(2)}, u32[]{:S(2)}) collective-permute-start(bf16[128,256]{1,0:T(8,128)(2,1)S(1)} %get-tuple-element.46), channel_id=1, source_target_pairs={{0,6},{2,4},{4,2},{6,0},{1,7},{3,5},{5,3},{7,1},{8,14},{10,12},{12... | collective-permute-start | bytes 196616 | tf_op jit(solution)/shard_map/ppermute | solution.py:284
  25.3 4.3 %collective-permute-start.9 = (bf16[128,256]{1,0:T(8,128)(2,1)S(1)}, bf16[128,256]{1,0:T(8,128)(2,1)S(1)}, u32[]{:S(2)}, u32[]{:S(2)}) collective-permute-start(bf16[128,256]{1,0:T(8,128)(2,1)S(1)} %get-tuple-element.47), channel_id=1, source_target_pairs={{0,2},{2,0},{4,6},{6,4},{1,3},{3,1},{5,7},{7,5},{8,10},{10,8},{12,... | collective-permute-start | bytes 196616 | tf_op jit(solution)/shard_map/ppermute | solution.py:284
  26.0 4.3 %collective-permute-start.10 = (bf16[128,256]{1,0:T(8,128)(2,1)S(1)}, bf16[128,256]{1,0:T(8,128)(2,1)S(1)}, u32[]{:S(2)}, u32[]{:S(2)}) collective-permute-start(bf16[128,256]{1,0:T(8,128)(2,1)S(1)} %get-tuple-element.48), channel_id=1, source_target_pairs={{0,4},{2,6},{4,0},{6,2},{1,5},{3,7},{5,1},{7,3},{8,12},{10,14},{12... | collective-permute-start | bytes 196616 | tf_op jit(solution)/shard_map/ppermute | solution.py:284
  27.9 2.3 %collective-permute-start.12 = (bf16[128,256]{1,0:T(8,128)(2,1)S(1)}, bf16[128,256]{1,0:T(8,128)(2,1)S(1)}, u32[]{:S(2)}, u32[]{:S(2)}) collective-permute-start(bf16[128,256]{1,0:T(8,128)(2,1)S(1)} %collective-permute-done.8.refs_1_), channel_id=1, source_target_pairs={{0,1},{1,0},{2,3},{3,2},{4,5},{5,4},{6,7},{7,6},{8,9},{9,8},{10,11... | collective-permute-start | bytes 196616 | tf_op jit(solution)/shard_map/ppermute | solution.py:284
  27.9 2.3 %collective-permute-start.11 = (bf16[128,256]{1,0:T(8,128)(2,1)S(1)}, bf16[128,256]{1,0:T(8,128)(2,1)S(1)}, u32[]{:S(2)}, u32[]{:S(2)}) collective-permute-start(bf16[128,256]{1,0:T(8,128)(2,1)S(1)} %get-tuple-element.45.refs_0_), channel_id=1, source_target_pairs={{0,1},{1,0},{2,3},{3,2},{4,5},{5,4},{6,7},{7,6},{8,9},{9,8},{10,11... | collective-permute-start | bytes 196616 | tf_op jit(solution)/shard_map/ppermute | solution.py:284
  29.7 1.3 %collective-permute-start.13 = (bf16[128,256]{1,0:T(8,128)(2,1)S(1)}, bf16[128,256]{1,0:T(8,128)(2,1)S(1)}, u32[]{:S(2)}, u32[]{:S(2)}) collective-permute-start(bf16[128,256]{1,0:T(8,128)(2,1)S(1)} %collective-permute-done.9.refs_2_), channel_id=1, source_target_pairs={{0,1},{1,0},{2,3},{3,2},{4,5},{5,4},{6,7},{7,6},{8,9},{9,8},{10,11... | collective-permute-start | bytes 196616 | tf_op jit(solution)/shard_map/ppermute | solution.py:284
  30.2 1.3 %collective-permute-start.14 = (bf16[128,256]{1,0:T(8,128)(2,1)S(1)}, bf16[128,256]{1,0:T(8,128)(2,1)S(1)}, u32[]{:S(2)}, u32[]{:S(2)}) collective-permute-start(bf16[128,256]{1,0:T(8,128)(2,1)S(1)} %collective-permute-done.10.refs_3_), channel_id=1, source_target_pairs={{0,1},{1,0},{2,3},{3,2},{4,5},{5,4},{6,7},{7,6},{8,9},{9,8},{10,11... | collective-permute-start | bytes 196616 | tf_op jit(solution)/shard_map/ppermute | solution.py:284

commit v10 on v9

--- a/solution.py
+++ b/solution.py
@@ -18,7 +18,7 @@
 EXTRA = 16
 OWN = 10**9
 NEAR = 1000000000
-MORE = 1
+MORE = 1000000000
 FAR = 1000000000
 VMEM = pl.BlockSpec(memory_space=pltpu.VMEM)
 HBM = pl.BlockSpec(memory_space=pltpu.HBM)
@@ -352,6 +352,10 @@
     def send_on(steps):
         blocks = [arrays.get(("block", step), arrays.get(("kv", step))) for step in steps]
         message = jnp.stack([block[: 2 * rows] for block in blocks])
+        if apart and steps == near[-1:]:
+            early = [first]
+            message, got = lax.optimization_barrier((message, [arrays[name] for name in early]))
+            arrays.update(zip(early, got))
         for offset in offsets:
             pairs = [(source, (source + offset) % groups) for source in range(groups)]
             arrays["halo", offset, tuple(steps)] = lax.ppermute(message, "group", pairs)
@@ -407,21 +411,19 @@
         arrays["block", step] = swapped(packed[step], "place", step)
     send_on([0])
     mix = {}
-    held = packed[near[-1] + 1 :] if apart else []
     if apart:
-        tied = lax.optimization_barrier((list(held), turned, [arrays["block", step] for step in near]))
-        held, turned, blocks = tied
-        arrays.update((("block", step), block) for step, block in zip(near, blocks))
+        blocks, queries = packed[:group], packed[group:]
+        tied = lax.optimization_barrier((queries, turned))
+        queries, turned = tied
+        arrays["q", apart[0]] = swapped(queries[0], "place", apart[0])
+        tied = lax.optimization_barrier((packed[apart[0]], turned, arrays["block", 1]))
+        block, turned, arrays["block", 1] = tied
+        arrays["kv", apart[0]] = swapped(block, "place", apart[0])
     for step in near:
         send_on([step])
-    for step, block in zip(apart, held):
-        arrays["kv", step] = swapped(block, "place", step)
     mix.update(stage(0, NEAR))
     if apart:
         send_on(apart)
-        for step, block in zip(apart, held[len(apart) :]):
-            block, arrays[first] = lax.optimization_barrier((block, arrays[first]))
-            arrays["q", step] = swapped(block, "place", step)
     for at in range(1, len(plan)):
         done = stage(at, MORE if at == 1 and apart else FAR)
         order = [step for step in sending_order(group) if step in done]

time: 32.8 us -> 36.5 us (1.11)
  waiting for transfers between devices: 7.78 us -> 14 us
  starting transfers between devices: 17.4 us -> 14.8 us
    ppermute x4, waiting for transfers between devices: 0.67 us -> 4.55 us  [send_on(): arrays['halo', offset, tuple(steps)] = lax.ppermute(message, 'group', pairs)]
    ppermute x11, waiting for transfers between devices: 7.11 us -> 9.42 us  [swapped(): lax.ppermute(value, axis, [(source, source ^ step) for source in range(co...]
    ppermute x4, starting transfers between devices: 6.46 us -> 4.95 us  [send_on(): arrays['halo', offset, tuple(steps)] = lax.ppermute(message, 'group', pairs)]
    ppermute x11, starting transfers between devices: 10.9 us -> 9.89 us  [swapped(): lax.ppermute(value, axis, [(source, source ^ step) for source in range(co...]
  transfers between devices with their start and end apart: 15 -> 15, of which waited for: 9 -> 9; matrix products, arithmetic and copies ran while one was open for 0% -> 0% of each run, Pallas kernels for 15% -> 14%
where the time goes in v10:
time: 36.5 us; the launch traced here: 36.3 us
  starting transfers between devices  14.8 us (41%)
  waiting for transfers between devices  14 us (38%)
  Pallas kernels  7.37 us (20%)
    ppermute x11, starting transfers between devices, swapped(): lax.ppermute(value, axis, [(source, source ^ step) for source in range(co...  9.89 us
    ppermute x11, waiting for transfers between devices, swapped(): lax.ppermute(value, axis, [(source, source ^ step) for source in range(co...  9.42 us
    ppermute x4, starting transfers between devices, send_on(): arrays['halo', offset, tuple(steps)] = lax.ppermute(message, 'group', pairs)  4.95 us
    ppermute x4, waiting for transfers between devices, send_on(): arrays['halo', offset, tuple(steps)] = lax.ppermute(message, 'group', pairs)  4.55 us
    pallas_call x4, Pallas kernels, stage(): pl.pallas_call(functools.partial(attend_kernel, names=names, work=work, s...  3.54 us
    pallas_call x1, Pallas kernels, on_device(): pl.pallas_call(functools.partial(turn_kernel, head_total=head_total), out...  1.44 us
    pallas_call x1, Pallas kernels, on_device(): pl.pallas_call(pack_kernel, out_shape=[shape((2 * rows, HD), bf16) if ste...  1.21 us
    pallas_call x1, Pallas kernels, on_device(): pl.pallas_call(functools.partial(project_kernel, group=group, head_total=...  1.19 us
  transfers between devices with their start and end apart: 15, of which 9 were waited for; matrix products, arithmetic and copies ran while one was open for 0% of the time, Pallas kernels for 14%

profile of v10, /device:TPU:0, one launch (start us, length us, event | category | flops | bytes accessed | tf_op | source)
XLA Modules:
  0.0 36.3 jit_solution(10385230378740634387)
XLA Ops:
  0.0 1.2 %pack.1 = (bf16[784,128]{1,0:T(8,128)(2,1)S(1)}, bf16[784,128]{1,0:T(8,128)(2,1)S(1)}, bf16[784,128]{1,0:T(8,128)(2,1)S(1)}, bf16[512,128]{1,0:T(8,128)(2,1)S(1)}, bf16[272,128]{1,0:T(8,128)(2,1)S(1)}) custom-call(bf16[256,512]{1,0:T(8,128)(2,1)} %query_ref.1, bf16[256,512]{1,0:T(8,128)(2,1)} %key_ref.1, bf16[256,512]{1,0:T(8,128)(2,1)} %value_ref.1, ...), custom_call_target="tpu_custom_call" | custom-call | tf_op jit(solution)/shard_map/pack/pallas_call | solution.py:299
  1.2 3.0 %collective-permute-start = (bf16[784,128]{1,0:T(8,128)(2,1)S(1)}, bf16[784,128]{1,0:T(8,128)(2,1)S(1)}, u32[]{:S(2)}, u32[]{:S(2)}) collective-permute-start(bf16[784,128]{1,0:T(8,128)(2,1)S(1)} %get-tuple-element.31), channel_id=1, source_target_pairs={{0,2},{2,0},{4,6},{6,4},{1,3},{3,1},{5,7},{7,5},{8,10},{10,8},{12,... | collective-permute-start | bytes 602120 | tf_op jit(solution)/shard_map/ppermute | solution.py:284
  4.2 1.6 %collective-permute-start.4 = (bf16[1,512,128]{2,1,0:T(8,128)(2,1)S(1)}, bf16[1,512,128]{2,1,0:T(8,128)(2,1)S(1)}, u32[]{:S(2)}, u32[]{:S(2)}) collective-permute-start(bf16[1,512,128]{2,1,0:T(8,128)(2,1)S(1)} %slice_bitcast_fusion.1), channel_id=1, source_target_pairs={{0,8},{8,16},{16,24},{24,0},{1,9},{9,17},{17,25},{25,1},{2,10},{10... | collective-permute-start | bytes 393224 | tf_op jit(solution)/shard_map/ppermute | solution.py:361
  5.9 1.5 %collective-permute-start.1 = (bf16[784,128]{1,0:T(8,128)(2,1)S(1)}, bf16[784,128]{1,0:T(8,128)(2,1)S(1)}, u32[]{:S(2)}, u32[]{:S(2)}) collective-permute-start(bf16[784,128]{1,0:T(8,128)(2,1)S(1)} %get-tuple-element.34), channel_id=1, source_target_pairs={{0,4},{2,6},{4,0},{6,2},{1,5},{3,7},{5,1},{7,3},{8,12},{10,14},{12... | collective-permute-start | bytes 602120 | tf_op jit(solution)/shard_map/ppermute | solution.py:284
  7.4 1.4 %turn.1.turned_ref = bf16[2,512,512]{2,1,0:T(8,128)(2,1)S(1)} custom-call(bf16[784,128]{1,0:T(8,128)(2,1)S(1)} %get-tuple-element.29.block_ref.refs_0_, bf16[1024,1024]{1,0:T(8,128)(2,1)} %weight_ref.1), custom_call_target="tpu_custom_call" | custom-call | flops 1000000000 | bytes 1 | tf_op jit(solution)/shard_map/turn/pallas_call | solution.py:328
  8.8 0.5 %collective-permute-start.2 = (bf16[272,128]{1,0:T(8,128)(2,1)S(1)}, bf16[272,128]{1,0:T(8,128)(2,1)S(1)}, u32[]{:S(2)}, u32[]{:S(2)}) collective-permute-start(bf16[272,128]{1,0:T(8,128)(2,1)S(1)} %get-tuple-element.35), channel_id=1, source_target_pairs={{0,6},{2,4},{4,2},{6,0},{1,7},{3,5},{5,3},{7,1},{8,14},{10,12},{12... | collective-permute-start | bytes 208904 | tf_op jit(solution)/shard_map/ppermute | solution.py:284
  9.4 0.0 collective-permute-done.refs_1_
  9.4 2.5 %collective-permute-start.6 = (bf16[512,128]{1,0:T(8,128)(2,1)S(1)}, bf16[512,128]{1,0:T(8,128)(2,1)S(1)}, u32[]{:S(2)}, u32[]{:S(2)}) collective-permute-start(bf16[512,128]{1,0:T(8,128)(2,1)S(1)} %get-tuple-element.38), channel_id=1, source_target_pairs={{0,6},{2,4},{4,2},{6,0},{1,7},{3,5},{5,3},{7,1},{8,14},{10,12},{12... | collective-permute-start | bytes 393224 | tf_op jit(solution)/shard_map/ppermute | solution.py:284
  11.9 4.4 %collective-permute-done.1.refs_2_ = bf16[784,128]{1,0:T(8,128)(2,1)S(1)} collective-permute-done((bf16[784,128]{1,0:T(8,128)(2,1)S(1)}, bf16[784,128]{1,0:T(8,128)(2,1)S(1)}, u32[]{:S(2)}, u32[]{:S(2)}) %collective-permute-start.1) | collective-permute-done | bytes 200736 | tf_op jit(solution)/shard_map/ppermute | solution.py:284
  16.4 0.0 collective-permute-done.4.refs_3_
  16.4 1.6 %collective-permute-start.3 = (bf16[1,512,128]{2,1,0:T(8,128)(2,1)S(1)}, bf16[1,512,128]{2,1,0:T(8,128)(2,1)S(1)}, u32[]{:S(2)}, u32[]{:S(2)}) collective-permute-start(bf16[1,512,128]{2,1,0:T(8,128)(2,1)S(1)} %slice_bitcast_fusion.2), channel_id=1, source_target_pairs={{0,8},{8,16},{16,24},{24,0},{1,9},{9,17},{17,25},{25,1},{2,10},{10... | collective-permute-start | bytes 393224 | tf_op jit(solution)/shard_map/ppermute | solution.py:361
  18.0 1.6 %collective-permute-start.5 = (bf16[1,512,128]{2,1,0:T(8,128)(2,1)S(1)}, bf16[1,512,128]{2,1,0:T(8,128)(2,1)S(1)}, u32[]{:S(2)}, u32[]{:S(2)}) collective-permute-start(bf16[1,512,128]{2,1,0:T(8,128)(2,1)S(1)} %slice_bitcast_fusion), channel_id=1, source_target_pairs={{0,8},{8,16},{16,24},{24,0},{1,9},{9,17},{17,25},{25,1},{2,10},{10... | collective-permute-start | bytes 393224 | tf_op jit(solution)/shard_map/ppermute | solution.py:361
  19.6 1.2 %attend.4 = (f32[4,128,256]{2,1,0:T(8,128)S(1)}, f32[4,8,256]{2,1,0:T(8,128)S(1)}) custom-call(bf16[784,128]{1,0:T(8,128)(2,1)S(1)} %get-tuple-element.29.block_ref.refs_0_, bf16[784,128]{1,0:T(8,128)(2,1)S(1)} %collective-permute-done.refs_1_, bf16[784,128]{1,0:T(8,128)(2,1)S(1)} %collective-permute-done.1.refs_2_, ...), custom_call_target="tpu_custom_call" | custom-call | flops 1000000000 | bytes 1 | tf_op jit(solution)/shard_map/attend/pallas_call | solution.py:389
  20.8 0.0 collective-permute-done.6.refs_5_
  20.8 0.1 collective-permute-start.7
  20.9 0.0 collective-permute-done.2.refs_4_.refs_3_
  20.9 0.8 %attend.5 = (f32[4,128,256]{2,1,0:T(8,128)S(1)}, f32[4,8,256]{2,1,0:T(8,128)S(1)}) custom-call(bf16[784,128]{1,0:T(8,128)(2,1)S(1)} %get-tuple-element.29.block_ref.refs_0_, bf16[784,128]{1,0:T(8,128)(2,1)S(1)} %collective-permute-done.refs_1_, bf16[784,128]{1,0:T(8,128)(2,1)S(1)} %collective-permute-done.1.refs_2_, ...), custom_call_target="tpu_custom_call" | custom-call | flops 1000000000 | bytes 1 | tf_op jit(solution)/shard_map/attend/pallas_call | solution.py:389
  21.7 1.5 %collective-permute-done.3.refs_4_ = bf16[1,512,128]{2,1,0:T(8,128)(2,1)S(1)} collective-permute-done((bf16[1,512,128]{2,1,0:T(8,128)(2,1)S(1)}, bf16[1,512,128]{2,1,0:T(8,128)(2,1)S(1)}, u32[]{:S(2)}, u32[]{:S(2)}) %collective-permute-start.3) | collective-permute-done | bytes 131104 | tf_op jit(solution)/shard_map/ppermute | solution.py:361
  23.2 1.6 %collective-permute-done.5.refs_5_ = bf16[1,512,128]{2,1,0:T(8,128)(2,1)S(1)} collective-permute-done((bf16[1,512,128]{2,1,0:T(8,128)(2,1)S(1)}, bf16[1,512,128]{2,1,0:T(8,128)(2,1)S(1)}, u32[]{:S(2)}, u32[]{:S(2)}) %collective-permute-start.5) | collective-permute-done | bytes 131104 | tf_op jit(solution)/shard_map/ppermute | solution.py:361
  24.8 0.6 %attend.6 = (bf16[128,256]{1,0:T(8,128)(2,1)S(1)}, f32[4,128,256]{2,1,0:T(8,128)S(1)}, f32[4,8,256]{2,1,0:T(8,128)S(1)}) custom-call(bf16[784,128]{1,0:T(8,128)(2,1)S(1)} %get-tuple-element.29.block_ref.refs_0_, bf16[784,128]{1,0:T(8,128)(2,1)S(1)} %collective-permute-done.refs_1_, bf16[784,128]{1,0:T(8,128)(2,1)S(1)} %collective-permute-done.1.refs_2_, ...), custom_call_target="tpu_custom_call" | custom-call | flops 1000000000 | bytes 1 | tf_op jit(solution)/shard_map/attend/pallas_call | solution.py:389
  25.3 0.8 %collective-permute-start.8 = (bf16[128,256]{1,0:T(8,128)(2,1)S(1)}, bf16[128,256]{1,0:T(8,128)(2,1)S(1)}, u32[]{:S(2)}, u32[]{:S(2)}) collective-permute-start(bf16[128,256]{1,0:T(8,128)(2,1)S(1)} %get-tuple-element.46), channel_id=1, source_target_pairs={{0,6},{2,4},{4,2},{6,0},{1,7},{3,5},{5,3},{7,1},{8,14},{10,12},{12... | collective-permute-start | bytes 196616 | tf_op jit(solution)/shard_map/ppermute | solution.py:284
  26.1 1.5 %collective-permute-done.7.refs_5_ = bf16[1,512,128]{2,1,0:T(8,128)(2,1)S(1)} collective-permute-done((bf16[1,512,128]{2,1,0:T(8,128)(2,1)S(1)}, bf16[1,512,128]{2,1,0:T(8,128)(2,1)S(1)}, u32[]{:S(2)}, u32[]{:S(2)}) %collective-permute-start.7) | collective-permute-done | bytes 131104 | tf_op jit(solution)/shard_map/ppermute | solution.py:361
  27.6 1.0 %attend.7 = (bf16[128,256]{1,0:T(8,128)(2,1)S(1)}, bf16[128,256]{1,0:T(8,128)(2,1)S(1)}, bf16[128,256]{1,0:T(8,128)(2,1)S(1)}) custom-call(bf16[784,128]{1,0:T(8,128)(2,1)S(1)} %get-tuple-element.29.block_ref.refs_0_, bf16[784,128]{1,0:T(8,128)(2,1)S(1)} %collective-permute-done.refs_1_, bf16[784,128]{1,0:T(8,128)(2,1)S(1)} %collective-permute-done.1.refs_2_, ...), custom_call_target="tpu_custom_call" | custom-call | flops 1000000000 | bytes 1 | tf_op jit(solution)/shard_map/attend/pallas_call | solution.py:389
  28.6 1.0 %collective-permute-start.9 = (bf16[128,256]{1,0:T(8,128)(2,1)S(1)}, bf16[128,256]{1,0:T(8,128)(2,1)S(1)}, u32[]{:S(2)}, u32[]{:S(2)}) collective-permute-start(bf16[128,256]{1,0:T(8,128)(2,1)S(1)} %get-tuple-element.47), channel_id=1, source_target_pairs={{0,2},{2,0},{4,6},{6,4},{1,3},{3,1},{5,7},{7,5},{8,10},{10,8},{12,... | collective-permute-start | bytes 196616 | tf_op jit(solution)/shard_map/ppermute | solution.py:284
  29.6 0.0 collective-permute-start.10
  29.6 1.0 %collective-permute-done.8.refs_1_ = bf16[128,256]{1,0:T(8,128)(2,1)S(1)} collective-permute-done((bf16[128,256]{1,0:T(8,128)(2,1)S(1)}, bf16[128,256]{1,0:T(8,128)(2,1)S(1)}, u32[]{:S(2)}, u32[]{:S(2)}) %collective-permute-start.8) | collective-permute-done | bytes 65568 | tf_op jit(solution)/shard_map/ppermute | solution.py:284
  30.6 0.0 collective-permute-start.12
  30.6 0.5 %collective-permute-start.11 = (bf16[128,256]{1,0:T(8,128)(2,1)S(1)}, bf16[128,256]{1,0:T(8,128)(2,1)S(1)}, u32[]{:S(2)}, u32[]{:S(2)}) collective-permute-start(bf16[128,256]{1,0:T(8,128)(2,1)S(1)} %get-tuple-element.45.refs_0_), channel_id=1, source_target_pairs={{0,1},{1,0},{2,3},{3,2},{4,5},{5,4},{6,7},{7,6},{8,9},{9,8},{10,11... | collective-permute-start | bytes 196616 | tf_op jit(solution)/shard_map/ppermute | solution.py:284
  31.1 1.9 %collective-permute-done.9.refs_2_ = bf16[128,256]{1,0:T(8,128)(2,1)S(1)} collective-permute-done((bf16[128,256]{1,0:T(8,128)(2,1)S(1)}, bf16[128,256]{1,0:T(8,128)(2,1)S(1)}, u32[]{:S(2)}, u32[]{:S(2)}) %collective-permute-start.9) | collective-permute-done | bytes 65568 | tf_op jit(solution)/shard_map/ppermute | solution.py:284
  32.9 0.0 collective-permute-start.13
  32.9 0.9 %collective-permute-done.10.refs_3_ = bf16[128,256]{1,0:T(8,128)(2,1)S(1)} collective-permute-done((bf16[128,256]{1,0:T(8,128)(2,1)S(1)}, bf16[128,256]{1,0:T(8,128)(2,1)S(1)}, u32[]{:S(2)}, u32[]{:S(2)}) %collective-permute-start.10) | collective-permute-done | bytes 65568 | tf_op jit(solution)/shard_map/ppermute | solution.py:284
  33.9 0.0 collective-permute-start.14
  33.9 0.0 collective-permute-done.12.refs_5_
  33.9 0.0 collective-permute-done.11.refs_4_
  33.9 0.3 collective-permute-done.13.refs_6_
  34.2 0.9 %collective-permute-done.14.refs_7_ = bf16[128,256]{1,0:T(8,128)(2,1)S(1)} collective-permute-done((bf16[128,256]{1,0:T(8,128)(2,1)S(1)}, bf16[128,256]{1,0:T(8,128)(2,1)S(1)}, u32[]{:S(2)}, u32[]{:S(2)}) %collective-permute-start.14) | collective-permute-done | bytes 65568 | tf_op jit(solution)/shard_map/ppermute | solution.py:284
  35.1 1.2 %project.1 = bf16[512,256]{1,0:T(8,128)(2,1)} custom-call(bf16[2,512,512]{2,1,0:T(8,128)(2,1)S(1)} %turn.1.turned_ref, bf16[128,256]{1,0:T(8,128)(2,1)S(1)} %get-tuple-element.45.refs_0_, bf16[128,256]{1,0:T(8,128)(2,1)S(1)} %collective-permute-done.8.refs_1_, bf16[128,256]{1,0:T(8,128)(2,1)S(1)} %collective-permute-done.9.refs_2_, ...), custom_call_target="tpu_custom_call" | custom-call | tf_op jit(solution)/shard_map/project/pallas_call | solution.py:435
  (3 shorter events, 0.0 us)
Async XLA Ops:
  1.2 8.2 %collective-permute-start = (bf16[784,128]{1,0:T(8,128)(2,1)S(1)}, bf16[784,128]{1,0:T(8,128)(2,1)S(1)}, u32[]{:S(2)}, u32[]{:S(2)}) collective-permute-start(bf16[784,128]{1,0:T(8,128)(2,1)S(1)} %get-tuple-element.31), channel_id=1, source_target_pairs={{0,2},{2,0},{4,6},{6,4},{1,3},{3,1},{5,7},{7,5},{8,10},{10,8},{12,... | collective-permute-start | bytes 602120 | tf_op jit(solution)/shard_map/ppermute | solution.py:284
  4.2 12.1 %collective-permute-start.4 = (bf16[1,512,128]{2,1,0:T(8,128)(2,1)S(1)}, bf16[1,512,128]{2,1,0:T(8,128)(2,1)S(1)}, u32[]{:S(2)}, u32[]{:S(2)}) collective-permute-start(bf16[1,512,128]{2,1,0:T(8,128)(2,1)S(1)} %slice_bitcast_fusion.1), channel_id=1, source_target_pairs={{0,8},{8,16},{16,24},{24,0},{1,9},{9,17},{17,25},{25,1},{2,10},{10... | collective-permute-start | bytes 393224 | tf_op jit(solution)/shard_map/ppermute | solution.py:361
  5.9 10.5 %collective-permute-start.1 = (bf16[784,128]{1,0:T(8,128)(2,1)S(1)}, bf16[784,128]{1,0:T(8,128)(2,1)S(1)}, u32[]{:S(2)}, u32[]{:S(2)}) collective-permute-start(bf16[784,128]{1,0:T(8,128)(2,1)S(1)} %get-tuple-element.34), channel_id=1, source_target_pairs={{0,4},{2,6},{4,0},{6,2},{1,5},{3,7},{5,1},{7,3},{8,12},{10,14},{12... | collective-permute-start | bytes 602120 | tf_op jit(solution)/shard_map/ppermute | solution.py:284
  8.8 12.1 %collective-permute-start.2 = (bf16[272,128]{1,0:T(8,128)(2,1)S(1)}, bf16[272,128]{1,0:T(8,128)(2,1)S(1)}, u32[]{:S(2)}, u32[]{:S(2)}) collective-permute-start(bf16[272,128]{1,0:T(8,128)(2,1)S(1)} %get-tuple-element.35), channel_id=1, source_target_pairs={{0,6},{2,4},{4,2},{6,0},{1,7},{3,5},{5,3},{7,1},{8,14},{10,12},{12... | collective-permute-start | bytes 208904 | tf_op jit(solution)/shard_map/ppermute | solution.py:284
  9.4 11.4 %collective-permute-start.6 = (bf16[512,128]{1,0:T(8,128)(2,1)S(1)}, bf16[512,128]{1,0:T(8,128)(2,1)S(1)}, u32[]{:S(2)}, u32[]{:S(2)}) collective-permute-start(bf16[512,128]{1,0:T(8,128)(2,1)S(1)} %get-tuple-element.38), channel_id=1, source_target_pairs={{0,6},{2,4},{4,2},{6,0},{1,7},{3,5},{5,3},{7,1},{8,14},{10,12},{12... | collective-permute-start | bytes 393224 | tf_op jit(solution)/shard_map/ppermute | solution.py:284
  16.4 6.8 %collective-permute-start.3 = (bf16[1,512,128]{2,1,0:T(8,128)(2,1)S(1)}, bf16[1,512,128]{2,1,0:T(8,128)(2,1)S(1)}, u32[]{:S(2)}, u32[]{:S(2)}) collective-permute-start(bf16[1,512,128]{2,1,0:T(8,128)(2,1)S(1)} %slice_bitcast_fusion.2), channel_id=1, source_target_pairs={{0,8},{8,16},{16,24},{24,0},{1,9},{9,17},{17,25},{25,1},{2,10},{10... | collective-permute-start | bytes 393224 | tf_op jit(solution)/shard_map/ppermute | solution.py:361
  18.0 6.8 %collective-permute-start.5 = (bf16[1,512,128]{2,1,0:T(8,128)(2,1)S(1)}, bf16[1,512,128]{2,1,0:T(8,128)(2,1)S(1)}, u32[]{:S(2)}, u32[]{:S(2)}) collective-permute-start(bf16[1,512,128]{2,1,0:T(8,128)(2,1)S(1)} %slice_bitcast_fusion), channel_id=1, source_target_pairs={{0,8},{8,16},{16,24},{24,0},{1,9},{9,17},{17,25},{25,1},{2,10},{10... | collective-permute-start | bytes 393224 | tf_op jit(solution)/shard_map/ppermute | solution.py:361
  20.8 6.8 %collective-permute-start.7 = (bf16[1,512,128]{2,1,0:T(8,128)(2,1)S(1)}, bf16[1,512,128]{2,1,0:T(8,128)(2,1)S(1)}, u32[]{:S(2)}, u32[]{:S(2)}) collective-permute-start(bf16[1,512,128]{2,1,0:T(8,128)(2,1)S(1)} %bitcast.9), channel_id=1, source_target_pairs={{0,8},{8,16},{16,24},{24,0},{1,9},{9,17},{17,25},{25,1},{2,10},{10... | collective-permute-start | bytes 393224 | tf_op jit(solution)/shard_map/ppermute | solution.py:361
  25.3 5.2 %collective-permute-start.8 = (bf16[128,256]{1,0:T(8,128)(2,1)S(1)}, bf16[128,256]{1,0:T(8,128)(2,1)S(1)}, u32[]{:S(2)}, u32[]{:S(2)}) collective-permute-start(bf16[128,256]{1,0:T(8,128)(2,1)S(1)} %get-tuple-element.46), channel_id=1, source_target_pairs={{0,6},{2,4},{4,2},{6,0},{1,7},{3,5},{5,3},{7,1},{8,14},{10,12},{12... | collective-permute-start | bytes 196616 | tf_op jit(solution)/shard_map/ppermute | solution.py:284
  28.6 4.3 %collective-permute-start.9 = (bf16[128,256]{1,0:T(8,128)(2,1)S(1)}, bf16[128,256]{1,0:T(8,128)(2,1)S(1)}, u32[]{:S(2)}, u32[]{:S(2)}) collective-permute-start(bf16[128,256]{1,0:T(8,128)(2,1)S(1)} %get-tuple-element.47), channel_id=1, source_target_pairs={{0,2},{2,0},{4,6},{6,4},{1,3},{3,1},{5,7},{7,5},{8,10},{10,8},{12,... | collective-permute-start | bytes 196616 | tf_op jit(solution)/shard_map/ppermute | solution.py:284
  29.6 4.3 %collective-permute-start.10 = (bf16[128,256]{1,0:T(8,128)(2,1)S(1)}, bf16[128,256]{1,0:T(8,128)(2,1)S(1)}, u32[]{:S(2)}, u32[]{:S(2)}) collective-permute-start(bf16[128,256]{1,0:T(8,128)(2,1)S(1)} %get-tuple-element.48), channel_id=1, source_target_pairs={{0,4},{2,6},{4,0},{6,2},{1,5},{3,7},{5,1},{7,3},{8,12},{10,14},{12... | collective-permute-start | bytes 196616 | tf_op jit(solution)/shard_map/ppermute | solution.py:284
  30.6 3.3 %collective-permute-start.12 = (bf16[128,256]{1,0:T(8,128)(2,1)S(1)}, bf16[128,256]{1,0:T(8,128)(2,1)S(1)}, u32[]{:S(2)}, u32[]{:S(2)}) collective-permute-start(bf16[128,256]{1,0:T(8,128)(2,1)S(1)} %collective-permute-done.8.refs_1_), channel_id=1, source_target_pairs={{0,1},{1,0},{2,3},{3,2},{4,5},{5,4},{6,7},{7,6},{8,9},{9,8},{10,11... | collective-permute-start | bytes 196616 | tf_op jit(solution)/shard_map/ppermute | solution.py:284
  30.6 3.3 %collective-permute-start.11 = (bf16[128,256]{1,0:T(8,128)(2,1)S(1)}, bf16[128,256]{1,0:T(8,128)(2,1)S(1)}, u32[]{:S(2)}, u32[]{:S(2)}) collective-permute-start(bf16[128,256]{1,0:T(8,128)(2,1)S(1)} %get-tuple-element.45.refs_0_), channel_id=1, source_target_pairs={{0,1},{1,0},{2,3},{3,2},{4,5},{5,4},{6,7},{7,6},{8,9},{9,8},{10,11... | collective-permute-start | bytes 196616 | tf_op jit(solution)/shard_map/ppermute | solution.py:284
  32.9 1.3 %collective-permute-start.13 = (bf16[128,256]{1,0:T(8,128)(2,1)S(1)}, bf16[128,256]{1,0:T(8,128)(2,1)S(1)}, u32[]{:S(2)}, u32[]{:S(2)}) collective-permute-start(bf16[128,256]{1,0:T(8,128)(2,1)S(1)} %collective-permute-done.9.refs_2_), channel_id=1, source_target_pairs={{0,1},{1,0},{2,3},{3,2},{4,5},{5,4},{6,7},{7,6},{8,9},{9,8},{10,11... | collective-permute-start | bytes 196616 | tf_op jit(solution)/shard_map/ppermute | solution.py:284
  33.9 1.3 %collective-permute-start.14 = (bf16[128,256]{1,0:T(8,128)(2,1)S(1)}, bf16[128,256]{1,0:T(8,128)(2,1)S(1)}, u32[]{:S(2)}, u32[]{:S(2)}) collective-permute-start(bf16[128,256]{1,0:T(8,128)(2,1)S(1)} %collective-permute-done.10.refs_3_), channel_id=1, source_target_pairs={{0,1},{1,0},{2,3},{3,2},{4,5},{5,4},{6,7},{7,6},{8,9},{9,8},{10,11... | collective-permute-start | bytes 196616 | tf_op jit(solution)/shard_map/ppermute | solution.py:284

commit v11 on v10

--- a/solution.py
+++ b/solution.py
@@ -352,7 +352,7 @@
     def send_on(steps):
         blocks = [arrays.get(("block", step), arrays.get(("kv", step))) for step in steps]
         message = jnp.stack([block[: 2 * rows] for block in blocks])
-        if apart and steps == near[-1:]:
+        if apart and steps == apart:
             early = [first]
             message, got = lax.optimization_barrier((message, [arrays[name] for name in early]))
             arrays.update(zip(early, got))
@@ -412,13 +412,14 @@
     send_on([0])
     mix = {}
     if apart:
-        blocks, queries = packed[:group], packed[group:]
-        tied = lax.optimization_barrier((queries, turned))
-        queries, turned = tied
+        queries, turned = lax.optimization_barrier((packed[group:], turned))
         arrays["q", apart[0]] = swapped(queries[0], "place", apart[0])
-        tied = lax.optimization_barrier((packed[apart[0]], turned, arrays["block", 1]))
-        block, turned, arrays["block", 1] = tied
-        arrays["kv", apart[0]] = swapped(block, "place", apart[0])
+        tied = lax.optimization_barrier(
+            (packed[apart[0]], turned, [arrays["block", step] for step in near])
+        )
+        far_block, turned, blocks = tied
+        arrays.update((("block", step), block) for step, block in zip(near, blocks))
+        arrays["kv", apart[0]] = swapped(far_block, "place", apart[0])
     for step in near:
         send_on([step])
     mix.update(stage(0, NEAR))

time: 36.5 us -> 33.6 us (0.921)
  waiting for transfers between devices: 14 us -> 7.87 us
  starting transfers between devices: 14.8 us -> 18.1 us
    ppermute x11, waiting for transfers between devices: 9.42 us -> 5.38 us  [swapped(): lax.ppermute(value, axis, [(source, source ^ step) for source in range(co...]
    ppermute x4, starting transfers between devices: 4.95 us -> 7.26 us  [send_on(): arrays['halo', offset, tuple(steps)] = lax.ppermute(message, 'group', pairs)]
    ppermute x4, waiting for transfers between devices: 4.55 us -> 2.49 us  [send_on(): arrays['halo', offset, tuple(steps)] = lax.ppermute(message, 'group', pairs)]
    ppermute x11, starting transfers between devices: 9.89 us -> 10.8 us  [swapped(): lax.ppermute(value, axis, [(source, source ^ step) for source in range(co...]
  transfers between devices with their start and end apart: 15 -> 15, of which waited for: 9 -> 8; matrix products, arithmetic and copies ran while one was open for 0% -> 0% of each run, Pallas kernels for 14% -> 15%
where the time goes in v11:
time: 33.6 us; the launch traced here: 33.5 us
  starting transfers between devices  18.1 us (54%)
  waiting for transfers between devices  7.87 us (23%)
  Pallas kernels  7.39 us (22%)
    ppermute x11, starting transfers between devices, swapped(): lax.ppermute(value, axis, [(source, source ^ step) for source in range(co...  10.8 us
    ppermute x4, starting transfers between devices, send_on(): arrays['halo', offset, tuple(steps)] = lax.ppermute(message, 'group', pairs)  7.26 us
    ppermute x11, waiting for transfers between devices, swapped(): lax.ppermute(value, axis, [(source, source ^ step) for source in range(co...  5.38 us
    pallas_call x4, Pallas kernels, stage(): pl.pallas_call(functools.partial(attend_kernel, names=names, work=work, s...  3.55 us
    ppermute x4, waiting for transfers between devices, send_on(): arrays['halo', offset, tuple(steps)] = lax.ppermute(message, 'group', pairs)  2.49 us
    pallas_call x1, Pallas kernels, on_device(): pl.pallas_call(functools.partial(turn_kernel, head_total=head_total), out...  1.44 us
    pallas_call x1, Pallas kernels, on_device(): pl.pallas_call(pack_kernel, out_shape=[shape((2 * rows, HD), bf16) if ste...  1.21 us
    pallas_call x1, Pallas kernels, on_device(): pl.pallas_call(functools.partial(project_kernel, group=group, head_total=...  1.19 us
  transfers between devices with their start and end apart: 15, of which 8 were waited for; matrix products, arithmetic and copies ran while one was open for 0% of the time, Pallas kernels for 15%

profile of v11, /device:TPU:0, one launch (start us, length us, event | category | flops | bytes accessed | tf_op | source)
XLA Modules:
  0.0 33.5 jit_solution(15757012722565965567)
XLA Ops:
  0.0 1.2 %pack.1 = (bf16[784,128]{1,0:T(8,128)(2,1)S(1)}, bf16[784,128]{1,0:T(8,128)(2,1)S(1)}, bf16[784,128]{1,0:T(8,128)(2,1)S(1)}, bf16[512,128]{1,0:T(8,128)(2,1)S(1)}, bf16[272,128]{1,0:T(8,128)(2,1)S(1)}) custom-call(bf16[256,512]{1,0:T(8,128)(2,1)} %query_ref.1, bf16[256,512]{1,0:T(8,128)(2,1)} %key_ref.1, bf16[256,512]{1,0:T(8,128)(2,1)} %value_ref.1, ...), custom_call_target="tpu_custom_call" | custom-call | tf_op jit(solution)/shard_map/pack/pallas_call | solution.py:299
  1.2 3.0 %collective-permute-start = (bf16[784,128]{1,0:T(8,128)(2,1)S(1)}, bf16[784,128]{1,0:T(8,128)(2,1)S(1)}, u32[]{:S(2)}, u32[]{:S(2)}) collective-permute-start(bf16[784,128]{1,0:T(8,128)(2,1)S(1)} %get-tuple-element.32), channel_id=1, source_target_pairs={{0,2},{2,0},{4,6},{6,4},{1,3},{3,1},{5,7},{7,5},{8,10},{10,8},{12,... | collective-permute-start | bytes 602120 | tf_op jit(solution)/shard_map/ppermute | solution.py:284
  4.2 1.5 %collective-permute-start.1 = (bf16[784,128]{1,0:T(8,128)(2,1)S(1)}, bf16[784,128]{1,0:T(8,128)(2,1)S(1)}, u32[]{:S(2)}, u32[]{:S(2)}) collective-permute-start(bf16[784,128]{1,0:T(8,128)(2,1)S(1)} %get-tuple-element.33), channel_id=1, source_target_pairs={{0,4},{2,6},{4,0},{6,2},{1,5},{3,7},{5,1},{7,3},{8,12},{10,14},{12... | collective-permute-start | bytes 602120 | tf_op jit(solution)/shard_map/ppermute | solution.py:284
  5.8 1.6 %collective-permute-start.6 = (bf16[1,512,128]{2,1,0:T(8,128)(2,1)S(1)}, bf16[1,512,128]{2,1,0:T(8,128)(2,1)S(1)}, u32[]{:S(2)}, u32[]{:S(2)}) collective-permute-start(bf16[1,512,128]{2,1,0:T(8,128)(2,1)S(1)} %slice_bitcast_fusion), channel_id=1, source_target_pairs={{0,8},{8,16},{16,24},{24,0},{1,9},{9,17},{17,25},{25,1},{2,10},{10... | collective-permute-start | bytes 393224 | tf_op jit(solution)/shard_map/ppermute | solution.py:361
  7.4 1.4 %turn.1.turned_ref = bf16[2,512,512]{2,1,0:T(8,128)(2,1)S(1)} custom-call(bf16[784,128]{1,0:T(8,128)(2,1)S(1)} %get-tuple-element.30.block_ref.refs_0_, bf16[1024,1024]{1,0:T(8,128)(2,1)} %weight_ref.1), custom_call_target="tpu_custom_call" | custom-call | flops 1000000000 | bytes 1 | tf_op jit(solution)/shard_map/turn/pallas_call | solution.py:328
  8.8 0.5 %collective-permute-start.2 = (bf16[272,128]{1,0:T(8,128)(2,1)S(1)}, bf16[272,128]{1,0:T(8,128)(2,1)S(1)}, u32[]{:S(2)}, u32[]{:S(2)}) collective-permute-start(bf16[272,128]{1,0:T(8,128)(2,1)S(1)} %get-tuple-element.37), channel_id=1, source_target_pairs={{0,6},{2,4},{4,2},{6,0},{1,7},{3,5},{5,3},{7,1},{8,14},{10,12},{12... | collective-permute-start | bytes 208904 | tf_op jit(solution)/shard_map/ppermute | solution.py:284
  9.4 0.0 collective-permute-done.refs_1_
  9.4 1.3 %collective-permute-done.1.refs_2_ = bf16[784,128]{1,0:T(8,128)(2,1)S(1)} collective-permute-done((bf16[784,128]{1,0:T(8,128)(2,1)S(1)}, bf16[784,128]{1,0:T(8,128)(2,1)S(1)}, u32[]{:S(2)}, u32[]{:S(2)}) %collective-permute-start.1) | collective-permute-done | bytes 200736 | tf_op jit(solution)/shard_map/ppermute | solution.py:284
  10.7 2.2 %collective-permute-start.5 = (bf16[512,128]{1,0:T(8,128)(2,1)S(1)}, bf16[512,128]{1,0:T(8,128)(2,1)S(1)}, u32[]{:S(2)}, u32[]{:S(2)}) collective-permute-start(bf16[512,128]{1,0:T(8,128)(2,1)S(1)} %get-tuple-element.38), channel_id=1, source_target_pairs={{0,6},{2,4},{4,2},{6,0},{1,7},{3,5},{5,3},{7,1},{8,14},{10,12},{12... | collective-permute-start | bytes 393224 | tf_op jit(solution)/shard_map/ppermute | solution.py:284
  12.9 1.6 %collective-permute-start.3 = (bf16[1,512,128]{2,1,0:T(8,128)(2,1)S(1)}, bf16[1,512,128]{2,1,0:T(8,128)(2,1)S(1)}, u32[]{:S(2)}, u32[]{:S(2)}) collective-permute-start(bf16[1,512,128]{2,1,0:T(8,128)(2,1)S(1)} %slice_bitcast_fusion.2), channel_id=1, source_target_pairs={{0,8},{8,16},{16,24},{24,0},{1,9},{9,17},{17,25},{25,1},{2,10},{10... | collective-permute-start | bytes 393224 | tf_op jit(solution)/shard_map/ppermute | solution.py:361
  14.6 1.6 %collective-permute-start.4 = (bf16[1,512,128]{2,1,0:T(8,128)(2,1)S(1)}, bf16[1,512,128]{2,1,0:T(8,128)(2,1)S(1)}, u32[]{:S(2)}, u32[]{:S(2)}) collective-permute-start(bf16[1,512,128]{2,1,0:T(8,128)(2,1)S(1)} %slice_bitcast_fusion.1), channel_id=1, source_target_pairs={{0,8},{8,16},{16,24},{24,0},{1,9},{9,17},{17,25},{25,1},{2,10},{10... | collective-permute-start | bytes 393224 | tf_op jit(solution)/shard_map/ppermute | solution.py:361
  16.2 0.0 collective-permute-done.6.refs_3_
  16.2 1.2 %attend.4 = (f32[4,128,256]{2,1,0:T(8,128)S(1)}, f32[4,8,256]{2,1,0:T(8,128)S(1)}) custom-call(bf16[784,128]{1,0:T(8,128)(2,1)S(1)} %get-tuple-element.30.block_ref.refs_0_, bf16[784,128]{1,0:T(8,128)(2,1)S(1)} %collective-permute-done.refs_1_, bf16[784,128]{1,0:T(8,128)(2,1)S(1)} %collective-permute-done.1.refs_2_, ...), custom_call_target="tpu_custom_call" | custom-call | flops 1000000000 | bytes 1 | tf_op jit(solution)/shard_map/attend/pallas_call | solution.py:389
  17.4 0.0 collective-permute-done.5.refs_5_
  17.4 2.4 %collective-permute-start.7 = (bf16[1,512,128]{2,1,0:T(8,128)(2,1)S(1)}, bf16[1,512,128]{2,1,0:T(8,128)(2,1)S(1)}, u32[]{:S(2)}, u32[]{:S(2)}) collective-permute-start(bf16[1,512,128]{2,1,0:T(8,128)(2,1)S(1)} %bitcast.9), channel_id=1, source_target_pairs={{0,8},{8,16},{16,24},{24,0},{1,9},{9,17},{17,25},{25,1},{2,10},{10... | collective-permute-start | bytes 393224 | tf_op jit(solution)/shard_map/ppermute | solution.py:361
  19.8 0.0 collective-permute-done.2.refs_4_.refs_3_
  19.8 0.8 %attend.5 = (f32[4,128,256]{2,1,0:T(8,128)S(1)}, f32[4,8,256]{2,1,0:T(8,128)S(1)}) custom-call(bf16[784,128]{1,0:T(8,128)(2,1)S(1)} %get-tuple-element.30.block_ref.refs_0_, bf16[784,128]{1,0:T(8,128)(2,1)S(1)} %collective-permute-done.refs_1_, bf16[784,128]{1,0:T(8,128)(2,1)S(1)} %collective-permute-done.1.refs_2_, ...), custom_call_target="tpu_custom_call" | custom-call | flops 1000000000 | bytes 1 | tf_op jit(solution)/shard_map/attend/pallas_call | solution.py:389
  20.6 0.7 %collective-permute-done.3.refs_4_ = bf16[1,512,128]{2,1,0:T(8,128)(2,1)S(1)} collective-permute-done((bf16[1,512,128]{2,1,0:T(8,128)(2,1)S(1)}, bf16[1,512,128]{2,1,0:T(8,128)(2,1)S(1)}, u32[]{:S(2)}, u32[]{:S(2)}) %collective-permute-start.3) | collective-permute-done | bytes 131104 | tf_op jit(solution)/shard_map/ppermute | solution.py:361
  21.3 1.7 %collective-permute-done.4.refs_5_ = bf16[1,512,128]{2,1,0:T(8,128)(2,1)S(1)} collective-permute-done((bf16[1,512,128]{2,1,0:T(8,128)(2,1)S(1)}, bf16[1,512,128]{2,1,0:T(8,128)(2,1)S(1)}, u32[]{:S(2)}, u32[]{:S(2)}) %collective-permute-start.4) | collective-permute-done | bytes 131104 | tf_op jit(solution)/shard_map/ppermute | solution.py:361
  23.1 0.6 %attend.6 = (bf16[128,256]{1,0:T(8,128)(2,1)S(1)}, f32[4,128,256]{2,1,0:T(8,128)S(1)}, f32[4,8,256]{2,1,0:T(8,128)S(1)}) custom-call(bf16[784,128]{1,0:T(8,128)(2,1)S(1)} %get-tuple-element.30.block_ref.refs_0_, bf16[784,128]{1,0:T(8,128)(2,1)S(1)} %collective-permute-done.refs_1_, bf16[784,128]{1,0:T(8,128)(2,1)S(1)} %collective-permute-done.1.refs_2_, ...), custom_call_target="tpu_custom_call" | custom-call | flops 1000000000 | bytes 1 | tf_op jit(solution)/shard_map/attend/pallas_call | solution.py:389
  23.6 0.9 %collective-permute-start.8 = (bf16[128,256]{1,0:T(8,128)(2,1)S(1)}, bf16[128,256]{1,0:T(8,128)(2,1)S(1)}, u32[]{:S(2)}, u32[]{:S(2)}) collective-permute-start(bf16[128,256]{1,0:T(8,128)(2,1)S(1)} %get-tuple-element.48), channel_id=1, source_target_pairs={{0,6},{2,4},{4,2},{6,0},{1,7},{3,5},{5,3},{7,1},{8,14},{10,12},{12... | collective-permute-start | bytes 196616 | tf_op jit(solution)/shard_map/ppermute | solution.py:284
  24.6 0.0 collective-permute-done.7.refs_5_
  24.6 1.0 %attend.7 = (bf16[128,256]{1,0:T(8,128)(2,1)S(1)}, bf16[128,256]{1,0:T(8,128)(2,1)S(1)}, bf16[128,256]{1,0:T(8,128)(2,1)S(1)}) custom-call(bf16[784,128]{1,0:T(8,128)(2,1)S(1)} %get-tuple-element.30.block_ref.refs_0_, bf16[784,128]{1,0:T(8,128)(2,1)S(1)} %collective-permute-done.refs_1_, bf16[784,128]{1,0:T(8,128)(2,1)S(1)} %collective-permute-done.1.refs_2_, ...), custom_call_target="tpu_custom_call" | custom-call | flops 1000000000 | bytes 1 | tf_op jit(solution)/shard_map/attend/pallas_call | solution.py:389
  25.6 1.2 %collective-permute-start.9 = (bf16[128,256]{1,0:T(8,128)(2,1)S(1)}, bf16[128,256]{1,0:T(8,128)(2,1)S(1)}, u32[]{:S(2)}, u32[]{:S(2)}) collective-permute-start(bf16[128,256]{1,0:T(8,128)(2,1)S(1)} %get-tuple-element.49), channel_id=1, source_target_pairs={{0,2},{2,0},{4,6},{6,4},{1,3},{3,1},{5,7},{7,5},{8,10},{10,8},{12,... | collective-permute-start | bytes 196616 | tf_op jit(solution)/shard_map/ppermute | solution.py:284
  26.8 0.9 %collective-permute-start.10 = (bf16[128,256]{1,0:T(8,128)(2,1)S(1)}, bf16[128,256]{1,0:T(8,128)(2,1)S(1)}, u32[]{:S(2)}, u32[]{:S(2)}) collective-permute-start(bf16[128,256]{1,0:T(8,128)(2,1)S(1)} %get-tuple-element.50), channel_id=1, source_target_pairs={{0,4},{2,6},{4,0},{6,2},{1,5},{3,7},{5,1},{7,3},{8,12},{10,14},{12... | collective-permute-start | bytes 196616 | tf_op jit(solution)/shard_map/ppermute | solution.py:284
  27.7 1.2 %collective-permute-done.8.refs_1_ = bf16[128,256]{1,0:T(8,128)(2,1)S(1)} collective-permute-done((bf16[128,256]{1,0:T(8,128)(2,1)S(1)}, bf16[128,256]{1,0:T(8,128)(2,1)S(1)}, u32[]{:S(2)}, u32[]{:S(2)}) %collective-permute-start.8) | collective-permute-done | bytes 65568 | tf_op jit(solution)/shard_map/ppermute | solution.py:284
  28.9 0.0 collective-permute-start.12
  28.9 0.5 %collective-permute-start.11 = (bf16[128,256]{1,0:T(8,128)(2,1)S(1)}, bf16[128,256]{1,0:T(8,128)(2,1)S(1)}, u32[]{:S(2)}, u32[]{:S(2)}) collective-permute-start(bf16[128,256]{1,0:T(8,128)(2,1)S(1)} %get-tuple-element.47.refs_0_), channel_id=1, source_target_pairs={{0,1},{1,0},{2,3},{3,2},{4,5},{5,4},{6,7},{7,6},{8,9},{9,8},{10,11... | collective-permute-start | bytes 196616 | tf_op jit(solution)/shard_map/ppermute | solution.py:284
  29.4 0.5 %collective-permute-done.9.refs_2_ = bf16[128,256]{1,0:T(8,128)(2,1)S(1)} collective-permute-done((bf16[128,256]{1,0:T(8,128)(2,1)S(1)}, bf16[128,256]{1,0:T(8,128)(2,1)S(1)}, u32[]{:S(2)}, u32[]{:S(2)}) %collective-permute-start.9) | collective-permute-done | bytes 65568 | tf_op jit(solution)/shard_map/ppermute | solution.py:284
  29.9 0.0 collective-permute-start.13
  29.9 1.1 %collective-permute-done.10.refs_3_ = bf16[128,256]{1,0:T(8,128)(2,1)S(1)} collective-permute-done((bf16[128,256]{1,0:T(8,128)(2,1)S(1)}, bf16[128,256]{1,0:T(8,128)(2,1)S(1)}, u32[]{:S(2)}, u32[]{:S(2)}) %collective-permute-start.10) | collective-permute-done | bytes 65568 | tf_op jit(solution)/shard_map/ppermute | solution.py:284
  31.0 0.0 collective-permute-start.14
  31.0 0.0 collective-permute-done.12.refs_5_
  31.0 0.0 collective-permute-done.11.refs_4_
  31.0 0.1 collective-permute-done.13.refs_6_
  31.2 1.1 %collective-permute-done.14.refs_7_ = bf16[128,256]{1,0:T(8,128)(2,1)S(1)} collective-permute-done((bf16[128,256]{1,0:T(8,128)(2,1)S(1)}, bf16[128,256]{1,0:T(8,128)(2,1)S(1)}, u32[]{:S(2)}, u32[]{:S(2)}) %collective-permute-start.14) | collective-permute-done | bytes 65568 | tf_op jit(solution)/shard_map/ppermute | solution.py:284
  32.3 1.2 %project.1 = bf16[512,256]{1,0:T(8,128)(2,1)} custom-call(bf16[2,512,512]{2,1,0:T(8,128)(2,1)S(1)} %turn.1.turned_ref, bf16[128,256]{1,0:T(8,128)(2,1)S(1)} %get-tuple-element.47.refs_0_, bf16[128,256]{1,0:T(8,128)(2,1)S(1)} %collective-permute-done.8.refs_1_, bf16[128,256]{1,0:T(8,128)(2,1)S(1)} %collective-permute-done.9.refs_2_, ...), custom_call_target="tpu_custom_call" | custom-call | tf_op jit(solution)/shard_map/project/pallas_call | solution.py:436
  (3 shorter events, 0.0 us)
Async XLA Ops:
  1.2 8.2 %collective-permute-start = (bf16[784,128]{1,0:T(8,128)(2,1)S(1)}, bf16[784,128]{1,0:T(8,128)(2,1)S(1)}, u32[]{:S(2)}, u32[]{:S(2)}) collective-permute-start(bf16[784,128]{1,0:T(8,128)(2,1)S(1)} %get-tuple-element.32), channel_id=1, source_target_pairs={{0,2},{2,0},{4,6},{6,4},{1,3},{3,1},{5,7},{7,5},{8,10},{10,8},{12,... | collective-permute-start | bytes 602120 | tf_op jit(solution)/shard_map/ppermute | solution.py:284
  4.2 6.4 %collective-permute-start.1 = (bf16[784,128]{1,0:T(8,128)(2,1)S(1)}, bf16[784,128]{1,0:T(8,128)(2,1)S(1)}, u32[]{:S(2)}, u32[]{:S(2)}) collective-permute-start(bf16[784,128]{1,0:T(8,128)(2,1)S(1)} %get-tuple-element.33), channel_id=1, source_target_pairs={{0,4},{2,6},{4,0},{6,2},{1,5},{3,7},{5,1},{7,3},{8,12},{10,14},{12... | collective-permute-start | bytes 602120 | tf_op jit(solution)/shard_map/ppermute | solution.py:284
  5.8 10.4 %collective-permute-start.6 = (bf16[1,512,128]{2,1,0:T(8,128)(2,1)S(1)}, bf16[1,512,128]{2,1,0:T(8,128)(2,1)S(1)}, u32[]{:S(2)}, u32[]{:S(2)}) collective-permute-start(bf16[1,512,128]{2,1,0:T(8,128)(2,1)S(1)} %slice_bitcast_fusion), channel_id=1, source_target_pairs={{0,8},{8,16},{16,24},{24,0},{1,9},{9,17},{17,25},{25,1},{2,10},{10... | collective-permute-start | bytes 393224 | tf_op jit(solution)/shard_map/ppermute | solution.py:361
  8.8 11.0 %collective-permute-start.2 = (bf16[272,128]{1,0:T(8,128)(2,1)S(1)}, bf16[272,128]{1,0:T(8,128)(2,1)S(1)}, u32[]{:S(2)}, u32[]{:S(2)}) collective-permute-start(bf16[272,128]{1,0:T(8,128)(2,1)S(1)} %get-tuple-element.37), channel_id=1, source_target_pairs={{0,6},{2,4},{4,2},{6,0},{1,7},{3,5},{5,3},{7,1},{8,14},{10,12},{12... | collective-permute-start | bytes 208904 | tf_op jit(solution)/shard_map/ppermute | solution.py:284
  10.7 6.7 %collective-permute-start.5 = (bf16[512,128]{1,0:T(8,128)(2,1)S(1)}, bf16[512,128]{1,0:T(8,128)(2,1)S(1)}, u32[]{:S(2)}, u32[]{:S(2)}) collective-permute-start(bf16[512,128]{1,0:T(8,128)(2,1)S(1)} %get-tuple-element.38), channel_id=1, source_target_pairs={{0,6},{2,4},{4,2},{6,0},{1,7},{3,5},{5,3},{7,1},{8,14},{10,12},{12... | collective-permute-start | bytes 393224 | tf_op jit(solution)/shard_map/ppermute | solution.py:284
  12.9 8.4 %collective-permute-start.3 = (bf16[1,512,128]{2,1,0:T(8,128)(2,1)S(1)}, bf16[1,512,128]{2,1,0:T(8,128)(2,1)S(1)}, u32[]{:S(2)}, u32[]{:S(2)}) collective-permute-start(bf16[1,512,128]{2,1,0:T(8,128)(2,1)S(1)} %slice_bitcast_fusion.2), channel_id=1, source_target_pairs={{0,8},{8,16},{16,24},{24,0},{1,9},{9,17},{17,25},{25,1},{2,10},{10... | collective-permute-start | bytes 393224 | tf_op jit(solution)/shard_map/ppermute | solution.py:361
  14.6 8.5 %collective-permute-start.4 = (bf16[1,512,128]{2,1,0:T(8,128)(2,1)S(1)}, bf16[1,512,128]{2,1,0:T(8,128)(2,1)S(1)}, u32[]{:S(2)}, u32[]{:S(2)}) collective-permute-start(bf16[1,512,128]{2,1,0:T(8,128)(2,1)S(1)} %slice_bitcast_fusion.1), channel_id=1, source_target_pairs={{0,8},{8,16},{16,24},{24,0},{1,9},{9,17},{17,25},{25,1},{2,10},{10... | collective-permute-start | bytes 393224 | tf_op jit(solution)/shard_map/ppermute | solution.py:361
  17.4 7.2 %collective-permute-start.7 = (bf16[1,512,128]{2,1,0:T(8,128)(2,1)S(1)}, bf16[1,512,128]{2,1,0:T(8,128)(2,1)S(1)}, u32[]{:S(2)}, u32[]{:S(2)}) collective-permute-start(bf16[1,512,128]{2,1,0:T(8,128)(2,1)S(1)} %bitcast.9), channel_id=1, source_target_pairs={{0,8},{8,16},{16,24},{24,0},{1,9},{9,17},{17,25},{25,1},{2,10},{10... | collective-permute-start | bytes 393224 | tf_op jit(solution)/shard_map/ppermute | solution.py:361
  23.6 5.2 %collective-permute-start.8 = (bf16[128,256]{1,0:T(8,128)(2,1)S(1)}, bf16[128,256]{1,0:T(8,128)(2,1)S(1)}, u32[]{:S(2)}, u32[]{:S(2)}) collective-permute-start(bf16[128,256]{1,0:T(8,128)(2,1)S(1)} %get-tuple-element.48), channel_id=1, source_target_pairs={{0,6},{2,4},{4,2},{6,0},{1,7},{3,5},{5,3},{7,1},{8,14},{10,12},{12... | collective-permute-start | bytes 196616 | tf_op jit(solution)/shard_map/ppermute | solution.py:284
  25.6 4.3 %collective-permute-start.9 = (bf16[128,256]{1,0:T(8,128)(2,1)S(1)}, bf16[128,256]{1,0:T(8,128)(2,1)S(1)}, u32[]{:S(2)}, u32[]{:S(2)}) collective-permute-start(bf16[128,256]{1,0:T(8,128)(2,1)S(1)} %get-tuple-element.49), channel_id=1, source_target_pairs={{0,2},{2,0},{4,6},{6,4},{1,3},{3,1},{5,7},{7,5},{8,10},{10,8},{12,... | collective-permute-start | bytes 196616 | tf_op jit(solution)/shard_map/ppermute | solution.py:284
  26.8 4.3 %collective-permute-start.10 = (bf16[128,256]{1,0:T(8,128)(2,1)S(1)}, bf16[128,256]{1,0:T(8,128)(2,1)S(1)}, u32[]{:S(2)}, u32[]{:S(2)}) collective-permute-start(bf16[128,256]{1,0:T(8,128)(2,1)S(1)} %get-tuple-element.50), channel_id=1, source_target_pairs={{0,4},{2,6},{4,0},{6,2},{1,5},{3,7},{5,1},{7,3},{8,12},{10,14},{12... | collective-permute-start | bytes 196616 | tf_op jit(solution)/shard_map/ppermute | solution.py:284
  28.9 2.2 %collective-permute-start.12 = (bf16[128,256]{1,0:T(8,128)(2,1)S(1)}, bf16[128,256]{1,0:T(8,128)(2,1)S(1)}, u32[]{:S(2)}, u32[]{:S(2)}) collective-permute-start(bf16[128,256]{1,0:T(8,128)(2,1)S(1)} %collective-permute-done.8.refs_1_), channel_id=1, source_target_pairs={{0,1},{1,0},{2,3},{3,2},{4,5},{5,4},{6,7},{7,6},{8,9},{9,8},{10,11... | collective-permute-start | bytes 196616 | tf_op jit(solution)/shard_map/ppermute | solution.py:284
  28.9 2.2 %collective-permute-start.11 = (bf16[128,256]{1,0:T(8,128)(2,1)S(1)}, bf16[128,256]{1,0:T(8,128)(2,1)S(1)}, u32[]{:S(2)}, u32[]{:S(2)}) collective-permute-start(bf16[128,256]{1,0:T(8,128)(2,1)S(1)} %get-tuple-element.47.refs_0_), channel_id=1, source_target_pairs={{0,1},{1,0},{2,3},{3,2},{4,5},{5,4},{6,7},{7,6},{8,9},{9,8},{10,11... | collective-permute-start | bytes 196616 | tf_op jit(solution)/shard_map/ppermute | solution.py:284
  29.9 1.3 %collective-permute-start.13 = (bf16[128,256]{1,0:T(8,128)(2,1)S(1)}, bf16[128,256]{1,0:T(8,128)(2,1)S(1)}, u32[]{:S(2)}, u32[]{:S(2)}) collective-permute-start(bf16[128,256]{1,0:T(8,128)(2,1)S(1)} %collective-permute-done.9.refs_2_), channel_id=1, source_target_pairs={{0,1},{1,0},{2,3},{3,2},{4,5},{5,4},{6,7},{7,6},{8,9},{9,8},{10,11... | collective-permute-start | bytes 196616 | tf_op jit(solution)/shard_map/ppermute | solution.py:284
  31.0 1.3 %collective-permute-start.14 = (bf16[128,256]{1,0:T(8,128)(2,1)S(1)}, bf16[128,256]{1,0:T(8,128)(2,1)S(1)}, u32[]{:S(2)}, u32[]{:S(2)}) collective-permute-start(bf16[128,256]{1,0:T(8,128)(2,1)S(1)} %collective-permute-done.10.refs_3_), channel_id=1, source_target_pairs={{0,1},{1,0},{2,3},{3,2},{4,5},{5,4},{6,7},{7,6},{8,9},{9,8},{10,11... | collective-permute-start | bytes 196616 | tf_op jit(solution)/shard_map/ppermute | solution.py:284

commit v12 on v11

--- a/solution.py
+++ b/solution.py
@@ -18,7 +18,6 @@
 EXTRA = 16
 OWN = 10**9
 NEAR = 1000000000
-MORE = 1000000000
 FAR = 1000000000
 VMEM = pl.BlockSpec(memory_space=pltpu.VMEM)
 HBM = pl.BlockSpec(memory_space=pltpu.HBM)
@@ -43,18 +42,9 @@
     return step.bit_count()
 
 
-def query_places(refs, group, rows):
-    apart = iter(refs[group:])
-    return [
-        next(apart) if hops(step) > 1 else refs[step].at[pl.ds(2 * rows, rows + EXTRA)]
-        for step in range(group)
-    ]
-
-
 def pack_kernel(query_ref, key_ref, value_ref, index_ref, count_ref, *refs):
     out_refs, (values, index, count, sem) = refs[:-4], refs[-4:]
     group = query_ref.shape[1] // HD
-    block_refs, query_refs = out_refs[:group], query_places(out_refs, group, query_ref.shape[0])
     rows = query_ref.shape[0]
     tiles = rows // TILE
     place = lax.axis_index("place")
@@ -71,10 +61,12 @@
         cols = pl.ds(pl.multiple_of(jnp.bitwise_xor(place, step) * HD, HD), HD)
         copies += [
             pltpu.make_async_copy(
-                key_ref.at[:, cols], block_refs[step].at[pl.ds(0, rows)], sem.at[3 + 2 * step]
+                key_ref.at[:, cols], out_refs[step].at[pl.ds(0, rows)], sem.at[3 + 2 * step]
             ),
             pltpu.make_async_copy(
-                query_ref.at[:, cols], query_refs[step].at[pl.ds(0, rows)], sem.at[4 + 2 * step]
+                query_ref.at[:, cols],
+                out_refs[step].at[pl.ds(2 * rows, rows)],
+                sem.at[4 + 2 * step],
             ),
         ]
     for copy in copies:
@@ -85,8 +77,8 @@
     value_copy.wait()
     for step in range(group):
         cols = pl.ds(pl.multiple_of(jnp.bitwise_xor(place, step) * HD, HD), HD)
-        out = block_refs[step]
-        query_refs[step][rows:] = uses
+        out = out_refs[step]
+        out[3 * rows :] = uses
         for at in range(0, rows, TILE):
             out[rows + at : rows + at + TILE] = values[at : at + TILE, cols].T
     for copy in copies:
@@ -178,8 +170,6 @@
     steps = list(range(group))
     near = [step for step in steps if hops(step) < 2]
     stages = [(near, lambda offset, step: hops(step) < 2 and (offset == 0 or step == 0))]
-    if len(near) < group:
-        stages.append((steps, lambda offset, step: offset == 0 or step == 0))
     stages.append((steps, lambda offset, step: offset == 0 or hops(step) < 2))
     if len(near) < group:
         stages.append((steps, lambda offset, step: True))
@@ -212,11 +202,9 @@
         for name in named:
             if name[0] == "halo" and name[1] == offset and step in name[2]:
                 return named[name].at[name[2].index(step)]
-        return named.get(("block", step), named.get(("kv", step)))
+        return named["block", step]
 
     def queries(step):
-        if ("q", step) in named:
-            return named["q", step]
         return named["block", step].at[pl.ds(2 * rows, rows + EXTRA)]
 
     here = lax.axis_index("place")
@@ -262,17 +250,18 @@
     return sorted(range(group), key=lambda step: (step > 0, -hops(step), step))
 
 
-def project_kernel(turned_ref, *refs, group, head_total):
-    mix_refs, out_ref, mix = refs[:-2], refs[-2], refs[-1]
+def project_kernel(turned_ref, *refs, group, others):
+    mix_refs, refs = refs[: len(others) * group], refs[len(others) * group :]
+    so_far, (out_ref, mix) = refs[:-2], refs[-2:]
     place = lax.axis_index("place")
-    for other in range(head_total):
+    for number in range(len(others)):
         for at, step in enumerate(sending_order(group)):
-            mix[other, jnp.bitwise_xor(place, step)] = mix_refs[other * group + at][...]
-    result = None
-    for other in range(head_total):
+            mix[number, jnp.bitwise_xor(place, step)] = mix_refs[number * group + at][...]
+    result = so_far[0][...] if so_far else None
+    for number, other in enumerate(others):
         part = jnp.dot(
             turned_ref[other],
-            mix[other].reshape(turned_ref.shape[2], out_ref.shape[1]),
+            mix[number].reshape(turned_ref.shape[2], out_ref.shape[1]),
             preferred_element_type=jnp.float32,
         )
         result = part if result is None else result + part
@@ -295,15 +284,11 @@
     shape = jax.ShapeDtypeStruct
 
     apart = [step for step in range(group) if hops(step) > 1]
-    whole_block, query_block = shape((3 * rows + EXTRA, HD), bf16), shape((rows + EXTRA, HD), bf16)
     packed = pl.pallas_call(
         pack_kernel,
-        out_shape=[
-            shape((2 * rows, HD), bf16) if step in apart else whole_block for step in range(group)
-        ]
-        + [query_block] * len(apart),
+        out_shape=[shape((3 * rows + EXTRA, HD), bf16)] * group,
         in_specs=[HBM] * 5,
-        out_specs=[VMEM] * (group + len(apart)),
+        out_specs=[VMEM] * group,
         scratch_shapes=[
             pltpu.VMEM((rows, width), bf16),
             pltpu.SMEM((rows // TILE, SLOTS, STEPS), jnp.int32),
@@ -350,12 +335,7 @@
     first = ("halo", 1, (0,))
 
     def send_on(steps):
-        blocks = [arrays.get(("block", step), arrays.get(("kv", step))) for step in steps]
-        message = jnp.stack([block[: 2 * rows] for block in blocks])
-        if apart and steps == apart:
-            early = [first]
-            message, got = lax.optimization_barrier((message, [arrays[name] for name in early]))
-            arrays.update(zip(early, got))
+        message = jnp.stack([arrays["block", step][: 2 * rows] for step in steps])
         for offset in offsets:
             pairs = [(source, (source + offset) % groups) for source in range(groups)]
             arrays["halo", offset, tuple(steps)] = lax.ppermute(message, "group", pairs)
@@ -375,10 +355,8 @@
         for name in arrays:
             if name[0] == "halo":
                 used = any((name[1], step) in keys for step in name[2])
-            elif name[0] in ("block", "kv"):
-                used = (0, name[1]) in keys or (name[0] == "block" and name[1] in dests)
-            elif name[0] == "q":
-                used = name[1] in dests
+            elif name[0] == "block":
+                used = (0, name[1]) in keys or name[1] in dests
             else:
                 used = bool(started)
             if used:
@@ -411,37 +389,45 @@
         arrays["block", step] = swapped(packed[step], "place", step)
     send_on([0])
     mix = {}
+    far_blocks = packed[len(near) + 1 :]
     if apart:
-        queries, turned = lax.optimization_barrier((packed[group:], turned))
-        arrays["q", apart[0]] = swapped(queries[0], "place", apart[0])
         tied = lax.optimization_barrier(
-            (packed[apart[0]], turned, [arrays["block", step] for step in near])
-        )
-        far_block, turned, blocks = tied
+            (far_blocks, turned, [arrays["block", step] for step in near])
+        )
+        far_blocks, turned, blocks = tied
         arrays.update((("block", step), block) for step, block in zip(near, blocks))
-        arrays["kv", apart[0]] = swapped(far_block, "place", apart[0])
+    for step, block in zip(apart, far_blocks):
+        arrays["block", step] = swapped(block, "place", step)
     for step in near:
         send_on([step])
     mix.update(stage(0, NEAR))
     if apart:
+        tied = lax.optimization_barrier((arrays["block", apart[0]], arrays["state",]))
+        arrays["block", apart[0]], arrays["state",] = tied
         send_on(apart)
     for at in range(1, len(plan)):
-        done = stage(at, MORE if at == 1 and apart else FAR)
+        done = stage(at, FAR)
         order = [step for step in sending_order(group) if step in done]
         mix.update((step, swapped(done[step], "place", step) if step else done[0]) for step in order)
 
     mixes = [mix[step] for step in sending_order(group)]
-    for other in range(1, head_total):
-        mixes += [swapped(entry, "head", other) for entry in mixes[:group]]
-    return pl.pallas_call(
-        functools.partial(project_kernel, group=group, head_total=head_total),
-        out_shape=shape((features, rows), bf16),
-        in_specs=[VMEM] * (1 + head_total * group),
-        out_specs=VMEM,
-        scratch_shapes=[pltpu.VMEM((head_total, group, HD, rows), bf16)],
-        compiler_params=PARAMS,
-        name="project",
-    )(turned, *mixes)
+    output = []
+    for others, kind in (([0], f32), (list(range(1, head_total)), bf16)):
+        parts = mixes
+        if output:
+            parts = [swapped(entry, "head", other) for other in others for entry in mixes]
+        output = [
+            pl.pallas_call(
+                functools.partial(project_kernel, group=group, others=others),
+                out_shape=shape((features, rows), kind),
+                in_specs=[VMEM] * (1 + len(parts) + len(output)),
+                out_specs=VMEM,
+                scratch_shapes=[pltpu.VMEM((len(others), group, HD, rows), bf16)],
+                compiler_params=PARAMS,
+                name="project",
+            )(turned, *parts, *output)
+        ]
+    return output[0]
 
 
 def solution(mesh):

time: 33.6 us -> 32.7 us (0.973)
  starting transfers between devices: 18.1 us -> 16.2 us
  waiting for transfers between devices: 7.87 us -> 8.92 us
    ppermute x11 -> x10, starting transfers between devices: 10.8 us -> 9.73 us  [swapped(): lax.ppermute(value, axis, [(source, source ^ step) for source in range(co...]
    ppermute x4, starting transfers between devices: 7.26 us -> 6.46 us  [send_on(): arrays['halo', offset, tuple(steps)] = lax.ppermute(message, 'group', pairs)]
    ppermute x4, waiting for transfers between devices: 2.49 us -> 3.18 us  [send_on(): arrays['halo', offset, tuple(steps)] = lax.ppermute(message, 'group', pairs)]
    ppermute x11 -> x10, waiting for transfers between devices: 5.38 us -> 5.75 us  [swapped(): lax.ppermute(value, axis, [(source, source ^ step) for source in range(co...]
    pallas_call x4 -> x3, Pallas kernels: 3.55 us -> 3.34 us  [stage(): pl.pallas_call(functools.partial(attend_kernel, names=names, work=work, s...]
    pallas_call x2 -> x3, Pallas kernels: 2.4 us -> 2.57 us  [the longest x2 1.35 us: on_device(): pl.pallas_call(functools.partial(project_kernel, group=group, others=othe...]
  transfers between devices with their start and end apart: 15 -> 14, of which waited for: 8 -> 10; matrix products, arithmetic and copies ran while one was open for 0% -> 0% of each run, Pallas kernels for 15% -> 16%
where the time goes in v12:
time: 32.7 us; the launch traced here: 32.6 us
  starting transfers between devices  16.2 us (50%)
  waiting for transfers between devices  8.92 us (27%)
  Pallas kernels  7.34 us (22%)
    ppermute x10, starting transfers between devices, swapped(): lax.ppermute(value, axis, [(source, source ^ step) for source in range(co...  9.73 us
    ppermute x4, starting transfers between devices, send_on(): arrays['halo', offset, tuple(steps)] = lax.ppermute(message, 'group', pairs)  6.46 us
    ppermute x10, waiting for transfers between devices, swapped(): lax.ppermute(value, axis, [(source, source ^ step) for source in range(co...  5.75 us
    pallas_call x3, Pallas kernels, stage(): pl.pallas_call(functools.partial(attend_kernel, names=names, work=work, s...  3.34 us
    ppermute x4, waiting for transfers between devices, send_on(): arrays['halo', offset, tuple(steps)] = lax.ppermute(message, 'group', pairs)  3.18 us
    pallas_call x1, Pallas kernels, on_device(): pl.pallas_call(functools.partial(turn_kernel, head_total=head_total), out...  1.44 us
    pallas_call x2, Pallas kernels, on_device(): pl.pallas_call(functools.partial(project_kernel, group=group, others=othe...  1.35 us
    pallas_call x1, Pallas kernels, on_device(): pl.pallas_call(pack_kernel, out_shape=[shape((3 * rows + EXTRA, HD), bf16...  1.21 us
  transfers between devices with their start and end apart: 14, of which 10 were waited for; matrix products, arithmetic and copies ran while one was open for 0% of the time, Pallas kernels for 16%

profile of v12, /device:TPU:0, one launch (start us, length us, event | category | flops | bytes accessed | tf_op | source)
XLA Modules:
  0.0 32.6 jit_solution(13302740782934030062)
XLA Ops:
  0.0 1.2 %pack.1 = (bf16[784,128]{1,0:T(8,128)(2,1)S(1)}, bf16[784,128]{1,0:T(8,128)(2,1)S(1)}, bf16[784,128]{1,0:T(8,128)(2,1)S(1)}, bf16[784,128]{1,0:T(8,128)(2,1)S(1)}) custom-call(bf16[256,512]{1,0:T(8,128)(2,1)} %query_ref.1, bf16[256,512]{1,0:T(8,128)(2,1)} %key_ref.1, bf16[256,512]{1,0:T(8,128)(2,1)} %value_ref.1, s32[2,2,4]{2,1,0:T(2,128)} %bitcast.10, ...), custom_call_target="tpu_custom_call" | custom-call | tf_op jit(solution)/shard_map/pack/pallas_call | solution.py:287
  1.2 3.0 %collective-permute-start = (bf16[784,128]{1,0:T(8,128)(2,1)S(1)}, bf16[784,128]{1,0:T(8,128)(2,1)S(1)}, u32[]{:S(2)}, u32[]{:S(2)}) collective-permute-start(bf16[784,128]{1,0:T(8,128)(2,1)S(1)} %get-tuple-element.25), channel_id=1, source_target_pairs={{0,2},{2,0},{4,6},{6,4},{1,3},{3,1},{5,7},{7,5},{8,10},{10,8},{12,... | collective-permute-start | bytes 602120 | tf_op jit(solution)/shard_map/ppermute | solution.py:273
  4.2 1.5 %collective-permute-start.1 = (bf16[784,128]{1,0:T(8,128)(2,1)S(1)}, bf16[784,128]{1,0:T(8,128)(2,1)S(1)}, u32[]{:S(2)}, u32[]{:S(2)}) collective-permute-start(bf16[784,128]{1,0:T(8,128)(2,1)S(1)} %get-tuple-element.26), channel_id=1, source_target_pairs={{0,4},{2,6},{4,0},{6,2},{1,5},{3,7},{5,1},{7,3},{8,12},{10,14},{12... | collective-permute-start | bytes 602120 | tf_op jit(solution)/shard_map/ppermute | solution.py:273
  5.8 1.6 %collective-permute-start.2 = (bf16[1,512,128]{2,1,0:T(8,128)(2,1)S(1)}, bf16[1,512,128]{2,1,0:T(8,128)(2,1)S(1)}, u32[]{:S(2)}, u32[]{:S(2)}) collective-permute-start(bf16[1,512,128]{2,1,0:T(8,128)(2,1)S(1)} %slice_bitcast_fusion.3), channel_id=1, source_target_pairs={{0,8},{8,16},{16,24},{24,0},{1,9},{9,17},{17,25},{25,1},{2,10},{10... | collective-permute-start | bytes 393224 | tf_op jit(solution)/shard_map/ppermute | solution.py:341
  7.4 1.4 %turn.1.turned_ref = bf16[2,512,512]{2,1,0:T(8,128)(2,1)S(1)} custom-call(bf16[784,128]{1,0:T(8,128)(2,1)S(1)} %get-tuple-element.24.block_ref.refs_0_, bf16[1024,1024]{1,0:T(8,128)(2,1)} %weight_ref.1), custom_call_target="tpu_custom_call" | custom-call | flops 1000000000 | bytes 1 | tf_op jit(solution)/shard_map/turn/pallas_call | solution.py:313
  8.8 0.4 %collective-permute-done.refs_1_ = bf16[784,128]{1,0:T(8,128)(2,1)S(1)} collective-permute-done((bf16[784,128]{1,0:T(8,128)(2,1)S(1)}, bf16[784,128]{1,0:T(8,128)(2,1)S(1)}, u32[]{:S(2)}, u32[]{:S(2)}) %collective-permute-start) | collective-permute-done | bytes 200736 | tf_op jit(solution)/shard_map/ppermute | solution.py:273
  9.2 1.5 %collective-permute-done.1.refs_2_ = bf16[784,128]{1,0:T(8,128)(2,1)S(1)} collective-permute-done((bf16[784,128]{1,0:T(8,128)(2,1)S(1)}, bf16[784,128]{1,0:T(8,128)(2,1)S(1)}, u32[]{:S(2)}, u32[]{:S(2)}) %collective-permute-start.1) | collective-permute-done | bytes 200736 | tf_op jit(solution)/shard_map/ppermute | solution.py:273
  10.7 1.6 %collective-permute-start.3 = (bf16[784,128]{1,0:T(8,128)(2,1)S(1)}, bf16[784,128]{1,0:T(8,128)(2,1)S(1)}, u32[]{:S(2)}, u32[]{:S(2)}) collective-permute-start(bf16[784,128]{1,0:T(8,128)(2,1)S(1)} %get-tuple-element.30), channel_id=1, source_target_pairs={{0,6},{2,4},{4,2},{6,0},{1,7},{3,5},{5,3},{7,1},{8,14},{10,12},{12... | collective-permute-start | bytes 602120 | tf_op jit(solution)/shard_map/ppermute | solution.py:273
  12.3 1.6 %collective-permute-start.5 = (bf16[1,512,128]{2,1,0:T(8,128)(2,1)S(1)}, bf16[1,512,128]{2,1,0:T(8,128)(2,1)S(1)}, u32[]{:S(2)}, u32[]{:S(2)}) collective-permute-start(bf16[1,512,128]{2,1,0:T(8,128)(2,1)S(1)} %slice_bitcast_fusion.1), channel_id=1, source_target_pairs={{0,8},{8,16},{16,24},{24,0},{1,9},{9,17},{17,25},{25,1},{2,10},{10... | collective-permute-start | bytes 393224 | tf_op jit(solution)/shard_map/ppermute | solution.py:341
  13.9 1.6 %collective-permute-start.4 = (bf16[1,512,128]{2,1,0:T(8,128)(2,1)S(1)}, bf16[1,512,128]{2,1,0:T(8,128)(2,1)S(1)}, u32[]{:S(2)}, u32[]{:S(2)}) collective-permute-start(bf16[1,512,128]{2,1,0:T(8,128)(2,1)S(1)} %slice_bitcast_fusion.2), channel_id=1, source_target_pairs={{0,8},{8,16},{16,24},{24,0},{1,9},{9,17},{17,25},{25,1},{2,10},{10... | collective-permute-start | bytes 393224 | tf_op jit(solution)/shard_map/ppermute | solution.py:341
  15.5 0.0 collective-permute-done.2.refs_3_
  15.5 1.2 %attend.3 = (f32[4,128,256]{2,1,0:T(8,128)S(1)}, f32[4,8,256]{2,1,0:T(8,128)S(1)}) custom-call(bf16[784,128]{1,0:T(8,128)(2,1)S(1)} %get-tuple-element.24.block_ref.refs_0_, bf16[784,128]{1,0:T(8,128)(2,1)S(1)} %collective-permute-done.refs_1_, bf16[784,128]{1,0:T(8,128)(2,1)S(1)} %collective-permute-done.1.refs_2_, ...), custom_call_target="tpu_custom_call" | custom-call | flops 1000000000 | bytes 1 | tf_op jit(solution)/shard_map/attend/pallas_call | solution.py:367
  16.7 0.7 %collective-permute-done.3.refs_4_ = bf16[784,128]{1,0:T(8,128)(2,1)S(1)} collective-permute-done((bf16[784,128]{1,0:T(8,128)(2,1)S(1)}, bf16[784,128]{1,0:T(8,128)(2,1)S(1)}, u32[]{:S(2)}, u32[]{:S(2)}) %collective-permute-start.3) | collective-permute-done | bytes 200736 | tf_op jit(solution)/shard_map/ppermute | solution.py:273
  17.4 1.6 %collective-permute-start.6 = (bf16[1,512,128]{2,1,0:T(8,128)(2,1)S(1)}, bf16[1,512,128]{2,1,0:T(8,128)(2,1)S(1)}, u32[]{:S(2)}, u32[]{:S(2)}) collective-permute-start(bf16[1,512,128]{2,1,0:T(8,128)(2,1)S(1)} %slice_bitcast_fusion), channel_id=1, source_target_pairs={{0,8},{8,16},{16,24},{24,0},{1,9},{9,17},{17,25},{25,1},{2,10},{10... | collective-permute-start | bytes 393224 | tf_op jit(solution)/shard_map/ppermute | solution.py:341
  19.0 0.4 %collective-permute-done.5.refs_6_ = bf16[1,512,128]{2,1,0:T(8,128)(2,1)S(1)} collective-permute-done((bf16[1,512,128]{2,1,0:T(8,128)(2,1)S(1)}, bf16[1,512,128]{2,1,0:T(8,128)(2,1)S(1)}, u32[]{:S(2)}, u32[]{:S(2)}) %collective-permute-start.5) | collective-permute-done | bytes 131104 | tf_op jit(solution)/shard_map/ppermute | solution.py:341
  19.4 2.8 %collective-permute-done.4.refs_5_ = bf16[1,512,128]{2,1,0:T(8,128)(2,1)S(1)} collective-permute-done((bf16[1,512,128]{2,1,0:T(8,128)(2,1)S(1)}, bf16[1,512,128]{2,1,0:T(8,128)(2,1)S(1)}, u32[]{:S(2)}, u32[]{:S(2)}) %collective-permute-start.4) | collective-permute-done | bytes 131104 | tf_op jit(solution)/shard_map/ppermute | solution.py:341
  22.2 1.2 %attend.4 = (bf16[128,256]{1,0:T(8,128)(2,1)S(1)}, f32[4,128,256]{2,1,0:T(8,128)S(1)}, f32[4,8,256]{2,1,0:T(8,128)S(1)}) custom-call(bf16[784,128]{1,0:T(8,128)(2,1)S(1)} %get-tuple-element.24.block_ref.refs_0_, bf16[784,128]{1,0:T(8,128)(2,1)S(1)} %collective-permute-done.refs_1_, bf16[784,128]{1,0:T(8,128)(2,1)S(1)} %collective-permute-done.1.refs_2_, ...), custom_call_target="tpu_custom_call" | custom-call | flops 1000000000 | bytes 1 | tf_op jit(solution)/shard_map/attend/pallas_call | solution.py:367
  23.3 1.5 %collective-permute-start.8 = (bf16[128,256]{1,0:T(8,128)(2,1)S(1)}, bf16[128,256]{1,0:T(8,128)(2,1)S(1)}, u32[]{:S(2)}, u32[]{:S(2)}) collective-permute-start(bf16[128,256]{1,0:T(8,128)(2,1)S(1)} %get-tuple-element.38), channel_id=1, source_target_pairs={{0,6},{2,4},{4,2},{6,0},{1,7},{3,5},{5,3},{7,1},{8,14},{10,12},{12... | collective-permute-start | bytes 196616 | tf_op jit(solution)/shard_map/ppermute | solution.py:273
  24.8 0.0 collective-permute-done.6.refs_5_
  24.8 1.0 %attend.5 = (bf16[128,256]{1,0:T(8,128)(2,1)S(1)}, bf16[128,256]{1,0:T(8,128)(2,1)S(1)}, bf16[128,256]{1,0:T(8,128)(2,1)S(1)}) custom-call(bf16[784,128]{1,0:T(8,128)(2,1)S(1)} %get-tuple-element.24.block_ref.refs_0_, bf16[784,128]{1,0:T(8,128)(2,1)S(1)} %collective-permute-done.refs_1_, bf16[784,128]{1,0:T(8,128)(2,1)S(1)} %collective-permute-done.1.refs_2_, ...), custom_call_target="tpu_custom_call" | custom-call | flops 1000000000 | bytes 1 | tf_op jit(solution)/shard_map/attend/pallas_call | solution.py:367
  25.8 0.1 collective-permute-start.10
  25.9 1.2 %collective-permute-start.12 = (bf16[128,256]{1,0:T(8,128)(2,1)S(1)}, bf16[128,256]{1,0:T(8,128)(2,1)S(1)}, u32[]{:S(2)}, u32[]{:S(2)}) collective-permute-start(bf16[128,256]{1,0:T(8,128)(2,1)S(1)} %get-tuple-element.40), channel_id=1, source_target_pairs={{0,4},{2,6},{4,0},{6,2},{1,5},{3,7},{5,1},{7,3},{8,12},{10,14},{12... | collective-permute-start | bytes 196616 | tf_op jit(solution)/shard_map/ppermute | solution.py:273
  27.1 1.5 %collective-permute-done.8.refs_1_ = bf16[128,256]{1,0:T(8,128)(2,1)S(1)} collective-permute-done((bf16[128,256]{1,0:T(8,128)(2,1)S(1)}, bf16[128,256]{1,0:T(8,128)(2,1)S(1)}, u32[]{:S(2)}, u32[]{:S(2)}) %collective-permute-start.8) | collective-permute-done | bytes 65568 | tf_op jit(solution)/shard_map/ppermute | solution.py:273
  28.6 0.0 collective-permute-start.9
  28.6 0.5 %collective-permute-start.7 = (bf16[128,256]{1,0:T(8,128)(2,1)S(1)}, bf16[128,256]{1,0:T(8,128)(2,1)S(1)}, u32[]{:S(2)}, u32[]{:S(2)}) collective-permute-start(bf16[128,256]{1,0:T(8,128)(2,1)S(1)} %get-tuple-element.37.refs_0_), channel_id=1, source_target_pairs={{0,1},{1,0},{2,3},{3,2},{4,5},{5,4},{6,7},{7,6},{8,9},{9,8},{10,11... | collective-permute-start | bytes 196616 | tf_op jit(solution)/shard_map/ppermute | solution.py:273
  29.1 1.1 %collective-permute-done.10.refs_2_ = bf16[128,256]{1,0:T(8,128)(2,1)S(1)} collective-permute-done((bf16[128,256]{1,0:T(8,128)(2,1)S(1)}, bf16[128,256]{1,0:T(8,128)(2,1)S(1)}, u32[]{:S(2)}, u32[]{:S(2)}) %collective-permute-start.10) | collective-permute-done | bytes 65568 | tf_op jit(solution)/shard_map/ppermute | solution.py:273
  30.1 0.0 collective-permute-start.11
  30.1 0.1 collective-permute-done.12.refs_3_
  30.2 0.4 %collective-permute-start.13 = (bf16[128,256]{1,0:T(8,128)(2,1)S(1)}, bf16[128,256]{1,0:T(8,128)(2,1)S(1)}, u32[]{:S(2)}, u32[]{:S(2)}) collective-permute-start(bf16[128,256]{1,0:T(8,128)(2,1)S(1)} %collective-permute-done.12.refs_3_), channel_id=1, source_target_pairs={{0,1},{1,0},{2,3},{3,2},{4,5},{5,4},{6,7},{7,6},{8,9},{9,8},{10,11... | collective-permute-start | bytes 196616 | tf_op jit(solution)/shard_map/ppermute | solution.py:273
  30.7 0.3 project.2.refs_4_
  31.0 0.0 collective-permute-done.9.refs_1_
  31.0 0.0 collective-permute-done.7.refs_0_
  31.0 0.4 %collective-permute-done.11.refs_2_ = bf16[128,256]{1,0:T(8,128)(2,1)S(1)} collective-permute-done((bf16[128,256]{1,0:T(8,128)(2,1)S(1)}, bf16[128,256]{1,0:T(8,128)(2,1)S(1)}, u32[]{:S(2)}, u32[]{:S(2)}) %collective-permute-start.11) | collective-permute-done | bytes 65568 | tf_op jit(solution)/shard_map/ppermute | solution.py:273
  31.4 0.2 collective-permute-done.13.refs_3_
  31.6 1.0 %project.3 = bf16[512,256]{1,0:T(8,128)(2,1)} custom-call(bf16[2,512,512]{2,1,0:T(8,128)(2,1)S(1)} %turn.1.turned_ref, bf16[128,256]{1,0:T(8,128)(2,1)S(1)} %collective-permute-done.7.refs_0_, bf16[128,256]{1,0:T(8,128)(2,1)S(1)} %collective-permute-done.9.refs_1_, bf16[128,256]{1,0:T(8,128)(2,1)S(1)} %collective-permute-done.11.refs_2_, ...), custom_call_target="tpu_custom_call" | custom-call | tf_op jit(solution)/shard_map/project/pallas_call | solution.py:420
  (4 shorter events, 0.0 us)
Async XLA Ops:
  1.2 8.0 %collective-permute-start = (bf16[784,128]{1,0:T(8,128)(2,1)S(1)}, bf16[784,128]{1,0:T(8,128)(2,1)S(1)}, u32[]{:S(2)}, u32[]{:S(2)}) collective-permute-start(bf16[784,128]{1,0:T(8,128)(2,1)S(1)} %get-tuple-element.25), channel_id=1, source_target_pairs={{0,2},{2,0},{4,6},{6,4},{1,3},{3,1},{5,7},{7,5},{8,10},{10,8},{12,... | collective-permute-start | bytes 602120 | tf_op jit(solution)/shard_map/ppermute | solution.py:273
  4.2 6.4 %collective-permute-start.1 = (bf16[784,128]{1,0:T(8,128)(2,1)S(1)}, bf16[784,128]{1,0:T(8,128)(2,1)S(1)}, u32[]{:S(2)}, u32[]{:S(2)}) collective-permute-start(bf16[784,128]{1,0:T(8,128)(2,1)S(1)} %get-tuple-element.26), channel_id=1, source_target_pairs={{0,4},{2,6},{4,0},{6,2},{1,5},{3,7},{5,1},{7,3},{8,12},{10,14},{12... | collective-permute-start | bytes 602120 | tf_op jit(solution)/shard_map/ppermute | solution.py:273
  5.8 9.7 %collective-permute-start.2 = (bf16[1,512,128]{2,1,0:T(8,128)(2,1)S(1)}, bf16[1,512,128]{2,1,0:T(8,128)(2,1)S(1)}, u32[]{:S(2)}, u32[]{:S(2)}) collective-permute-start(bf16[1,512,128]{2,1,0:T(8,128)(2,1)S(1)} %slice_bitcast_fusion.3), channel_id=1, source_target_pairs={{0,8},{8,16},{16,24},{24,0},{1,9},{9,17},{17,25},{25,1},{2,10},{10... | collective-permute-start | bytes 393224 | tf_op jit(solution)/shard_map/ppermute | solution.py:341
  10.7 6.7 %collective-permute-start.3 = (bf16[784,128]{1,0:T(8,128)(2,1)S(1)}, bf16[784,128]{1,0:T(8,128)(2,1)S(1)}, u32[]{:S(2)}, u32[]{:S(2)}) collective-permute-start(bf16[784,128]{1,0:T(8,128)(2,1)S(1)} %get-tuple-element.30), channel_id=1, source_target_pairs={{0,6},{2,4},{4,2},{6,0},{1,7},{3,5},{5,3},{7,1},{8,14},{10,12},{12... | collective-permute-start | bytes 602120 | tf_op jit(solution)/shard_map/ppermute | solution.py:273
  12.3 7.2 %collective-permute-start.5 = (bf16[1,512,128]{2,1,0:T(8,128)(2,1)S(1)}, bf16[1,512,128]{2,1,0:T(8,128)(2,1)S(1)}, u32[]{:S(2)}, u32[]{:S(2)}) collective-permute-start(bf16[1,512,128]{2,1,0:T(8,128)(2,1)S(1)} %slice_bitcast_fusion.1), channel_id=1, source_target_pairs={{0,8},{8,16},{16,24},{24,0},{1,9},{9,17},{17,25},{25,1},{2,10},{10... | collective-permute-start | bytes 393224 | tf_op jit(solution)/shard_map/ppermute | solution.py:341
  13.9 8.3 %collective-permute-start.4 = (bf16[1,512,128]{2,1,0:T(8,128)(2,1)S(1)}, bf16[1,512,128]{2,1,0:T(8,128)(2,1)S(1)}, u32[]{:S(2)}, u32[]{:S(2)}) collective-permute-start(bf16[1,512,128]{2,1,0:T(8,128)(2,1)S(1)} %slice_bitcast_fusion.2), channel_id=1, source_target_pairs={{0,8},{8,16},{16,24},{24,0},{1,9},{9,17},{17,25},{25,1},{2,10},{10... | collective-permute-start | bytes 393224 | tf_op jit(solution)/shard_map/ppermute | solution.py:341
  17.4 7.4 %collective-permute-start.6 = (bf16[1,512,128]{2,1,0:T(8,128)(2,1)S(1)}, bf16[1,512,128]{2,1,0:T(8,128)(2,1)S(1)}, u32[]{:S(2)}, u32[]{:S(2)}) collective-permute-start(bf16[1,512,128]{2,1,0:T(8,128)(2,1)S(1)} %slice_bitcast_fusion), channel_id=1, source_target_pairs={{0,8},{8,16},{16,24},{24,0},{1,9},{9,17},{17,25},{25,1},{2,10},{10... | collective-permute-start | bytes 393224 | tf_op jit(solution)/shard_map/ppermute | solution.py:341
  23.3 5.2 %collective-permute-start.8 = (bf16[128,256]{1,0:T(8,128)(2,1)S(1)}, bf16[128,256]{1,0:T(8,128)(2,1)S(1)}, u32[]{:S(2)}, u32[]{:S(2)}) collective-permute-start(bf16[128,256]{1,0:T(8,128)(2,1)S(1)} %get-tuple-element.38), channel_id=1, source_target_pairs={{0,6},{2,4},{4,2},{6,0},{1,7},{3,5},{5,3},{7,1},{8,14},{10,12},{12... | collective-permute-start | bytes 196616 | tf_op jit(solution)/shard_map/ppermute | solution.py:273
  25.8 4.3 %collective-permute-start.10 = (bf16[128,256]{1,0:T(8,128)(2,1)S(1)}, bf16[128,256]{1,0:T(8,128)(2,1)S(1)}, u32[]{:S(2)}, u32[]{:S(2)}) collective-permute-start(bf16[128,256]{1,0:T(8,128)(2,1)S(1)} %get-tuple-element.39), channel_id=1, source_target_pairs={{0,2},{2,0},{4,6},{6,4},{1,3},{3,1},{5,7},{7,5},{8,10},{10,8},{12,... | collective-permute-start | bytes 196616 | tf_op jit(solution)/shard_map/ppermute | solution.py:273
  25.9 4.3 %collective-permute-start.12 = (bf16[128,256]{1,0:T(8,128)(2,1)S(1)}, bf16[128,256]{1,0:T(8,128)(2,1)S(1)}, u32[]{:S(2)}, u32[]{:S(2)}) collective-permute-start(bf16[128,256]{1,0:T(8,128)(2,1)S(1)} %get-tuple-element.40), channel_id=1, source_target_pairs={{0,4},{2,6},{4,0},{6,2},{1,5},{3,7},{5,1},{7,3},{8,12},{10,14},{12... | collective-permute-start | bytes 196616 | tf_op jit(solution)/shard_map/ppermute | solution.py:273
  28.6 2.4 %collective-permute-start.9 = (bf16[128,256]{1,0:T(8,128)(2,1)S(1)}, bf16[128,256]{1,0:T(8,128)(2,1)S(1)}, u32[]{:S(2)}, u32[]{:S(2)}) collective-permute-start(bf16[128,256]{1,0:T(8,128)(2,1)S(1)} %collective-permute-done.8.refs_1_), channel_id=1, source_target_pairs={{0,1},{1,0},{2,3},{3,2},{4,5},{5,4},{6,7},{7,6},{8,9},{9,8},{10,11... | collective-permute-start | bytes 196616 | tf_op jit(solution)/shard_map/ppermute | solution.py:273
  28.6 2.4 %collective-permute-start.7 = (bf16[128,256]{1,0:T(8,128)(2,1)S(1)}, bf16[128,256]{1,0:T(8,128)(2,1)S(1)}, u32[]{:S(2)}, u32[]{:S(2)}) collective-permute-start(bf16[128,256]{1,0:T(8,128)(2,1)S(1)} %get-tuple-element.37.refs_0_), channel_id=1, source_target_pairs={{0,1},{1,0},{2,3},{3,2},{4,5},{5,4},{6,7},{7,6},{8,9},{9,8},{10,11... | collective-permute-start | bytes 196616 | tf_op jit(solution)/shard_map/ppermute | solution.py:273
  30.1 1.3 %collective-permute-start.11 = (bf16[128,256]{1,0:T(8,128)(2,1)S(1)}, bf16[128,256]{1,0:T(8,128)(2,1)S(1)}, u32[]{:S(2)}, u32[]{:S(2)}) collective-permute-start(bf16[128,256]{1,0:T(8,128)(2,1)S(1)} %collective-permute-done.10.refs_2_), channel_id=1, source_target_pairs={{0,1},{1,0},{2,3},{3,2},{4,5},{5,4},{6,7},{7,6},{8,9},{9,8},{10,11... | collective-permute-start | bytes 196616 | tf_op jit(solution)/shard_map/ppermute | solution.py:273
  30.2 1.3 %collective-permute-start.13 = (bf16[128,256]{1,0:T(8,128)(2,1)S(1)}, bf16[128,256]{1,0:T(8,128)(2,1)S(1)}, u32[]{:S(2)}, u32[]{:S(2)}) collective-permute-start(bf16[128,256]{1,0:T(8,128)(2,1)S(1)} %collective-permute-done.12.refs_3_), channel_id=1, source_target_pairs={{0,1},{1,0},{2,3},{3,2},{4,5},{5,4},{6,7},{7,6},{8,9},{9,8},{10,11... | collective-permute-start | bytes 196616 | tf_op jit(solution)/shard_map/ppermute | solution.py:273

commit v13 on v12

--- a/solution.py
+++ b/solution.py
@@ -16,7 +16,7 @@
 SCALE = LOG2E * HD ** (-0.5)
 MASKED = -1e30
 EXTRA = 16
-OWN = 10**9
+OWN = 1000000000
 NEAR = 1000000000
 FAR = 1000000000
 VMEM = pl.BlockSpec(memory_space=pltpu.VMEM)
@@ -387,23 +387,29 @@
 
     for step in near:
         arrays["block", step] = swapped(packed[step], "place", step)
+    arrays["block", 0], turned = lax.optimization_barrier((packed[0], turned))
     send_on([0])
     mix = {}
     far_blocks = packed[len(near) + 1 :]
+    for step in near[:1]:
+        send_on([step])
     if apart:
+        watch = near
         tied = lax.optimization_barrier(
-            (far_blocks, turned, [arrays["block", step] for step in near])
+            (far_blocks, turned, [arrays["block", step] for step in watch])
         )
         far_blocks, turned, blocks = tied
-        arrays.update((("block", step), block) for step, block in zip(near, blocks))
+        arrays.update((("block", step), block) for step, block in zip(watch, blocks))
+    for step in near[1:]:
+        send_on([step])
     for step, block in zip(apart, far_blocks):
         arrays["block", step] = swapped(block, "place", step)
-    for step in near:
-        send_on([step])
     mix.update(stage(0, NEAR))
     if apart:
-        tied = lax.optimization_barrier((arrays["block", apart[0]], arrays["state",]))
-        arrays["block", apart[0]], arrays["state",] = tied
+        names = [("state",)]
+        tied = lax.optimization_barrier((arrays["block", apart[0]], [arrays[name] for name in names]))
+        arrays["block", apart[0]], got = tied
+        arrays.update(zip(names, got))
         send_on(apart)
     for at in range(1, len(plan)):
         done = stage(at, FAR)

time: 32.7 us -> 33.5 us (1.024)
  starting transfers between devices: 16.2 us -> 17.7 us
  waiting for transfers between devices: 8.92 us -> 8.2 us
    ppermute x10, starting transfers between devices: 9.73 us -> 10.9 us  [swapped(): lax.ppermute(value, axis, [(source, source ^ step) for source in range(co...]
    ppermute x4, waiting for transfers between devices: 3.18 us -> 2.68 us  [send_on(): arrays['halo', offset, tuple(steps)] = lax.ppermute(message, 'group', pairs)]
  transfers between devices with their start and end apart: 14 -> 14, of which waited for: 10 -> 7; matrix products, arithmetic and copies ran while one was open for 0% -> 0% of each run, Pallas kernels for 16% -> 15%
where the time goes in v13:
time: 33.5 us; the launch traced here: 33.4 us
  starting transfers between devices  17.7 us (53%)
  waiting for transfers between devices  8.2 us (24%)
  Pallas kernels  7.36 us (22%)
    ppermute x10, starting transfers between devices, swapped(): lax.ppermute(value, axis, [(source, source ^ step) for source in range(co...  10.9 us
    ppermute x4, starting transfers between devices, send_on(): arrays['halo', offset, tuple(steps)] = lax.ppermute(message, 'group', pairs)  6.76 us
    ppermute x10, waiting for transfers between devices, swapped(): lax.ppermute(value, axis, [(source, source ^ step) for source in range(co...  5.51 us
    pallas_call x3, Pallas kernels, stage(): pl.pallas_call(functools.partial(attend_kernel, names=names, work=work, s...  3.35 us
    ppermute x4, waiting for transfers between devices, send_on(): arrays['halo', offset, tuple(steps)] = lax.ppermute(message, 'group', pairs)  2.68 us
    pallas_call x1, Pallas kernels, on_device(): pl.pallas_call(functools.partial(turn_kernel, head_total=head_total), out...  1.44 us
    pallas_call x2, Pallas kernels, on_device(): pl.pallas_call(functools.partial(project_kernel, group=group, others=othe...  1.35 us
    pallas_call x1, Pallas kernels, on_device(): pl.pallas_call(pack_kernel, out_shape=[shape((3 * rows + EXTRA, HD), bf16...  1.21 us
  transfers between devices with their start and end apart: 14, of which 7 were waited for; matrix products, arithmetic and copies ran while one was open for 0% of the time, Pallas kernels for 15%

profile of v13, /device:TPU:0, one launch (start us, length us, event | category | flops | bytes accessed | tf_op | source)
XLA Modules:
  0.0 33.4 jit_solution(6059240950812307100)
XLA Ops:
  0.0 1.2 %pack.1 = (bf16[784,128]{1,0:T(8,128)(2,1)S(1)}, bf16[784,128]{1,0:T(8,128)(2,1)S(1)}, bf16[784,128]{1,0:T(8,128)(2,1)S(1)}, bf16[784,128]{1,0:T(8,128)(2,1)S(1)}) custom-call(bf16[256,512]{1,0:T(8,128)(2,1)} %query_ref.1, bf16[256,512]{1,0:T(8,128)(2,1)} %key_ref.1, bf16[256,512]{1,0:T(8,128)(2,1)} %value_ref.1, s32[2,2,4]{2,1,0:T(2,128)} %bitcast.10, ...), custom_call_target="tpu_custom_call" | custom-call | tf_op jit(solution)/shard_map/pack/pallas_call | solution.py:287
  1.2 3.0 %collective-permute-start = (bf16[784,128]{1,0:T(8,128)(2,1)S(1)}, bf16[784,128]{1,0:T(8,128)(2,1)S(1)}, u32[]{:S(2)}, u32[]{:S(2)}) collective-permute-start(bf16[784,128]{1,0:T(8,128)(2,1)S(1)} %get-tuple-element.28), channel_id=1, source_target_pairs={{0,2},{2,0},{4,6},{6,4},{1,3},{3,1},{5,7},{7,5},{8,10},{10,8},{12,... | collective-permute-start | bytes 602120 | tf_op jit(solution)/shard_map/ppermute | solution.py:273
  4.2 1.5 %collective-permute-start.1 = (bf16[784,128]{1,0:T(8,128)(2,1)S(1)}, bf16[784,128]{1,0:T(8,128)(2,1)S(1)}, u32[]{:S(2)}, u32[]{:S(2)}) collective-permute-start(bf16[784,128]{1,0:T(8,128)(2,1)S(1)} %get-tuple-element.29), channel_id=1, source_target_pairs={{0,4},{2,6},{4,0},{6,2},{1,5},{3,7},{5,1},{7,3},{8,12},{10,14},{12... | collective-permute-start | bytes 602120 | tf_op jit(solution)/shard_map/ppermute | solution.py:273
  5.7 1.4 %turn.1.turned_ref = bf16[2,512,512]{2,1,0:T(8,128)(2,1)S(1)} custom-call(bf16[784,128]{1,0:T(8,128)(2,1)S(1)} %get-tuple-element.31.block_ref.refs_0_, bf16[1024,1024]{1,0:T(8,128)(2,1)} %weight_ref.1), custom_call_target="tpu_custom_call" | custom-call | flops 1000000000 | bytes 1 | tf_op jit(solution)/shard_map/turn/pallas_call | solution.py:313
  7.2 1.6 %collective-permute-start.2 = (bf16[1,512,128]{2,1,0:T(8,128)(2,1)S(1)}, bf16[1,512,128]{2,1,0:T(8,128)(2,1)S(1)}, u32[]{:S(2)}, u32[]{:S(2)}) collective-permute-start(bf16[1,512,128]{2,1,0:T(8,128)(2,1)S(1)} %slice_bitcast_fusion.3), channel_id=1, source_target_pairs={{0,8},{8,16},{16,24},{24,0},{1,9},{9,17},{17,25},{25,1},{2,10},{10... | collective-permute-start | bytes 393224 | tf_op jit(solution)/shard_map/ppermute | solution.py:341
  8.8 0.4 %collective-permute-done.refs_1_ = bf16[784,128]{1,0:T(8,128)(2,1)S(1)} collective-permute-done((bf16[784,128]{1,0:T(8,128)(2,1)S(1)}, bf16[784,128]{1,0:T(8,128)(2,1)S(1)}, u32[]{:S(2)}, u32[]{:S(2)}) %collective-permute-start) | collective-permute-done | bytes 200736 | tf_op jit(solution)/shard_map/ppermute | solution.py:273
  9.2 1.9 %collective-permute-start.3 = (bf16[1,512,128]{2,1,0:T(8,128)(2,1)S(1)}, bf16[1,512,128]{2,1,0:T(8,128)(2,1)S(1)}, u32[]{:S(2)}, u32[]{:S(2)}) collective-permute-start(bf16[1,512,128]{2,1,0:T(8,128)(2,1)S(1)} %slice_bitcast_fusion), channel_id=1, source_target_pairs={{0,8},{8,16},{16,24},{24,0},{1,9},{9,17},{17,25},{25,1},{2,10},{10... | collective-permute-start | bytes 393224 | tf_op jit(solution)/shard_map/ppermute | solution.py:341
  11.1 0.0 collective-permute-done.1.refs_2_
  11.1 2.4 %collective-permute-start.5 = (bf16[784,128]{1,0:T(8,128)(2,1)S(1)}, bf16[784,128]{1,0:T(8,128)(2,1)S(1)}, u32[]{:S(2)}, u32[]{:S(2)}) collective-permute-start(bf16[784,128]{1,0:T(8,128)(2,1)S(1)} %get-tuple-element.34), channel_id=1, source_target_pairs={{0,6},{2,4},{4,2},{6,0},{1,7},{3,5},{5,3},{7,1},{8,14},{10,12},{12... | collective-permute-start | bytes 602120 | tf_op jit(solution)/shard_map/ppermute | solution.py:273
  13.6 1.6 %collective-permute-start.4 = (bf16[1,512,128]{2,1,0:T(8,128)(2,1)S(1)}, bf16[1,512,128]{2,1,0:T(8,128)(2,1)S(1)}, u32[]{:S(2)}, u32[]{:S(2)}) collective-permute-start(bf16[1,512,128]{2,1,0:T(8,128)(2,1)S(1)} %slice_bitcast_fusion.2), channel_id=1, source_target_pairs={{0,8},{8,16},{16,24},{24,0},{1,9},{9,17},{17,25},{25,1},{2,10},{10... | collective-permute-start | bytes 393224 | tf_op jit(solution)/shard_map/ppermute | solution.py:341
  15.2 0.0 collective-permute-done.2.refs_3_
  15.2 1.2 %attend.3 = (f32[4,128,256]{2,1,0:T(8,128)S(1)}, f32[4,8,256]{2,1,0:T(8,128)S(1)}) custom-call(bf16[784,128]{1,0:T(8,128)(2,1)S(1)} %get-tuple-element.31.block_ref.refs_0_, bf16[784,128]{1,0:T(8,128)(2,1)S(1)} %collective-permute-done.refs_1_, bf16[784,128]{1,0:T(8,128)(2,1)S(1)} %collective-permute-done.1.refs_2_, ...), custom_call_target="tpu_custom_call" | custom-call | flops 1000000000 | bytes 1 | tf_op jit(solution)/shard_map/attend/pallas_call | solution.py:367
  16.4 1.3 %collective-permute-done.5.refs_6_ = bf16[784,128]{1,0:T(8,128)(2,1)S(1)} collective-permute-done((bf16[784,128]{1,0:T(8,128)(2,1)S(1)}, bf16[784,128]{1,0:T(8,128)(2,1)S(1)}, u32[]{:S(2)}, u32[]{:S(2)}) %collective-permute-start.5) | collective-permute-done | bytes 200736 | tf_op jit(solution)/shard_map/ppermute | solution.py:273
  17.7 1.6 %collective-permute-start.6 = (bf16[1,512,128]{2,1,0:T(8,128)(2,1)S(1)}, bf16[1,512,128]{2,1,0:T(8,128)(2,1)S(1)}, u32[]{:S(2)}, u32[]{:S(2)}) collective-permute-start(bf16[1,512,128]{2,1,0:T(8,128)(2,1)S(1)} %slice_bitcast_fusion.1), channel_id=1, source_target_pairs={{0,8},{8,16},{16,24},{24,0},{1,9},{9,17},{17,25},{25,1},{2,10},{10... | collective-permute-start | bytes 393224 | tf_op jit(solution)/shard_map/ppermute | solution.py:341
  19.4 0.0 collective-permute-done.3.refs_4_
  19.4 1.4 %collective-permute-done.4.refs_5_ = bf16[1,512,128]{2,1,0:T(8,128)(2,1)S(1)} collective-permute-done((bf16[1,512,128]{2,1,0:T(8,128)(2,1)S(1)}, bf16[1,512,128]{2,1,0:T(8,128)(2,1)S(1)}, u32[]{:S(2)}, u32[]{:S(2)}) %collective-permute-start.4) | collective-permute-done | bytes 131104 | tf_op jit(solution)/shard_map/ppermute | solution.py:341
  20.8 1.2 %attend.4 = (bf16[128,256]{1,0:T(8,128)(2,1)S(1)}, f32[4,128,256]{2,1,0:T(8,128)S(1)}, f32[4,8,256]{2,1,0:T(8,128)S(1)}) custom-call(bf16[784,128]{1,0:T(8,128)(2,1)S(1)} %get-tuple-element.31.block_ref.refs_0_, bf16[784,128]{1,0:T(8,128)(2,1)S(1)} %collective-permute-done.refs_1_, bf16[784,128]{1,0:T(8,128)(2,1)S(1)} %collective-permute-done.1.refs_2_, ...), custom_call_target="tpu_custom_call" | custom-call | flops 1000000000 | bytes 1 | tf_op jit(solution)/shard_map/attend/pallas_call | solution.py:367
  21.9 1.3 %collective-permute-start.8 = (bf16[128,256]{1,0:T(8,128)(2,1)S(1)}, bf16[128,256]{1,0:T(8,128)(2,1)S(1)}, u32[]{:S(2)}, u32[]{:S(2)}) collective-permute-start(bf16[128,256]{1,0:T(8,128)(2,1)S(1)} %get-tuple-element.42), channel_id=1, source_target_pairs={{0,6},{2,4},{4,2},{6,0},{1,7},{3,5},{5,3},{7,1},{8,14},{10,12},{12... | collective-permute-start | bytes 196616 | tf_op jit(solution)/shard_map/ppermute | solution.py:273
  23.3 1.3 %collective-permute-done.6.refs_5_ = bf16[1,512,128]{2,1,0:T(8,128)(2,1)S(1)} collective-permute-done((bf16[1,512,128]{2,1,0:T(8,128)(2,1)S(1)}, bf16[1,512,128]{2,1,0:T(8,128)(2,1)S(1)}, u32[]{:S(2)}, u32[]{:S(2)}) %collective-permute-start.6) | collective-permute-done | bytes 131104 | tf_op jit(solution)/shard_map/ppermute | solution.py:341
  24.6 1.0 %attend.5 = (bf16[128,256]{1,0:T(8,128)(2,1)S(1)}, bf16[128,256]{1,0:T(8,128)(2,1)S(1)}, bf16[128,256]{1,0:T(8,128)(2,1)S(1)}) custom-call(bf16[784,128]{1,0:T(8,128)(2,1)S(1)} %get-tuple-element.31.block_ref.refs_0_, bf16[784,128]{1,0:T(8,128)(2,1)S(1)} %collective-permute-done.refs_1_, bf16[784,128]{1,0:T(8,128)(2,1)S(1)} %collective-permute-done.1.refs_2_, ...), custom_call_target="tpu_custom_call" | custom-call | flops 1000000000 | bytes 1 | tf_op jit(solution)/shard_map/attend/pallas_call | solution.py:367
  25.6 1.3 %collective-permute-start.10 = (bf16[128,256]{1,0:T(8,128)(2,1)S(1)}, bf16[128,256]{1,0:T(8,128)(2,1)S(1)}, u32[]{:S(2)}, u32[]{:S(2)}) collective-permute-start(bf16[128,256]{1,0:T(8,128)(2,1)S(1)} %get-tuple-element.43), channel_id=1, source_target_pairs={{0,2},{2,0},{4,6},{6,4},{1,3},{3,1},{5,7},{7,5},{8,10},{10,8},{12,... | collective-permute-start | bytes 196616 | tf_op jit(solution)/shard_map/ppermute | solution.py:273
  26.8 0.8 %collective-permute-start.12 = (bf16[128,256]{1,0:T(8,128)(2,1)S(1)}, bf16[128,256]{1,0:T(8,128)(2,1)S(1)}, u32[]{:S(2)}, u32[]{:S(2)}) collective-permute-start(bf16[128,256]{1,0:T(8,128)(2,1)S(1)} %get-tuple-element.44), channel_id=1, source_target_pairs={{0,4},{2,6},{4,0},{6,2},{1,5},{3,7},{5,1},{7,3},{8,12},{10,14},{12... | collective-permute-start | bytes 196616 | tf_op jit(solution)/shard_map/ppermute | solution.py:273
  27.7 0.0 collective-permute-done.8.refs_1_
  27.7 0.0 collective-permute-start.9
  27.7 0.5 %collective-permute-start.7 = (bf16[128,256]{1,0:T(8,128)(2,1)S(1)}, bf16[128,256]{1,0:T(8,128)(2,1)S(1)}, u32[]{:S(2)}, u32[]{:S(2)}) collective-permute-start(bf16[128,256]{1,0:T(8,128)(2,1)S(1)} %get-tuple-element.41.refs_0_), channel_id=1, source_target_pairs={{0,1},{1,0},{2,3},{3,2},{4,5},{5,4},{6,7},{7,6},{8,9},{9,8},{10,11... | collective-permute-start | bytes 196616 | tf_op jit(solution)/shard_map/ppermute | solution.py:273
  28.2 1.7 %collective-permute-done.10.refs_2_ = bf16[128,256]{1,0:T(8,128)(2,1)S(1)} collective-permute-done((bf16[128,256]{1,0:T(8,128)(2,1)S(1)}, bf16[128,256]{1,0:T(8,128)(2,1)S(1)}, u32[]{:S(2)}, u32[]{:S(2)}) %collective-permute-start.10) | collective-permute-done | bytes 65568 | tf_op jit(solution)/shard_map/ppermute | solution.py:273
  29.9 0.0 collective-permute-start.11
  29.9 1.2 %collective-permute-done.12.refs_3_ = bf16[128,256]{1,0:T(8,128)(2,1)S(1)} collective-permute-done((bf16[128,256]{1,0:T(8,128)(2,1)S(1)}, bf16[128,256]{1,0:T(8,128)(2,1)S(1)}, u32[]{:S(2)}, u32[]{:S(2)}) %collective-permute-start.12) | collective-permute-done | bytes 65568 | tf_op jit(solution)/shard_map/ppermute | solution.py:273
  31.1 0.0 collective-permute-start.13
  31.1 0.3 project.2.refs_4_
  31.4 0.0 collective-permute-done.9.refs_1_
  31.4 0.0 collective-permute-done.7.refs_0_
  31.5 0.0 collective-permute-done.11.refs_2_
  31.5 0.9 %collective-permute-done.13.refs_3_ = bf16[128,256]{1,0:T(8,128)(2,1)S(1)} collective-permute-done((bf16[128,256]{1,0:T(8,128)(2,1)S(1)}, bf16[128,256]{1,0:T(8,128)(2,1)S(1)}, u32[]{:S(2)}, u32[]{:S(2)}) %collective-permute-start.13) | collective-permute-done | bytes 65568 | tf_op jit(solution)/shard_map/ppermute | solution.py:273
  32.4 1.0 %project.3 = bf16[512,256]{1,0:T(8,128)(2,1)} custom-call(bf16[2,512,512]{2,1,0:T(8,128)(2,1)S(1)} %turn.1.turned_ref, bf16[128,256]{1,0:T(8,128)(2,1)S(1)} %collective-permute-done.7.refs_0_, bf16[128,256]{1,0:T(8,128)(2,1)S(1)} %collective-permute-done.9.refs_1_, bf16[128,256]{1,0:T(8,128)(2,1)S(1)} %collective-permute-done.11.refs_2_, ...), custom_call_target="tpu_custom_call" | custom-call | tf_op jit(solution)/shard_map/project/pallas_call | solution.py:426
  (4 shorter events, 0.0 us)
Async XLA Ops:
  1.2 8.0 %collective-permute-start = (bf16[784,128]{1,0:T(8,128)(2,1)S(1)}, bf16[784,128]{1,0:T(8,128)(2,1)S(1)}, u32[]{:S(2)}, u32[]{:S(2)}) collective-permute-start(bf16[784,128]{1,0:T(8,128)(2,1)S(1)} %get-tuple-element.28), channel_id=1, source_target_pairs={{0,2},{2,0},{4,6},{6,4},{1,3},{3,1},{5,7},{7,5},{8,10},{10,8},{12,... | collective-permute-start | bytes 602120 | tf_op jit(solution)/shard_map/ppermute | solution.py:273
  4.2 6.9 %collective-permute-start.1 = (bf16[784,128]{1,0:T(8,128)(2,1)S(1)}, bf16[784,128]{1,0:T(8,128)(2,1)S(1)}, u32[]{:S(2)}, u32[]{:S(2)}) collective-permute-start(bf16[784,128]{1,0:T(8,128)(2,1)S(1)} %get-tuple-element.29), channel_id=1, source_target_pairs={{0,4},{2,6},{4,0},{6,2},{1,5},{3,7},{5,1},{7,3},{8,12},{10,14},{12... | collective-permute-start | bytes 602120 | tf_op jit(solution)/shard_map/ppermute | solution.py:273
  7.2 8.0 %collective-permute-start.2 = (bf16[1,512,128]{2,1,0:T(8,128)(2,1)S(1)}, bf16[1,512,128]{2,1,0:T(8,128)(2,1)S(1)}, u32[]{:S(2)}, u32[]{:S(2)}) collective-permute-start(bf16[1,512,128]{2,1,0:T(8,128)(2,1)S(1)} %slice_bitcast_fusion.3), channel_id=1, source_target_pairs={{0,8},{8,16},{16,24},{24,0},{1,9},{9,17},{17,25},{25,1},{2,10},{10... | collective-permute-start | bytes 393224 | tf_op jit(solution)/shard_map/ppermute | solution.py:341
  9.2 10.1 %collective-permute-start.3 = (bf16[1,512,128]{2,1,0:T(8,128)(2,1)S(1)}, bf16[1,512,128]{2,1,0:T(8,128)(2,1)S(1)}, u32[]{:S(2)}, u32[]{:S(2)}) collective-permute-start(bf16[1,512,128]{2,1,0:T(8,128)(2,1)S(1)} %slice_bitcast_fusion), channel_id=1, source_target_pairs={{0,8},{8,16},{16,24},{24,0},{1,9},{9,17},{17,25},{25,1},{2,10},{10... | collective-permute-start | bytes 393224 | tf_op jit(solution)/shard_map/ppermute | solution.py:341
  11.1 6.6 %collective-permute-start.5 = (bf16[784,128]{1,0:T(8,128)(2,1)S(1)}, bf16[784,128]{1,0:T(8,128)(2,1)S(1)}, u32[]{:S(2)}, u32[]{:S(2)}) collective-permute-start(bf16[784,128]{1,0:T(8,128)(2,1)S(1)} %get-tuple-element.34), channel_id=1, source_target_pairs={{0,6},{2,4},{4,2},{6,0},{1,7},{3,5},{5,3},{7,1},{8,14},{10,12},{12... | collective-permute-start | bytes 602120 | tf_op jit(solution)/shard_map/ppermute | solution.py:273
  13.6 7.2 %collective-permute-start.4 = (bf16[1,512,128]{2,1,0:T(8,128)(2,1)S(1)}, bf16[1,512,128]{2,1,0:T(8,128)(2,1)S(1)}, u32[]{:S(2)}, u32[]{:S(2)}) collective-permute-start(bf16[1,512,128]{2,1,0:T(8,128)(2,1)S(1)} %slice_bitcast_fusion.2), channel_id=1, source_target_pairs={{0,8},{8,16},{16,24},{24,0},{1,9},{9,17},{17,25},{25,1},{2,10},{10... | collective-permute-start | bytes 393224 | tf_op jit(solution)/shard_map/ppermute | solution.py:341
  17.7 6.8 %collective-permute-start.6 = (bf16[1,512,128]{2,1,0:T(8,128)(2,1)S(1)}, bf16[1,512,128]{2,1,0:T(8,128)(2,1)S(1)}, u32[]{:S(2)}, u32[]{:S(2)}) collective-permute-start(bf16[1,512,128]{2,1,0:T(8,128)(2,1)S(1)} %slice_bitcast_fusion.1), channel_id=1, source_target_pairs={{0,8},{8,16},{16,24},{24,0},{1,9},{9,17},{17,25},{25,1},{2,10},{10... | collective-permute-start | bytes 393224 | tf_op jit(solution)/shard_map/ppermute | solution.py:341
  21.9 5.7 %collective-permute-start.8 = (bf16[128,256]{1,0:T(8,128)(2,1)S(1)}, bf16[128,256]{1,0:T(8,128)(2,1)S(1)}, u32[]{:S(2)}, u32[]{:S(2)}) collective-permute-start(bf16[128,256]{1,0:T(8,128)(2,1)S(1)} %get-tuple-element.42), channel_id=1, source_target_pairs={{0,6},{2,4},{4,2},{6,0},{1,7},{3,5},{5,3},{7,1},{8,14},{10,12},{12... | collective-permute-start | bytes 196616 | tf_op jit(solution)/shard_map/ppermute | solution.py:273
  25.6 4.3 %collective-permute-start.10 = (bf16[128,256]{1,0:T(8,128)(2,1)S(1)}, bf16[128,256]{1,0:T(8,128)(2,1)S(1)}, u32[]{:S(2)}, u32[]{:S(2)}) collective-permute-start(bf16[128,256]{1,0:T(8,128)(2,1)S(1)} %get-tuple-element.43), channel_id=1, source_target_pairs={{0,2},{2,0},{4,6},{6,4},{1,3},{3,1},{5,7},{7,5},{8,10},{10,8},{12,... | collective-permute-start | bytes 196616 | tf_op jit(solution)/shard_map/ppermute | solution.py:273
  26.8 4.3 %collective-permute-start.12 = (bf16[128,256]{1,0:T(8,128)(2,1)S(1)}, bf16[128,256]{1,0:T(8,128)(2,1)S(1)}, u32[]{:S(2)}, u32[]{:S(2)}) collective-permute-start(bf16[128,256]{1,0:T(8,128)(2,1)S(1)} %get-tuple-element.44), channel_id=1, source_target_pairs={{0,4},{2,6},{4,0},{6,2},{1,5},{3,7},{5,1},{7,3},{8,12},{10,14},{12... | collective-permute-start | bytes 196616 | tf_op jit(solution)/shard_map/ppermute | solution.py:273
  27.7 3.8 %collective-permute-start.9 = (bf16[128,256]{1,0:T(8,128)(2,1)S(1)}, bf16[128,256]{1,0:T(8,128)(2,1)S(1)}, u32[]{:S(2)}, u32[]{:S(2)}) collective-permute-start(bf16[128,256]{1,0:T(8,128)(2,1)S(1)} %collective-permute-done.8.refs_1_), channel_id=1, source_target_pairs={{0,1},{1,0},{2,3},{3,2},{4,5},{5,4},{6,7},{7,6},{8,9},{9,8},{10,11... | collective-permute-start | bytes 196616 | tf_op jit(solution)/shard_map/ppermute | solution.py:273
  27.7 3.8 %collective-permute-start.7 = (bf16[128,256]{1,0:T(8,128)(2,1)S(1)}, bf16[128,256]{1,0:T(8,128)(2,1)S(1)}, u32[]{:S(2)}, u32[]{:S(2)}) collective-permute-start(bf16[128,256]{1,0:T(8,128)(2,1)S(1)} %get-tuple-element.41.refs_0_), channel_id=1, source_target_pairs={{0,1},{1,0},{2,3},{3,2},{4,5},{5,4},{6,7},{7,6},{8,9},{9,8},{10,11... | collective-permute-start | bytes 196616 | tf_op jit(solution)/shard_map/ppermute | solution.py:273
  29.9 1.6 %collective-permute-start.11 = (bf16[128,256]{1,0:T(8,128)(2,1)S(1)}, bf16[128,256]{1,0:T(8,128)(2,1)S(1)}, u32[]{:S(2)}, u32[]{:S(2)}) collective-permute-start(bf16[128,256]{1,0:T(8,128)(2,1)S(1)} %collective-permute-done.10.refs_2_), channel_id=1, source_target_pairs={{0,1},{1,0},{2,3},{3,2},{4,5},{5,4},{6,7},{7,6},{8,9},{9,8},{10,11... | collective-permute-start | bytes 196616 | tf_op jit(solution)/shard_map/ppermute | solution.py:273
  31.1 1.3 %collective-permute-start.13 = (bf16[128,256]{1,0:T(8,128)(2,1)S(1)}, bf16[128,256]{1,0:T(8,128)(2,1)S(1)}, u32[]{:S(2)}, u32[]{:S(2)}) collective-permute-start(bf16[128,256]{1,0:T(8,128)(2,1)S(1)} %collective-permute-done.12.refs_3_), channel_id=1, source_target_pairs={{0,1},{1,0},{2,3},{3,2},{4,5},{5,4},{6,7},{7,6},{8,9},{9,8},{10,11... | collective-permute-start | bytes 196616 | tf_op jit(solution)/shard_map/ppermute | solution.py:273

commit v14 on v13

--- a/solution.py
+++ b/solution.py
@@ -170,9 +170,7 @@
     steps = list(range(group))
     near = [step for step in steps if hops(step) < 2]
     stages = [(near, lambda offset, step: hops(step) < 2 and (offset == 0 or step == 0))]
-    stages.append((steps, lambda offset, step: offset == 0 or hops(step) < 2))
-    if len(near) < group:
-        stages.append((steps, lambda offset, step: True))
+    stages.append((steps, lambda offset, step: True))
     plan, taken = [], set()
     for dests, there in stages:
         work = []
@@ -340,6 +338,18 @@
             pairs = [(source, (source + offset) % groups) for source in range(groups)]
             arrays["halo", offset, tuple(steps)] = lax.ppermute(message, "group", pairs)
 
+    def send_across(step):
+        for offset in offsets:
+            pairs = [
+                (at * group + p, (at + offset) % groups * group + (p ^ step))
+                for at in range(groups)
+                for p in range(group)
+            ]
+            message = packed[step][None, : 2 * rows]
+            message, arrays["block", 0] = lax.optimization_barrier((message, arrays["block", 0]))
+            arrived = lax.ppermute(message, ("group", "place"), pairs)
+            arrays["halo", offset, (step,)] = arrived
+
     def stage(at, cost):
         work = plan[at]
         started = [
@@ -348,7 +358,7 @@
             if finish[step] >= at and any(step in table for work in plan[:at] for table in work)
         ]
         active = sorted(set(started) | {step for table in work for step in table})
-        ready = [step for step in active if finish[step] == at]
+        ready = [step for step in sending_order(group) if step in active and finish[step] == at]
         keys = {key for table in work for todo in table.values() for key, _ in todo}
         dests = {step for table in work for step in table}
         names = []
@@ -391,26 +401,25 @@
     send_on([0])
     mix = {}
     far_blocks = packed[len(near) + 1 :]
+    for step in apart:
+        send_across(step)
     for step in near[:1]:
         send_on([step])
     if apart:
-        watch = near
         tied = lax.optimization_barrier(
-            (far_blocks, turned, [arrays["block", step] for step in watch])
+            (far_blocks, turned, [arrays["block", step] for step in near])
         )
         far_blocks, turned, blocks = tied
-        arrays.update((("block", step), block) for step, block in zip(watch, blocks))
+        arrays.update((("block", step), block) for step, block in zip(near, blocks))
     for step in near[1:]:
         send_on([step])
     for step, block in zip(apart, far_blocks):
         arrays["block", step] = swapped(block, "place", step)
+    if apart:
+        far_halo = ("halo", 1, tuple(apart))
+        tied = lax.optimization_barrier((arrays["block", 0], arrays[far_halo]))
+        arrays["block", 0], arrays[far_halo] = tied
     mix.update(stage(0, NEAR))
-    if apart:
-        names = [("state",)]
-        tied = lax.optimization_barrier((arrays["block", apart[0]], [arrays[name] for name in names]))
-        arrays["block", apart[0]], got = tied
-        arrays.update(zip(names, got))
-        send_on(apart)
     for at in range(1, len(plan)):
         done = stage(at, FAR)
         order = [step for step in sending_order(group) if step in done]

time: 33.5 us -> 32.7 us (0.976)
  starting transfers between devices: 17.7 us -> 16.5 us
  waiting for transfers between devices: 8.2 us -> 9.1 us
  Pallas kernels: 7.36 us -> 6.78 us
    ppermute x0 -> x1, waiting for transfers between devices: none -> 3.79 us  [send_across(): arrived = lax.ppermute(message, ('group', 'place'), pairs)]
    ppermute x4 -> x3, starting transfers between devices: 6.76 us -> 3.95 us  [send_on(): arrays['halo', offset, tuple(steps)] = lax.ppermute(message, 'group', pairs)]
    ppermute x10, waiting for transfers between devices: 5.51 us -> 3.27 us  [swapped(): lax.ppermute(value, axis, [(source, source ^ step) for source in range(co...]
    ppermute x0 -> x1, starting transfers between devices: none -> 1.54 us  [send_across(): arrived = lax.ppermute(message, ('group', 'place'), pairs)]
    ppermute x4 -> x3, waiting for transfers between devices: 2.68 us -> 2.04 us  [send_on(): arrays['halo', offset, tuple(steps)] = lax.ppermute(message, 'group', pairs)]
    pallas_call x3 -> x2, Pallas kernels: 3.35 us -> 2.78 us  [stage(): pl.pallas_call(functools.partial(attend_kernel, names=names, work=work, s...]
  transfers between devices with their start and end apart: 14 -> 14, of which waited for: 7 -> 6; matrix products, arithmetic and copies ran while one was open for 0% -> 0% of each run, Pallas kernels for 15% -> 9%
where the time goes in v14:
time: 32.7 us; the launch traced here: 32.5 us
  starting transfers between devices  16.5 us (50%)
  waiting for transfers between devices  9.1 us (28%)
  Pallas kernels  6.78 us (21%)
    ppermute x10, starting transfers between devices, swapped(): lax.ppermute(value, axis, [(source, source ^ step) for source in range(co...  11 us
    ppermute x3, starting transfers between devices, send_on(): arrays['halo', offset, tuple(steps)] = lax.ppermute(message, 'group', pairs)  3.95 us
    ppermute x1, waiting for transfers between devices, send_across(): arrived = lax.ppermute(message, ('group', 'place'), pairs)  3.79 us
    ppermute x10, waiting for transfers between devices, swapped(): lax.ppermute(value, axis, [(source, source ^ step) for source in range(co...  3.27 us
    pallas_call x2, Pallas kernels, stage(): pl.pallas_call(functools.partial(attend_kernel, names=names, work=work, s...  2.78 us
    ppermute x3, waiting for transfers between devices, send_on(): arrays['halo', offset, tuple(steps)] = lax.ppermute(message, 'group', pairs)  2.04 us
    ppermute x1, starting transfers between devices, send_across(): arrived = lax.ppermute(message, ('group', 'place'), pairs)  1.54 us
    pallas_call x1, Pallas kernels, on_device(): pl.pallas_call(functools.partial(turn_kernel, head_total=head_total), out...  1.44 us
  transfers between devices with their start and end apart: 14, of which 6 were waited for; matrix products, arithmetic and copies ran while one was open for 0% of the time, Pallas kernels for 9%

profile of v14, /device:TPU:0, one launch (start us, length us, event | category | flops | bytes accessed | tf_op | source)
XLA Modules:
  0.0 32.5 jit_solution(16509243415070402021)
XLA Ops:
  0.0 1.2 %pack.1 = (bf16[784,128]{1,0:T(8,128)(2,1)S(1)}, bf16[784,128]{1,0:T(8,128)(2,1)S(1)}, bf16[784,128]{1,0:T(8,128)(2,1)S(1)}, bf16[784,128]{1,0:T(8,128)(2,1)S(1)}) custom-call(bf16[256,512]{1,0:T(8,128)(2,1)} %query_ref.1, bf16[256,512]{1,0:T(8,128)(2,1)} %key_ref.1, bf16[256,512]{1,0:T(8,128)(2,1)} %value_ref.1, s32[2,2,4]{2,1,0:T(2,128)} %bitcast.10, ...), custom_call_target="tpu_custom_call" | custom-call | tf_op jit(solution)/shard_map/pack/pallas_call | solution.py:285
  1.2 3.0 %collective-permute-start = (bf16[784,128]{1,0:T(8,128)(2,1)S(1)}, bf16[784,128]{1,0:T(8,128)(2,1)S(1)}, u32[]{:S(2)}, u32[]{:S(2)}) collective-permute-start(bf16[784,128]{1,0:T(8,128)(2,1)S(1)} %get-tuple-element.28), channel_id=1, source_target_pairs={{0,2},{2,0},{4,6},{6,4},{1,3},{3,1},{5,7},{7,5},{8,10},{10,8},{12,... | collective-permute-start | bytes 602120 | tf_op jit(solution)/shard_map/ppermute | solution.py:271
  4.2 1.5 %collective-permute-start.1 = (bf16[784,128]{1,0:T(8,128)(2,1)S(1)}, bf16[784,128]{1,0:T(8,128)(2,1)S(1)}, u32[]{:S(2)}, u32[]{:S(2)}) collective-permute-start(bf16[784,128]{1,0:T(8,128)(2,1)S(1)} %get-tuple-element.29), channel_id=1, source_target_pairs={{0,4},{2,6},{4,0},{6,2},{1,5},{3,7},{5,1},{7,3},{8,12},{10,14},{12... | collective-permute-start | bytes 602120 | tf_op jit(solution)/shard_map/ppermute | solution.py:271
  5.7 1.4 %turn.1.turned_ref = bf16[2,512,512]{2,1,0:T(8,128)(2,1)S(1)} custom-call(bf16[784,128]{1,0:T(8,128)(2,1)S(1)} %get-tuple-element.34.block_ref.refs_0_, bf16[1024,1024]{1,0:T(8,128)(2,1)} %weight_ref.1), custom_call_target="tpu_custom_call" | custom-call | flops 1000000000 | bytes 1 | tf_op jit(solution)/shard_map/turn/pallas_call | solution.py:311
  7.2 1.6 %collective-permute-start.3 = (bf16[1,512,128]{2,1,0:T(8,128)(2,1)S(1)}, bf16[1,512,128]{2,1,0:T(8,128)(2,1)S(1)}, u32[]{:S(2)}, u32[]{:S(2)}) collective-permute-start(bf16[1,512,128]{2,1,0:T(8,128)(2,1)S(1)} %slice_bitcast_fusion.2), channel_id=1, source_target_pairs={{0,8},{8,16},{16,24},{24,0},{1,9},{9,17},{17,25},{25,1},{2,10},{10... | collective-permute-start | bytes 393224 | tf_op jit(solution)/shard_map/ppermute | solution.py:339
  8.9 1.5 %collective-permute-start.2 = (bf16[1,512,128]{2,1,0:T(8,128)(2,1)S(1)}, bf16[1,512,128]{2,1,0:T(8,128)(2,1)S(1)}, u32[]{:S(2)}, u32[]{:S(2)}) collective-permute-start(bf16[1,512,128]{2,1,0:T(8,128)(2,1)S(1)} %slice_bitcast_fusion.3), channel_id=1, source_target_pairs={{0,14},{2,12},{4,10},{6,8},{8,22},{10,20},{12,18},{14,16},{16,30},... | collective-permute-start | bytes 393224 | tf_op jit(solution)/shard_map/ppermute | solution.py:350
  10.4 0.0 collective-permute-done.refs_1_
  10.4 1.6 %collective-permute-start.4 = (bf16[1,512,128]{2,1,0:T(8,128)(2,1)S(1)}, bf16[1,512,128]{2,1,0:T(8,128)(2,1)S(1)}, u32[]{:S(2)}, u32[]{:S(2)}) collective-permute-start(bf16[1,512,128]{2,1,0:T(8,128)(2,1)S(1)} %slice_bitcast_fusion), channel_id=1, source_target_pairs={{0,8},{8,16},{16,24},{24,0},{1,9},{9,17},{17,25},{25,1},{2,10},{10... | collective-permute-start | bytes 393224 | tf_op jit(solution)/shard_map/ppermute | solution.py:339
  12.0 0.0 collective-permute-done.1.refs_2_
  12.0 2.4 %collective-permute-start.6 = (bf16[784,128]{1,0:T(8,128)(2,1)S(1)}, bf16[784,128]{1,0:T(8,128)(2,1)S(1)}, u32[]{:S(2)}, u32[]{:S(2)}) collective-permute-start(bf16[784,128]{1,0:T(8,128)(2,1)S(1)} %get-tuple-element.38), channel_id=1, source_target_pairs={{0,6},{2,4},{4,2},{6,0},{1,7},{3,5},{5,3},{7,1},{8,14},{10,12},{12... | collective-permute-start | bytes 602120 | tf_op jit(solution)/shard_map/ppermute | solution.py:271
  14.5 0.7 %collective-permute-start.5 = (bf16[1,512,128]{2,1,0:T(8,128)(2,1)S(1)}, bf16[1,512,128]{2,1,0:T(8,128)(2,1)S(1)}, u32[]{:S(2)}, u32[]{:S(2)}) collective-permute-start(bf16[1,512,128]{2,1,0:T(8,128)(2,1)S(1)} %slice_bitcast_fusion.1), channel_id=1, source_target_pairs={{0,8},{8,16},{16,24},{24,0},{1,9},{9,17},{17,25},{25,1},{2,10},{10... | collective-permute-start | bytes 393224 | tf_op jit(solution)/shard_map/ppermute | solution.py:339
  15.2 3.8 %collective-permute-done.2.refs_4_ = bf16[1,512,128]{2,1,0:T(8,128)(2,1)S(1)} collective-permute-done((bf16[1,512,128]{2,1,0:T(8,128)(2,1)S(1)}, bf16[1,512,128]{2,1,0:T(8,128)(2,1)S(1)}, u32[]{:S(2)}, u32[]{:S(2)}) %collective-permute-start.2) | collective-permute-done | bytes 131104 | tf_op jit(solution)/shard_map/ppermute | solution.py:350
  19.0 0.0 collective-permute-done.3.refs_3_
  19.0 1.2 %attend.2 = (f32[4,128,256]{2,1,0:T(8,128)S(1)}, f32[4,8,256]{2,1,0:T(8,128)S(1)}) custom-call(bf16[784,128]{1,0:T(8,128)(2,1)S(1)} %get-tuple-element.34.block_ref.refs_0_, bf16[784,128]{1,0:T(8,128)(2,1)S(1)} %collective-permute-done.refs_1_, bf16[784,128]{1,0:T(8,128)(2,1)S(1)} %collective-permute-done.1.refs_2_, ...), custom_call_target="tpu_custom_call" | custom-call | flops 1000000000 | bytes 1 | tf_op jit(solution)/shard_map/attend/pallas_call | solution.py:377
  20.2 0.6 %collective-permute-done.4.refs_5_ = bf16[1,512,128]{2,1,0:T(8,128)(2,1)S(1)} collective-permute-done((bf16[1,512,128]{2,1,0:T(8,128)(2,1)S(1)}, bf16[1,512,128]{2,1,0:T(8,128)(2,1)S(1)}, u32[]{:S(2)}, u32[]{:S(2)}) %collective-permute-start.4) | collective-permute-done | bytes 131104 | tf_op jit(solution)/shard_map/ppermute | solution.py:339
  20.8 1.4 %collective-permute-done.5.refs_6_ = bf16[1,512,128]{2,1,0:T(8,128)(2,1)S(1)} collective-permute-done((bf16[1,512,128]{2,1,0:T(8,128)(2,1)S(1)}, bf16[1,512,128]{2,1,0:T(8,128)(2,1)S(1)}, u32[]{:S(2)}, u32[]{:S(2)}) %collective-permute-start.5) | collective-permute-done | bytes 131104 | tf_op jit(solution)/shard_map/ppermute | solution.py:339
  22.2 0.0 collective-permute-done.6.refs_7_
  22.2 1.6 %attend.3 = (bf16[128,256]{1,0:T(8,128)(2,1)S(1)}, bf16[128,256]{1,0:T(8,128)(2,1)S(1)}, bf16[128,256]{1,0:T(8,128)(2,1)S(1)}, bf16[128,256]{1,0:T(8,128)(2,1)S(1)}) custom-call(bf16[784,128]{1,0:T(8,128)(2,1)S(1)} %get-tuple-element.34.block_ref.refs_0_, bf16[784,128]{1,0:T(8,128)(2,1)S(1)} %collective-permute-done.refs_1_, ...), custom_call_target="tpu_custom_call" | custom-call | flops 1000000000 | bytes 1 | tf_op jit(solution)/shard_map/attend/pallas_call | solution.py:377
  23.8 0.7 %collective-permute-start.8 = (bf16[128,256]{1,0:T(8,128)(2,1)S(1)}, bf16[128,256]{1,0:T(8,128)(2,1)S(1)}, u32[]{:S(2)}, u32[]{:S(2)}) collective-permute-start(bf16[128,256]{1,0:T(8,128)(2,1)S(1)} %get-tuple-element.42), channel_id=1, source_target_pairs={{0,6},{2,4},{4,2},{6,0},{1,7},{3,5},{5,3},{7,1},{8,14},{10,12},{12... | collective-permute-start | bytes 196616 | tf_op jit(solution)/shard_map/ppermute | solution.py:271
  24.6 1.4 %collective-permute-start.10 = (bf16[128,256]{1,0:T(8,128)(2,1)S(1)}, bf16[128,256]{1,0:T(8,128)(2,1)S(1)}, u32[]{:S(2)}, u32[]{:S(2)}) collective-permute-start(bf16[128,256]{1,0:T(8,128)(2,1)S(1)} %get-tuple-element.43), channel_id=1, source_target_pairs={{0,2},{2,0},{4,6},{6,4},{1,3},{3,1},{5,7},{7,5},{8,10},{10,8},{12,... | collective-permute-start | bytes 196616 | tf_op jit(solution)/shard_map/ppermute | solution.py:271
  26.0 1.4 %collective-permute-start.12 = (bf16[128,256]{1,0:T(8,128)(2,1)S(1)}, bf16[128,256]{1,0:T(8,128)(2,1)S(1)}, u32[]{:S(2)}, u32[]{:S(2)}) collective-permute-start(bf16[128,256]{1,0:T(8,128)(2,1)S(1)} %get-tuple-element.44), channel_id=1, source_target_pairs={{0,4},{2,6},{4,0},{6,2},{1,5},{3,7},{5,1},{7,3},{8,12},{10,14},{12... | collective-permute-start | bytes 196616 | tf_op jit(solution)/shard_map/ppermute | solution.py:271
  27.4 0.0 collective-permute-start.7
  27.4 1.7 %collective-permute-done.8.refs_1_ = bf16[128,256]{1,0:T(8,128)(2,1)S(1)} collective-permute-done((bf16[128,256]{1,0:T(8,128)(2,1)S(1)}, bf16[128,256]{1,0:T(8,128)(2,1)S(1)}, u32[]{:S(2)}, u32[]{:S(2)}) %collective-permute-start.8) | collective-permute-done | bytes 65568 | tf_op jit(solution)/shard_map/ppermute | solution.py:271
  29.1 0.0 collective-permute-start.9
  29.1 0.0 collective-permute-done.10.refs_2_
  29.1 0.5 %collective-permute-start.11 = (bf16[128,256]{1,0:T(8,128)(2,1)S(1)}, bf16[128,256]{1,0:T(8,128)(2,1)S(1)}, u32[]{:S(2)}, u32[]{:S(2)}) collective-permute-start(bf16[128,256]{1,0:T(8,128)(2,1)S(1)} %collective-permute-done.10.refs_2_), channel_id=1, source_target_pairs={{0,1},{1,0},{2,3},{3,2},{4,5},{5,4},{6,7},{7,6},{8,9},{9,8},{10,11... | collective-permute-start | bytes 196616 | tf_op jit(solution)/shard_map/ppermute | solution.py:271
  29.6 0.7 %collective-permute-done.12.refs_3_ = bf16[128,256]{1,0:T(8,128)(2,1)S(1)} collective-permute-done((bf16[128,256]{1,0:T(8,128)(2,1)S(1)}, bf16[128,256]{1,0:T(8,128)(2,1)S(1)}, u32[]{:S(2)}, u32[]{:S(2)}) %collective-permute-start.12) | collective-permute-done | bytes 65568 | tf_op jit(solution)/shard_map/ppermute | solution.py:271
  30.3 0.0 collective-permute-start.13
  30.3 0.3 project.2.refs_4_
  30.6 0.0 collective-permute-done.7.refs_0_
  30.6 0.0 collective-permute-done.9.refs_1_
  30.6 0.0 collective-permute-done.11.refs_2_
  30.6 0.9 %collective-permute-done.13.refs_3_ = bf16[128,256]{1,0:T(8,128)(2,1)S(1)} collective-permute-done((bf16[128,256]{1,0:T(8,128)(2,1)S(1)}, bf16[128,256]{1,0:T(8,128)(2,1)S(1)}, u32[]{:S(2)}, u32[]{:S(2)}) %collective-permute-start.13) | collective-permute-done | bytes 65568 | tf_op jit(solution)/shard_map/ppermute | solution.py:271
  31.5 1.0 %project.3 = bf16[512,256]{1,0:T(8,128)(2,1)} custom-call(bf16[2,512,512]{2,1,0:T(8,128)(2,1)S(1)} %turn.1.turned_ref, bf16[128,256]{1,0:T(8,128)(2,1)S(1)} %collective-permute-done.7.refs_0_, bf16[128,256]{1,0:T(8,128)(2,1)S(1)} %collective-permute-done.9.refs_1_, bf16[128,256]{1,0:T(8,128)(2,1)S(1)} %collective-permute-done.11.refs_2_, ...), custom_call_target="tpu_custom_call" | custom-call | tf_op jit(solution)/shard_map/project/pallas_call | solution.py:435
  (4 shorter events, 0.0 us)
Async XLA Ops:
  1.2 9.2 %collective-permute-start = (bf16[784,128]{1,0:T(8,128)(2,1)S(1)}, bf16[784,128]{1,0:T(8,128)(2,1)S(1)}, u32[]{:S(2)}, u32[]{:S(2)}) collective-permute-start(bf16[784,128]{1,0:T(8,128)(2,1)S(1)} %get-tuple-element.28), channel_id=1, source_target_pairs={{0,2},{2,0},{4,6},{6,4},{1,3},{3,1},{5,7},{7,5},{8,10},{10,8},{12,... | collective-permute-start | bytes 602120 | tf_op jit(solution)/shard_map/ppermute | solution.py:271
  4.2 7.8 %collective-permute-start.1 = (bf16[784,128]{1,0:T(8,128)(2,1)S(1)}, bf16[784,128]{1,0:T(8,128)(2,1)S(1)}, u32[]{:S(2)}, u32[]{:S(2)}) collective-permute-start(bf16[784,128]{1,0:T(8,128)(2,1)S(1)} %get-tuple-element.29), channel_id=1, source_target_pairs={{0,4},{2,6},{4,0},{6,2},{1,5},{3,7},{5,1},{7,3},{8,12},{10,14},{12... | collective-permute-start | bytes 602120 | tf_op jit(solution)/shard_map/ppermute | solution.py:271
  7.2 11.8 %collective-permute-start.3 = (bf16[1,512,128]{2,1,0:T(8,128)(2,1)S(1)}, bf16[1,512,128]{2,1,0:T(8,128)(2,1)S(1)}, u32[]{:S(2)}, u32[]{:S(2)}) collective-permute-start(bf16[1,512,128]{2,1,0:T(8,128)(2,1)S(1)} %slice_bitcast_fusion.2), channel_id=1, source_target_pairs={{0,8},{8,16},{16,24},{24,0},{1,9},{9,17},{17,25},{25,1},{2,10},{10... | collective-permute-start | bytes 393224 | tf_op jit(solution)/shard_map/ppermute | solution.py:339
  8.9 10.1 %collective-permute-start.2 = (bf16[1,512,128]{2,1,0:T(8,128)(2,1)S(1)}, bf16[1,512,128]{2,1,0:T(8,128)(2,1)S(1)}, u32[]{:S(2)}, u32[]{:S(2)}) collective-permute-start(bf16[1,512,128]{2,1,0:T(8,128)(2,1)S(1)} %slice_bitcast_fusion.3), channel_id=1, source_target_pairs={{0,14},{2,12},{4,10},{6,8},{8,22},{10,20},{12,18},{14,16},{16,30},... | collective-permute-start | bytes 393224 | tf_op jit(solution)/shard_map/ppermute | solution.py:350
  10.4 10.4 %collective-permute-start.4 = (bf16[1,512,128]{2,1,0:T(8,128)(2,1)S(1)}, bf16[1,512,128]{2,1,0:T(8,128)(2,1)S(1)}, u32[]{:S(2)}, u32[]{:S(2)}) collective-permute-start(bf16[1,512,128]{2,1,0:T(8,128)(2,1)S(1)} %slice_bitcast_fusion), channel_id=1, source_target_pairs={{0,8},{8,16},{16,24},{24,0},{1,9},{9,17},{17,25},{25,1},{2,10},{10... | collective-permute-start | bytes 393224 | tf_op jit(solution)/shard_map/ppermute | solution.py:339
  12.0 10.2 %collective-permute-start.6 = (bf16[784,128]{1,0:T(8,128)(2,1)S(1)}, bf16[784,128]{1,0:T(8,128)(2,1)S(1)}, u32[]{:S(2)}, u32[]{:S(2)}) collective-permute-start(bf16[784,128]{1,0:T(8,128)(2,1)S(1)} %get-tuple-element.38), channel_id=1, source_target_pairs={{0,6},{2,4},{4,2},{6,0},{1,7},{3,5},{5,3},{7,1},{8,14},{10,12},{12... | collective-permute-start | bytes 602120 | tf_op jit(solution)/shard_map/ppermute | solution.py:271
  14.5 7.7 %collective-permute-start.5 = (bf16[1,512,128]{2,1,0:T(8,128)(2,1)S(1)}, bf16[1,512,128]{2,1,0:T(8,128)(2,1)S(1)}, u32[]{:S(2)}, u32[]{:S(2)}) collective-permute-start(bf16[1,512,128]{2,1,0:T(8,128)(2,1)S(1)} %slice_bitcast_fusion.1), channel_id=1, source_target_pairs={{0,8},{8,16},{16,24},{24,0},{1,9},{9,17},{17,25},{25,1},{2,10},{10... | collective-permute-start | bytes 393224 | tf_op jit(solution)/shard_map/ppermute | solution.py:339
  23.8 5.2 %collective-permute-start.8 = (bf16[128,256]{1,0:T(8,128)(2,1)S(1)}, bf16[128,256]{1,0:T(8,128)(2,1)S(1)}, u32[]{:S(2)}, u32[]{:S(2)}) collective-permute-start(bf16[128,256]{1,0:T(8,128)(2,1)S(1)} %get-tuple-element.42), channel_id=1, source_target_pairs={{0,6},{2,4},{4,2},{6,0},{1,7},{3,5},{5,3},{7,1},{8,14},{10,12},{12... | collective-permute-start | bytes 196616 | tf_op jit(solution)/shard_map/ppermute | solution.py:271
  24.6 4.5 %collective-permute-start.10 = (bf16[128,256]{1,0:T(8,128)(2,1)S(1)}, bf16[128,256]{1,0:T(8,128)(2,1)S(1)}, u32[]{:S(2)}, u32[]{:S(2)}) collective-permute-start(bf16[128,256]{1,0:T(8,128)(2,1)S(1)} %get-tuple-element.43), channel_id=1, source_target_pairs={{0,2},{2,0},{4,6},{6,4},{1,3},{3,1},{5,7},{7,5},{8,10},{10,8},{12,... | collective-permute-start | bytes 196616 | tf_op jit(solution)/shard_map/ppermute | solution.py:271
  26.0 4.3 %collective-permute-start.12 = (bf16[128,256]{1,0:T(8,128)(2,1)S(1)}, bf16[128,256]{1,0:T(8,128)(2,1)S(1)}, u32[]{:S(2)}, u32[]{:S(2)}) collective-permute-start(bf16[128,256]{1,0:T(8,128)(2,1)S(1)} %get-tuple-element.44), channel_id=1, source_target_pairs={{0,4},{2,6},{4,0},{6,2},{1,5},{3,7},{5,1},{7,3},{8,12},{10,14},{12... | collective-permute-start | bytes 196616 | tf_op jit(solution)/shard_map/ppermute | solution.py:271
  27.4 3.2 %collective-permute-start.7 = (bf16[128,256]{1,0:T(8,128)(2,1)S(1)}, bf16[128,256]{1,0:T(8,128)(2,1)S(1)}, u32[]{:S(2)}, u32[]{:S(2)}) collective-permute-start(bf16[128,256]{1,0:T(8,128)(2,1)S(1)} %get-tuple-element.41.refs_0_), channel_id=1, source_target_pairs={{0,1},{1,0},{2,3},{3,2},{4,5},{5,4},{6,7},{7,6},{8,9},{9,8},{10,11... | collective-permute-start | bytes 196616 | tf_op jit(solution)/shard_map/ppermute | solution.py:271
  29.1 1.6 %collective-permute-start.9 = (bf16[128,256]{1,0:T(8,128)(2,1)S(1)}, bf16[128,256]{1,0:T(8,128)(2,1)S(1)}, u32[]{:S(2)}, u32[]{:S(2)}) collective-permute-start(bf16[128,256]{1,0:T(8,128)(2,1)S(1)} %collective-permute-done.8.refs_1_), channel_id=1, source_target_pairs={{0,1},{1,0},{2,3},{3,2},{4,5},{5,4},{6,7},{7,6},{8,9},{9,8},{10,11... | collective-permute-start | bytes 196616 | tf_op jit(solution)/shard_map/ppermute | solution.py:271
  29.1 1.6 %collective-permute-start.11 = (bf16[128,256]{1,0:T(8,128)(2,1)S(1)}, bf16[128,256]{1,0:T(8,128)(2,1)S(1)}, u32[]{:S(2)}, u32[]{:S(2)}) collective-permute-start(bf16[128,256]{1,0:T(8,128)(2,1)S(1)} %collective-permute-done.10.refs_2_), channel_id=1, source_target_pairs={{0,1},{1,0},{2,3},{3,2},{4,5},{5,4},{6,7},{7,6},{8,9},{9,8},{10,11... | collective-permute-start | bytes 196616 | tf_op jit(solution)/shard_map/ppermute | solution.py:271
  30.3 1.3 %collective-permute-start.13 = (bf16[128,256]{1,0:T(8,128)(2,1)S(1)}, bf16[128,256]{1,0:T(8,128)(2,1)S(1)}, u32[]{:S(2)}, u32[]{:S(2)}) collective-permute-start(bf16[128,256]{1,0:T(8,128)(2,1)S(1)} %collective-permute-done.12.refs_3_), channel_id=1, source_target_pairs={{0,1},{1,0},{2,3},{3,2},{4,5},{5,4},{6,7},{7,6},{8,9},{9,8},{10,11... | collective-permute-start | bytes 196616 | tf_op jit(solution)/shard_map/ppermute | solution.py:271

commit v15 on v14

--- a/solution.py
+++ b/solution.py
@@ -332,23 +332,25 @@
     near = [step for step in range(1, group) if hops(step) < 2]
     first = ("halo", 1, (0,))
 
-    def send_on(steps):
-        message = jnp.stack([arrays["block", step][: 2 * rows] for step in steps])
+    def send(message, step, across):
         for offset in offsets:
-            pairs = [(source, (source + offset) % groups) for source in range(groups)]
-            arrays["halo", offset, tuple(steps)] = lax.ppermute(message, "group", pairs)
-
-    def send_across(step):
-        for offset in offsets:
-            pairs = [
-                (at * group + p, (at + offset) % groups * group + (p ^ step))
-                for at in range(groups)
-                for p in range(group)
-            ]
-            message = packed[step][None, : 2 * rows]
-            message, arrays["block", 0] = lax.optimization_barrier((message, arrays["block", 0]))
+            first = max(0, offset * group - STEPS + 1)
+            pairs = []
+            for at in range(groups):
+                for p in range(group):
+                    slab, target = (p, p ^ step) if across else (p ^ step, p)
+                    goal = (at + offset) % groups if slab >= first else at
+                    pairs.append((at * group + p, goal * group + target))
             arrived = lax.ppermute(message, ("group", "place"), pairs)
             arrays["halo", offset, (step,)] = arrived
+
+    def send_on(step):
+        send(arrays["block", step][None, : 2 * rows], step, False)
+
+    def send_across(step):
+        message = packed[step][None, : 2 * rows]
+        message, arrays["block", 0] = lax.optimization_barrier((message, arrays["block", 0]))
+        send(message, step, True)
 
     def stage(at, cost):
         work = plan[at]
@@ -398,13 +400,13 @@
     for step in near:
         arrays["block", step] = swapped(packed[step], "place", step)
     arrays["block", 0], turned = lax.optimization_barrier((packed[0], turned))
-    send_on([0])
+    send_on(0)
     mix = {}
     far_blocks = packed[len(near) + 1 :]
     for step in apart:
         send_across(step)
     for step in near[:1]:
-        send_on([step])
+        send_on(step)
     if apart:
         tied = lax.optimization_barrier(
             (far_blocks, turned, [arrays["block", step] for step in near])
@@ -412,7 +414,7 @@
         far_blocks, turned, blocks = tied
         arrays.update((("block", step), block) for step, block in zip(near, blocks))
     for step in near[1:]:
-        send_on([step])
+        send_on(step)
     for step, block in zip(apart, far_blocks):
         arrays["block", step] = swapped(block, "place", step)
     if apart:

time: 32.7 us -> 35.9 us (1.098)
  starting transfers between devices: 16.5 us -> 21.1 us
  waiting for transfers between devices: 9.1 us -> 7.66 us
    ppermute x4, starting transfers between devices: 5.49 us -> 11 us  [send(): arrived = lax.ppermute(message, ('group', 'place'), pairs)]
    ppermute x4, waiting for transfers between devices: 5.83 us -> 3.96 us  [send(): arrived = lax.ppermute(message, ('group', 'place'), pairs)]
    ppermute x10, starting transfers between devices: 11 us -> 10.1 us  [swapped(): lax.ppermute(value, axis, [(source, source ^ step) for source in range(co...]
    ppermute x10, waiting for transfers between devices: 3.27 us -> 3.7 us  [swapped(): lax.ppermute(value, axis, [(source, source ^ step) for source in range(co...]
  transfers between devices with their start and end apart: 14 -> 14, of which waited for: 6 -> 6; matrix products, arithmetic and copies ran while one was open for 0% -> 0% of each run, Pallas kernels for 9% -> 8%
where the time goes in v15:
time: 35.9 us; the launch traced here: 35.7 us
  starting transfers between devices  21.1 us (59%)
  waiting for transfers between devices  7.66 us (21%)
  Pallas kernels  6.78 us (19%)
    ppermute x4, starting transfers between devices, send(): arrived = lax.ppermute(message, ('group', 'place'), pairs)  11 us
    ppermute x10, starting transfers between devices, swapped(): lax.ppermute(value, axis, [(source, source ^ step) for source in range(co...  10.1 us
    ppermute x4, waiting for transfers between devices, send(): arrived = lax.ppermute(message, ('group', 'place'), pairs)  3.96 us
    ppermute x10, waiting for transfers between devices, swapped(): lax.ppermute(value, axis, [(source, source ^ step) for source in range(co...  3.7 us
    pallas_call x2, Pallas kernels, stage(): pl.pallas_call(functools.partial(attend_kernel, names=names, work=work, s...  2.78 us
    pallas_call x1, Pallas kernels, on_device(): pl.pallas_call(functools.partial(turn_kernel, head_total=head_total), out...  1.44 us
    pallas_call x2, Pallas kernels, on_device(): pl.pallas_call(functools.partial(project_kernel, group=group, others=othe...  1.35 us
    pallas_call x1, Pallas kernels, on_device(): pl.pallas_call(pack_kernel, out_shape=[shape((3 * rows + EXTRA, HD), bf16...  1.21 us
  transfers between devices with their start and end apart: 14, of which 6 were waited for; matrix products, arithmetic and copies ran while one was open for 0% of the time, Pallas kernels for 8%

profile of v15, /device:TPU:0, one launch (start us, length us, event | category | flops | bytes accessed | tf_op | source)
XLA Modules:
  0.0 35.7 jit_solution(17164015035869023357)
XLA Ops:
  0.0 1.2 %pack.1 = (bf16[784,128]{1,0:T(8,128)(2,1)S(1)}, bf16[784,128]{1,0:T(8,128)(2,1)S(1)}, bf16[784,128]{1,0:T(8,128)(2,1)S(1)}, bf16[784,128]{1,0:T(8,128)(2,1)S(1)}) custom-call(bf16[256,512]{1,0:T(8,128)(2,1)} %query_ref.1, bf16[256,512]{1,0:T(8,128)(2,1)} %key_ref.1, bf16[256,512]{1,0:T(8,128)(2,1)} %value_ref.1, s32[2,2,4]{2,1,0:T(2,128)} %bitcast.10, ...), custom_call_target="tpu_custom_call" | custom-call | tf_op jit(solution)/shard_map/pack/pallas_call | solution.py:285
  1.2 3.0 %collective-permute-start = (bf16[784,128]{1,0:T(8,128)(2,1)S(1)}, bf16[784,128]{1,0:T(8,128)(2,1)S(1)}, u32[]{:S(2)}, u32[]{:S(2)}) collective-permute-start(bf16[784,128]{1,0:T(8,128)(2,1)S(1)} %get-tuple-element.28), channel_id=1, source_target_pairs={{0,2},{2,0},{4,6},{6,4},{1,3},{3,1},{5,7},{7,5},{8,10},{10,8},{12,... | collective-permute-start | bytes 602120 | tf_op jit(solution)/shard_map/ppermute | solution.py:271
  4.2 1.5 %collective-permute-start.1 = (bf16[784,128]{1,0:T(8,128)(2,1)S(1)}, bf16[784,128]{1,0:T(8,128)(2,1)S(1)}, u32[]{:S(2)}, u32[]{:S(2)}) collective-permute-start(bf16[784,128]{1,0:T(8,128)(2,1)S(1)} %get-tuple-element.29), channel_id=1, source_target_pairs={{0,4},{2,6},{4,0},{6,2},{1,5},{3,7},{5,1},{7,3},{8,12},{10,14},{12... | collective-permute-start | bytes 602120 | tf_op jit(solution)/shard_map/ppermute | solution.py:271
  5.7 1.4 %turn.1.turned_ref = bf16[2,512,512]{2,1,0:T(8,128)(2,1)S(1)} custom-call(bf16[784,128]{1,0:T(8,128)(2,1)S(1)} %get-tuple-element.34.block_ref.refs_0_, bf16[1024,1024]{1,0:T(8,128)(2,1)} %weight_ref.1), custom_call_target="tpu_custom_call" | custom-call | flops 1000000000 | bytes 1 | tf_op jit(solution)/shard_map/turn/pallas_call | solution.py:311
  7.2 0.7 %collective-permute-start.3 = (bf16[1,512,128]{2,1,0:T(8,128)(2,1)S(1)}, bf16[1,512,128]{2,1,0:T(8,128)(2,1)S(1)}, u32[]{:S(2)}, u32[]{:S(2)}) collective-permute-start(bf16[1,512,128]{2,1,0:T(8,128)(2,1)S(1)} %slice_bitcast_fusion.2), channel_id=1, source_target_pairs={{0,0},{2,10},{4,12},{6,14},{8,8},{10,18},{12,20},{14,22},{16,16},{... | collective-permute-start | bytes 393224 | tf_op jit(solution)/shard_map/ppermute | solution.py:344
  7.9 3.3 %collective-permute-start.2 = (bf16[1,512,128]{2,1,0:T(8,128)(2,1)S(1)}, bf16[1,512,128]{2,1,0:T(8,128)(2,1)S(1)}, u32[]{:S(2)}, u32[]{:S(2)}) collective-permute-start(bf16[1,512,128]{2,1,0:T(8,128)(2,1)S(1)} %slice_bitcast_fusion.3), channel_id=1, source_target_pairs={{0,6},{2,12},{4,10},{6,8},{8,14},{10,20},{12,18},{14,16},{16,22},{... | collective-permute-start | bytes 393224 | tf_op jit(solution)/shard_map/ppermute | solution.py:344
  11.2 0.0 collective-permute-done.refs_1_
  11.3 3.5 %collective-permute-start.4 = (bf16[1,512,128]{2,1,0:T(8,128)(2,1)S(1)}, bf16[1,512,128]{2,1,0:T(8,128)(2,1)S(1)}, u32[]{:S(2)}, u32[]{:S(2)}) collective-permute-start(bf16[1,512,128]{2,1,0:T(8,128)(2,1)S(1)} %slice_bitcast_fusion), channel_id=1, source_target_pairs={{0,8},{2,2},{4,12},{6,14},{8,16},{10,10},{12,20},{14,22},{16,24},{... | collective-permute-start | bytes 393224 | tf_op jit(solution)/shard_map/ppermute | solution.py:344
  14.8 0.0 collective-permute-done.1.refs_2_
  14.8 0.7 %collective-permute-start.6 = (bf16[784,128]{1,0:T(8,128)(2,1)S(1)}, bf16[784,128]{1,0:T(8,128)(2,1)S(1)}, u32[]{:S(2)}, u32[]{:S(2)}) collective-permute-start(bf16[784,128]{1,0:T(8,128)(2,1)S(1)} %get-tuple-element.38), channel_id=1, source_target_pairs={{0,6},{2,4},{4,2},{6,0},{1,7},{3,5},{5,3},{7,1},{8,14},{10,12},{12... | collective-permute-start | bytes 602120 | tf_op jit(solution)/shard_map/ppermute | solution.py:271
  15.5 3.5 %collective-permute-start.5 = (bf16[1,512,128]{2,1,0:T(8,128)(2,1)S(1)}, bf16[1,512,128]{2,1,0:T(8,128)(2,1)S(1)}, u32[]{:S(2)}, u32[]{:S(2)}) collective-permute-start(bf16[1,512,128]{2,1,0:T(8,128)(2,1)S(1)} %slice_bitcast_fusion.1), channel_id=1, source_target_pairs={{0,8},{2,10},{4,4},{6,14},{8,16},{10,18},{12,12},{14,22},{16,24},{... | collective-permute-start | bytes 393224 | tf_op jit(solution)/shard_map/ppermute | solution.py:344
  19.0 0.9 %collective-permute-done.2.refs_4_ = bf16[1,512,128]{2,1,0:T(8,128)(2,1)S(1)} collective-permute-done((bf16[1,512,128]{2,1,0:T(8,128)(2,1)S(1)}, bf16[1,512,128]{2,1,0:T(8,128)(2,1)S(1)}, u32[]{:S(2)}, u32[]{:S(2)}) %collective-permute-start.2) | collective-permute-done | bytes 131104 | tf_op jit(solution)/shard_map/ppermute | solution.py:344
  19.9 0.0 collective-permute-done.3.refs_3_
  19.9 1.2 %attend.2 = (f32[4,128,256]{2,1,0:T(8,128)S(1)}, f32[4,8,256]{2,1,0:T(8,128)S(1)}) custom-call(bf16[784,128]{1,0:T(8,128)(2,1)S(1)} %get-tuple-element.34.block_ref.refs_0_, bf16[784,128]{1,0:T(8,128)(2,1)S(1)} %collective-permute-done.refs_1_, bf16[784,128]{1,0:T(8,128)(2,1)S(1)} %collective-permute-done.1.refs_2_, ...), custom_call_target="tpu_custom_call" | custom-call | flops 1000000000 | bytes 1 | tf_op jit(solution)/shard_map/attend/pallas_call | solution.py:379
  21.1 0.0 collective-permute-done.4.refs_5_
  21.1 3.1 %collective-permute-done.5.refs_6_ = bf16[1,512,128]{2,1,0:T(8,128)(2,1)S(1)} collective-permute-done((bf16[1,512,128]{2,1,0:T(8,128)(2,1)S(1)}, bf16[1,512,128]{2,1,0:T(8,128)(2,1)S(1)}, u32[]{:S(2)}, u32[]{:S(2)}) %collective-permute-start.5) | collective-permute-done | bytes 131104 | tf_op jit(solution)/shard_map/ppermute | solution.py:344
  24.2 0.0 collective-permute-done.6.refs_7_
  24.2 1.6 %attend.3 = (bf16[128,256]{1,0:T(8,128)(2,1)S(1)}, bf16[128,256]{1,0:T(8,128)(2,1)S(1)}, bf16[128,256]{1,0:T(8,128)(2,1)S(1)}, bf16[128,256]{1,0:T(8,128)(2,1)S(1)}) custom-call(bf16[784,128]{1,0:T(8,128)(2,1)S(1)} %get-tuple-element.34.block_ref.refs_0_, bf16[784,128]{1,0:T(8,128)(2,1)S(1)} %collective-permute-done.refs_1_, ...), custom_call_target="tpu_custom_call" | custom-call | flops 1000000000 | bytes 1 | tf_op jit(solution)/shard_map/attend/pallas_call | solution.py:379
  25.8 2.1 %collective-permute-start.8 = (bf16[128,256]{1,0:T(8,128)(2,1)S(1)}, bf16[128,256]{1,0:T(8,128)(2,1)S(1)}, u32[]{:S(2)}, u32[]{:S(2)}) collective-permute-start(bf16[128,256]{1,0:T(8,128)(2,1)S(1)} %get-tuple-element.42), channel_id=1, source_target_pairs={{0,6},{2,4},{4,2},{6,0},{1,7},{3,5},{5,3},{7,1},{8,14},{10,12},{12... | collective-permute-start | bytes 196616 | tf_op jit(solution)/shard_map/ppermute | solution.py:271
  27.9 1.3 %collective-permute-start.10 = (bf16[128,256]{1,0:T(8,128)(2,1)S(1)}, bf16[128,256]{1,0:T(8,128)(2,1)S(1)}, u32[]{:S(2)}, u32[]{:S(2)}) collective-permute-start(bf16[128,256]{1,0:T(8,128)(2,1)S(1)} %get-tuple-element.43), channel_id=1, source_target_pairs={{0,2},{2,0},{4,6},{6,4},{1,3},{3,1},{5,7},{7,5},{8,10},{10,8},{12,... | collective-permute-start | bytes 196616 | tf_op jit(solution)/shard_map/ppermute | solution.py:271
  29.2 1.4 %collective-permute-start.12 = (bf16[128,256]{1,0:T(8,128)(2,1)S(1)}, bf16[128,256]{1,0:T(8,128)(2,1)S(1)}, u32[]{:S(2)}, u32[]{:S(2)}) collective-permute-start(bf16[128,256]{1,0:T(8,128)(2,1)S(1)} %get-tuple-element.44), channel_id=1, source_target_pairs={{0,4},{2,6},{4,0},{6,2},{1,5},{3,7},{5,1},{7,3},{8,12},{10,14},{12... | collective-permute-start | bytes 196616 | tf_op jit(solution)/shard_map/ppermute | solution.py:271
  30.6 0.0 collective-permute-start.7
  30.6 0.4 %collective-permute-done.8.refs_1_ = bf16[128,256]{1,0:T(8,128)(2,1)S(1)} collective-permute-done((bf16[128,256]{1,0:T(8,128)(2,1)S(1)}, bf16[128,256]{1,0:T(8,128)(2,1)S(1)}, u32[]{:S(2)}, u32[]{:S(2)}) %collective-permute-start.8) | collective-permute-done | bytes 65568 | tf_op jit(solution)/shard_map/ppermute | solution.py:271
  31.0 0.1 collective-permute-start.9
  31.1 1.1 %collective-permute-done.10.refs_2_ = bf16[128,256]{1,0:T(8,128)(2,1)S(1)} collective-permute-done((bf16[128,256]{1,0:T(8,128)(2,1)S(1)}, bf16[128,256]{1,0:T(8,128)(2,1)S(1)}, u32[]{:S(2)}, u32[]{:S(2)}) %collective-permute-start.10) | collective-permute-done | bytes 65568 | tf_op jit(solution)/shard_map/ppermute | solution.py:271
  32.1 0.0 collective-permute-start.11
  32.1 1.3 %collective-permute-done.12.refs_3_ = bf16[128,256]{1,0:T(8,128)(2,1)S(1)} collective-permute-done((bf16[128,256]{1,0:T(8,128)(2,1)S(1)}, bf16[128,256]{1,0:T(8,128)(2,1)S(1)}, u32[]{:S(2)}, u32[]{:S(2)}) %collective-permute-start.12) | collective-permute-done | bytes 65568 | tf_op jit(solution)/shard_map/ppermute | solution.py:271
  33.4 0.0 collective-permute-start.13
  33.4 0.3 project.2.refs_4_
  33.8 0.0 collective-permute-done.7.refs_0_
  33.8 0.0 collective-permute-done.9.refs_1_
  33.8 0.0 collective-permute-done.11.refs_2_
  33.8 0.9 %collective-permute-done.13.refs_3_ = bf16[128,256]{1,0:T(8,128)(2,1)S(1)} collective-permute-done((bf16[128,256]{1,0:T(8,128)(2,1)S(1)}, bf16[128,256]{1,0:T(8,128)(2,1)S(1)}, u32[]{:S(2)}, u32[]{:S(2)}) %collective-permute-start.13) | collective-permute-done | bytes 65568 | tf_op jit(solution)/shard_map/ppermute | solution.py:271
  34.7 1.0 %project.3 = bf16[512,256]{1,0:T(8,128)(2,1)} custom-call(bf16[2,512,512]{2,1,0:T(8,128)(2,1)S(1)} %turn.1.turned_ref, bf16[128,256]{1,0:T(8,128)(2,1)S(1)} %collective-permute-done.7.refs_0_, bf16[128,256]{1,0:T(8,128)(2,1)S(1)} %collective-permute-done.9.refs_1_, bf16[128,256]{1,0:T(8,128)(2,1)S(1)} %collective-permute-done.11.refs_2_, ...), custom_call_target="tpu_custom_call" | custom-call | tf_op jit(solution)/shard_map/project/pallas_call | solution.py:437
  (4 shorter events, 0.0 us)
Async XLA Ops:
  1.2 10.0 %collective-permute-start = (bf16[784,128]{1,0:T(8,128)(2,1)S(1)}, bf16[784,128]{1,0:T(8,128)(2,1)S(1)}, u32[]{:S(2)}, u32[]{:S(2)}) collective-permute-start(bf16[784,128]{1,0:T(8,128)(2,1)S(1)} %get-tuple-element.28), channel_id=1, source_target_pairs={{0,2},{2,0},{4,6},{6,4},{1,3},{3,1},{5,7},{7,5},{8,10},{10,8},{12,... | collective-permute-start | bytes 602120 | tf_op jit(solution)/shard_map/ppermute | solution.py:271
  4.2 10.5 %collective-permute-start.1 = (bf16[784,128]{1,0:T(8,128)(2,1)S(1)}, bf16[784,128]{1,0:T(8,128)(2,1)S(1)}, u32[]{:S(2)}, u32[]{:S(2)}) collective-permute-start(bf16[784,128]{1,0:T(8,128)(2,1)S(1)} %get-tuple-element.29), channel_id=1, source_target_pairs={{0,4},{2,6},{4,0},{6,2},{1,5},{3,7},{5,1},{7,3},{8,12},{10,14},{12... | collective-permute-start | bytes 602120 | tf_op jit(solution)/shard_map/ppermute | solution.py:271
  7.2 12.7 %collective-permute-start.3 = (bf16[1,512,128]{2,1,0:T(8,128)(2,1)S(1)}, bf16[1,512,128]{2,1,0:T(8,128)(2,1)S(1)}, u32[]{:S(2)}, u32[]{:S(2)}) collective-permute-start(bf16[1,512,128]{2,1,0:T(8,128)(2,1)S(1)} %slice_bitcast_fusion.2), channel_id=1, source_target_pairs={{0,0},{2,10},{4,12},{6,14},{8,8},{10,18},{12,20},{14,22},{16,16},{... | collective-permute-start | bytes 393224 | tf_op jit(solution)/shard_map/ppermute | solution.py:344
  7.9 12.0 %collective-permute-start.2 = (bf16[1,512,128]{2,1,0:T(8,128)(2,1)S(1)}, bf16[1,512,128]{2,1,0:T(8,128)(2,1)S(1)}, u32[]{:S(2)}, u32[]{:S(2)}) collective-permute-start(bf16[1,512,128]{2,1,0:T(8,128)(2,1)S(1)} %slice_bitcast_fusion.3), channel_id=1, source_target_pairs={{0,6},{2,12},{4,10},{6,8},{8,14},{10,20},{12,18},{14,16},{16,22},{... | collective-permute-start | bytes 393224 | tf_op jit(solution)/shard_map/ppermute | solution.py:344
  11.3 9.8 %collective-permute-start.4 = (bf16[1,512,128]{2,1,0:T(8,128)(2,1)S(1)}, bf16[1,512,128]{2,1,0:T(8,128)(2,1)S(1)}, u32[]{:S(2)}, u32[]{:S(2)}) collective-permute-start(bf16[1,512,128]{2,1,0:T(8,128)(2,1)S(1)} %slice_bitcast_fusion), channel_id=1, source_target_pairs={{0,8},{2,2},{4,12},{6,14},{8,16},{10,10},{12,20},{14,22},{16,24},{... | collective-permute-start | bytes 393224 | tf_op jit(solution)/shard_map/ppermute | solution.py:344
  14.8 9.4 %collective-permute-start.6 = (bf16[784,128]{1,0:T(8,128)(2,1)S(1)}, bf16[784,128]{1,0:T(8,128)(2,1)S(1)}, u32[]{:S(2)}, u32[]{:S(2)}) collective-permute-start(bf16[784,128]{1,0:T(8,128)(2,1)S(1)} %get-tuple-element.38), channel_id=1, source_target_pairs={{0,6},{2,4},{4,2},{6,0},{1,7},{3,5},{5,3},{7,1},{8,14},{10,12},{12... | collective-permute-start | bytes 602120 | tf_op jit(solution)/shard_map/ppermute | solution.py:271
  15.5 8.7 %collective-permute-start.5 = (bf16[1,512,128]{2,1,0:T(8,128)(2,1)S(1)}, bf16[1,512,128]{2,1,0:T(8,128)(2,1)S(1)}, u32[]{:S(2)}, u32[]{:S(2)}) collective-permute-start(bf16[1,512,128]{2,1,0:T(8,128)(2,1)S(1)} %slice_bitcast_fusion.1), channel_id=1, source_target_pairs={{0,8},{2,10},{4,4},{6,14},{8,16},{10,18},{12,12},{14,22},{16,24},{... | collective-permute-start | bytes 393224 | tf_op jit(solution)/shard_map/ppermute | solution.py:344
  25.8 5.2 %collective-permute-start.8 = (bf16[128,256]{1,0:T(8,128)(2,1)S(1)}, bf16[128,256]{1,0:T(8,128)(2,1)S(1)}, u32[]{:S(2)}, u32[]{:S(2)}) collective-permute-start(bf16[128,256]{1,0:T(8,128)(2,1)S(1)} %get-tuple-element.42), channel_id=1, source_target_pairs={{0,6},{2,4},{4,2},{6,0},{1,7},{3,5},{5,3},{7,1},{8,14},{10,12},{12... | collective-permute-start | bytes 196616 | tf_op jit(solution)/shard_map/ppermute | solution.py:271
  27.9 4.3 %collective-permute-start.10 = (bf16[128,256]{1,0:T(8,128)(2,1)S(1)}, bf16[128,256]{1,0:T(8,128)(2,1)S(1)}, u32[]{:S(2)}, u32[]{:S(2)}) collective-permute-start(bf16[128,256]{1,0:T(8,128)(2,1)S(1)} %get-tuple-element.43), channel_id=1, source_target_pairs={{0,2},{2,0},{4,6},{6,4},{1,3},{3,1},{5,7},{7,5},{8,10},{10,8},{12,... | collective-permute-start | bytes 196616 | tf_op jit(solution)/shard_map/ppermute | solution.py:271
  29.2 4.3 %collective-permute-start.12 = (bf16[128,256]{1,0:T(8,128)(2,1)S(1)}, bf16[128,256]{1,0:T(8,128)(2,1)S(1)}, u32[]{:S(2)}, u32[]{:S(2)}) collective-permute-start(bf16[128,256]{1,0:T(8,128)(2,1)S(1)} %get-tuple-element.44), channel_id=1, source_target_pairs={{0,4},{2,6},{4,0},{6,2},{1,5},{3,7},{5,1},{7,3},{8,12},{10,14},{12... | collective-permute-start | bytes 196616 | tf_op jit(solution)/shard_map/ppermute | solution.py:271
  30.6 3.2 %collective-permute-start.7 = (bf16[128,256]{1,0:T(8,128)(2,1)S(1)}, bf16[128,256]{1,0:T(8,128)(2,1)S(1)}, u32[]{:S(2)}, u32[]{:S(2)}) collective-permute-start(bf16[128,256]{1,0:T(8,128)(2,1)S(1)} %get-tuple-element.41.refs_0_), channel_id=1, source_target_pairs={{0,1},{1,0},{2,3},{3,2},{4,5},{5,4},{6,7},{7,6},{8,9},{9,8},{10,11... | collective-permute-start | bytes 196616 | tf_op jit(solution)/shard_map/ppermute | solution.py:271
  31.0 2.8 %collective-permute-start.9 = (bf16[128,256]{1,0:T(8,128)(2,1)S(1)}, bf16[128,256]{1,0:T(8,128)(2,1)S(1)}, u32[]{:S(2)}, u32[]{:S(2)}) collective-permute-start(bf16[128,256]{1,0:T(8,128)(2,1)S(1)} %collective-permute-done.8.refs_1_), channel_id=1, source_target_pairs={{0,1},{1,0},{2,3},{3,2},{4,5},{5,4},{6,7},{7,6},{8,9},{9,8},{10,11... | collective-permute-start | bytes 196616 | tf_op jit(solution)/shard_map/ppermute | solution.py:271
  32.1 1.6 %collective-permute-start.11 = (bf16[128,256]{1,0:T(8,128)(2,1)S(1)}, bf16[128,256]{1,0:T(8,128)(2,1)S(1)}, u32[]{:S(2)}, u32[]{:S(2)}) collective-permute-start(bf16[128,256]{1,0:T(8,128)(2,1)S(1)} %collective-permute-done.10.refs_2_), channel_id=1, source_target_pairs={{0,1},{1,0},{2,3},{3,2},{4,5},{5,4},{6,7},{7,6},{8,9},{9,8},{10,11... | collective-permute-start | bytes 196616 | tf_op jit(solution)/shard_map/ppermute | solution.py:271
  33.4 1.3 %collective-permute-start.13 = (bf16[128,256]{1,0:T(8,128)(2,1)S(1)}, bf16[128,256]{1,0:T(8,128)(2,1)S(1)}, u32[]{:S(2)}, u32[]{:S(2)}) collective-permute-start(bf16[128,256]{1,0:T(8,128)(2,1)S(1)} %collective-permute-done.12.refs_3_), channel_id=1, source_target_pairs={{0,1},{1,0},{2,3},{3,2},{4,5},{5,4},{6,7},{7,6},{8,9},{9,8},{10,11... | collective-permute-start | bytes 196616 | tf_op jit(solution)/shard_map/ppermute | solution.py:271

commit v16 on v14

--- a/solution.py
+++ b/solution.py
@@ -170,6 +170,7 @@
     steps = list(range(group))
     near = [step for step in steps if hops(step) < 2]
     stages = [(near, lambda offset, step: hops(step) < 2 and (offset == 0 or step == 0))]
+    stages.append((steps, lambda offset, step: offset == 0 or step != near[-1]))
     stages.append((steps, lambda offset, step: True))
     plan, taken = [], set()
     for dests, there in stages:
@@ -245,7 +246,8 @@
 
 
 def sending_order(group):
-    return sorted(range(group), key=lambda step: (step > 0, -hops(step), step))
+    last = max(step for step in range(group) if hops(step) < 2)
+    return sorted(range(group), key=lambda step: (step > 0, step != last, -hops(step), step))
 
 
 def project_kernel(turned_ref, *refs, group, others):
@@ -415,10 +417,6 @@
         send_on([step])
     for step, block in zip(apart, far_blocks):
         arrays["block", step] = swapped(block, "place", step)
-    if apart:
-        far_halo = ("halo", 1, tuple(apart))
-        tied = lax.optimization_barrier((arrays["block", 0], arrays[far_halo]))
-        arrays["block", 0], arrays[far_halo] = tied
     mix.update(stage(0, NEAR))
     for at in range(1, len(plan)):
         done = stage(at, FAR)

time: 32.7 us -> 31.4 us (0.960)
  waiting for transfers between devices: 9.1 us -> 7.61 us
  Pallas kernels: 6.78 us -> 7.14 us
    ppermute x1, waiting for transfers between devices: 3.79 us -> 2.22 us  [send_across(): arrived = lax.ppermute(message, ('group', 'place'), pairs)]
    ppermute x10, starting transfers between devices: 11 us -> 10.6 us  [swapped(): lax.ppermute(value, axis, [(source, source ^ step) for source in range(co...]
    pallas_call x2 -> x3, Pallas kernels: 2.78 us -> 3.14 us  [stage(): pl.pallas_call(functools.partial(attend_kernel, names=names, work=work, s...]
  transfers between devices with their start and end apart: 14 -> 14, of which waited for: 6 -> 10; matrix products, arithmetic and copies ran while one was open for 0% -> 0% of each run, Pallas kernels for 9% -> 13%
where the time goes in v16:
time: 31.4 us; the launch traced here: 31.2 us
  starting transfers between devices  16.3 us (52%)
  waiting for transfers between devices  7.61 us (24%)
  Pallas kernels  7.14 us (23%)
    ppermute x10, starting transfers between devices, swapped(): lax.ppermute(value, axis, [(source, source ^ step) for source in range(co...  10.6 us
    ppermute x3, starting transfers between devices, send_on(): arrays['halo', offset, tuple(steps)] = lax.ppermute(message, 'group', pairs)  4.2 us
    ppermute x10, waiting for transfers between devices, swapped(): lax.ppermute(value, axis, [(source, source ^ step) for source in range(co...  3.28 us
    pallas_call x3, Pallas kernels, stage(): pl.pallas_call(functools.partial(attend_kernel, names=names, work=work, s...  3.14 us
    ppermute x1, waiting for transfers between devices, send_across(): arrived = lax.ppermute(message, ('group', 'place'), pairs)  2.22 us
    ppermute x3, waiting for transfers between devices, send_on(): arrays['halo', offset, tuple(steps)] = lax.ppermute(message, 'group', pairs)  2.11 us
    ppermute x1, starting transfers between devices, send_across(): arrived = lax.ppermute(message, ('group', 'place'), pairs)  1.54 us
    pallas_call x1, Pallas kernels, on_device(): pl.pallas_call(functools.partial(turn_kernel, head_total=head_total), out...  1.44 us
  transfers between devices with their start and end apart: 14, of which 10 were waited for; matrix products, arithmetic and copies ran while one was open for 0% of the time, Pallas kernels for 13%

profile of v16, /device:TPU:0, one launch (start us, length us, event | category | flops | bytes accessed | tf_op | source)
XLA Modules:
  0.0 31.2 jit_solution(4206941612581191394)
XLA Ops:
  0.0 1.2 %pack.1 = (bf16[784,128]{1,0:T(8,128)(2,1)S(1)}, bf16[784,128]{1,0:T(8,128)(2,1)S(1)}, bf16[784,128]{1,0:T(8,128)(2,1)S(1)}, bf16[784,128]{1,0:T(8,128)(2,1)S(1)}) custom-call(bf16[256,512]{1,0:T(8,128)(2,1)} %query_ref.1, bf16[256,512]{1,0:T(8,128)(2,1)} %key_ref.1, bf16[256,512]{1,0:T(8,128)(2,1)} %value_ref.1, s32[2,2,4]{2,1,0:T(2,128)} %bitcast.10, ...), custom_call_target="tpu_custom_call" | custom-call | tf_op jit(solution)/shard_map/pack/pallas_call | solution.py:287
  1.2 3.0 %collective-permute-start = (bf16[784,128]{1,0:T(8,128)(2,1)S(1)}, bf16[784,128]{1,0:T(8,128)(2,1)S(1)}, u32[]{:S(2)}, u32[]{:S(2)}) collective-permute-start(bf16[784,128]{1,0:T(8,128)(2,1)S(1)} %get-tuple-element.28), channel_id=1, source_target_pairs={{0,2},{2,0},{4,6},{6,4},{1,3},{3,1},{5,7},{7,5},{8,10},{10,8},{12,... | collective-permute-start | bytes 602120 | tf_op jit(solution)/shard_map/ppermute | solution.py:273
  4.2 1.5 %collective-permute-start.1 = (bf16[784,128]{1,0:T(8,128)(2,1)S(1)}, bf16[784,128]{1,0:T(8,128)(2,1)S(1)}, u32[]{:S(2)}, u32[]{:S(2)}) collective-permute-start(bf16[784,128]{1,0:T(8,128)(2,1)S(1)} %get-tuple-element.29), channel_id=1, source_target_pairs={{0,4},{2,6},{4,0},{6,2},{1,5},{3,7},{5,1},{7,3},{8,12},{10,14},{12... | collective-permute-start | bytes 602120 | tf_op jit(solution)/shard_map/ppermute | solution.py:273
  5.7 1.4 %turn.1.turned_ref = bf16[2,512,512]{2,1,0:T(8,128)(2,1)S(1)} custom-call(bf16[784,128]{1,0:T(8,128)(2,1)S(1)} %get-tuple-element.32.block_ref.refs_0_, bf16[1024,1024]{1,0:T(8,128)(2,1)} %weight_ref.1), custom_call_target="tpu_custom_call" | custom-call | flops 1000000000 | bytes 1 | tf_op jit(solution)/shard_map/turn/pallas_call | solution.py:313
  7.2 1.6 %collective-permute-start.4 = (bf16[1,512,128]{2,1,0:T(8,128)(2,1)S(1)}, bf16[1,512,128]{2,1,0:T(8,128)(2,1)S(1)}, u32[]{:S(2)}, u32[]{:S(2)}) collective-permute-start(bf16[1,512,128]{2,1,0:T(8,128)(2,1)S(1)} %slice_bitcast_fusion.1), channel_id=1, source_target_pairs={{0,8},{8,16},{16,24},{24,0},{1,9},{9,17},{17,25},{25,1},{2,10},{10... | collective-permute-start | bytes 393224 | tf_op jit(solution)/shard_map/ppermute | solution.py:341
  8.9 1.5 %collective-permute-start.5 = (bf16[1,512,128]{2,1,0:T(8,128)(2,1)S(1)}, bf16[1,512,128]{2,1,0:T(8,128)(2,1)S(1)}, u32[]{:S(2)}, u32[]{:S(2)}) collective-permute-start(bf16[1,512,128]{2,1,0:T(8,128)(2,1)S(1)} %slice_bitcast_fusion.3), channel_id=1, source_target_pairs={{0,14},{2,12},{4,10},{6,8},{8,22},{10,20},{12,18},{14,16},{16,30},... | collective-permute-start | bytes 393224 | tf_op jit(solution)/shard_map/ppermute | solution.py:352
  10.4 0.0 collective-permute-done.refs_1_
  10.4 0.3 collective-permute-done.1.refs_2_
  10.7 2.2 %collective-permute-start.3 = (bf16[784,128]{1,0:T(8,128)(2,1)S(1)}, bf16[784,128]{1,0:T(8,128)(2,1)S(1)}, u32[]{:S(2)}, u32[]{:S(2)}) collective-permute-start(bf16[784,128]{1,0:T(8,128)(2,1)S(1)} %get-tuple-element.35), channel_id=1, source_target_pairs={{0,6},{2,4},{4,2},{6,0},{1,7},{3,5},{5,3},{7,1},{8,14},{10,12},{12... | collective-permute-start | bytes 602120 | tf_op jit(solution)/shard_map/ppermute | solution.py:273
  12.9 1.6 %collective-permute-start.6 = (bf16[1,512,128]{2,1,0:T(8,128)(2,1)S(1)}, bf16[1,512,128]{2,1,0:T(8,128)(2,1)S(1)}, u32[]{:S(2)}, u32[]{:S(2)}) collective-permute-start(bf16[1,512,128]{2,1,0:T(8,128)(2,1)S(1)} %slice_bitcast_fusion), channel_id=1, source_target_pairs={{0,8},{8,16},{16,24},{24,0},{1,9},{9,17},{17,25},{25,1},{2,10},{10... | collective-permute-start | bytes 393224 | tf_op jit(solution)/shard_map/ppermute | solution.py:341
  14.5 0.9 %collective-permute-start.2 = (bf16[1,512,128]{2,1,0:T(8,128)(2,1)S(1)}, bf16[1,512,128]{2,1,0:T(8,128)(2,1)S(1)}, u32[]{:S(2)}, u32[]{:S(2)}) collective-permute-start(bf16[1,512,128]{2,1,0:T(8,128)(2,1)S(1)} %slice_bitcast_fusion.2), channel_id=1, source_target_pairs={{0,8},{8,16},{16,24},{24,0},{1,9},{9,17},{17,25},{25,1},{2,10},{10... | collective-permute-start | bytes 393224 | tf_op jit(solution)/shard_map/ppermute | solution.py:341
  15.4 0.0 collective-permute-done.4.refs_3_
  15.5 1.2 %attend.3 = (f32[4,128,256]{2,1,0:T(8,128)S(1)}, f32[4,8,256]{2,1,0:T(8,128)S(1)}) custom-call(bf16[784,128]{1,0:T(8,128)(2,1)S(1)} %get-tuple-element.32.block_ref.refs_0_, bf16[784,128]{1,0:T(8,128)(2,1)S(1)} %collective-permute-done.refs_1_, bf16[784,128]{1,0:T(8,128)(2,1)S(1)} %collective-permute-done.1.refs_2_, ...), custom_call_target="tpu_custom_call" | custom-call | flops 1000000000 | bytes 1 | tf_op jit(solution)/shard_map/attend/pallas_call | solution.py:379
  16.7 2.2 %collective-permute-done.5.refs_4_ = bf16[1,512,128]{2,1,0:T(8,128)(2,1)S(1)} collective-permute-done((bf16[1,512,128]{2,1,0:T(8,128)(2,1)S(1)}, bf16[1,512,128]{2,1,0:T(8,128)(2,1)S(1)}, u32[]{:S(2)}, u32[]{:S(2)}) %collective-permute-start.5) | collective-permute-done | bytes 131104 | tf_op jit(solution)/shard_map/ppermute | solution.py:352
  18.9 2.0 %collective-permute-done.6.refs_5_ = bf16[1,512,128]{2,1,0:T(8,128)(2,1)S(1)} collective-permute-done((bf16[1,512,128]{2,1,0:T(8,128)(2,1)S(1)}, bf16[1,512,128]{2,1,0:T(8,128)(2,1)S(1)}, u32[]{:S(2)}, u32[]{:S(2)}) %collective-permute-start.6) | collective-permute-done | bytes 131104 | tf_op jit(solution)/shard_map/ppermute | solution.py:341
  20.8 0.0 collective-permute-done.3.refs_6_.refs_3_
  20.8 1.2 %attend.4 = (bf16[128,256]{1,0:T(8,128)(2,1)S(1)}, f32[4,128,256]{2,1,0:T(8,128)S(1)}, f32[4,8,256]{2,1,0:T(8,128)S(1)}) custom-call(bf16[784,128]{1,0:T(8,128)(2,1)S(1)} %get-tuple-element.32.block_ref.refs_0_, bf16[784,128]{1,0:T(8,128)(2,1)S(1)} %collective-permute-done.refs_1_, bf16[784,128]{1,0:T(8,128)(2,1)S(1)} %collective-permute-done.1.refs_2_, ...), custom_call_target="tpu_custom_call" | custom-call | flops 1000000000 | bytes 1 | tf_op jit(solution)/shard_map/attend/pallas_call | solution.py:379
  22.1 0.2 collective-permute-done.2.refs_2_
  22.2 0.7 %attend.5 = (bf16[128,256]{1,0:T(8,128)(2,1)S(1)}, bf16[128,256]{1,0:T(8,128)(2,1)S(1)}, bf16[128,256]{1,0:T(8,128)(2,1)S(1)}) custom-call(bf16[784,128]{1,0:T(8,128)(2,1)S(1)} %get-tuple-element.32.block_ref.refs_0_, bf16[784,128]{1,0:T(8,128)(2,1)S(1)} %collective-permute-done.refs_1_, bf16[1,512,128]{2,1,0:T(8,128)(2,1)S(1)} %collective-permute-done.2.refs_2_, ...), custom_call_target="tpu_custom_call" | custom-call | flops 1000000000 | bytes 1 | tf_op jit(solution)/shard_map/attend/pallas_call | solution.py:379
  23.0 1.1 %collective-permute-start.10 = (bf16[128,256]{1,0:T(8,128)(2,1)S(1)}, bf16[128,256]{1,0:T(8,128)(2,1)S(1)}, u32[]{:S(2)}, u32[]{:S(2)}) collective-permute-start(bf16[128,256]{1,0:T(8,128)(2,1)S(1)} %get-tuple-element.43), channel_id=1, source_target_pairs={{0,6},{2,4},{4,2},{6,0},{1,7},{3,5},{5,3},{7,1},{8,14},{10,12},{12... | collective-permute-start | bytes 196616 | tf_op jit(solution)/shard_map/ppermute | solution.py:273
  24.1 0.6 %collective-permute-start.12 = (bf16[128,256]{1,0:T(8,128)(2,1)S(1)}, bf16[128,256]{1,0:T(8,128)(2,1)S(1)}, u32[]{:S(2)}, u32[]{:S(2)}) collective-permute-start(bf16[128,256]{1,0:T(8,128)(2,1)S(1)} %get-tuple-element.44), channel_id=1, source_target_pairs={{0,2},{2,0},{4,6},{6,4},{1,3},{3,1},{5,7},{7,5},{8,10},{10,8},{12,... | collective-permute-start | bytes 196616 | tf_op jit(solution)/shard_map/ppermute | solution.py:273
  24.7 1.8 %collective-permute-start.8 = (bf16[128,256]{1,0:T(8,128)(2,1)S(1)}, bf16[128,256]{1,0:T(8,128)(2,1)S(1)}, u32[]{:S(2)}, u32[]{:S(2)}) collective-permute-start(bf16[128,256]{1,0:T(8,128)(2,1)S(1)} %get-tuple-element.42), channel_id=1, source_target_pairs={{0,4},{2,6},{4,0},{6,2},{1,5},{3,7},{5,1},{7,3},{8,12},{10,14},{12... | collective-permute-start | bytes 196616 | tf_op jit(solution)/shard_map/ppermute | solution.py:273
  26.5 0.0 collective-permute-start.7
  26.5 1.7 %collective-permute-done.10.refs_2_ = bf16[128,256]{1,0:T(8,128)(2,1)S(1)} collective-permute-done((bf16[128,256]{1,0:T(8,128)(2,1)S(1)}, bf16[128,256]{1,0:T(8,128)(2,1)S(1)}, u32[]{:S(2)}, u32[]{:S(2)}) %collective-permute-start.10) | collective-permute-done | bytes 65568 | tf_op jit(solution)/shard_map/ppermute | solution.py:273
  28.2 0.0 collective-permute-start.11
  28.2 0.2 collective-permute-done.12.refs_3_
  28.4 0.3 %collective-permute-start.13 = (bf16[128,256]{1,0:T(8,128)(2,1)S(1)}, bf16[128,256]{1,0:T(8,128)(2,1)S(1)}, u32[]{:S(2)}, u32[]{:S(2)}) collective-permute-start(bf16[128,256]{1,0:T(8,128)(2,1)S(1)} %collective-permute-done.12.refs_3_), channel_id=1, source_target_pairs={{0,1},{1,0},{2,3},{3,2},{4,5},{5,4},{6,7},{7,6},{8,9},{9,8},{10,11... | collective-permute-start | bytes 196616 | tf_op jit(solution)/shard_map/ppermute | solution.py:273
  28.7 0.2 collective-permute-done.8.refs_1_
  28.9 0.0 collective-permute-start.9
  28.9 0.3 %project.2.refs_4_ = f32[512,256]{1,0:T(8,128)S(1)} custom-call(bf16[2,512,512]{2,1,0:T(8,128)(2,1)S(1)} %turn.1.turned_ref, bf16[128,256]{1,0:T(8,128)(2,1)S(1)} %get-tuple-element.41.refs_0_, bf16[128,256]{1,0:T(8,128)(2,1)S(1)} %collective-permute-done.8.refs_1_, bf16[128,256]{1,0:T(8,128)(2,1)S(1)} %collective-permute-done.10.refs_2_, ...), custom_call_target="tpu_custom_call" | custom-call | tf_op jit(solution)/shard_map/project/pallas_call | solution.py:433
  29.3 0.0 collective-permute-done.7.refs_0_
  29.3 0.2 collective-permute-done.11.refs_2_
  29.4 0.2 collective-permute-done.13.refs_3_
  29.6 0.6 %collective-permute-done.9.refs_1_ = bf16[128,256]{1,0:T(8,128)(2,1)S(1)} collective-permute-done((bf16[128,256]{1,0:T(8,128)(2,1)S(1)}, bf16[128,256]{1,0:T(8,128)(2,1)S(1)}, u32[]{:S(2)}, u32[]{:S(2)}) %collective-permute-start.9) | collective-permute-done | bytes 65568 | tf_op jit(solution)/shard_map/ppermute | solution.py:273
  30.2 1.0 %project.3 = bf16[512,256]{1,0:T(8,128)(2,1)} custom-call(bf16[2,512,512]{2,1,0:T(8,128)(2,1)S(1)} %turn.1.turned_ref, bf16[128,256]{1,0:T(8,128)(2,1)S(1)} %collective-permute-done.7.refs_0_, bf16[128,256]{1,0:T(8,128)(2,1)S(1)} %collective-permute-done.9.refs_1_, bf16[128,256]{1,0:T(8,128)(2,1)S(1)} %collective-permute-done.11.refs_2_, ...), custom_call_target="tpu_custom_call" | custom-call | tf_op jit(solution)/shard_map/project/pallas_call | solution.py:433
  (4 shorter events, 0.0 us)
Async XLA Ops:
  1.2 9.2 %collective-permute-start = (bf16[784,128]{1,0:T(8,128)(2,1)S(1)}, bf16[784,128]{1,0:T(8,128)(2,1)S(1)}, u32[]{:S(2)}, u32[]{:S(2)}) collective-permute-start(bf16[784,128]{1,0:T(8,128)(2,1)S(1)} %get-tuple-element.28), channel_id=1, source_target_pairs={{0,2},{2,0},{4,6},{6,4},{1,3},{3,1},{5,7},{7,5},{8,10},{10,8},{12,... | collective-permute-start | bytes 602120 | tf_op jit(solution)/shard_map/ppermute | solution.py:273
  4.2 6.4 %collective-permute-start.1 = (bf16[784,128]{1,0:T(8,128)(2,1)S(1)}, bf16[784,128]{1,0:T(8,128)(2,1)S(1)}, u32[]{:S(2)}, u32[]{:S(2)}) collective-permute-start(bf16[784,128]{1,0:T(8,128)(2,1)S(1)} %get-tuple-element.29), channel_id=1, source_target_pairs={{0,4},{2,6},{4,0},{6,2},{1,5},{3,7},{5,1},{7,3},{8,12},{10,14},{12... | collective-permute-start | bytes 602120 | tf_op jit(solution)/shard_map/ppermute | solution.py:273
  7.2 8.2 %collective-permute-start.4 = (bf16[1,512,128]{2,1,0:T(8,128)(2,1)S(1)}, bf16[1,512,128]{2,1,0:T(8,128)(2,1)S(1)}, u32[]{:S(2)}, u32[]{:S(2)}) collective-permute-start(bf16[1,512,128]{2,1,0:T(8,128)(2,1)S(1)} %slice_bitcast_fusion.1), channel_id=1, source_target_pairs={{0,8},{8,16},{16,24},{24,0},{1,9},{9,17},{17,25},{25,1},{2,10},{10... | collective-permute-start | bytes 393224 | tf_op jit(solution)/shard_map/ppermute | solution.py:341
  8.9 10.0 %collective-permute-start.5 = (bf16[1,512,128]{2,1,0:T(8,128)(2,1)S(1)}, bf16[1,512,128]{2,1,0:T(8,128)(2,1)S(1)}, u32[]{:S(2)}, u32[]{:S(2)}) collective-permute-start(bf16[1,512,128]{2,1,0:T(8,128)(2,1)S(1)} %slice_bitcast_fusion.3), channel_id=1, source_target_pairs={{0,14},{2,12},{4,10},{6,8},{8,22},{10,20},{12,18},{14,16},{16,30},... | collective-permute-start | bytes 393224 | tf_op jit(solution)/shard_map/ppermute | solution.py:352
  10.7 10.2 %collective-permute-start.3 = (bf16[784,128]{1,0:T(8,128)(2,1)S(1)}, bf16[784,128]{1,0:T(8,128)(2,1)S(1)}, u32[]{:S(2)}, u32[]{:S(2)}) collective-permute-start(bf16[784,128]{1,0:T(8,128)(2,1)S(1)} %get-tuple-element.35), channel_id=1, source_target_pairs={{0,6},{2,4},{4,2},{6,0},{1,7},{3,5},{5,3},{7,1},{8,14},{10,12},{12... | collective-permute-start | bytes 602120 | tf_op jit(solution)/shard_map/ppermute | solution.py:273
  12.9 8.0 %collective-permute-start.6 = (bf16[1,512,128]{2,1,0:T(8,128)(2,1)S(1)}, bf16[1,512,128]{2,1,0:T(8,128)(2,1)S(1)}, u32[]{:S(2)}, u32[]{:S(2)}) collective-permute-start(bf16[1,512,128]{2,1,0:T(8,128)(2,1)S(1)} %slice_bitcast_fusion), channel_id=1, source_target_pairs={{0,8},{8,16},{16,24},{24,0},{1,9},{9,17},{17,25},{25,1},{2,10},{10... | collective-permute-start | bytes 393224 | tf_op jit(solution)/shard_map/ppermute | solution.py:341
  14.5 7.7 %collective-permute-start.2 = (bf16[1,512,128]{2,1,0:T(8,128)(2,1)S(1)}, bf16[1,512,128]{2,1,0:T(8,128)(2,1)S(1)}, u32[]{:S(2)}, u32[]{:S(2)}) collective-permute-start(bf16[1,512,128]{2,1,0:T(8,128)(2,1)S(1)} %slice_bitcast_fusion.2), channel_id=1, source_target_pairs={{0,8},{8,16},{16,24},{24,0},{1,9},{9,17},{17,25},{25,1},{2,10},{10... | collective-permute-start | bytes 393224 | tf_op jit(solution)/shard_map/ppermute | solution.py:341
  23.0 5.2 %collective-permute-start.10 = (bf16[128,256]{1,0:T(8,128)(2,1)S(1)}, bf16[128,256]{1,0:T(8,128)(2,1)S(1)}, u32[]{:S(2)}, u32[]{:S(2)}) collective-permute-start(bf16[128,256]{1,0:T(8,128)(2,1)S(1)} %get-tuple-element.43), channel_id=1, source_target_pairs={{0,6},{2,4},{4,2},{6,0},{1,7},{3,5},{5,3},{7,1},{8,14},{10,12},{12... | collective-permute-start | bytes 196616 | tf_op jit(solution)/shard_map/ppermute | solution.py:273
  24.1 4.3 %collective-permute-start.12 = (bf16[128,256]{1,0:T(8,128)(2,1)S(1)}, bf16[128,256]{1,0:T(8,128)(2,1)S(1)}, u32[]{:S(2)}, u32[]{:S(2)}) collective-permute-start(bf16[128,256]{1,0:T(8,128)(2,1)S(1)} %get-tuple-element.44), channel_id=1, source_target_pairs={{0,2},{2,0},{4,6},{6,4},{1,3},{3,1},{5,7},{7,5},{8,10},{10,8},{12,... | collective-permute-start | bytes 196616 | tf_op jit(solution)/shard_map/ppermute | solution.py:273
  24.7 4.3 %collective-permute-start.8 = (bf16[128,256]{1,0:T(8,128)(2,1)S(1)}, bf16[128,256]{1,0:T(8,128)(2,1)S(1)}, u32[]{:S(2)}, u32[]{:S(2)}) collective-permute-start(bf16[128,256]{1,0:T(8,128)(2,1)S(1)} %get-tuple-element.42), channel_id=1, source_target_pairs={{0,4},{2,6},{4,0},{6,2},{1,5},{3,7},{5,1},{7,3},{8,12},{10,14},{12... | collective-permute-start | bytes 196616 | tf_op jit(solution)/shard_map/ppermute | solution.py:273
  26.5 2.8 %collective-permute-start.7 = (bf16[128,256]{1,0:T(8,128)(2,1)S(1)}, bf16[128,256]{1,0:T(8,128)(2,1)S(1)}, u32[]{:S(2)}, u32[]{:S(2)}) collective-permute-start(bf16[128,256]{1,0:T(8,128)(2,1)S(1)} %get-tuple-element.41.refs_0_), channel_id=1, source_target_pairs={{0,1},{1,0},{2,3},{3,2},{4,5},{5,4},{6,7},{7,6},{8,9},{9,8},{10,11... | collective-permute-start | bytes 196616 | tf_op jit(solution)/shard_map/ppermute | solution.py:273
  28.2 1.3 %collective-permute-start.11 = (bf16[128,256]{1,0:T(8,128)(2,1)S(1)}, bf16[128,256]{1,0:T(8,128)(2,1)S(1)}, u32[]{:S(2)}, u32[]{:S(2)}) collective-permute-start(bf16[128,256]{1,0:T(8,128)(2,1)S(1)} %collective-permute-done.10.refs_2_), channel_id=1, source_target_pairs={{0,1},{1,0},{2,3},{3,2},{4,5},{5,4},{6,7},{7,6},{8,9},{9,8},{10,11... | collective-permute-start | bytes 196616 | tf_op jit(solution)/shard_map/ppermute | solution.py:273
  28.4 1.3 %collective-permute-start.13 = (bf16[128,256]{1,0:T(8,128)(2,1)S(1)}, bf16[128,256]{1,0:T(8,128)(2,1)S(1)}, u32[]{:S(2)}, u32[]{:S(2)}) collective-permute-start(bf16[128,256]{1,0:T(8,128)(2,1)S(1)} %collective-permute-done.12.refs_3_), channel_id=1, source_target_pairs={{0,1},{1,0},{2,3},{3,2},{4,5},{5,4},{6,7},{7,6},{8,9},{9,8},{10,11... | collective-permute-start | bytes 196616 | tf_op jit(solution)/shard_map/ppermute | solution.py:273
  28.9 1.3 %collective-permute-start.9 = (bf16[128,256]{1,0:T(8,128)(2,1)S(1)}, bf16[128,256]{1,0:T(8,128)(2,1)S(1)}, u32[]{:S(2)}, u32[]{:S(2)}) collective-permute-start(bf16[128,256]{1,0:T(8,128)(2,1)S(1)} %collective-permute-done.8.refs_1_), channel_id=1, source_target_pairs={{0,1},{1,0},{2,3},{3,2},{4,5},{5,4},{6,7},{7,6},{8,9},{9,8},{10,11... | collective-permute-start | bytes 196616 | tf_op jit(solution)/shard_map/ppermute | solution.py:273

commit v17 on v16

--- a/solution.py
+++ b/solution.py
@@ -169,8 +169,9 @@
 def stage_plan(group):
     steps = list(range(group))
     near = [step for step in steps if hops(step) < 2]
-    stages = [(near, lambda offset, step: hops(step) < 2 and (offset == 0 or step == 0))]
-    stages.append((steps, lambda offset, step: offset == 0 or step != near[-1]))
+    stages = [(near, lambda offset, step: offset == 0 and hops(step) < 2)]
+    if len(near) < group:
+        stages.append((steps, lambda offset, step: offset == 0 or step == 1 or hops(step) > 1))
     stages.append((steps, lambda offset, step: True))
     plan, taken = [], set()
     for dests, there in stages:
@@ -400,19 +401,23 @@
     for step in near:
         arrays["block", step] = swapped(packed[step], "place", step)
     arrays["block", 0], turned = lax.optimization_barrier((packed[0], turned))
-    send_on([0])
     mix = {}
     far_blocks = packed[len(near) + 1 :]
-    for step in apart:
+    for step in near[:1] + apart:
         send_across(step)
-    for step in near[:1]:
-        send_on([step])
     if apart:
         tied = lax.optimization_barrier(
             (far_blocks, turned, [arrays["block", step] for step in near])
         )
         far_blocks, turned, blocks = tied
         arrays.update((("block", step), block) for step, block in zip(near, blocks))
+    early_own = arrays["block", 0]
+    if near:
+        late = ("block", near[-1])
+        tied = lax.optimization_barrier((early_own, arrays[late]))
+        arrays["block", 0], arrays[late] = tied
+    send_on([0])
+    arrays["block", 0] = early_own
     for step in near[1:]:
         send_on([step])
     for step, block in zip(apart, far_blocks):

time: 31.4 us -> 34.6 us (1.10)
  starting transfers between devices: 16.3 us -> 21.2 us
  waiting for transfers between devices: 7.61 us -> 5.86 us
    ppermute x3 -> x2, starting transfers between devices: 4.2 us -> 7.11 us  [send_on(): arrays['halo', offset, tuple(steps)] = lax.ppermute(message, 'group', pairs)]
    ppermute x1 -> x2, starting transfers between devices: 1.54 us -> 4.05 us  [send_across(): arrived = lax.ppermute(message, ('group', 'place'), pairs)]
    ppermute x1 -> x2, waiting for transfers between devices: 2.22 us -> 0.01 us  [send_across(): arrived = lax.ppermute(message, ('group', 'place'), pairs)]
    ppermute x10, waiting for transfers between devices: 3.28 us -> 4.72 us  [swapped(): lax.ppermute(value, axis, [(source, source ^ step) for source in range(co...]
    ppermute x3 -> x2, waiting for transfers between devices: 2.11 us -> 1.13 us  [send_on(): arrays['halo', offset, tuple(steps)] = lax.ppermute(message, 'group', pairs)]
    ppermute x10, starting transfers between devices: 10.6 us -> 10.1 us  [swapped(): lax.ppermute(value, axis, [(source, source ^ step) for source in range(co...]
  transfers between devices with their start and end apart: 14 -> 14, of which waited for: 10 -> 5; matrix products, arithmetic and copies ran while one was open for 0% -> 0% of each run, Pallas kernels for 13% -> 12%
where the time goes in v17:
time: 34.6 us; the launch traced here: 34.4 us
  starting transfers between devices  21.2 us (61%)
  Pallas kernels  7.15 us (21%)
  waiting for transfers between devices  5.86 us (17%)
    ppermute x10, starting transfers between devices, swapped(): lax.ppermute(value, axis, [(source, source ^ step) for source in range(co...  10.1 us
    ppermute x2, starting transfers between devices, send_on(): arrays['halo', offset, tuple(steps)] = lax.ppermute(message, 'group', pairs)  7.11 us
    ppermute x10, waiting for transfers between devices, swapped(): lax.ppermute(value, axis, [(source, source ^ step) for source in range(co...  4.72 us
    ppermute x2, starting transfers between devices, send_across(): arrived = lax.ppermute(message, ('group', 'place'), pairs)  4.05 us
    pallas_call x3, Pallas kernels, stage(): pl.pallas_call(functools.partial(attend_kernel, names=names, work=work, s...  3.15 us
    pallas_call x1, Pallas kernels, on_device(): pl.pallas_call(functools.partial(turn_kernel, head_total=head_total), out...  1.44 us
    pallas_call x2, Pallas kernels, on_device(): pl.pallas_call(functools.partial(project_kernel, group=group, others=othe...  1.35 us
    pallas_call x1, Pallas kernels, on_device(): pl.pallas_call(pack_kernel, out_shape=[shape((3 * rows + EXTRA, HD), bf16...  1.21 us
  transfers between devices with their start and end apart: 14, of which 5 were waited for; matrix products, arithmetic and copies ran while one was open for 0% of the time, Pallas kernels for 12%

profile of v17, /device:TPU:0, one launch (start us, length us, event | category | flops | bytes accessed | tf_op | source)
XLA Modules:
  0.0 34.4 jit_solution(16880288517332420959)
XLA Ops:
  0.0 1.2 %pack.1 = (bf16[784,128]{1,0:T(8,128)(2,1)S(1)}, bf16[784,128]{1,0:T(8,128)(2,1)S(1)}, bf16[784,128]{1,0:T(8,128)(2,1)S(1)}, bf16[784,128]{1,0:T(8,128)(2,1)S(1)}) custom-call(bf16[256,512]{1,0:T(8,128)(2,1)} %query_ref.1, bf16[256,512]{1,0:T(8,128)(2,1)} %key_ref.1, bf16[256,512]{1,0:T(8,128)(2,1)} %value_ref.1, s32[2,2,4]{2,1,0:T(2,128)} %bitcast.10, ...), custom_call_target="tpu_custom_call" | custom-call | tf_op jit(solution)/shard_map/pack/pallas_call | solution.py:288
  1.2 3.0 %collective-permute-start = (bf16[784,128]{1,0:T(8,128)(2,1)S(1)}, bf16[784,128]{1,0:T(8,128)(2,1)S(1)}, u32[]{:S(2)}, u32[]{:S(2)}) collective-permute-start(bf16[784,128]{1,0:T(8,128)(2,1)S(1)} %get-tuple-element.32), channel_id=1, source_target_pairs={{0,2},{2,0},{4,6},{6,4},{1,3},{3,1},{5,7},{7,5},{8,10},{10,8},{12,... | collective-permute-start | bytes 602120 | tf_op jit(solution)/shard_map/ppermute | solution.py:274
  4.2 1.5 %collective-permute-start.1 = (bf16[784,128]{1,0:T(8,128)(2,1)S(1)}, bf16[784,128]{1,0:T(8,128)(2,1)S(1)}, u32[]{:S(2)}, u32[]{:S(2)}) collective-permute-start(bf16[784,128]{1,0:T(8,128)(2,1)S(1)} %get-tuple-element.33), channel_id=1, source_target_pairs={{0,4},{2,6},{4,0},{6,2},{1,5},{3,7},{5,1},{7,3},{8,12},{10,14},{12... | collective-permute-start | bytes 602120 | tf_op jit(solution)/shard_map/ppermute | solution.py:274
  5.7 1.4 %turn.1.turned_ref = bf16[2,512,512]{2,1,0:T(8,128)(2,1)S(1)} custom-call(bf16[784,128]{1,0:T(8,128)(2,1)S(1)} %get-tuple-element.41.block_ref.refs_0_, bf16[1024,1024]{1,0:T(8,128)(2,1)} %weight_ref.1), custom_call_target="tpu_custom_call" | custom-call | flops 1000000000 | bytes 1 | tf_op jit(solution)/shard_map/turn/pallas_call | solution.py:314
  7.2 1.5 %collective-permute-start.6 = (bf16[1,512,128]{2,1,0:T(8,128)(2,1)S(1)}, bf16[1,512,128]{2,1,0:T(8,128)(2,1)S(1)}, u32[]{:S(2)}, u32[]{:S(2)}) collective-permute-start(bf16[1,512,128]{2,1,0:T(8,128)(2,1)S(1)} %get-tuple-element.44), channel_id=1, source_target_pairs={{0,14},{2,12},{4,10},{6,8},{8,22},{10,20},{12,18},{14,16},{16,30},... | collective-permute-start | bytes 393224 | tf_op jit(solution)/shard_map/ppermute | solution.py:353
  8.8 2.5 %collective-permute-start.5 = (bf16[1,512,128]{2,1,0:T(8,128)(2,1)S(1)}, bf16[1,512,128]{2,1,0:T(8,128)(2,1)S(1)}, u32[]{:S(2)}, u32[]{:S(2)}) collective-permute-start(bf16[1,512,128]{2,1,0:T(8,128)(2,1)S(1)} %get-tuple-element.43), channel_id=1, source_target_pairs={{0,10},{2,8},{4,14},{6,12},{8,18},{10,16},{12,22},{14,20},{16,26},... | collective-permute-start | bytes 393224 | tf_op jit(solution)/shard_map/ppermute | solution.py:353
  11.3 0.0 collective-permute-done.refs_1_
  11.3 0.0 collective-permute-done.1.refs_2_
  11.3 1.5 %collective-permute-start.4 = (bf16[784,128]{1,0:T(8,128)(2,1)S(1)}, bf16[784,128]{1,0:T(8,128)(2,1)S(1)}, u32[]{:S(2)}, u32[]{:S(2)}) collective-permute-start(bf16[784,128]{1,0:T(8,128)(2,1)S(1)} %get-tuple-element.42), channel_id=1, source_target_pairs={{0,6},{2,4},{4,2},{6,0},{1,7},{3,5},{5,3},{7,1},{8,14},{10,12},{12... | collective-permute-start | bytes 602120 | tf_op jit(solution)/shard_map/ppermute | solution.py:274
  12.8 5.4 %collective-permute-start.3 = (bf16[1,512,128]{2,1,0:T(8,128)(2,1)S(1)}, bf16[1,512,128]{2,1,0:T(8,128)(2,1)S(1)}, u32[]{:S(2)}, u32[]{:S(2)}) collective-permute-start(bf16[1,512,128]{2,1,0:T(8,128)(2,1)S(1)} %slice_bitcast_fusion), channel_id=1, source_target_pairs={{0,8},{8,16},{16,24},{24,0},{1,9},{9,17},{17,25},{25,1},{2,10},{10... | collective-permute-start | bytes 393224 | tf_op jit(solution)/shard_map/ppermute | solution.py:342
  18.2 1.7 %collective-permute-start.2 = (bf16[1,512,128]{2,1,0:T(8,128)(2,1)S(1)}, bf16[1,512,128]{2,1,0:T(8,128)(2,1)S(1)}, u32[]{:S(2)}, u32[]{:S(2)}) collective-permute-start(bf16[1,512,128]{2,1,0:T(8,128)(2,1)S(1)} %slice_bitcast_fusion.1), channel_id=1, source_target_pairs={{0,8},{8,16},{16,24},{24,0},{1,9},{9,17},{17,25},{25,1},{2,10},{10... | collective-permute-start | bytes 393224 | tf_op jit(solution)/shard_map/ppermute | solution.py:342
  19.9 1.2 %attend.3 = (f32[4,128,256]{2,1,0:T(8,128)S(1)}, f32[4,8,256]{2,1,0:T(8,128)S(1)}) custom-call(bf16[784,128]{1,0:T(8,128)(2,1)S(1)} %get-tuple-element.41.block_ref.refs_0_, bf16[784,128]{1,0:T(8,128)(2,1)S(1)} %collective-permute-done.refs_1_, bf16[784,128]{1,0:T(8,128)(2,1)S(1)} %collective-permute-done.1.refs_2_), custom_call_target="tpu_custom_call" | custom-call | flops 1000000000 | bytes 1 | tf_op jit(solution)/shard_map/attend/pallas_call | solution.py:380
  21.1 0.0 collective-permute-done.6.refs_4_
  21.1 0.0 collective-permute-done.5.refs_3_
  21.1 1.5 %collective-permute-done.4.refs_5_ = bf16[784,128]{1,0:T(8,128)(2,1)S(1)} collective-permute-done((bf16[784,128]{1,0:T(8,128)(2,1)S(1)}, bf16[784,128]{1,0:T(8,128)(2,1)S(1)}, u32[]{:S(2)}, u32[]{:S(2)}) %collective-permute-start.4) | collective-permute-done | bytes 200736 | tf_op jit(solution)/shard_map/ppermute | solution.py:274
  22.7 1.2 %attend.4 = (f32[4,128,256]{2,1,0:T(8,128)S(1)}, f32[4,8,256]{2,1,0:T(8,128)S(1)}) custom-call(bf16[784,128]{1,0:T(8,128)(2,1)S(1)} %get-tuple-element.41.block_ref.refs_0_, bf16[784,128]{1,0:T(8,128)(2,1)S(1)} %collective-permute-done.refs_1_, bf16[784,128]{1,0:T(8,128)(2,1)S(1)} %collective-permute-done.1.refs_2_, ...), custom_call_target="tpu_custom_call" | custom-call | flops 1000000000 | bytes 1 | tf_op jit(solution)/shard_map/attend/pallas_call | solution.py:380
  23.9 0.0 collective-permute-done.3.refs_4_
  23.9 1.1 %collective-permute-done.2.refs_3_ = bf16[1,512,128]{2,1,0:T(8,128)(2,1)S(1)} collective-permute-done((bf16[1,512,128]{2,1,0:T(8,128)(2,1)S(1)}, bf16[1,512,128]{2,1,0:T(8,128)(2,1)S(1)}, u32[]{:S(2)}, u32[]{:S(2)}) %collective-permute-start.2) | collective-permute-done | bytes 131104 | tf_op jit(solution)/shard_map/ppermute | solution.py:342
  25.0 0.7 %attend.5 = (bf16[128,256]{1,0:T(8,128)(2,1)S(1)}, bf16[128,256]{1,0:T(8,128)(2,1)S(1)}, bf16[128,256]{1,0:T(8,128)(2,1)S(1)}, bf16[128,256]{1,0:T(8,128)(2,1)S(1)}) custom-call(bf16[784,128]{1,0:T(8,128)(2,1)S(1)} %get-tuple-element.41.block_ref.refs_0_, bf16[784,128]{1,0:T(8,128)(2,1)S(1)} %collective-permute-done.refs_1_, ...), custom_call_target="tpu_custom_call" | custom-call | flops 1000000000 | bytes 1 | tf_op jit(solution)/shard_map/attend/pallas_call | solution.py:380
  25.8 0.4 %collective-permute-start.10 = (bf16[128,256]{1,0:T(8,128)(2,1)S(1)}, bf16[128,256]{1,0:T(8,128)(2,1)S(1)}, u32[]{:S(2)}, u32[]{:S(2)}) collective-permute-start(bf16[128,256]{1,0:T(8,128)(2,1)S(1)} %get-tuple-element.51), channel_id=1, source_target_pairs={{0,6},{2,4},{4,2},{6,0},{1,7},{3,5},{5,3},{7,1},{8,14},{10,12},{12... | collective-permute-start | bytes 196616 | tf_op jit(solution)/shard_map/ppermute | solution.py:274
  26.1 1.7 %collective-permute-start.12 = (bf16[128,256]{1,0:T(8,128)(2,1)S(1)}, bf16[128,256]{1,0:T(8,128)(2,1)S(1)}, u32[]{:S(2)}, u32[]{:S(2)}) collective-permute-start(bf16[128,256]{1,0:T(8,128)(2,1)S(1)} %get-tuple-element.52), channel_id=1, source_target_pairs={{0,2},{2,0},{4,6},{6,4},{1,3},{3,1},{5,7},{7,5},{8,10},{10,8},{12,... | collective-permute-start | bytes 196616 | tf_op jit(solution)/shard_map/ppermute | solution.py:274
  27.9 1.5 %collective-permute-start.8 = (bf16[128,256]{1,0:T(8,128)(2,1)S(1)}, bf16[128,256]{1,0:T(8,128)(2,1)S(1)}, u32[]{:S(2)}, u32[]{:S(2)}) collective-permute-start(bf16[128,256]{1,0:T(8,128)(2,1)S(1)} %get-tuple-element.50), channel_id=1, source_target_pairs={{0,4},{2,6},{4,0},{6,2},{1,5},{3,7},{5,1},{7,3},{8,12},{10,14},{12... | collective-permute-start | bytes 196616 | tf_op jit(solution)/shard_map/ppermute | solution.py:274
  29.3 0.0 collective-permute-start.7
  29.3 1.7 %collective-permute-done.10.refs_2_ = bf16[128,256]{1,0:T(8,128)(2,1)S(1)} collective-permute-done((bf16[128,256]{1,0:T(8,128)(2,1)S(1)}, bf16[128,256]{1,0:T(8,128)(2,1)S(1)}, u32[]{:S(2)}, u32[]{:S(2)}) %collective-permute-start.10) | collective-permute-done | bytes 65568 | tf_op jit(solution)/shard_map/ppermute | solution.py:274
  31.0 0.0 collective-permute-start.11
  31.0 0.0 collective-permute-done.12.refs_3_
  31.0 0.5 %collective-permute-start.13 = (bf16[128,256]{1,0:T(8,128)(2,1)S(1)}, bf16[128,256]{1,0:T(8,128)(2,1)S(1)}, u32[]{:S(2)}, u32[]{:S(2)}) collective-permute-start(bf16[128,256]{1,0:T(8,128)(2,1)S(1)} %collective-permute-done.12.refs_3_), channel_id=1, source_target_pairs={{0,1},{1,0},{2,3},{3,2},{4,5},{5,4},{6,7},{7,6},{8,9},{9,8},{10,11... | collective-permute-start | bytes 196616 | tf_op jit(solution)/shard_map/ppermute | solution.py:274
  31.5 0.6 %collective-permute-done.8.refs_1_ = bf16[128,256]{1,0:T(8,128)(2,1)S(1)} collective-permute-done((bf16[128,256]{1,0:T(8,128)(2,1)S(1)}, bf16[128,256]{1,0:T(8,128)(2,1)S(1)}, u32[]{:S(2)}, u32[]{:S(2)}) %collective-permute-start.8) | collective-permute-done | bytes 65568 | tf_op jit(solution)/shard_map/ppermute | solution.py:274
  32.1 0.0 collective-permute-start.9
  32.1 0.3 project.2.refs_4_
  32.5 0.0 collective-permute-done.7.refs_0_
  32.5 0.0 collective-permute-done.11.refs_2_
  32.5 0.0 collective-permute-done.13.refs_3_
  32.5 0.9 %collective-permute-done.9.refs_1_ = bf16[128,256]{1,0:T(8,128)(2,1)S(1)} collective-permute-done((bf16[128,256]{1,0:T(8,128)(2,1)S(1)}, bf16[128,256]{1,0:T(8,128)(2,1)S(1)}, u32[]{:S(2)}, u32[]{:S(2)}) %collective-permute-start.9) | collective-permute-done | bytes 65568 | tf_op jit(solution)/shard_map/ppermute | solution.py:274
  33.4 1.0 %project.3 = bf16[512,256]{1,0:T(8,128)(2,1)} custom-call(bf16[2,512,512]{2,1,0:T(8,128)(2,1)S(1)} %turn.1.turned_ref, bf16[128,256]{1,0:T(8,128)(2,1)S(1)} %collective-permute-done.7.refs_0_, bf16[128,256]{1,0:T(8,128)(2,1)S(1)} %collective-permute-done.9.refs_1_, bf16[128,256]{1,0:T(8,128)(2,1)S(1)} %collective-permute-done.11.refs_2_, ...), custom_call_target="tpu_custom_call" | custom-call | tf_op jit(solution)/shard_map/project/pallas_call | solution.py:438
  (3 shorter events, 0.0 us)
Async XLA Ops:
  1.2 10.0 %collective-permute-start = (bf16[784,128]{1,0:T(8,128)(2,1)S(1)}, bf16[784,128]{1,0:T(8,128)(2,1)S(1)}, u32[]{:S(2)}, u32[]{:S(2)}) collective-permute-start(bf16[784,128]{1,0:T(8,128)(2,1)S(1)} %get-tuple-element.32), channel_id=1, source_target_pairs={{0,2},{2,0},{4,6},{6,4},{1,3},{3,1},{5,7},{7,5},{8,10},{10,8},{12,... | collective-permute-start | bytes 602120 | tf_op jit(solution)/shard_map/ppermute | solution.py:274
  4.2 7.0 %collective-permute-start.1 = (bf16[784,128]{1,0:T(8,128)(2,1)S(1)}, bf16[784,128]{1,0:T(8,128)(2,1)S(1)}, u32[]{:S(2)}, u32[]{:S(2)}) collective-permute-start(bf16[784,128]{1,0:T(8,128)(2,1)S(1)} %get-tuple-element.33), channel_id=1, source_target_pairs={{0,4},{2,6},{4,0},{6,2},{1,5},{3,7},{5,1},{7,3},{8,12},{10,14},{12... | collective-permute-start | bytes 602120 | tf_op jit(solution)/shard_map/ppermute | solution.py:274
  7.2 13.9 %collective-permute-start.6 = (bf16[1,512,128]{2,1,0:T(8,128)(2,1)S(1)}, bf16[1,512,128]{2,1,0:T(8,128)(2,1)S(1)}, u32[]{:S(2)}, u32[]{:S(2)}) collective-permute-start(bf16[1,512,128]{2,1,0:T(8,128)(2,1)S(1)} %get-tuple-element.44), channel_id=1, source_target_pairs={{0,14},{2,12},{4,10},{6,8},{8,22},{10,20},{12,18},{14,16},{16,30},... | collective-permute-start | bytes 393224 | tf_op jit(solution)/shard_map/ppermute | solution.py:353
  8.8 12.4 %collective-permute-start.5 = (bf16[1,512,128]{2,1,0:T(8,128)(2,1)S(1)}, bf16[1,512,128]{2,1,0:T(8,128)(2,1)S(1)}, u32[]{:S(2)}, u32[]{:S(2)}) collective-permute-start(bf16[1,512,128]{2,1,0:T(8,128)(2,1)S(1)} %get-tuple-element.43), channel_id=1, source_target_pairs={{0,10},{2,8},{4,14},{6,12},{8,18},{10,16},{12,22},{14,20},{16,26},... | collective-permute-start | bytes 393224 | tf_op jit(solution)/shard_map/ppermute | solution.py:353
  11.3 11.4 %collective-permute-start.4 = (bf16[784,128]{1,0:T(8,128)(2,1)S(1)}, bf16[784,128]{1,0:T(8,128)(2,1)S(1)}, u32[]{:S(2)}, u32[]{:S(2)}) collective-permute-start(bf16[784,128]{1,0:T(8,128)(2,1)S(1)} %get-tuple-element.42), channel_id=1, source_target_pairs={{0,6},{2,4},{4,2},{6,0},{1,7},{3,5},{5,3},{7,1},{8,14},{10,12},{12... | collective-permute-start | bytes 602120 | tf_op jit(solution)/shard_map/ppermute | solution.py:274
  12.8 11.1 %collective-permute-start.3 = (bf16[1,512,128]{2,1,0:T(8,128)(2,1)S(1)}, bf16[1,512,128]{2,1,0:T(8,128)(2,1)S(1)}, u32[]{:S(2)}, u32[]{:S(2)}) collective-permute-start(bf16[1,512,128]{2,1,0:T(8,128)(2,1)S(1)} %slice_bitcast_fusion), channel_id=1, source_target_pairs={{0,8},{8,16},{16,24},{24,0},{1,9},{9,17},{17,25},{25,1},{2,10},{10... | collective-permute-start | bytes 393224 | tf_op jit(solution)/shard_map/ppermute | solution.py:342
  18.2 6.8 %collective-permute-start.2 = (bf16[1,512,128]{2,1,0:T(8,128)(2,1)S(1)}, bf16[1,512,128]{2,1,0:T(8,128)(2,1)S(1)}, u32[]{:S(2)}, u32[]{:S(2)}) collective-permute-start(bf16[1,512,128]{2,1,0:T(8,128)(2,1)S(1)} %slice_bitcast_fusion.1), channel_id=1, source_target_pairs={{0,8},{8,16},{16,24},{24,0},{1,9},{9,17},{17,25},{25,1},{2,10},{10... | collective-permute-start | bytes 393224 | tf_op jit(solution)/shard_map/ppermute | solution.py:342
  25.8 5.2 %collective-permute-start.10 = (bf16[128,256]{1,0:T(8,128)(2,1)S(1)}, bf16[128,256]{1,0:T(8,128)(2,1)S(1)}, u32[]{:S(2)}, u32[]{:S(2)}) collective-permute-start(bf16[128,256]{1,0:T(8,128)(2,1)S(1)} %get-tuple-element.51), channel_id=1, source_target_pairs={{0,6},{2,4},{4,2},{6,0},{1,7},{3,5},{5,3},{7,1},{8,14},{10,12},{12... | collective-permute-start | bytes 196616 | tf_op jit(solution)/shard_map/ppermute | solution.py:274
  26.1 4.9 %collective-permute-start.12 = (bf16[128,256]{1,0:T(8,128)(2,1)S(1)}, bf16[128,256]{1,0:T(8,128)(2,1)S(1)}, u32[]{:S(2)}, u32[]{:S(2)}) collective-permute-start(bf16[128,256]{1,0:T(8,128)(2,1)S(1)} %get-tuple-element.52), channel_id=1, source_target_pairs={{0,2},{2,0},{4,6},{6,4},{1,3},{3,1},{5,7},{7,5},{8,10},{10,8},{12,... | collective-permute-start | bytes 196616 | tf_op jit(solution)/shard_map/ppermute | solution.py:274
  27.9 4.3 %collective-permute-start.8 = (bf16[128,256]{1,0:T(8,128)(2,1)S(1)}, bf16[128,256]{1,0:T(8,128)(2,1)S(1)}, u32[]{:S(2)}, u32[]{:S(2)}) collective-permute-start(bf16[128,256]{1,0:T(8,128)(2,1)S(1)} %get-tuple-element.50), channel_id=1, source_target_pairs={{0,4},{2,6},{4,0},{6,2},{1,5},{3,7},{5,1},{7,3},{8,12},{10,14},{12... | collective-permute-start | bytes 196616 | tf_op jit(solution)/shard_map/ppermute | solution.py:274
  29.3 3.1 %collective-permute-start.7 = (bf16[128,256]{1,0:T(8,128)(2,1)S(1)}, bf16[128,256]{1,0:T(8,128)(2,1)S(1)}, u32[]{:S(2)}, u32[]{:S(2)}) collective-permute-start(bf16[128,256]{1,0:T(8,128)(2,1)S(1)} %get-tuple-element.49.refs_0_), channel_id=1, source_target_pairs={{0,1},{1,0},{2,3},{3,2},{4,5},{5,4},{6,7},{7,6},{8,9},{9,8},{10,11... | collective-permute-start | bytes 196616 | tf_op jit(solution)/shard_map/ppermute | solution.py:274
  31.0 1.5 %collective-permute-start.11 = (bf16[128,256]{1,0:T(8,128)(2,1)S(1)}, bf16[128,256]{1,0:T(8,128)(2,1)S(1)}, u32[]{:S(2)}, u32[]{:S(2)}) collective-permute-start(bf16[128,256]{1,0:T(8,128)(2,1)S(1)} %collective-permute-done.10.refs_2_), channel_id=1, source_target_pairs={{0,1},{1,0},{2,3},{3,2},{4,5},{5,4},{6,7},{7,6},{8,9},{9,8},{10,11... | collective-permute-start | bytes 196616 | tf_op jit(solution)/shard_map/ppermute | solution.py:274
  31.0 1.5 %collective-permute-start.13 = (bf16[128,256]{1,0:T(8,128)(2,1)S(1)}, bf16[128,256]{1,0:T(8,128)(2,1)S(1)}, u32[]{:S(2)}, u32[]{:S(2)}) collective-permute-start(bf16[128,256]{1,0:T(8,128)(2,1)S(1)} %collective-permute-done.12.refs_3_), channel_id=1, source_target_pairs={{0,1},{1,0},{2,3},{3,2},{4,5},{5,4},{6,7},{7,6},{8,9},{9,8},{10,11... | collective-permute-start | bytes 196616 | tf_op jit(solution)/shard_map/ppermute | solution.py:274
  32.1 1.3 %collective-permute-start.9 = (bf16[128,256]{1,0:T(8,128)(2,1)S(1)}, bf16[128,256]{1,0:T(8,128)(2,1)S(1)}, u32[]{:S(2)}, u32[]{:S(2)}) collective-permute-start(bf16[128,256]{1,0:T(8,128)(2,1)S(1)} %collective-permute-done.8.refs_1_), channel_id=1, source_target_pairs={{0,1},{1,0},{2,3},{3,2},{4,5},{5,4},{6,7},{7,6},{8,9},{9,8},{10,11... | collective-permute-start | bytes 196616 | tf_op jit(solution)/shard_map/ppermute | solution.py:274

commit v18 on v16

--- a/solution.py
+++ b/solution.py
@@ -399,8 +399,8 @@
 
     for step in near:
         arrays["block", step] = swapped(packed[step], "place", step)
+    send_on([0])
     arrays["block", 0], turned = lax.optimization_barrier((packed[0], turned))
-    send_on([0])
     mix = {}
     far_blocks = packed[len(near) + 1 :]
     for step in apart:

time: 31.4 us -> 31.3 us (level)
    ppermute x10, waiting for transfers between devices: 3.28 us -> 4.32 us  [swapped(): lax.ppermute(value, axis, [(source, source ^ step) for source in range(co...]
    ppermute x3, waiting for transfers between devices: 2.11 us -> 1.25 us  [send_on(): arrays['halo', offset, tuple(steps)] = lax.ppermute(message, 'group', pairs)]
  transfers between devices with their start and end apart: 14 -> 14, of which waited for: 10 -> 9; matrix products, arithmetic and copies ran while one was open for 0% -> 0% of each run, Pallas kernels for 13% -> 13%
where the time goes in v18:
time: 31.3 us; the launch traced here: 31.1 us
  starting transfers between devices  16.1 us (51%)
  waiting for transfers between devices  7.78 us (25%)
  Pallas kernels  7.14 us (23%)
    ppermute x10, starting transfers between devices, swapped(): lax.ppermute(value, axis, [(source, source ^ step) for source in range(co...  10.3 us
    ppermute x10, waiting for transfers between devices, swapped(): lax.ppermute(value, axis, [(source, source ^ step) for source in range(co...  4.32 us
    ppermute x3, starting transfers between devices, send_on(): arrays['halo', offset, tuple(steps)] = lax.ppermute(message, 'group', pairs)  4.2 us
    pallas_call x3, Pallas kernels, stage(): pl.pallas_call(functools.partial(attend_kernel, names=names, work=work, s...  3.14 us
    ppermute x1, waiting for transfers between devices, send_across(): arrived = lax.ppermute(message, ('group', 'place'), pairs)  2.22 us
    ppermute x1, starting transfers between devices, send_across(): arrived = lax.ppermute(message, ('group', 'place'), pairs)  1.54 us
    pallas_call x1, Pallas kernels, on_device(): pl.pallas_call(functools.partial(turn_kernel, head_total=head_total), out...  1.44 us
    pallas_call x2, Pallas kernels, on_device(): pl.pallas_call(functools.partial(project_kernel, group=group, others=othe...  1.34 us
  transfers between devices with their start and end apart: 14, of which 9 were waited for; matrix products, arithmetic and copies ran while one was open for 0% of the time, Pallas kernels for 13%

profile of v18, /device:TPU:0, one launch (start us, length us, event | category | flops | bytes accessed | tf_op | source)
XLA Modules:
  0.0 31.1 jit_solution(15140828639625971344)
XLA Ops:
  0.0 1.2 %pack.1 = (bf16[784,128]{1,0:T(8,128)(2,1)S(1)}, bf16[784,128]{1,0:T(8,128)(2,1)S(1)}, bf16[784,128]{1,0:T(8,128)(2,1)S(1)}, bf16[784,128]{1,0:T(8,128)(2,1)S(1)}) custom-call(bf16[256,512]{1,0:T(8,128)(2,1)} %query_ref.1, bf16[256,512]{1,0:T(8,128)(2,1)} %key_ref.1, bf16[256,512]{1,0:T(8,128)(2,1)} %value_ref.1, s32[2,2,4]{2,1,0:T(2,128)} %bitcast.10, ...), custom_call_target="tpu_custom_call" | custom-call | tf_op jit(solution)/shard_map/pack/pallas_call | solution.py:287
  1.2 3.0 %collective-permute-start = (bf16[784,128]{1,0:T(8,128)(2,1)S(1)}, bf16[784,128]{1,0:T(8,128)(2,1)S(1)}, u32[]{:S(2)}, u32[]{:S(2)}) collective-permute-start(bf16[784,128]{1,0:T(8,128)(2,1)S(1)} %get-tuple-element.28), channel_id=1, source_target_pairs={{0,2},{2,0},{4,6},{6,4},{1,3},{3,1},{5,7},{7,5},{8,10},{10,8},{12,... | collective-permute-start | bytes 602120 | tf_op jit(solution)/shard_map/ppermute | solution.py:273
  4.2 1.5 %collective-permute-start.1 = (bf16[784,128]{1,0:T(8,128)(2,1)S(1)}, bf16[784,128]{1,0:T(8,128)(2,1)S(1)}, u32[]{:S(2)}, u32[]{:S(2)}) collective-permute-start(bf16[784,128]{1,0:T(8,128)(2,1)S(1)} %get-tuple-element.29), channel_id=1, source_target_pairs={{0,4},{2,6},{4,0},{6,2},{1,5},{3,7},{5,1},{7,3},{8,12},{10,14},{12... | collective-permute-start | bytes 602120 | tf_op jit(solution)/shard_map/ppermute | solution.py:273
  5.8 1.6 %collective-permute-start.4 = (bf16[1,512,128]{2,1,0:T(8,128)(2,1)S(1)}, bf16[1,512,128]{2,1,0:T(8,128)(2,1)S(1)}, u32[]{:S(2)}, u32[]{:S(2)}) collective-permute-start(bf16[1,512,128]{2,1,0:T(8,128)(2,1)S(1)} %slice_bitcast_fusion.1), channel_id=1, source_target_pairs={{0,8},{8,16},{16,24},{24,0},{1,9},{9,17},{17,25},{25,1},{2,10},{10... | collective-permute-start | bytes 393224 | tf_op jit(solution)/shard_map/ppermute | solution.py:341
  7.4 1.4 %turn.1.turned_ref = bf16[2,512,512]{2,1,0:T(8,128)(2,1)S(1)} custom-call(bf16[784,128]{1,0:T(8,128)(2,1)S(1)} %get-tuple-element.32.block_ref.refs_0_, bf16[1024,1024]{1,0:T(8,128)(2,1)} %weight_ref.1), custom_call_target="tpu_custom_call" | custom-call | flops 1000000000 | bytes 1 | tf_op jit(solution)/shard_map/turn/pallas_call | solution.py:313
  8.9 1.5 %collective-permute-start.5 = (bf16[1,512,128]{2,1,0:T(8,128)(2,1)S(1)}, bf16[1,512,128]{2,1,0:T(8,128)(2,1)S(1)}, u32[]{:S(2)}, u32[]{:S(2)}) collective-permute-start(bf16[1,512,128]{2,1,0:T(8,128)(2,1)S(1)} %slice_bitcast_fusion.3), channel_id=1, source_target_pairs={{0,14},{2,12},{4,10},{6,8},{8,22},{10,20},{12,18},{14,16},{16,30},... | collective-permute-start | bytes 393224 | tf_op jit(solution)/shard_map/ppermute | solution.py:352
  10.4 0.0 collective-permute-done.refs_1_
  10.4 0.3 collective-permute-done.1.refs_2_
  10.7 2.2 %collective-permute-start.3 = (bf16[784,128]{1,0:T(8,128)(2,1)S(1)}, bf16[784,128]{1,0:T(8,128)(2,1)S(1)}, u32[]{:S(2)}, u32[]{:S(2)}) collective-permute-start(bf16[784,128]{1,0:T(8,128)(2,1)S(1)} %get-tuple-element.35), channel_id=1, source_target_pairs={{0,6},{2,4},{4,2},{6,0},{1,7},{3,5},{5,3},{7,1},{8,14},{10,12},{12... | collective-permute-start | bytes 602120 | tf_op jit(solution)/shard_map/ppermute | solution.py:273
  12.9 1.6 %collective-permute-start.6 = (bf16[1,512,128]{2,1,0:T(8,128)(2,1)S(1)}, bf16[1,512,128]{2,1,0:T(8,128)(2,1)S(1)}, u32[]{:S(2)}, u32[]{:S(2)}) collective-permute-start(bf16[1,512,128]{2,1,0:T(8,128)(2,1)S(1)} %slice_bitcast_fusion), channel_id=1, source_target_pairs={{0,8},{8,16},{16,24},{24,0},{1,9},{9,17},{17,25},{25,1},{2,10},{10... | collective-permute-start | bytes 393224 | tf_op jit(solution)/shard_map/ppermute | solution.py:341
  14.5 0.9 %collective-permute-start.2 = (bf16[1,512,128]{2,1,0:T(8,128)(2,1)S(1)}, bf16[1,512,128]{2,1,0:T(8,128)(2,1)S(1)}, u32[]{:S(2)}, u32[]{:S(2)}) collective-permute-start(bf16[1,512,128]{2,1,0:T(8,128)(2,1)S(1)} %slice_bitcast_fusion.2), channel_id=1, source_target_pairs={{0,8},{8,16},{16,24},{24,0},{1,9},{9,17},{17,25},{25,1},{2,10},{10... | collective-permute-start | bytes 393224 | tf_op jit(solution)/shard_map/ppermute | solution.py:341
  15.4 0.0 collective-permute-done.4.refs_3_
  15.5 1.2 %attend.3 = (f32[4,128,256]{2,1,0:T(8,128)S(1)}, f32[4,8,256]{2,1,0:T(8,128)S(1)}) custom-call(bf16[784,128]{1,0:T(8,128)(2,1)S(1)} %get-tuple-element.32.block_ref.refs_0_, bf16[784,128]{1,0:T(8,128)(2,1)S(1)} %collective-permute-done.refs_1_, bf16[784,128]{1,0:T(8,128)(2,1)S(1)} %collective-permute-done.1.refs_2_, ...), custom_call_target="tpu_custom_call" | custom-call | flops 1000000000 | bytes 1 | tf_op jit(solution)/shard_map/attend/pallas_call | solution.py:379
  16.7 2.2 %collective-permute-done.5.refs_4_ = bf16[1,512,128]{2,1,0:T(8,128)(2,1)S(1)} collective-permute-done((bf16[1,512,128]{2,1,0:T(8,128)(2,1)S(1)}, bf16[1,512,128]{2,1,0:T(8,128)(2,1)S(1)}, u32[]{:S(2)}, u32[]{:S(2)}) %collective-permute-start.5) | collective-permute-done | bytes 131104 | tf_op jit(solution)/shard_map/ppermute | solution.py:352
  18.9 1.1 %collective-permute-done.6.refs_5_ = bf16[1,512,128]{2,1,0:T(8,128)(2,1)S(1)} collective-permute-done((bf16[1,512,128]{2,1,0:T(8,128)(2,1)S(1)}, bf16[1,512,128]{2,1,0:T(8,128)(2,1)S(1)}, u32[]{:S(2)}, u32[]{:S(2)}) %collective-permute-start.6) | collective-permute-done | bytes 131104 | tf_op jit(solution)/shard_map/ppermute | solution.py:341
  20.0 0.0 collective-permute-done.3.refs_6_.refs_3_
  20.0 1.2 %attend.4 = (bf16[128,256]{1,0:T(8,128)(2,1)S(1)}, f32[4,128,256]{2,1,0:T(8,128)S(1)}, f32[4,8,256]{2,1,0:T(8,128)S(1)}) custom-call(bf16[784,128]{1,0:T(8,128)(2,1)S(1)} %get-tuple-element.32.block_ref.refs_0_, bf16[784,128]{1,0:T(8,128)(2,1)S(1)} %collective-permute-done.refs_1_, bf16[784,128]{1,0:T(8,128)(2,1)S(1)} %collective-permute-done.1.refs_2_, ...), custom_call_target="tpu_custom_call" | custom-call | flops 1000000000 | bytes 1 | tf_op jit(solution)/shard_map/attend/pallas_call | solution.py:379
  21.2 0.2 collective-permute-done.2.refs_2_
  21.4 0.7 %attend.5 = (bf16[128,256]{1,0:T(8,128)(2,1)S(1)}, bf16[128,256]{1,0:T(8,128)(2,1)S(1)}, bf16[128,256]{1,0:T(8,128)(2,1)S(1)}) custom-call(bf16[784,128]{1,0:T(8,128)(2,1)S(1)} %get-tuple-element.32.block_ref.refs_0_, bf16[784,128]{1,0:T(8,128)(2,1)S(1)} %collective-permute-done.refs_1_, bf16[1,512,128]{2,1,0:T(8,128)(2,1)S(1)} %collective-permute-done.2.refs_2_, ...), custom_call_target="tpu_custom_call" | custom-call | flops 1000000000 | bytes 1 | tf_op jit(solution)/shard_map/attend/pallas_call | solution.py:379
  22.1 2.0 %collective-permute-start.10 = (bf16[128,256]{1,0:T(8,128)(2,1)S(1)}, bf16[128,256]{1,0:T(8,128)(2,1)S(1)}, u32[]{:S(2)}, u32[]{:S(2)}) collective-permute-start(bf16[128,256]{1,0:T(8,128)(2,1)S(1)} %get-tuple-element.43), channel_id=1, source_target_pairs={{0,6},{2,4},{4,2},{6,0},{1,7},{3,5},{5,3},{7,1},{8,14},{10,12},{12... | collective-permute-start | bytes 196616 | tf_op jit(solution)/shard_map/ppermute | solution.py:273
  24.1 0.5 %collective-permute-start.12 = (bf16[128,256]{1,0:T(8,128)(2,1)S(1)}, bf16[128,256]{1,0:T(8,128)(2,1)S(1)}, u32[]{:S(2)}, u32[]{:S(2)}) collective-permute-start(bf16[128,256]{1,0:T(8,128)(2,1)S(1)} %get-tuple-element.44), channel_id=1, source_target_pairs={{0,2},{2,0},{4,6},{6,4},{1,3},{3,1},{5,7},{7,5},{8,10},{10,8},{12,... | collective-permute-start | bytes 196616 | tf_op jit(solution)/shard_map/ppermute | solution.py:273
  24.6 1.1 %collective-permute-start.8 = (bf16[128,256]{1,0:T(8,128)(2,1)S(1)}, bf16[128,256]{1,0:T(8,128)(2,1)S(1)}, u32[]{:S(2)}, u32[]{:S(2)}) collective-permute-start(bf16[128,256]{1,0:T(8,128)(2,1)S(1)} %get-tuple-element.42), channel_id=1, source_target_pairs={{0,4},{2,6},{4,0},{6,2},{1,5},{3,7},{5,1},{7,3},{8,12},{10,14},{12... | collective-permute-start | bytes 196616 | tf_op jit(solution)/shard_map/ppermute | solution.py:273
  25.6 0.0 collective-permute-start.7
  25.6 1.9 %collective-permute-done.10.refs_2_ = bf16[128,256]{1,0:T(8,128)(2,1)S(1)} collective-permute-done((bf16[128,256]{1,0:T(8,128)(2,1)S(1)}, bf16[128,256]{1,0:T(8,128)(2,1)S(1)}, u32[]{:S(2)}, u32[]{:S(2)}) %collective-permute-start.10) | collective-permute-done | bytes 65568 | tf_op jit(solution)/shard_map/ppermute | solution.py:273
  27.6 0.0 collective-permute-start.11
  27.6 0.8 %collective-permute-done.12.refs_3_ = bf16[128,256]{1,0:T(8,128)(2,1)S(1)} collective-permute-done((bf16[128,256]{1,0:T(8,128)(2,1)S(1)}, bf16[128,256]{1,0:T(8,128)(2,1)S(1)}, u32[]{:S(2)}, u32[]{:S(2)}) %collective-permute-start.12) | collective-permute-done | bytes 65568 | tf_op jit(solution)/shard_map/ppermute | solution.py:273
  28.4 0.0 collective-permute-start.13
  28.4 0.5 %collective-permute-done.8.refs_1_ = bf16[128,256]{1,0:T(8,128)(2,1)S(1)} collective-permute-done((bf16[128,256]{1,0:T(8,128)(2,1)S(1)}, bf16[128,256]{1,0:T(8,128)(2,1)S(1)}, u32[]{:S(2)}, u32[]{:S(2)}) %collective-permute-start.8) | collective-permute-done | bytes 65568 | tf_op jit(solution)/shard_map/ppermute | solution.py:273
  28.8 0.0 collective-permute-start.9
  28.9 0.3 %project.2.refs_4_ = f32[512,256]{1,0:T(8,128)S(1)} custom-call(bf16[2,512,512]{2,1,0:T(8,128)(2,1)S(1)} %turn.1.turned_ref, bf16[128,256]{1,0:T(8,128)(2,1)S(1)} %get-tuple-element.41.refs_0_, bf16[128,256]{1,0:T(8,128)(2,1)S(1)} %collective-permute-done.8.refs_1_, bf16[128,256]{1,0:T(8,128)(2,1)S(1)} %collective-permute-done.10.refs_2_, ...), custom_call_target="tpu_custom_call" | custom-call | tf_op jit(solution)/shard_map/project/pallas_call | solution.py:433
  29.2 0.0 collective-permute-done.7.refs_0_
  29.2 0.0 collective-permute-done.11.refs_2_
  29.2 0.4 %collective-permute-done.13.refs_3_ = bf16[128,256]{1,0:T(8,128)(2,1)S(1)} collective-permute-done((bf16[128,256]{1,0:T(8,128)(2,1)S(1)}, bf16[128,256]{1,0:T(8,128)(2,1)S(1)}, u32[]{:S(2)}, u32[]{:S(2)}) %collective-permute-start.13) | collective-permute-done | bytes 65568 | tf_op jit(solution)/shard_map/ppermute | solution.py:273
  29.6 0.5 %collective-permute-done.9.refs_1_ = bf16[128,256]{1,0:T(8,128)(2,1)S(1)} collective-permute-done((bf16[128,256]{1,0:T(8,128)(2,1)S(1)}, bf16[128,256]{1,0:T(8,128)(2,1)S(1)}, u32[]{:S(2)}, u32[]{:S(2)}) %collective-permute-start.9) | collective-permute-done | bytes 65568 | tf_op jit(solution)/shard_map/ppermute | solution.py:273
  30.1 1.0 %project.3 = bf16[512,256]{1,0:T(8,128)(2,1)} custom-call(bf16[2,512,512]{2,1,0:T(8,128)(2,1)S(1)} %turn.1.turned_ref, bf16[128,256]{1,0:T(8,128)(2,1)S(1)} %collective-permute-done.7.refs_0_, bf16[128,256]{1,0:T(8,128)(2,1)S(1)} %collective-permute-done.9.refs_1_, bf16[128,256]{1,0:T(8,128)(2,1)S(1)} %collective-permute-done.11.refs_2_, ...), custom_call_target="tpu_custom_call" | custom-call | tf_op jit(solution)/shard_map/project/pallas_call | solution.py:433
  (4 shorter events, 0.0 us)
Async XLA Ops:
  1.2 9.2 %collective-permute-start = (bf16[784,128]{1,0:T(8,128)(2,1)S(1)}, bf16[784,128]{1,0:T(8,128)(2,1)S(1)}, u32[]{:S(2)}, u32[]{:S(2)}) collective-permute-start(bf16[784,128]{1,0:T(8,128)(2,1)S(1)} %get-tuple-element.28), channel_id=1, source_target_pairs={{0,2},{2,0},{4,6},{6,4},{1,3},{3,1},{5,7},{7,5},{8,10},{10,8},{12,... | collective-permute-start | bytes 602120 | tf_op jit(solution)/shard_map/ppermute | solution.py:273
  4.2 6.4 %collective-permute-start.1 = (bf16[784,128]{1,0:T(8,128)(2,1)S(1)}, bf16[784,128]{1,0:T(8,128)(2,1)S(1)}, u32[]{:S(2)}, u32[]{:S(2)}) collective-permute-start(bf16[784,128]{1,0:T(8,128)(2,1)S(1)} %get-tuple-element.29), channel_id=1, source_target_pairs={{0,4},{2,6},{4,0},{6,2},{1,5},{3,7},{5,1},{7,3},{8,12},{10,14},{12... | collective-permute-start | bytes 602120 | tf_op jit(solution)/shard_map/ppermute | solution.py:273
  5.8 9.7 %collective-permute-start.4 = (bf16[1,512,128]{2,1,0:T(8,128)(2,1)S(1)}, bf16[1,512,128]{2,1,0:T(8,128)(2,1)S(1)}, u32[]{:S(2)}, u32[]{:S(2)}) collective-permute-start(bf16[1,512,128]{2,1,0:T(8,128)(2,1)S(1)} %slice_bitcast_fusion.1), channel_id=1, source_target_pairs={{0,8},{8,16},{16,24},{24,0},{1,9},{9,17},{17,25},{25,1},{2,10},{10... | collective-permute-start | bytes 393224 | tf_op jit(solution)/shard_map/ppermute | solution.py:341
  8.9 10.0 %collective-permute-start.5 = (bf16[1,512,128]{2,1,0:T(8,128)(2,1)S(1)}, bf16[1,512,128]{2,1,0:T(8,128)(2,1)S(1)}, u32[]{:S(2)}, u32[]{:S(2)}) collective-permute-start(bf16[1,512,128]{2,1,0:T(8,128)(2,1)S(1)} %slice_bitcast_fusion.3), channel_id=1, source_target_pairs={{0,14},{2,12},{4,10},{6,8},{8,22},{10,20},{12,18},{14,16},{16,30},... | collective-permute-start | bytes 393224 | tf_op jit(solution)/shard_map/ppermute | solution.py:352
  10.7 9.3 %collective-permute-start.3 = (bf16[784,128]{1,0:T(8,128)(2,1)S(1)}, bf16[784,128]{1,0:T(8,128)(2,1)S(1)}, u32[]{:S(2)}, u32[]{:S(2)}) collective-permute-start(bf16[784,128]{1,0:T(8,128)(2,1)S(1)} %get-tuple-element.35), channel_id=1, source_target_pairs={{0,6},{2,4},{4,2},{6,0},{1,7},{3,5},{5,3},{7,1},{8,14},{10,12},{12... | collective-permute-start | bytes 602120 | tf_op jit(solution)/shard_map/ppermute | solution.py:273
  12.9 7.1 %collective-permute-start.6 = (bf16[1,512,128]{2,1,0:T(8,128)(2,1)S(1)}, bf16[1,512,128]{2,1,0:T(8,128)(2,1)S(1)}, u32[]{:S(2)}, u32[]{:S(2)}) collective-permute-start(bf16[1,512,128]{2,1,0:T(8,128)(2,1)S(1)} %slice_bitcast_fusion), channel_id=1, source_target_pairs={{0,8},{8,16},{16,24},{24,0},{1,9},{9,17},{17,25},{25,1},{2,10},{10... | collective-permute-start | bytes 393224 | tf_op jit(solution)/shard_map/ppermute | solution.py:341
  14.5 6.9 %collective-permute-start.2 = (bf16[1,512,128]{2,1,0:T(8,128)(2,1)S(1)}, bf16[1,512,128]{2,1,0:T(8,128)(2,1)S(1)}, u32[]{:S(2)}, u32[]{:S(2)}) collective-permute-start(bf16[1,512,128]{2,1,0:T(8,128)(2,1)S(1)} %slice_bitcast_fusion.2), channel_id=1, source_target_pairs={{0,8},{8,16},{16,24},{24,0},{1,9},{9,17},{17,25},{25,1},{2,10},{10... | collective-permute-start | bytes 393224 | tf_op jit(solution)/shard_map/ppermute | solution.py:341
  22.1 5.5 %collective-permute-start.10 = (bf16[128,256]{1,0:T(8,128)(2,1)S(1)}, bf16[128,256]{1,0:T(8,128)(2,1)S(1)}, u32[]{:S(2)}, u32[]{:S(2)}) collective-permute-start(bf16[128,256]{1,0:T(8,128)(2,1)S(1)} %get-tuple-element.43), channel_id=1, source_target_pairs={{0,6},{2,4},{4,2},{6,0},{1,7},{3,5},{5,3},{7,1},{8,14},{10,12},{12... | collective-permute-start | bytes 196616 | tf_op jit(solution)/shard_map/ppermute | solution.py:273
  24.1 4.3 %collective-permute-start.12 = (bf16[128,256]{1,0:T(8,128)(2,1)S(1)}, bf16[128,256]{1,0:T(8,128)(2,1)S(1)}, u32[]{:S(2)}, u32[]{:S(2)}) collective-permute-start(bf16[128,256]{1,0:T(8,128)(2,1)S(1)} %get-tuple-element.44), channel_id=1, source_target_pairs={{0,2},{2,0},{4,6},{6,4},{1,3},{3,1},{5,7},{7,5},{8,10},{10,8},{12,... | collective-permute-start | bytes 196616 | tf_op jit(solution)/shard_map/ppermute | solution.py:273
  24.6 4.3 %collective-permute-start.8 = (bf16[128,256]{1,0:T(8,128)(2,1)S(1)}, bf16[128,256]{1,0:T(8,128)(2,1)S(1)}, u32[]{:S(2)}, u32[]{:S(2)}) collective-permute-start(bf16[128,256]{1,0:T(8,128)(2,1)S(1)} %get-tuple-element.42), channel_id=1, source_target_pairs={{0,4},{2,6},{4,0},{6,2},{1,5},{3,7},{5,1},{7,3},{8,12},{10,14},{12... | collective-permute-start | bytes 196616 | tf_op jit(solution)/shard_map/ppermute | solution.py:273
  25.6 3.6 %collective-permute-start.7 = (bf16[128,256]{1,0:T(8,128)(2,1)S(1)}, bf16[128,256]{1,0:T(8,128)(2,1)S(1)}, u32[]{:S(2)}, u32[]{:S(2)}) collective-permute-start(bf16[128,256]{1,0:T(8,128)(2,1)S(1)} %get-tuple-element.41.refs_0_), channel_id=1, source_target_pairs={{0,1},{1,0},{2,3},{3,2},{4,5},{5,4},{6,7},{7,6},{8,9},{9,8},{10,11... | collective-permute-start | bytes 196616 | tf_op jit(solution)/shard_map/ppermute | solution.py:273
  27.6 1.6 %collective-permute-start.11 = (bf16[128,256]{1,0:T(8,128)(2,1)S(1)}, bf16[128,256]{1,0:T(8,128)(2,1)S(1)}, u32[]{:S(2)}, u32[]{:S(2)}) collective-permute-start(bf16[128,256]{1,0:T(8,128)(2,1)S(1)} %collective-permute-done.10.refs_2_), channel_id=1, source_target_pairs={{0,1},{1,0},{2,3},{3,2},{4,5},{5,4},{6,7},{7,6},{8,9},{9,8},{10,11... | collective-permute-start | bytes 196616 | tf_op jit(solution)/shard_map/ppermute | solution.py:273
  28.4 1.3 %collective-permute-start.13 = (bf16[128,256]{1,0:T(8,128)(2,1)S(1)}, bf16[128,256]{1,0:T(8,128)(2,1)S(1)}, u32[]{:S(2)}, u32[]{:S(2)}) collective-permute-start(bf16[128,256]{1,0:T(8,128)(2,1)S(1)} %collective-permute-done.12.refs_3_), channel_id=1, source_target_pairs={{0,1},{1,0},{2,3},{3,2},{4,5},{5,4},{6,7},{7,6},{8,9},{9,8},{10,11... | collective-permute-start | bytes 196616 | tf_op jit(solution)/shard_map/ppermute | solution.py:273
  28.8 1.3 %collective-permute-start.9 = (bf16[128,256]{1,0:T(8,128)(2,1)S(1)}, bf16[128,256]{1,0:T(8,128)(2,1)S(1)}, u32[]{:S(2)}, u32[]{:S(2)}) collective-permute-start(bf16[128,256]{1,0:T(8,128)(2,1)S(1)} %collective-permute-done.8.refs_1_), channel_id=1, source_target_pairs={{0,1},{1,0},{2,3},{3,2},{4,5},{5,4},{6,7},{7,6},{8,9},{9,8},{10,11... | collective-permute-start | bytes 196616 | tf_op jit(solution)/shard_map/ppermute | solution.py:273
